TPU v7x, 32 devices: a whole 2x2x4 slice. The times are simulated.
32 devices in a mesh: dp: 4 (over x, core), seq: 8 (over z, y).
Axes of the slice: x: 2, y: 2, z: 4, core: 2. Of those that a mesh axis runs over, the one named last changes fastest.
Arguments:
- bases: int32 [4, 32768], P('dp', 'seq'), may hold values from 0 to 3
- stem_table: bfloat16 [15, 4, 768], replicated, may hold values from -1.5 to 1.5
- conv_weight: bfloat16 [768, 3840], P('seq'), may hold values from -0.09375 to 0.09375
- query_weight: bfloat16 [768, 128], replicated, may hold values from -0.21875 to 0.21875
- key_weight: bfloat16 [768, 128], replicated, may hold values from -0.21875 to 0.21875
- pair_grad: float32 [4, 16, 16], P('dp', 'seq'), may hold values from -6 to 6
Outputs:
- conv_grad: float32 [768, 3840], P('seq')
- query_grad: float32 [768, 128], P('seq')
- key_grad: float32 [768, 128], P('seq')
Inputs may be any that keep to these rules, and one draw needn't show every extreme that they name: `bases`: 0, 1, 2, 3 stand for A, C, G, T.
All inputs are finite; a program needn't handle non-finite values.
Results may differ from a plain program's by a relative error of at most 0.0084.
Values may be sent and summed in bfloat16 or wider, within the bound.
No kernel may reach another device: no remote copies, remote signals or barrier semaphores. Data moves between devices by JAX's collectives and lax.ppermute only.
A program may use at most 128 MiB of HBM per device.

v0:
```python
import jax
import jax.numpy as jnp
from jax import lax
from jax.sharding import PartitionSpec as P

C0 = 768
C1 = 768
PC = 128
K0 = 15
K1 = 5
POOL = 8
BASE_DEV = 4096
BIN_ROWS = 256
POS_DEV = 2


root_coeff = 0.7978845608028654


def padded_2(x, sides, width):
    for axis, dim in sides:
        size, length = (lax.axis_size(axis), x.shape[dim])
        up = [(i, (i + 1) % size) for i in range(size - 1)]
        down = [(j, i) for i, j in up]
        last = lax.slice_in_dim(x, length - width, length, axis=dim)
        leading = lax.slice_in_dim(x, 0, width, axis=dim)
        before = lax.ppermute(last, axis, up)
        after = lax.ppermute(leading, axis, down)
        x = jnp.concatenate([before, x, after], axis=dim)
    return x


def gelu_slope(value):
    tangent = jnp.tanh(root_coeff * (value + 0.044715 * value * value * value))
    return 0.5 * (1.0 + tangent) + 0.5 * value * (1.0 - tangent * tangent) * root_coeff * (
        1.0 + 3.0 * 0.044715 * value * value
    )


def forward_taps(padded, weights, rows):
    total = jnp.zeros((rows, weights.shape[0]), jnp.float32)
    for tap in range(K1):
        total = total + lax.dot_general(
            padded[tap : tap + rows],
            weights[:, tap * C0 : (tap + 1) * C0],
            (((1,), (1,)), ((), ())),
            preferred_element_type=jnp.float32,
        )
    return total


def body(bases, stem_table, conv_weight, query_weight, key_weight, pair_grad):
    high = lax.Precision.HIGHEST
    scale = PC ** (-0.5)
    rows = BASE_DEV // POOL
    extended = padded_2(bases + 1, (("seq", 1),), K0 // 2)
    taps = jnp.stack([extended[0, t : t + BASE_DEV] for t in range(K0)], axis=1)
    onehot = (
        (taps[:, :, None] == jnp.arange(1, 5, dtype=jnp.int32))
        .astype(jnp.bfloat16)
        .reshape(BASE_DEV, K0 * 4)
    )
    stem = jnp.dot(onehot, stem_table.reshape(K0 * 4, C0), preferred_element_type=jnp.float32)
    pooled = jax.nn.gelu(stem).reshape(rows, POOL, C0).max(axis=1).astype(jnp.bfloat16)
    padded = padded_2(pooled, (("seq", 0),), K1 // 2)
    grad_block = pair_grad[0]
    conv = forward_taps(padded, lax.all_gather(conv_weight, "seq", axis=0, tiled=True), rows)
    embed_own = jax.nn.gelu(conv).reshape(POS_DEV, BIN_ROWS, C1).mean(axis=1).astype(jnp.bfloat16)
    embed_all = lax.all_gather(embed_own, "seq", axis=0, tiled=True)
    query_own = jnp.dot(embed_own, query_weight, preferred_element_type=jnp.float32)
    keys_all = jnp.dot(embed_all, key_weight, preferred_element_type=jnp.float32)
    dquery = jnp.dot(grad_block, keys_all, precision=high) * scale
    dkeys_part = jnp.dot(grad_block.T, query_own, precision=high) * scale
    dkeys = lax.psum_scatter(dkeys_part, "seq", scatter_dimension=0, tiled=True)
    dembed = jnp.dot(dquery, query_weight.astype(jnp.float32).T, precision=high) + jnp.dot(
        dkeys, key_weight.astype(jnp.float32).T, precision=high
    )
    embed_f = embed_own.astype(jnp.float32)
    query_grad, key_grad = (
        lax.psum_scatter(
            jnp.dot(embed_f.T, dquery, precision=high), "seq", scatter_dimension=0, tiled=True
        ),
        lax.psum_scatter(
            jnp.dot(embed_f.T, dkeys, precision=high), "seq", scatter_dimension=0, tiled=True
        ),
    )
    dconv = (
        (gelu_slope(conv).reshape(POS_DEV, BIN_ROWS, C1) * dembed[:, None, :] / BIN_ROWS)
        .reshape(rows, C1)
        .astype(jnp.bfloat16)
    )
    blocks = [
        lax.dot_general(
            dconv,
            padded[t : t + rows],
            (((0,), (0,)), ((), ())),
            preferred_element_type=jnp.float32,
        )
        for t in range(K1)
    ]
    conv_part = lax.psum_scatter(
        jnp.concatenate(blocks, axis=1), "seq", scatter_dimension=0, tiled=True
    )
    conv_grad, query_total, key_total = lax.psum((conv_part, query_grad, key_grad), "dp")
    return (conv_grad, query_total, key_total)


def solution(mesh):
    return jax.shard_map(
        body,
        mesh=mesh,
        in_specs=(P("dp", "seq"), P(), P("seq", None), P(), P(), P("dp", "seq", None)),
        out_specs=(P("seq", None), P("seq", None), P("seq", None)),
        check_vma=False,
    )
```

profile of v0, /device:TPU:0, one launch (start us, length us, event | category | flops | bytes accessed | tf_op | source)
XLA Modules:
  0.0 606.5 jit_solution(17297356835633447112)
XLA Ops:
  7.2 0.0 copy-start
  7.2 0.0 all-gather.3.cloned.1.call-start
  7.2 0.7 all-gather.3.cloned.1.call-update
  7.9 0.0 reduce-scatter.10.cloned.1.call-start
  8.0 0.7 fusion.80
  8.7 0.1 fusion.86
  8.8 4.9 collective-permute-start
  13.7 1.3 collective-permute-start.1
  15.0 1.2 dynamic-slice
  16.9 0.0 collective-permute-done
  16.9 2.2 collective-permute-done.1
  19.1 0.1 fusion.68
  19.2 0.3 fusion.55
  19.5 0.3 fusion.56
  19.8 0.4 stack.3
  20.2 0.0 copy-done.4
  20.2 7.5 %fusion.8 = bf16[512,768]{1,0:T(8,128)(2,1)S(1)} fusion(s32[4096,15]{0,1:T(8,128)S(1)} %stack.3, s32[4]{0:T(128)S(1)} %iota_add_fusion, bf16[15,4,768]{2,1,0:T(4,128)(2,1)S(1)} %copy-done.4), kind=kOutput, calls=%fused_computation.9 | convolution fusion | flops 405651456 | bytes 1124368 | tf_op jit(solution)/shard_map/dot_general | solution.py:63
  27.7 4.3 collective-permute-start.2
  32.0 1.3 collective-permute-start.3
  33.3 73.9 %all-gather.3.cloned.1.call-done = bf16[768,3840]{1,0:T(8,128)(2,1)} async-done(((bf16[96,3840]{1,0:T(8,128)(2,1)}), bf16[768,3840]{1,0:T(8,128)(2,1)}) %all-gather.3.cloned.1.call-update) | async-done | bytes 5898256 | tf_op jit(solution)/shard_map/all_gather | solution.py:67
  107.2 2.2 fusion.30
  109.5 0.0 collective-permute-done.2
  109.5 2.1 fusion.32
  111.6 0.8 fusion.34
  112.4 0.0 collective-permute-done.3
  112.4 0.8 fusion.28
  113.2 0.0 copy-start.1
  113.3 0.0 copy-start.3
  113.3 1.3 bitcast_reduce_fusion
  114.6 30.3 %all-gather = bf16[8,2,768]{2,1,0:T(2,128)(2,1)S(1)} all-gather(bf16[1,2,768]{2,1,0:T(2,128)(2,1)S(1)} %fusion.110), channel_id=1, replica_groups=mesh['dp'=4,'seq'=8] {'seq'}, dimensions={0}, use_global_device_ids=true | all-gather | bytes 27648 | tf_op jit(solution)/shard_map/all_gather | solution.py:69
  144.9 0.1 fusion.89
  145.1 0.2 fusion.87
  145.2 0.1 convolution_multiply_fusion.1
  145.4 0.3 fusion.88
  145.6 0.2 fusion.36
  145.9 18.9 %all-reduce = f32[16,128]{1,0:T(8,128)S(1)} all-reduce(f32[16,128]{1,0:T(8,128)S(1)} %fusion.36), channel_id=2, replica_groups=mesh['dp'=4,'seq'=8] {'seq'}, use_global_device_ids=true, to_apply=%region_2.0.clone | all-reduce | flops 2048 | bytes 16384
  164.8 0.3 convolution_add_fusion
  165.0 1.1 fusion.16
  166.1 2.3 convolution_dynamic-update-slice_fusion.4
  168.4 2.3 convolution_dynamic-update-slice_fusion.3
  170.7 2.2 convolution_dynamic-update-slice_fusion.2
  172.9 2.2 convolution_dynamic-update-slice_fusion.1
  175.1 2.3 convolution_dynamic-update-slice_fusion
  177.4 12.4 %copy.13 = f32[768,3840]{1,0:T(8,128)} copy(f32[768,3840]{0,1:T(8,128)} %convolution_dynamic-update-slice_fusion) | data formatting | bytes 23592960
  189.8 0.0 reduce-scatter.10.cloned.1.call-update
  189.8 0.0 reduce-scatter.6.cloned.1.call-start
  189.9 1.1 fusion.90
  191.0 0.0 reduce-scatter.6.cloned.1.call-update
  191.0 0.0 reduce-scatter.8.cloned.1.call-start
  191.1 1.2 fusion.71
  192.2 0.0 reduce-scatter.8.cloned.1.call-update
  192.2 0.0 all-reduce.5.cloned.1.call-start
  192.3 191.4 %reduce-scatter.10.cloned.1.call-done = f32[96,3840]{1,0:T(8,128)} async-done(((f32[768,3840]{1,0:T(8,128)}), f32[96,3840]{1,0:T(8,128)}) %reduce-scatter.10.cloned.1.call-update) | async-done | bytes 1474576
  383.7 2.8 copy.14
  386.5 0.0 all-reduce.5.cloned.1.call-update
  386.5 0.0 all-reduce.7.cloned.1.call-start
  386.5 61.8 %reduce-scatter.6.cloned.1.call-done = f32[96,128]{1,0:T(8,128)} async-done(((f32[768,128]{1,0:T(8,128)}), f32[96,128]{1,0:T(8,128)}) %reduce-scatter.6.cloned.1.call-update) | async-done | bytes 49168 | tf_op jit(solution)/shard_map/reduce_scatter | solution.py:80
  448.4 63.9 %reduce-scatter.8.cloned.1.call-done = f32[96,128]{1,0:T(8,128)} async-done(((f32[768,128]{1,0:T(8,128)}), f32[96,128]{1,0:T(8,128)}) %reduce-scatter.8.cloned.1.call-update) | async-done | bytes 49168 | tf_op jit(solution)/shard_map/reduce_scatter | solution.py:83
  512.3 0.0 all-reduce.7.cloned.1.call-update
  512.3 50.7 %all-reduce.5.cloned.1.call-done = f32[96,3840]{0,1:T(8,128)} async-done(((f32[96,3840]{0,1:T(8,128)}), f32[96,3840]{0,1:T(8,128)}) %all-reduce.5.cloned.1.call-update) | async-done | bytes 1474576 | tf_op jit(solution)/shard_map/psum | solution.py:104
  563.0 2.7 copy.12
  565.7 31.1 %all-reduce.7.cloned.1.call-done = (f32[96,128]{1,0:T(8,128)}, f32[96,128]{1,0:T(8,128)}) async-done(((f32[96,128]{1,0:T(8,128)}, f32[96,128]{1,0:T(8,128)}), (f32[96,128]{1,0:T(8,128)}, f32[96,128]{1,0:T(8,128)})) %all-reduce.7.cloned.1.call-update) | async-done | bytes 98320 | tf_op jit(solution)/shard_map/psum | solution.py:104
  596.8 1.4 copy.24
  598.2 1.4 copy.25
  (10 shorter events, 0.0 us)
Async XLA Ops:
  7.2 137.9 %copy-start = (bf16[768,128]{1,0:T(8,128)(2,1)S(1)}, bf16[768,128]{1,0:T(8,128)(2,1)}, u32[]{:S(2)}) copy-start(bf16[768,128]{1,0:T(8,128)(2,1)} %param.10) | copy-start | bytes 589828
  7.2 13.0 %copy-start.4 = (bf16[15,4,768]{2,1,0:T(4,128)(2,1)S(1)}, bf16[15,4,768]{2,1,0:T(4,128)(2,1)}, u32[]{:S(2)}) copy-start(bf16[15,4,768]{2,1,0:T(4,128)(2,1)} %param.7) | copy-start | bytes 276484
  7.2 100.0 %all-gather.3.cloned.1.call-start = ((), (), s32[]{:S(2)}) async-start(), calls=%async_computation.3 | async-start | bytes 6635520 | tf_op jit(solution)/shard_map/all_gather | solution.py:67
  7.9 375.7 %reduce-scatter.10.cloned.1.call-start = ((), (), s32[]{:S(2)}) async-start(), calls=%async_computation.7 | async-start | bytes 13271040
  8.8 8.1 %collective-permute-start = (s32[1,7]{1,0:T(1,128)S(1)}, s32[1,7]{1,0:T(1,128)S(1)}, u32[]{:S(2)}, u32[]{:S(2)}) collective-permute-start(s32[1,7]{1,0:T(1,128)S(1)} %get-tuple-element.28), channel_id=1, source_target_pairs={{0,1},{1,2},{2,3},{3,4},{4,5},{5,6},{6,7},{8,9},{9,10},{10,11},{11... | collective-permute-start | bytes 92 | tf_op jit(solution)/shard_map/ppermute | solution.py:27
  13.7 5.4 collective-permute-start.1
  27.7 81.8 %collective-permute-start.2 = (bf16[2,768]{1,0:T(2,128)(2,1)S(1)}, bf16[2,768]{1,0:T(2,128)(2,1)S(1)}, u32[]{:S(2)}, u32[]{:S(2)}) collective-permute-start(bf16[2,768]{1,0:T(2,128)(2,1)S(1)} %get-tuple-element.11), channel_id=1, source_target_pairs={{0,1},{1,2},{2,3},{3,4},{4,5},{5,6},{6,7},{8,9},{9,10},{10,11},{11... | collective-permute-start | bytes 9224 | tf_op jit(solution)/shard_map/ppermute | solution.py:27
  32.0 80.4 %collective-permute-start.3 = (bf16[2,768]{1,0:T(2,128)(2,1)S(1)}, bf16[2,768]{1,0:T(2,128)(2,1)S(1)}, u32[]{:S(2)}, u32[]{:S(2)}) collective-permute-start(bf16[2,768]{1,0:T(2,128)(2,1)S(1)} %get-tuple-element.12), channel_id=1, source_target_pairs={{1,0},{2,1},{3,2},{4,3},{5,4},{6,5},{7,6},{9,8},{10,9},{11,10},{12... | collective-permute-start | bytes 9224 | tf_op jit(solution)/shard_map/ppermute | solution.py:28
  107.2 4.3 copy-start.2
  113.2 31.7 %copy-start.1 = (bf16[768,128]{1,0:T(8,128)(2,1)S(1)}, bf16[768,128]{1,0:T(8,128)(2,1)}, u32[]{:S(2)}) copy-start(bf16[768,128]{1,0:T(8,128)(2,1)} %param.9) | copy-start | bytes 589828
  113.3 32.0 %copy-start.3 = (f32[1,2,16]{2,1,0:T(2,128)S(1)}, f32[1,2,16]{2,1,0:T(2,128)}, u32[]{:S(2)}) copy-start(f32[1,2,16]{2,1,0:T(2,128)} %param.11) | copy-start | bytes 388
  189.8 258.6 %reduce-scatter.6.cloned.1.call-start = ((), (), s32[]{:S(2)}) async-start(), calls=%async_computation.5 | async-start | bytes 442368 | tf_op jit(solution)/shard_map/reduce_scatter | solution.py:80
  191.0 321.3 %reduce-scatter.8.cloned.1.call-start = ((), (), s32[]{:S(2)}) async-start(), calls=%async_computation.6 | async-start | bytes 442368 | tf_op jit(solution)/shard_map/reduce_scatter | solution.py:83
  192.2 370.7 %all-reduce.5.cloned.1.call-start = ((), (), s32[]{:S(2)}) async-start(), calls=%async_computation.4 | async-start | bytes 3932160 | tf_op jit(solution)/shard_map/psum | solution.py:104
  386.5 210.3 %all-reduce.7.cloned.1.call-start = ((), (), s32[]{:S(2)}) async-start(), calls=%async_computation.8 | async-start | bytes 196608 | tf_op jit(solution)/shard_map/psum | solution.py:104
Sparse Core Ops, SparseCore 0:
  10.2 96.9 all-gather.2
  189.9 193.6 reduce-scatter.9
  387.9 60.4 reduce-scatter.5
  451.8 60.3 reduce-scatter.7
  514.6 48.3 all-reduce.4
  565.3 31.4 all-reduce.6
where the time goes:
time: 607 us; the launch traced here: 606 us
  waiting for transfers between devices  476 us (78%)
  blocking collectives  49.2 us (8%)
  matrix products  29.5 us (5%)
  local copies, waits for them, and re-layouts  22.5 us (4%)
  between operations  15 us (2%)
  starting transfers between devices  12 us (2%)
    unnamed x7, waiting for transfers between devices  192 us
    psum x2, waiting for transfers between devices, body(): lax.psum((conv_part, query_grad, key_grad), 'dp')  81.8 us
    all_gather x1, waiting for transfers between devices, body(): lax.all_gather(conv_weight, 'seq', axis=0, tiled=True)  73.9 us
    reduce_scatter x1, waiting for transfers between devices, body(): lax.psum_scatter(jnp.dot(embed_f.T, dkeys, precision=high), 'seq', scatte...  63.9 us
    reduce_scatter x1, waiting for transfers between devices, body(): lax.psum_scatter(jnp.dot(embed_f.T, dquery, precision=high), 'seq', scatt...  61.8 us
    all_gather x1, blocking collectives, body(): embed_all = lax.all_gather(embed_own, 'seq', axis=0, tiled=True)  30.3 us
    unnamed x17, local copies, waits for them, and re-layouts  22 us
    unnamed x1, blocking collectives  18.9 us
  transfers between devices with their start and end apart: 10, of which 7 were waited for; matrix products, arithmetic and copies ran while one was open for 4% of the time, Pallas kernels for 0%

commit v1 on v0

v1 whole, which is shorter than its diff:
```python
import functools

import jax
import jax.numpy as jnp
from jax import lax
from jax.experimental import pallas as pl
from jax.experimental.pallas import tpu as pltpu
from jax.sharding import PartitionSpec as P

C0 = 768
C1 = 768
PC = 128
K0 = 15
K1 = 5
POOL = 8
BIN_ROWS = 256
WINDOW = 24
CHUNK = 64
PAD = 128
GRAD_BLOCK = 512

ROOT = 0.7978845608028654
CUBE = 0.044715
HIGH = lax.Precision.HIGHEST
VMEM_LIMIT = 56 * 1024 * 1024


def params():
    return pltpu.CompilerParams(vmem_limit_bytes=VMEM_LIMIT)


def swap(x, axis, bit):
    size = lax.axis_size(axis)
    return lax.ppermute(x, axis, [(i, i ^ bit) for i in range(size)])


def gather_xor(x, axis, dim):
    bit = 1
    while bit < lax.axis_size(axis):
        x = jnp.concatenate([x, swap(x, axis, bit)], axis=dim)
        bit *= 2
    return x


def twice_gelu(v):
    return v + v * jnp.tanh(v * (ROOT + (ROOT * CUBE) * (v * v)))


def stem_kernel(
    n, rows_dev, co, pay_ref, t0_ref, w_ref, p_ref, slope_ref, emb_ref, bases, table, weights, ybuf, sums
):
    step = pl.program_id(0)
    rows = n * rows_dev
    blocks = rows // BIN_ROWS

    @pl.when(step == 0)
    def _():
        me = lax.axis_index("seq")
        bases[...] = jnp.full(bases.shape, -1.0, jnp.float32)
        for slab in range(n):
            slot = jnp.bitwise_xor(me, slab)
            start = pl.multiple_of(slot * rows_dev, 128)
            block = pay_ref[:, pl.ds(start, rows_dev)].astype(jnp.float32)
            bases[:, PAD + slab * rows_dev : PAD + (slab + 1) * rows_dev] = block[:POOL]
        for chunk in range(C0 // CHUNK):
            part = t0_ref[chunk * CHUNK : (chunk + 1) * CHUNK, :]
            for pos in range(POOL):
                shifted = part if pos == 0 else pltpu.roll(part, pos, 1)
                first = (chunk * POOL + pos) * CHUNK
                table[first : first + CHUNK, :] = shifted.astype(jnp.bfloat16)
        for tap in range(K1):
            weights[tap * co : (tap + 1) * co, :] = w_ref[:, tap * C0 : (tap + 1) * C0]
        ybuf[:, :PAD] = jnp.zeros((K1 * co, PAD), jnp.float32)
        ybuf[:, PAD + rows :] = jnp.zeros((K1 * co, PAD), jnp.float32)
        sums[...] = jnp.zeros(sums.shape, jnp.float32)

    @pl.when(step < blocks)
    def _():
        first = pl.multiple_of(step * BIN_ROWS, 128)
        near = bases[:, pl.ds(first, BIN_ROWS + 2 * PAD)]
        window = jnp.concatenate(
            [near[:, PAD + q : PAD + q + BIN_ROWS] for q in (-1, 0, 1)], axis=0
        )
        onehot = jnp.concatenate(
            [(window == b).astype(jnp.float32) for b in range(4)]
            + [jnp.zeros((128 - 4 * WINDOW, BIN_ROWS), jnp.float32)],
            axis=0,
        ).astype(jnp.bfloat16)
        for chunk in range(C0 // CHUNK):
            stem = jnp.dot(
                table[chunk * POOL * CHUNK : (chunk + 1) * POOL * CHUNK, :],
                onehot,
                preferred_element_type=jnp.float32,
            )
            most = least = stem[:CHUNK]
            for pos in range(1, POOL):
                part = stem[pos * CHUNK : (pos + 1) * CHUNK]
                most = jnp.maximum(most, part)
                least = jnp.minimum(least, part)
            pooled = 0.5 * jnp.maximum(twice_gelu(most), twice_gelu(least))
            p_ref[chunk * CHUNK : (chunk + 1) * CHUNK, :] = pooled.astype(jnp.bfloat16)
        ybuf[:, pl.ds(first + PAD, BIN_ROWS)] = jnp.dot(
            weights[...], p_ref[...], preferred_element_type=jnp.float32
        )

    @pl.when(step >= 1)
    def _():
        first = pl.multiple_of((step - 1) * BIN_ROWS, 128)
        conv = None
        for tap in range(K1):
            near = ybuf[tap * co : (tap + 1) * co, pl.ds(first, BIN_ROWS + 2 * PAD)]
            begin = PAD + tap - K1 // 2
            part = near[:, begin : begin + BIN_ROWS]
            conv = part if conv is None else conv + part
        square = conv * conv
        tangent = jnp.tanh(conv * (ROOT + (ROOT * CUBE) * square))
        half = 0.5 * conv
        gelu = half + half * tangent
        slope_ref[...] = (0.5 + 0.5 * tangent) + half * (1.0 - tangent * tangent) * (
            ROOT + (3.0 * ROOT * CUBE) * square
        )
        mean = jnp.sum(gelu, axis=1, keepdims=True) * (1.0 / BIN_ROWS)
        lane = lax.broadcasted_iota(jnp.int32, sums.shape, 1)
        sums[...] = jnp.where(lane == step - 1, mean, sums[...])

    @pl.when(step == blocks)
    def _():
        emb_ref[...] = sums[...].T[: emb_ref.shape[0], :].astype(jnp.bfloat16)


def stem_and_conv(n, payload, first_table, conv_weight):
    co = conv_weight.shape[0]
    rows = payload.shape[1]
    blocks = rows // BIN_ROWS
    return pl.pallas_call(
        functools.partial(stem_kernel, n, rows // n, co),
        grid=(blocks + 1,),
        in_specs=[
            pl.BlockSpec(payload.shape, lambda i: (0, 0)),
            pl.BlockSpec(first_table.shape, lambda i: (0, 0)),
            pl.BlockSpec(conv_weight.shape, lambda i: (0, 0)),
        ],
        out_specs=[
            pl.BlockSpec((C0, BIN_ROWS), lambda i: (0, jnp.minimum(i, blocks - 1))),
            pl.BlockSpec((co, BIN_ROWS), lambda i: (0, jnp.maximum(i - 1, 0))),
            pl.BlockSpec((blocks, co), lambda i: (0, 0)),
        ],
        out_shape=[
            jax.ShapeDtypeStruct((C0, rows), jnp.bfloat16),
            jax.ShapeDtypeStruct((co, rows), jnp.float32),
            jax.ShapeDtypeStruct((blocks, co), jnp.bfloat16),
        ],
        scratch_shapes=[
            pltpu.VMEM((POOL, rows + 2 * PAD), jnp.float32),
            pltpu.VMEM((POOL * C0, 128), jnp.bfloat16),
            pltpu.VMEM((K1 * co, C0), jnp.bfloat16),
            pltpu.VMEM((K1 * co, rows + 2 * PAD), jnp.float32),
            pltpu.VMEM((co, 128), jnp.float32),
        ],
        compiler_params=params(),
        name="stem_and_conv",
    )(payload, first_table, conv_weight)


def grad_kernel(
    n, rows_dev, co, pay_ref, emb_ref, wq_ref, wk_ref, slope_ref, p_ref, keep_ref, send_ref, dpad, acc, qk
):
    step = pl.program_id(0)
    rows = n * rows_dev
    npos = rows // BIN_ROWS
    own_pos = npos // n
    scale = PC**-0.5

    @pl.when(step == 0)
    def _():
        me = lax.axis_index("seq")
        query = jnp.zeros((npos, PC), jnp.float32)
        keys = jnp.zeros((npos, PC), jnp.float32)
        for slot in range(n):
            first = pl.multiple_of(jnp.bitwise_xor(me, slot) * co, 16)
            embed = emb_ref[slot * npos : (slot + 1) * npos, :]
            query = query + jnp.dot(
                embed, wq_ref[pl.ds(first, co), :], preferred_element_type=jnp.float32
            )
            keys = keys + jnp.dot(
                embed, wk_ref[pl.ds(first, co), :], preferred_element_type=jnp.float32
            )
        pieces = []
        for slab in range(n):
            start = pl.multiple_of(jnp.bitwise_xor(me, slab) * rows_dev, 128)
            block = pay_ref[:, pl.ds(start, 128)].astype(jnp.float32)
            for row in range(own_pos):
                at = POOL + 3 * row
                pieces.append(block[at : at + 1] + block[at + 1 : at + 2] + block[at + 2 : at + 3])
        grad = jnp.concatenate(pieces, axis=0)[:, :npos]
        dquery = jnp.dot(grad, keys, precision=HIGH, preferred_element_type=jnp.float32) * scale
        dkeys = (
            lax.dot_general(
                grad, query, (((0,), (0,)), ((), ())), precision=HIGH,
                preferred_element_type=jnp.float32,
            )
            * scale
        )
        first = pl.multiple_of(me * co, 16)
        dembed = None
        for w_ref, cotangent in ((wq_ref, dquery), (wk_ref, dkeys)):
            part = lax.dot_general(
                w_ref[pl.ds(first, co), :].astype(jnp.float32), cotangent,
                (((1,), (1,)), ((), ())), precision=HIGH, preferred_element_type=jnp.float32,
            )
            dembed = part if dembed is None else dembed + part
        dembed = dembed * (1.0 / BIN_ROWS)
        own = emb_ref[:npos, :].astype(jnp.float32)
        for at, cotangent in enumerate((dquery, dkeys)):
            qk[:, at * PC : (at + 1) * PC] = lax.dot_general(
                own, cotangent, (((0,), (0,)), ((), ())), precision=HIGH,
                preferred_element_type=jnp.float32,
            )
        dpad[:, :PAD] = jnp.zeros((co, PAD), jnp.float32)
        dpad[:, PAD + rows :] = jnp.zeros((co, PAD), jnp.float32)
        for pos in range(npos):
            dpad[:, PAD + pos * BIN_ROWS : PAD + (pos + 1) * BIN_ROWS] = (
                slope_ref[:, pos * BIN_ROWS : (pos + 1) * BIN_ROWS] * dembed[:, pos : pos + 1]
            )
        acc[...] = jnp.zeros(acc.shape, jnp.float32)

    first = pl.multiple_of(step * GRAD_BLOCK, 128)
    near = dpad[:, pl.ds(first, GRAD_BLOCK + 2 * PAD)]
    shifted = jnp.concatenate(
        [
            near[:, PAD - tap + K1 // 2 : PAD - tap + K1 // 2 + GRAD_BLOCK].astype(jnp.bfloat16)
            for tap in range(K1)
        ],
        axis=0,
    )
    acc[...] += lax.dot_general(
        shifted, p_ref[...], (((1,), (1,)), ((), ())), preferred_element_type=jnp.float32
    )

    @pl.when(step == rows // GRAD_BLOCK - 1)
    def _():
        core = lax.axis_index("dp") % 2

        def write(low, high, kind_low, kind_high):
            taps = [acc[tap * co : (tap + 1) * co, :] for tap in range(K1)]
            low[:, : 2 * C0] = jnp.concatenate(taps[:2], axis=1).astype(kind_low)
            low[:, 2 * C0 :] = taps[2][:, : 2 * C0 // 3].astype(kind_low)
            high[:, : C0 // 3] = taps[2][:, 2 * C0 // 3 :].astype(kind_high)
            high[:, C0 // 3 : C0 // 3 + 2 * C0] = jnp.concatenate(taps[3:], axis=1).astype(kind_high)
            high[:, C0 // 3 + 2 * C0 :] = qk[...].astype(kind_high)

        @pl.when(core == 0)
        def _():
            write(keep_ref, send_ref, jnp.float32, jnp.bfloat16)

        @pl.when(core == 1)
        def _():
            write(send_ref, keep_ref, jnp.bfloat16, jnp.float32)


def gradients(n, payload, embed, query_weight, key_weight, slope, pooled):
    co, rows = slope.shape
    half = (K1 * C0 + 2 * PC) // 2
    whole = lambda i: (0, 0)
    return pl.pallas_call(
        functools.partial(grad_kernel, n, rows // n, co),
        grid=(rows // GRAD_BLOCK,),
        in_specs=[pl.BlockSpec(x.shape, whole) for x in (payload, embed, query_weight, key_weight, slope)]
        + [pl.BlockSpec((C0, GRAD_BLOCK), lambda i: (0, i))],
        out_specs=[pl.BlockSpec((co, half), whole)] * 2,
        out_shape=[
            jax.ShapeDtypeStruct((co, half), jnp.float32),
            jax.ShapeDtypeStruct((co, half), jnp.bfloat16),
        ],
        scratch_shapes=[
            pltpu.VMEM((co, rows + 2 * PAD), jnp.float32),
            pltpu.VMEM((K1 * co, C0), jnp.float32),
            pltpu.VMEM((co, 2 * PC), jnp.float32),
        ],
        compiler_params=params(),
        name="gradients",
    )(payload, embed, query_weight, key_weight, slope, pooled)


def add_kernel(a_ref, b_ref, out_ref):
    out_ref[...] = (a_ref[...].astype(jnp.float32) + b_ref[...].astype(jnp.float32)).astype(
        jnp.bfloat16
    )


def add_half(a, b):
    return pl.pallas_call(
        add_kernel,
        out_shape=jax.ShapeDtypeStruct(b.shape, jnp.bfloat16),
        compiler_params=params(),
        name="add_half",
    )(a, b)


def join_kernel(mine_ref, other_ref, conv_ref, query_ref, key_ref):
    half = mine_ref.shape[1]
    rest = K1 * C0 - half
    core = lax.axis_index("dp") % 2

    def write(low, high):
        conv_ref[:, :half] = low[...].astype(jnp.float32)
        conv_ref[:, half:] = high[:, :rest].astype(jnp.float32)
        query_ref[...] = high[:, rest : rest + PC].astype(jnp.float32)
        key_ref[...] = high[:, rest + PC :].astype(jnp.float32)

    @pl.when(core == 0)
    def _():
        write(mine_ref, other_ref)

    @pl.when(core == 1)
    def _():
        write(other_ref, mine_ref)


def join(mine, other):
    co = mine.shape[0]
    return pl.pallas_call(
        join_kernel,
        out_shape=[
            jax.ShapeDtypeStruct((co, K1 * C0), jnp.float32),
            jax.ShapeDtypeStruct((co, PC), jnp.float32),
            jax.ShapeDtypeStruct((co, PC), jnp.float32),
        ],
        compiler_params=params(),
        name="join",
    )(mine, other)


def body(bases, stem_table, conv_weight, query_weight, key_weight, pair_grad):
    n = lax.axis_size("seq")
    rows_dev = bases.shape[1] // POOL
    own_pos, npos = pair_grad.shape[1:]

    rest = pair_grad[0]
    parts = []
    for _ in range(3):
        part = lax.reduce_precision(rest, 8, 7)
        parts.append(part)
        rest = rest - part
    grad_rows = jnp.stack(parts, axis=1).reshape(3 * own_pos, npos).astype(jnp.bfloat16)
    grad_rows = jnp.pad(grad_rows, ((0, 8 - 3 * own_pos), (0, rows_dev - npos)))
    base_rows = bases.reshape(rows_dev, POOL).T.astype(jnp.bfloat16)
    payload = gather_xor(jnp.concatenate([base_rows, grad_rows], axis=0), "seq", 1)

    first_table = jnp.pad(
        stem_table.transpose(2, 1, 0), ((0, 0), (0, 0), (1, WINDOW - 1 - K0))
    ).reshape(C0, 4 * WINDOW)
    first_table = jnp.pad(first_table, ((0, 0), (0, 128 - 4 * WINDOW))).astype(jnp.float32)

    pooled, slope, embed = stem_and_conv(n, payload, first_table, conv_weight)
    embed_all = gather_xor(embed, "seq", 0)
    keep, send = gradients(n, payload, embed_all, query_weight, key_weight, slope, pooled)

    mine = add_half(keep, swap(send, "dp", 1))
    bit = 2
    while bit < lax.axis_size("dp"):
        mine = add_half(mine, swap(mine, "dp", bit))
        bit *= 2
    return tuple(join(mine, swap(mine, "dp", 1)))


def solution(mesh):
    return jax.shard_map(
        body,
        mesh=mesh,
        in_specs=(P("dp", "seq"), P(), P("seq", None), P(), P(), P("dp", "seq", None)),
        out_specs=(P("seq", None), P("seq", None), P("seq", None)),
        check_vma=False,
    )
```

time: 607 us -> 105 us (0.17)
  waiting for transfers between devices: 476 us -> 22.9 us
  Pallas kernels: 0 us -> 55.4 us
  blocking collectives: 49.2 us -> 0 us
  matrix products: 29.5 us -> 0 us
  local copies, waits for them, and re-layouts: 22.5 us -> 3.61 us
  between operations: 15 us -> 0.69 us
    unnamed x7 -> x0, waiting for transfers between devices: 192 us -> none
    reduce_scatter x2 -> x0, waiting for transfers between devices: 126 us -> none  [the longest x1 63.9 us: body(): lax.psum_scatter(jnp.dot(embed_f.T, dkeys, precision=high), 'seq', scatte...]
    psum x2 -> x0, waiting for transfers between devices: 81.8 us -> none  [body(): lax.psum((conv_part, query_grad, key_grad), 'dp')]
    all_gather x1 -> x0, waiting for transfers between devices: 73.9 us -> none  [body(): lax.all_gather(conv_weight, 'seq', axis=0, tiled=True)]
    pallas_call x0 -> x5, Pallas kernels: none -> 55.4 us  [the longest x1 37.6 us: stem_and_conv(): pl.pallas_call(functools.partial(stem_kernel, n, rows // n, co), grid=(bl...]
    all_gather x1 -> x0, blocking collectives: 30.3 us -> none  [body(): embed_all = lax.all_gather(embed_own, 'seq', axis=0, tiled=True)]
    dot_general x19 -> x0, matrix products: 29.5 us -> none  [the longest x5 11.3 us: body(): lax.dot_general(dconv, padded[t:t + rows], (((0,), (0,)), ((), ())), pref...]
    ppermute x4 -> x9, waiting for transfers between devices: 2.22 us -> 22.9 us  [swap(): return lax.ppermute(x, axis, [(i, i ^ bit) for i in range(size)])]
  transfers between devices with their start and end apart: 10 -> 9, of which waited for: 7 -> 9; matrix products, arithmetic and copies ran while one was open for 4% -> 2% of each run, Pallas kernels for 0% -> 0%
where the time goes in v1:
time: 105 us
  Pallas kernels  55.4 us (53%)
  waiting for transfers between devices  22.9 us (22%)
  starting transfers between devices  16.7 us (16%)
  other arithmetic  5.61 us (5%)
  local copies, waits for them, and re-layouts  3.61 us (3%)
    pallas_call x1, Pallas kernels, stem_and_conv(): pl.pallas_call(functools.partial(stem_kernel, n, rows // n, co), grid=(bl...  37.6 us
    ppermute x9, waiting for transfers between devices, swap(): return lax.ppermute(x, axis, [(i, i ^ bit) for i in range(size)])  22.9 us
    ppermute x9, starting transfers between devices, swap(): return lax.ppermute(x, axis, [(i, i ^ bit) for i in range(size)])  16.7 us
    pallas_call x1, Pallas kernels, gradients(): pl.pallas_call(functools.partial(grad_kernel, n, rows // n, co), grid=(ro...  11.5 us
    pallas_call x2, Pallas kernels, add_half(): pl.pallas_call(add_kernel, out_shape=jax.ShapeDtypeStruct(b.shape, jnp.bf...  3.99 us
    concatenate x6, other arithmetic, gather_xor(): x = jnp.concatenate([x, swap(x, axis, bit)], axis=dim)  3.36 us
    unnamed x7, local copies, waits for them, and re-layouts  3.13 us
    pallas_call x1, Pallas kernels, join(): pl.pallas_call(join_kernel, out_shape=[jax.ShapeDtypeStruct((co, K1 * C0)...  2.35 us
  transfers between devices with their start and end apart: 9, of which 9 were waited for; matrix products, arithmetic and copies ran while one was open for 2% of the time, Pallas kernels for 0%

profile of v1, /device:TPU:0, one launch (start us, length us, event | category | flops | bytes accessed | tf_op | source)
XLA Modules:
  0.0 104.9 jit_solution(11797132932948215974)
XLA Ops:
  0.6 0.7 reduce-precision_convert_fusion.1
  1.4 0.8 convert_reduce_fusion
  2.1 0.2 convert_element_type.23
  2.3 0.1 copy.11
  2.4 3.0 %collective-permute-start = (bf16[16,512]{1,0:T(8,128)(2,1)S(1)}, bf16[16,512]{1,0:T(8,128)(2,1)S(1)}, u32[]{:S(2)}, u32[]{:S(2)}) collective-permute-start(bf16[16,512]{1,0:T(8,128)(2,1)S(1)} %pad_maximum_fusion.4), channel_id=1, source_target_pairs={{0,1},{1,0},{2,3},{3,2},{4,5},{5,4},{6,7},{7,6},{8,9},{9,8},{10,11... | collective-permute-start | bytes 49160 | tf_op jit(solution)/shard_map/ppermute | solution.py:34
  5.4 1.7 %collective-permute-done = bf16[16,512]{1,0:T(8,128)(2,1)S(1)} collective-permute-done((bf16[16,512]{1,0:T(8,128)(2,1)S(1)}, bf16[16,512]{1,0:T(8,128)(2,1)S(1)}, u32[]{:S(2)}, u32[]{:S(2)}) %collective-permute-start) | collective-permute-done | bytes 16416 | tf_op jit(solution)/shard_map/ppermute | solution.py:34
  7.2 2.1 %collective-permute-start.1 = (bf16[16,1024]{1,0:T(8,128)(2,1)S(1)}, bf16[16,1024]{1,0:T(8,128)(2,1)S(1)}, u32[]{:S(2)}, u32[]{:S(2)}) collective-permute-start(bf16[16,1024]{1,0:T(8,128)(2,1)S(1)} %pad_maximum_fusion.2), channel_id=1, source_target_pairs={{0,2},{1,3},{2,0},{3,1},{4,6},{5,7},{6,4},{7,5},{8,10},{9,11},{10,... | collective-permute-start | bytes 98312 | tf_op jit(solution)/shard_map/ppermute | solution.py:34
  9.2 0.9 copy.16
  10.2 0.2 copy.14
  10.4 0.8 collective-permute-done.1
  11.1 3.0 %collective-permute-start.2 = (bf16[16,2048]{1,0:T(8,128)(2,1)S(1)}, bf16[16,2048]{1,0:T(8,128)(2,1)S(1)}, u32[]{:S(2)}, u32[]{:S(2)}) collective-permute-start(bf16[16,2048]{1,0:T(8,128)(2,1)S(1)} %pad_maximum_fusion.1), channel_id=1, source_target_pairs={{0,4},{1,5},{2,6},{3,7},{4,0},{5,1},{6,2},{7,3},{8,12},{9,13},{10,... | collective-permute-start | bytes 196616 | tf_op jit(solution)/shard_map/ppermute | solution.py:34
  14.2 0.8 pad_convert_fusion.t0_ref
  14.9 1.5 %collective-permute-done.2 = bf16[16,2048]{1,0:T(8,128)(2,1)S(1)} collective-permute-done((bf16[16,2048]{1,0:T(8,128)(2,1)S(1)}, bf16[16,2048]{1,0:T(8,128)(2,1)S(1)}, u32[]{:S(2)}, u32[]{:S(2)}) %collective-permute-start.2) | collective-permute-done | bytes 65568 | tf_op jit(solution)/shard_map/ppermute | solution.py:34
  16.4 0.7 pad_maximum_fusion.pay_ref
  17.1 37.6 %stem_and_conv.1 = (bf16[768,4096]{1,0:T(8,128)(2,1)}, f32[96,4096]{1,0:T(8,128)}, bf16[16,96]{1,0:T(8,128)(2,1)}) custom-call(bf16[16,4096]{1,0:T(8,128)(2,1)} %pad_maximum_fusion.pay_ref, f32[768,128]{1,0:T(8,128)} %pad_convert_fusion.t0_ref, bf16[96,3840]{1,0:T(8,128)(2,1)} %w_ref.1), custom_call_target="tpu_custom_call" | custom-call | tf_op jit(solution)/shard_map/stem_and_conv/pallas_call | solution.py:135
  54.6 1.9 %collective-permute-start.3 = (bf16[16,96]{1,0:T(8,128)(2,1)}, bf16[16,96]{1,0:T(8,128)(2,1)S(1)}, u32[]{:S(2)}, u32[]{:S(2)}) collective-permute-start(bf16[16,96]{1,0:T(8,128)(2,1)} %get-tuple-element.8), channel_id=1, source_target_pairs={{0,1},{1,0},{2,3},{3,2},{4,5},{5,4},{6,7},{7,6},{8,9},{9,8},{10,11... | collective-permute-start | bytes 9224 | tf_op jit(solution)/shard_map/ppermute | solution.py:34
  56.5 2.0 %collective-permute-done.3 = bf16[16,96]{1,0:T(8,128)(2,1)S(1)} collective-permute-done((bf16[16,96]{1,0:T(8,128)(2,1)}, bf16[16,96]{1,0:T(8,128)(2,1)S(1)}, u32[]{:S(2)}, u32[]{:S(2)}) %collective-permute-start.3) | collective-permute-done | bytes 3104 | tf_op jit(solution)/shard_map/ppermute | solution.py:34
  58.5 0.7 pad_maximum_fusion.6
  59.2 1.9 %collective-permute-start.4 = (bf16[32,96]{1,0:T(8,128)(2,1)S(1)}, bf16[32,96]{1,0:T(8,128)(2,1)S(1)}, u32[]{:S(2)}, u32[]{:S(2)}) collective-permute-start(bf16[32,96]{1,0:T(8,128)(2,1)S(1)} %pad_maximum_fusion.6), channel_id=1, source_target_pairs={{0,2},{1,3},{2,0},{3,1},{4,6},{5,7},{6,4},{7,5},{8,10},{9,11},{10,... | collective-permute-start | bytes 18440 | tf_op jit(solution)/shard_map/ppermute | solution.py:34
  61.1 1.7 %collective-permute-done.4 = bf16[32,96]{1,0:T(8,128)(2,1)S(1)} collective-permute-done((bf16[32,96]{1,0:T(8,128)(2,1)S(1)}, bf16[32,96]{1,0:T(8,128)(2,1)S(1)}, u32[]{:S(2)}, u32[]{:S(2)}) %collective-permute-start.4) | collective-permute-done | bytes 6176 | tf_op jit(solution)/shard_map/ppermute | solution.py:34
  62.8 0.7 pad_maximum_fusion.5
  63.5 3.1 %collective-permute-start.5 = (bf16[64,96]{1,0:T(8,128)(2,1)S(1)}, bf16[64,96]{1,0:T(8,128)(2,1)S(1)}, u32[]{:S(2)}, u32[]{:S(2)}) collective-permute-start(bf16[64,96]{1,0:T(8,128)(2,1)S(1)} %pad_maximum_fusion.5), channel_id=1, source_target_pairs={{0,4},{1,5},{2,6},{3,7},{4,0},{5,1},{6,2},{7,3},{8,12},{9,13},{10,... | collective-permute-start | bytes 36872 | tf_op jit(solution)/shard_map/ppermute | solution.py:34
  66.6 1.7 %collective-permute-done.5 = bf16[64,96]{1,0:T(8,128)(2,1)S(1)} collective-permute-done((bf16[64,96]{1,0:T(8,128)(2,1)S(1)}, bf16[64,96]{1,0:T(8,128)(2,1)S(1)}, u32[]{:S(2)}, u32[]{:S(2)}) %collective-permute-start.5) | collective-permute-done | bytes 12320 | tf_op jit(solution)/shard_map/ppermute | solution.py:34
  68.3 1.3 %pad_maximum_fusion.3.emb_ref = bf16[128,96]{1,0:T(8,128)(2,1)} fusion(bf16[64,96]{1,0:T(8,128)(2,1)S(1)} %collective-permute-done.5, bf16[32,96]{1,0:T(8,128)(2,1)S(1)} %collective-permute-done.4, bf16[16,96]{1,0:T(8,128)(2,1)S(1)} %collective-permute-done.3, bf16[16,96]{1,0:T(8,128)(2,1)} %get-tuple-element.8), kind=kLoop, calls=%fused_computation.5 | loop fusion | flops 98304 | bytes 49152 | tf_op jit(solution)/shard_map/concatenate | solution.py:40
  69.6 11.5 %gradients.1 = (f32[96,2048]{1,0:T(8,128)}, bf16[96,2048]{1,0:T(8,128)(2,1)}) custom-call(bf16[16,4096]{1,0:T(8,128)(2,1)} %pad_maximum_fusion.pay_ref, bf16[128,96]{1,0:T(8,128)(2,1)} %pad_maximum_fusion.3.emb_ref, bf16[768,128]{1,0:T(8,128)(2,1)} %wq_ref.1, bf16[768,128]{1,0:T(8,128)(2,1)} %wk_ref.1, f32[96,4096]{1,0:T(8,128)} %get-tuple-element.9.slope_ref, ...), custom_call_target="tpu_custom_call" | custom-call | tf_op jit(solution)/shard_map/gradients/pallas_call | solution.py:265
  81.1 0.0 collective-permute-start.6
  81.1 1.9 %collective-permute-done.6.b_ref = bf16[96,2048]{1,0:T(8,128)(2,1)S(1)} collective-permute-done((bf16[96,2048]{1,0:T(8,128)(2,1)}, bf16[96,2048]{1,0:T(8,128)(2,1)S(1)}, u32[]{:S(2)}, u32[]{:S(2)}) %collective-permute-start.6) | collective-permute-done | bytes 393248 | tf_op jit(solution)/shard_map/ppermute | solution.py:34
  83.0 0.0 copy-start.1
  83.0 0.7 copy-done.1
  83.8 2.0 %add_half.2.a_ref = bf16[96,2048]{1,0:T(8,128)(2,1)} custom-call(f32[96,2048]{1,0:T(8,128)} %get-tuple-element.11.a_ref, bf16[96,2048]{1,0:T(8,128)(2,1)} %copy-done.1), custom_call_target="tpu_custom_call" | custom-call | tf_op jit(solution)/shard_map/add_half/pallas_call | solution.py:292
  85.8 1.7 %collective-permute-start.7 = (bf16[96,2048]{1,0:T(8,128)(2,1)}, bf16[96,2048]{1,0:T(8,128)(2,1)S(1)}, u32[]{:S(2)}, u32[]{:S(2)}) collective-permute-start(bf16[96,2048]{1,0:T(8,128)(2,1)} %add_half.2.a_ref), channel_id=1, source_target_pairs={{0,16},{8,24},{16,0},{24,8},{1,17},{9,25},{17,1},{25,9},{2,18},{10... | collective-permute-start | bytes 1179656 | tf_op jit(solution)/shard_map/ppermute | solution.py:34
  87.5 9.7 %collective-permute-done.7.b_ref = bf16[96,2048]{1,0:T(8,128)(2,1)S(1)} collective-permute-done((bf16[96,2048]{1,0:T(8,128)(2,1)}, bf16[96,2048]{1,0:T(8,128)(2,1)S(1)}, u32[]{:S(2)}, u32[]{:S(2)}) %collective-permute-start.7) | collective-permute-done | bytes 393248 | tf_op jit(solution)/shard_map/ppermute | solution.py:34
  97.2 0.0 copy-start.2
  97.2 0.7 copy-done.2
  97.9 1.9 %add_half.3.mine_ref = bf16[96,2048]{1,0:T(8,128)(2,1)} custom-call(bf16[96,2048]{1,0:T(8,128)(2,1)} %add_half.2.a_ref, bf16[96,2048]{1,0:T(8,128)(2,1)} %copy-done.2), custom_call_target="tpu_custom_call" | custom-call | tf_op jit(solution)/shard_map/add_half/pallas_call | solution.py:292
  99.9 0.0 collective-permute-start.8
  99.9 1.9 %collective-permute-done.8.other_ref = bf16[96,2048]{1,0:T(8,128)(2,1)S(1)} collective-permute-done((bf16[96,2048]{1,0:T(8,128)(2,1)}, bf16[96,2048]{1,0:T(8,128)(2,1)S(1)}, u32[]{:S(2)}, u32[]{:S(2)}) %collective-permute-start.8) | collective-permute-done | bytes 393248 | tf_op jit(solution)/shard_map/ppermute | solution.py:34
  101.8 0.0 copy-start
  101.8 0.7 copy-done
  102.5 2.3 %join.1 = (f32[96,3840]{1,0:T(8,128)}, f32[96,128]{1,0:T(8,128)}, f32[96,128]{1,0:T(8,128)}) custom-call(bf16[96,2048]{1,0:T(8,128)(2,1)} %add_half.3.mine_ref, bf16[96,2048]{1,0:T(8,128)(2,1)} %copy-done), custom_call_target="tpu_custom_call" | custom-call | tf_op jit(solution)/shard_map/join/pallas_call | solution.py:322
  (8 shorter events, 0.1 us)
Async XLA Ops:
  2.4 4.8 %collective-permute-start = (bf16[16,512]{1,0:T(8,128)(2,1)S(1)}, bf16[16,512]{1,0:T(8,128)(2,1)S(1)}, u32[]{:S(2)}, u32[]{:S(2)}) collective-permute-start(bf16[16,512]{1,0:T(8,128)(2,1)S(1)} %pad_maximum_fusion.4), channel_id=1, source_target_pairs={{0,1},{1,0},{2,3},{3,2},{4,5},{5,4},{6,7},{7,6},{8,9},{9,8},{10,11... | collective-permute-start | bytes 49160 | tf_op jit(solution)/shard_map/ppermute | solution.py:34
  7.2 4.0 %collective-permute-start.1 = (bf16[16,1024]{1,0:T(8,128)(2,1)S(1)}, bf16[16,1024]{1,0:T(8,128)(2,1)S(1)}, u32[]{:S(2)}, u32[]{:S(2)}) collective-permute-start(bf16[16,1024]{1,0:T(8,128)(2,1)S(1)} %pad_maximum_fusion.2), channel_id=1, source_target_pairs={{0,2},{1,3},{2,0},{3,1},{4,6},{5,7},{6,4},{7,5},{8,10},{9,11},{10,... | collective-permute-start | bytes 98312 | tf_op jit(solution)/shard_map/ppermute | solution.py:34
  11.1 5.3 %collective-permute-start.2 = (bf16[16,2048]{1,0:T(8,128)(2,1)S(1)}, bf16[16,2048]{1,0:T(8,128)(2,1)S(1)}, u32[]{:S(2)}, u32[]{:S(2)}) collective-permute-start(bf16[16,2048]{1,0:T(8,128)(2,1)S(1)} %pad_maximum_fusion.1), channel_id=1, source_target_pairs={{0,4},{1,5},{2,6},{3,7},{4,0},{5,1},{6,2},{7,3},{8,12},{9,13},{10,... | collective-permute-start | bytes 196616 | tf_op jit(solution)/shard_map/ppermute | solution.py:34
  54.6 3.8 %collective-permute-start.3 = (bf16[16,96]{1,0:T(8,128)(2,1)}, bf16[16,96]{1,0:T(8,128)(2,1)S(1)}, u32[]{:S(2)}, u32[]{:S(2)}) collective-permute-start(bf16[16,96]{1,0:T(8,128)(2,1)} %get-tuple-element.8), channel_id=1, source_target_pairs={{0,1},{1,0},{2,3},{3,2},{4,5},{5,4},{6,7},{7,6},{8,9},{9,8},{10,11... | collective-permute-start | bytes 9224 | tf_op jit(solution)/shard_map/ppermute | solution.py:34
  59.2 3.7 %collective-permute-start.4 = (bf16[32,96]{1,0:T(8,128)(2,1)S(1)}, bf16[32,96]{1,0:T(8,128)(2,1)S(1)}, u32[]{:S(2)}, u32[]{:S(2)}) collective-permute-start(bf16[32,96]{1,0:T(8,128)(2,1)S(1)} %pad_maximum_fusion.6), channel_id=1, source_target_pairs={{0,2},{1,3},{2,0},{3,1},{4,6},{5,7},{6,4},{7,5},{8,10},{9,11},{10,... | collective-permute-start | bytes 18440 | tf_op jit(solution)/shard_map/ppermute | solution.py:34
  63.5 4.8 %collective-permute-start.5 = (bf16[64,96]{1,0:T(8,128)(2,1)S(1)}, bf16[64,96]{1,0:T(8,128)(2,1)S(1)}, u32[]{:S(2)}, u32[]{:S(2)}) collective-permute-start(bf16[64,96]{1,0:T(8,128)(2,1)S(1)} %pad_maximum_fusion.5), channel_id=1, source_target_pairs={{0,4},{1,5},{2,6},{3,7},{4,0},{5,1},{6,2},{7,3},{8,12},{9,13},{10,... | collective-permute-start | bytes 36872 | tf_op jit(solution)/shard_map/ppermute | solution.py:34
  81.1 1.9 %collective-permute-start.6 = (bf16[96,2048]{1,0:T(8,128)(2,1)}, bf16[96,2048]{1,0:T(8,128)(2,1)S(1)}, u32[]{:S(2)}, u32[]{:S(2)}) collective-permute-start(bf16[96,2048]{1,0:T(8,128)(2,1)} %get-tuple-element.12), channel_id=1, source_target_pairs={{0,8},{8,0},{16,24},{24,16},{1,9},{9,1},{17,25},{25,17},{2,10},{10... | collective-permute-start | bytes 1179656 | tf_op jit(solution)/shard_map/ppermute | solution.py:34
  83.0 0.7 copy-start.1
  85.8 11.4 %collective-permute-start.7 = (bf16[96,2048]{1,0:T(8,128)(2,1)}, bf16[96,2048]{1,0:T(8,128)(2,1)S(1)}, u32[]{:S(2)}, u32[]{:S(2)}) collective-permute-start(bf16[96,2048]{1,0:T(8,128)(2,1)} %add_half.2.a_ref), channel_id=1, source_target_pairs={{0,16},{8,24},{16,0},{24,8},{1,17},{9,25},{17,1},{25,9},{2,18},{10... | collective-permute-start | bytes 1179656 | tf_op jit(solution)/shard_map/ppermute | solution.py:34
  97.2 0.7 copy-start.2
  99.9 1.9 %collective-permute-start.8 = (bf16[96,2048]{1,0:T(8,128)(2,1)}, bf16[96,2048]{1,0:T(8,128)(2,1)S(1)}, u32[]{:S(2)}, u32[]{:S(2)}) collective-permute-start(bf16[96,2048]{1,0:T(8,128)(2,1)} %add_half.3.mine_ref), channel_id=1, source_target_pairs={{0,8},{8,0},{16,24},{24,16},{1,9},{9,1},{17,25},{25,17},{2,10},{10... | collective-permute-start | bytes 1179656 | tf_op jit(solution)/shard_map/ppermute | solution.py:34
  101.8 0.7 copy-start

commit v2 on v0

v2 whole, which is shorter than its diff:
```python
import functools

import jax
import jax.numpy as jnp
from jax import lax
from jax.experimental import pallas as pl
from jax.experimental.pallas import tpu as pltpu
from jax.sharding import PartitionSpec as P

C0 = 768
C1 = 768
PC = 128
K0 = 15
K1 = 5
POOL = 8
BIN_ROWS = 256
WINDOW = 24
CHUNK = 128
BLOCK = 512
LAG = 3
PAD = 128
SLOT = 128

ROOT = 0.7978845608028654
CUBE = 0.044715
HIGH = lax.Precision.HIGHEST
MIB = 1024 * 1024


def params(mib):
    return pltpu.CompilerParams(vmem_limit_bytes=mib * MIB)


def swap(x, axis, bit):
    size = lax.axis_size(axis)
    return lax.ppermute(x, axis, [(i, i ^ bit) for i in range(size)])


def gather_xor(x, axis):
    x = x[None]
    bit = 1
    while bit < lax.axis_size(axis):
        x = jnp.concatenate([x, swap(x, axis, bit)], axis=0)
        bit *= 2
    return x


def gather_direct(x, axis):
    return lax.all_to_all(jnp.broadcast_to(x[None], (lax.axis_size(axis),) + x.shape), axis, 0, 0)


def twice_gelu(v):
    return v + v * jnp.tanh(v * (ROOT + (ROOT * CUBE) * (v * v)))


def prepare_kernel(n, co, t0_ref, w_ref, wq_ref, wk_ref, table_ref, weights_ref, proj_ref):
    for chunk in range(C0 // CHUNK):
        part = t0_ref[chunk * CHUNK : (chunk + 1) * CHUNK, :]
        for pos in range(POOL):
            shifted = part if pos == 0 else pltpu.roll(part, pos, 1)
            first = (chunk * POOL + pos) * CHUNK
            table_ref[first : first + CHUNK, :] = shifted.astype(jnp.bfloat16)
    for tap in range(K1):
        weights_ref[tap * co : (tap + 1) * co, :] = w_ref[:, tap * C0 : (tap + 1) * C0]
    for slot in range(n):
        rows = slice(slot * co, (slot + 1) * co)
        proj_ref[slot * SLOT : slot * SLOT + co, :PC] = wq_ref[rows, :]
        proj_ref[slot * SLOT : slot * SLOT + co, PC:] = wk_ref[rows, :]
        proj_ref[slot * SLOT + co : (slot + 1) * SLOT, :] = jnp.zeros(
            (SLOT - co, 2 * PC), jnp.bfloat16
        )


def prepare(n, first_table, conv_weight, query_weight, key_weight):
    co = conv_weight.shape[0]
    return pl.pallas_call(
        functools.partial(prepare_kernel, n, co),
        out_shape=[
            jax.ShapeDtypeStruct((POOL * C0, 128), jnp.bfloat16),
            jax.ShapeDtypeStruct((K1 * co, C0), jnp.bfloat16),
            jax.ShapeDtypeStruct((n * SLOT, 2 * PC), jnp.bfloat16),
        ],
        compiler_params=params(8),
        cost_estimate=pl.CostEstimate(flops=0, bytes_accessed=5 * MIB, transcendentals=0),
        name="prepare",
    )(first_table, conv_weight, query_weight, key_weight)


def stem_kernel(
    n, rows_dev, co, pay_ref, table, weights, grad_ref, p_ref, slope_ref, emb_ref, bases, ybuf, prev, sums, sa, sb, slopes
):
    step = pl.program_id(0)
    rows = n * rows_dev
    blocks = rows // BLOCK
    front = LAG * BLOCK + PAD
    piece = 256

    def convolve(block):
        first = pl.multiple_of((block + LAG) * BLOCK, 128)
        conv = None
        for tap in range(K1):
            near = ybuf[tap * co : (tap + 1) * co, pl.ds(first, BLOCK + 2 * PAD)]
            begin = PAD + tap - K1 // 2
            part = near[:, begin : begin + BLOCK]
            conv = part if conv is None else conv + part
        square = conv * conv
        tangent = jnp.tanh(conv * (ROOT + (ROOT * CUBE) * square))
        half = 0.5 * conv
        gelu = half + half * tangent
        slopes[...] = (0.5 + 0.5 * tangent) + half * (1.0 - tangent * tangent) * (
            ROOT + (3.0 * ROOT * CUBE) * square
        )
        lane = lax.broadcasted_iota(jnp.int32, (co, 128), 1)
        total = sums[:co, :]
        for part in range(BLOCK // BIN_ROWS):
            mean = jnp.sum(
                gelu[:, part * BIN_ROWS : (part + 1) * BIN_ROWS], axis=1, keepdims=True
            ) * (1.0 / BIN_ROWS)
            total = jnp.where(lane == block * (BLOCK // BIN_ROWS) + part, mean, total)
        sums[:co, :] = total

    def taps(block):
        ybuf[:, pl.ds(pl.multiple_of(front + block * BLOCK, 128), BLOCK)] = jnp.dot(
            weights[...], prev[...], preferred_element_type=jnp.float32
        )

    @pl.when(step == 0)
    def _():
        me = lax.axis_index("seq")
        bases[:, :PAD] = jnp.full((POOL, PAD), -1.0, jnp.float32)
        bases[:, PAD + rows :] = jnp.full((POOL, PAD), -1.0, jnp.float32)
        half = rows_dev // 2
        for slab in range(n):
            block = pay_ref[jnp.bitwise_xor(me, slab)].astype(jnp.float32)
            first = PAD + slab * rows_dev
            bases[:, first : first + half] = block[:POOL]
            bases[:, first + half : first + 2 * half] = block[POOL:]
        ybuf[:, front + rows :] = jnp.zeros((K1 * co, PAD), jnp.float32)
        prev[...] = jnp.zeros(prev.shape, jnp.bfloat16)
        sums[...] = jnp.zeros(sums.shape, jnp.float32)

    @pl.when(step < blocks)
    def _():
        first = pl.multiple_of(step * BLOCK, 128)
        near = bases[:, pl.ds(first, BLOCK + 2 * PAD)]
        window = jnp.concatenate(
            [near[:, PAD + q : PAD + q + BLOCK] for q in (-1, 0, 1)], axis=0
        )
        onehot = jnp.concatenate(
            [(window == b).astype(jnp.float32) for b in range(4)]
            + [jnp.zeros((128 - 4 * WINDOW, BLOCK), jnp.float32)],
            axis=0,
        ).astype(jnp.bfloat16)
        convolve(step - LAG)
        taps(step - 1)
        stage = (sa, sb)

        def multiply(chunk, at):
            stage[chunk % 2][:, at : at + piece] = jnp.dot(
                table[chunk * POOL * CHUNK : (chunk + 1) * POOL * CHUNK, :],
                onehot[:, at : at + piece],
                preferred_element_type=jnp.float32,
            )

        def pool(chunk, at):
            stem = stage[chunk % 2]
            for row in range(0, CHUNK, 16):
                most = least = stem[row : row + 16, at : at + piece]
                for pos in range(1, POOL):
                    part = stem[pos * CHUNK + row : pos * CHUNK + row + 16, at : at + piece]
                    most = jnp.maximum(most, part)
                    least = jnp.minimum(least, part)
                pooled = (0.5 * jnp.maximum(twice_gelu(most), twice_gelu(least))).astype(jnp.bfloat16)
                to = chunk * CHUNK + row
                prev[to : to + 16, at : at + piece] = pooled

        chunks = C0 // CHUNK
        for at in range(0, BLOCK, piece):
            multiply(0, at)
        for chunk in range(chunks):
            for at in range(0, BLOCK, piece):
                if chunk + 1 < chunks:
                    multiply(chunk + 1, at)
                pool(chunk, at)
        p_ref[...] = prev[...]
        slope_ref[...] = slopes[...]

    @pl.when(step >= blocks)
    def _():
        @pl.when(step == blocks)
        def _():
            taps(blocks - 1)

        convolve(step - LAG)
        slope_ref[...] = slopes[...]

    @pl.when(step == blocks + LAG - 1)
    def _():
        own_pos, npos = grad_ref.shape
        embed = sums[...].T[:npos, :].astype(jnp.bfloat16).astype(jnp.float32)
        rest = grad_ref[...]
        parts = []
        for _ in range(3):
            part = rest.astype(jnp.bfloat16).astype(jnp.float32)
            parts.append(part)
            rest = rest - part
        grads = jnp.concatenate(
            parts + [jnp.zeros((npos - 3 * own_pos, npos), jnp.float32)], axis=0
        )
        emb_ref[...] = jnp.concatenate(
            [embed[:, :co], grads, jnp.zeros((npos, SLOT - co - npos), jnp.float32)], axis=1
        ).astype(jnp.bfloat16)


def stem_and_conv(n, payload, table, weights, pair_grad):
    co = weights.shape[0] // K1
    rows_dev = payload.shape[2] * 2
    rows = n * rows_dev
    npos = rows // BIN_ROWS
    blocks = rows // BLOCK
    whole = lambda i: (0, 0)
    return pl.pallas_call(
        functools.partial(stem_kernel, n, rows_dev, co),
        grid=(blocks + LAG,),
        in_specs=[
            pl.BlockSpec(payload.shape, lambda i: (0, 0, 0)),
            pl.BlockSpec(table.shape, whole),
            pl.BlockSpec(weights.shape, whole),
            pl.BlockSpec(pair_grad.shape, whole),
        ],
        out_specs=[
            pl.BlockSpec((C0, BLOCK), lambda i: (0, jnp.minimum(i, blocks - 1))),
            pl.BlockSpec((co, BLOCK), lambda i: (0, jnp.maximum(i - LAG, 0))),
            pl.BlockSpec((npos, SLOT), whole),
        ],
        out_shape=[
            jax.ShapeDtypeStruct((C0, rows), jnp.bfloat16),
            jax.ShapeDtypeStruct((co, rows), jnp.float32),
            jax.ShapeDtypeStruct((npos, SLOT), jnp.bfloat16),
        ],
        scratch_shapes=[
            pltpu.VMEM((POOL, rows + 2 * PAD), jnp.float32),
            pltpu.VMEM((K1 * co, LAG * BLOCK + rows + 2 * PAD), jnp.float32),
            pltpu.VMEM((C0, BLOCK), jnp.bfloat16),
            pltpu.VMEM((128, 128), jnp.float32),
            pltpu.VMEM((POOL * CHUNK, BLOCK), jnp.float32),
            pltpu.VMEM((POOL * CHUNK, BLOCK), jnp.float32),
            pltpu.VMEM((co, BLOCK), jnp.float32),
        ],
        compiler_params=params(36),
        name="stem_and_conv",
    )(payload, table, weights, pair_grad)


WIDE = K1 * C0 + 2 * PC
PARTS = ((0, K1 * C0), (K1 * C0, K1 * C0 + PC), (K1 * C0 + PC, WIDE))
CODED = WIDE + 128


def encode(values, out_ref):
    exponents = []
    for (begin, end), x in zip(PARTS, values):
        top = jnp.maximum(jnp.max(jnp.abs(x), axis=1, keepdims=True), 1e-30)
        exponent = jnp.floor(jnp.log2(32000.0 / top))
        scaled = jnp.floor(x * jnp.exp2(exponent) + 0.5)
        out_ref[:, begin:end] = scaled.astype(jnp.int32).astype(jnp.int16)
        exponents.append(exponent)
    lane = lax.broadcasted_iota(jnp.int32, (out_ref.shape[0], 128), 1)
    packed = jnp.where(lane == 0, exponents[0], jnp.where(lane == 1, exponents[1], exponents[2]))
    out_ref[:, WIDE:] = packed.astype(jnp.int32).astype(jnp.int16)


def decode(ref):
    exponents = ref[:, WIDE:].astype(jnp.int32).astype(jnp.float32)
    return [
        ref[:, begin:end].astype(jnp.int32).astype(jnp.float32) * jnp.exp2(-exponents[:, at : at + 1])
        for at, (begin, end) in enumerate(PARTS)
    ]


def half_gradient(half, dconv, qk_ref, pooled_ref, out_ref, shifted):
    size = out_ref.shape[0]
    held = dconv.shape[1]
    rows = pooled_ref.shape[1]
    shifted[K1 * held :, :] = jnp.zeros((shifted.shape[0] - K1 * held, rows), jnp.bfloat16)
    for first in range(0, rows, BLOCK):
        near = dconv[half, :, first : first + BLOCK + 2 * PAD]
        for tap in range(K1):
            begin = PAD - tap + K1 // 2
            shifted[tap * held : (tap + 1) * held, first : first + BLOCK] = near[
                :, begin : begin + BLOCK
            ]
    product = lax.dot_general(
        pooled_ref[...], shifted[...], (((1,), (1,)), ((), ())), preferred_element_type=jnp.float32
    ).T
    conv = jnp.concatenate(
        [product[tap * held : tap * held + size, :] for tap in range(K1)], axis=1
    )
    if out_ref.dtype == jnp.int16:
        qk = qk_ref[half]
        encode((conv, qk[:, :PC], qk[:, PC:]), out_ref)
    else:
        out_ref[:, : K1 * C0] = conv
        out_ref[:, K1 * C0 :] = qk_ref[half]


def send_kernel(n, emb_ref, proj_ref, slope_ref, pooled_ref, send_ref, dconv_ref, qk_ref, shifted):
    co, rows = slope_ref.shape
    size, held = co // 2, dconv_ref.shape[1]
    npos = rows // BIN_ROWS
    own_pos = npos // n
    scale = PC**-0.5
    me = lax.axis_index("seq")
    both = jnp.dot(
        jnp.concatenate([emb_ref[slot] for slot in range(n)], axis=1),
        proj_ref[...],
        preferred_element_type=jnp.float32,
    )
    query, keys = both[:, :PC], both[:, PC:]
    pieces = []
    for slab in range(n):
        block = emb_ref[slab].astype(jnp.float32)
        total = block[:own_pos]
        for part in range(1, 3):
            total = total + block[part * own_pos : (part + 1) * own_pos]
        pieces.append(total)
    grad = jnp.concatenate(pieces, axis=0)[:, co : co + npos]
    dquery = jnp.dot(grad, keys, precision=HIGH, preferred_element_type=jnp.float32) * scale
    dkeys = (
        lax.dot_general(
            grad, query, (((0,), (0,)), ((), ())), precision=HIGH,
            preferred_element_type=jnp.float32,
        )
        * scale
    )
    cotangent = jnp.concatenate([dquery, dkeys], axis=1)
    own = pl.ds(pl.multiple_of(me * SLOT, SLOT), SLOT)
    dembed = lax.dot_general(
        proj_ref[own, :].astype(jnp.float32), cotangent,
        (((1,), (1,)), ((), ())), precision=HIGH, preferred_element_type=jnp.float32,
    ) * (1.0 / BIN_ROWS)
    qk = lax.dot_general(
        emb_ref[me].astype(jnp.float32), cotangent, (((0,), (0,)), ((), ())),
        precision=HIGH, preferred_element_type=jnp.float32,
    )
    edge = jnp.zeros((held, PAD), jnp.bfloat16)
    for half in range(2):
        channels = slice(half * size, (half + 1) * size)
        qk_ref[half] = qk[channels]
        dconv_ref[half, :, :PAD] = edge
        dconv_ref[half, :, PAD + rows :] = edge
        for pos in range(npos):
            part = slope_ref[channels, pos * BIN_ROWS : (pos + 1) * BIN_ROWS] * dembed[
                channels, pos : pos + 1
            ]
            if held > size:
                part = jnp.concatenate(
                    [part, jnp.zeros((held - size, BIN_ROWS), jnp.float32)], axis=0
                )
            dconv_ref[half, :, PAD + pos * BIN_ROWS : PAD + (pos + 1) * BIN_ROWS] = part.astype(
                jnp.bfloat16
            )
    half_gradient(1 - lax.axis_index("dp") % 2, dconv_ref, qk_ref, pooled_ref, send_ref, shifted)


def keep_kernel(dconv_ref, qk_ref, pooled_ref, keep_ref, shifted):
    half_gradient(lax.axis_index("dp") % 2, dconv_ref, qk_ref, pooled_ref, keep_ref, shifted)


def send_half(n, embed, proj, slope, pooled):
    co, rows = slope.shape
    size = co // 2
    held = -(-size // 16) * 16
    return pl.pallas_call(
        functools.partial(send_kernel, n),
        out_shape=[
            jax.ShapeDtypeStruct((size, CODED), jnp.int16),
            jax.ShapeDtypeStruct((2, held, rows + 2 * PAD), jnp.bfloat16),
            jax.ShapeDtypeStruct((2, size, 2 * PC), jnp.float32),
        ],
        scratch_shapes=[pltpu.VMEM((256, rows), jnp.bfloat16)],
        compiler_params=params(32),
        name="send_half",
    )(embed, proj, slope, pooled)


def keep_half(dconv, qk, pooled):
    size, rows = qk.shape[1], pooled.shape[1]
    return pl.pallas_call(
        keep_kernel,
        out_shape=jax.ShapeDtypeStruct((size, WIDE), jnp.float32),
        scratch_shapes=[pltpu.VMEM((256, rows), jnp.bfloat16)],
        compiler_params=params(32),
        cost_estimate=pl.CostEstimate(
            flops=2 * K1 * size * C0 * rows, bytes_accessed=12 * MIB, transcendentals=0
        ),
        name="keep_half",
    )(dconv, qk, pooled)


def add_kernel(a_ref, b_ref, out_ref):
    if a_ref.dtype == jnp.int16:
        a = decode(a_ref)
    else:
        a = [a_ref[:, begin:end] for begin, end in PARTS]
    encode([x + y for x, y in zip(a, decode(b_ref))], out_ref)


def add_half(a, b):
    return pl.pallas_call(
        add_kernel,
        out_shape=jax.ShapeDtypeStruct(b.shape, jnp.int16),
        compiler_params=params(8),
        name="add_half",
    )(a, b)


def join_kernel(mine_ref, other_ref, conv_ref, query_ref, key_ref):
    size = mine_ref.shape[0]
    core = lax.axis_index("dp") % 2
    for half, ref in ((core, mine_ref), (1 - core, other_ref)):
        rows = pl.ds(pl.multiple_of(half * size, 8), size)
        for x, out_ref in zip(decode(ref), (conv_ref, query_ref, key_ref)):
            out_ref[rows, :] = x


def join(mine, other):
    co = 2 * mine.shape[0]
    return pl.pallas_call(
        join_kernel,
        out_shape=[
            jax.ShapeDtypeStruct((co, K1 * C0), jnp.float32),
            jax.ShapeDtypeStruct((co, PC), jnp.float32),
            jax.ShapeDtypeStruct((co, PC), jnp.float32),
        ],
        compiler_params=params(8),
        name="join",
    )(mine, other)


def body(bases, stem_table, conv_weight, query_weight, key_weight, pair_grad):
    n = lax.axis_size("seq")
    rows_dev = bases.shape[1] // POOL

    own = bases.astype(jnp.bfloat16).reshape(2, rows_dev // 2, POOL).transpose(0, 2, 1)
    payload = gather_xor(own.reshape(2 * POOL, rows_dev // 2), "seq")

    first_table = jnp.pad(
        stem_table.transpose(2, 1, 0), ((0, 0), (0, 0), (1, WINDOW - 1 - K0))
    ).reshape(C0, 4 * WINDOW)
    first_table = jnp.pad(first_table, ((0, 0), (0, 128 - 4 * WINDOW))).astype(jnp.float32)
    table, weights, proj = prepare(n, first_table, conv_weight, query_weight, key_weight)

    pooled, slope, embed = stem_and_conv(n, payload, table, weights, pair_grad[0])
    embed_all = gather_direct(embed, "seq")
    send, dconv, qk = send_half(n, embed_all, proj, slope, pooled)
    received = swap(send, "dp", 1)
    keep = keep_half(dconv, qk, pooled)

    mine = add_half(keep, received)
    bit = 2
    while bit < lax.axis_size("dp"):
        mine = add_half(mine, swap(mine, "dp", bit))
        bit *= 2
    return tuple(join(mine, swap(mine, "dp", 1)))


def solution(mesh):
    return jax.shard_map(
        body,
        mesh=mesh,
        in_specs=(P("dp", "seq"), P(), P("seq", None), P(), P(), P("dp", "seq", None)),
        out_specs=(P("seq", None), P("seq", None), P("seq", None)),
        check_vma=False,
    )
```

time: 607 us -> 82.2 us (0.14)
  waiting for transfers between devices: 476 us -> 15.5 us
  Pallas kernels: 0 us -> 40.6 us
  blocking collectives: 49.2 us -> 12.9 us
  matrix products: 29.5 us -> 0 us
  local copies, waits for them, and re-layouts: 22.5 us -> 1.39 us
  between operations: 15 us -> 0.79 us
    unnamed x7 -> x0, waiting for transfers between devices: 192 us -> none
    reduce_scatter x2 -> x0, waiting for transfers between devices: 126 us -> none  [the longest x1 63.9 us: body(): lax.psum_scatter(jnp.dot(embed_f.T, dkeys, precision=high), 'seq', scatte...]
    psum x2 -> x0, waiting for transfers between devices: 81.8 us -> none  [body(): lax.psum((conv_part, query_grad, key_grad), 'dp')]
    all_gather x1 -> x0, waiting for transfers between devices: 73.9 us -> none  [body(): lax.all_gather(conv_weight, 'seq', axis=0, tiled=True)]
    pallas_call x0 -> x7, Pallas kernels: none -> 40.6 us  [the longest x1 32.4 us: stem_and_conv(): pl.pallas_call(functools.partial(stem_kernel, n, rows_dev, co), grid=(blo...]
    all_gather x1 -> x0, blocking collectives: 30.3 us -> none  [body(): embed_all = lax.all_gather(embed_own, 'seq', axis=0, tiled=True)]
    dot_general x19 -> x0, matrix products: 29.5 us -> none  [the longest x5 11.3 us: body(): lax.dot_general(dconv, padded[t:t + rows], (((0,), (0,)), ((), ())), pref...]
    unnamed x17 -> x9, local copies, waits for them, and re-layouts: 22 us -> 0.92 us
  transfers between devices with their start and end apart: 10 -> 6, of which waited for: 7 -> 5; matrix products, arithmetic and copies ran while one was open for 4% -> 1% of each run, Pallas kernels for 0% -> 3%
where the time goes in v2:
time: 82.2 us; the launch traced here: 82 us
  Pallas kernels  40.6 us (49%)
  waiting for transfers between devices  15.5 us (19%)
  blocking collectives  12.9 us (16%)
  starting transfers between devices  9.86 us (12%)
  local copies, waits for them, and re-layouts  1.39 us (2%)
  other arithmetic  0.9 us (1%)
    pallas_call x1, Pallas kernels, stem_and_conv(): pl.pallas_call(functools.partial(stem_kernel, n, rows_dev, co), grid=(blo...  32.4 us
    ppermute x6, waiting for transfers between devices, swap(): return lax.ppermute(x, axis, [(i, i ^ bit) for i in range(size)])  15.5 us
    all_to_all x1, blocking collectives, gather_direct(): lax.all_to_all(jnp.broadcast_to(x[None], (lax.axis_size(axis),) + x.shape...  12.9 us
    ppermute x6, starting transfers between devices, swap(): return lax.ppermute(x, axis, [(i, i ^ bit) for i in range(size)])  9.86 us
    pallas_call x1, Pallas kernels, send_half(): pl.pallas_call(functools.partial(send_kernel, n), out_shape=[jax.ShapeDty...  3.54 us
    pallas_call x1, Pallas kernels, keep_half(): pl.pallas_call(keep_kernel, out_shape=jax.ShapeDtypeStruct((size, WIDE),...  2.07 us
  transfers between devices with their start and end apart: 6, of which 5 were waited for; matrix products, arithmetic and copies ran while one was open for 1% of the time, Pallas kernels for 3%

profile of v2, /device:TPU:0, one launch (start us, length us, event | category | flops | bytes accessed | tf_op | source)
XLA Modules:
  0.0 82.0 jit_solution(3064506635162084353)
XLA Ops:
  0.6 0.0 copy-start.2
  0.6 0.0 copy-start.1
  0.7 0.0 copy-start
  0.7 0.9 %convert_reduce_fusion = bf16[4096]{0:T(1024)(128)(2,1)S(1)} fusion(s32[1,4096]{1,0:T(1,128)} %param.6), kind=kLoop, calls=%fused_computation.5 | loop fusion | flops 4096 | bytes 24576 | tf_op jit(solution)/shard_map/convert_element_type | solution.py:445
  1.5 0.2 reshape.13
  1.7 0.1 copy.11
  1.8 0.0 copy-start.3
  1.8 3.0 %collective-permute-start = (bf16[1,16,256]{2,1,0:T(8,128)(2,1)S(1)}, bf16[1,16,256]{2,1,0:T(8,128)(2,1)S(1)}, u32[]{:S(2)}, u32[]{:S(2)}) collective-permute-start(bf16[1,16,256]{2,1,0:T(8,128)(2,1)S(1)} %bitcast.11), channel_id=1, source_target_pairs={{0,1},{1,0},{2,3},{3,2},{4,5},{5,4},{6,7},{7,6},{8,9},{9,8},{10,11... | collective-permute-start | bytes 24584 | tf_op jit(solution)/shard_map/ppermute | solution.py:36
  4.8 1.6 %collective-permute-done = bf16[1,16,256]{2,1,0:T(8,128)(2,1)S(1)} collective-permute-done((bf16[1,16,256]{2,1,0:T(8,128)(2,1)S(1)}, bf16[1,16,256]{2,1,0:T(8,128)(2,1)S(1)}, u32[]{:S(2)}, u32[]{:S(2)}) %collective-permute-start) | collective-permute-done | bytes 8224 | tf_op jit(solution)/shard_map/ppermute | solution.py:36
  6.4 2.1 %collective-permute-start.1 = (bf16[2,16,256]{2,1,0:T(8,128)(2,1)S(1)}, bf16[2,16,256]{2,1,0:T(8,128)(2,1)S(1)}, u32[]{:S(2)}, u32[]{:S(2)}) collective-permute-start(bf16[2,16,256]{2,1,0:T(8,128)(2,1)S(1)} %pad_maximum_fusion.2), channel_id=1, source_target_pairs={{0,2},{1,3},{2,0},{3,1},{4,6},{5,7},{6,4},{7,5},{8,10},{9,11},{10,... | collective-permute-start | bytes 49160 | tf_op jit(solution)/shard_map/ppermute | solution.py:36
  8.5 0.9 %copy.15 = bf16[15,4,768]{2,0,1:T(8,128)(2,1)S(1)} copy(bf16[15,4,768]{2,1,0:T(4,128)(2,1)} %param.7) | data formatting | bytes 184320 | tf_op args[1]
  9.5 0.2 copy.13
  9.6 0.6 collective-permute-done.1
  10.2 3.0 %collective-permute-start.2 = (bf16[4,16,256]{2,1,0:T(8,128)(2,1)S(1)}, bf16[4,16,256]{2,1,0:T(8,128)(2,1)S(1)}, u32[]{:S(2)}, u32[]{:S(2)}) collective-permute-start(bf16[4,16,256]{2,1,0:T(8,128)(2,1)S(1)} %pad_maximum_fusion.1), channel_id=1, source_target_pairs={{0,4},{1,5},{2,6},{3,7},{4,0},{5,1},{6,2},{7,3},{8,12},{9,13},{10,... | collective-permute-start | bytes 98312 | tf_op jit(solution)/shard_map/ppermute | solution.py:36
  13.3 0.0 copy-done.2
  13.3 0.0 copy-done.1
  13.3 0.0 copy-done
  13.3 0.5 prepare.1
  13.8 1.3 %collective-permute-done.2 = bf16[4,16,256]{2,1,0:T(8,128)(2,1)S(1)} collective-permute-done((bf16[4,16,256]{2,1,0:T(8,128)(2,1)S(1)}, bf16[4,16,256]{2,1,0:T(8,128)(2,1)S(1)}, u32[]{:S(2)}, u32[]{:S(2)}) %collective-permute-start.2) | collective-permute-done | bytes 32800 | tf_op jit(solution)/shard_map/ppermute | solution.py:36
  15.2 0.0 copy-done.3
  15.2 32.4 %stem_and_conv.1 = (bf16[768,4096]{1,0:T(8,128)(2,1)S(1)}, f32[96,4096]{1,0:T(8,128)S(1)}, bf16[16,128]{1,0:T(8,128)(2,1)S(1)}) custom-call(bf16[8,16,256]{2,1,0:T(8,128)(2,1)S(1)} %pad_maximum_fusion.pay_ref, bf16[6144,128]{1,0:T(8,128)(2,1)S(1)} %get-tuple-element.12.table, bf16[480,768]{1,0:T(8,128)(2,1)S(1)} %get-tuple-element.13.weights, ...), custom_call_target="tpu_custom_call" | custom-call | tf_op jit(solution)/shard_map/stem_and_conv/pallas_call | solution.py:222
  47.6 12.9 %all_to_all.5.emb_ref = bf16[8,16,128]{2,1,0:T(8,128)(2,1)S(1)} all-to-all(bf16[8,16,128]{2,1,0:T(8,128)(2,1)S(1)} %broadcast_in_dim.2), channel_id=1, replica_groups=mesh['dp'=4,'seq'=8] {'seq'}, dimensions={0} | all-to-all | bytes 65536 | tf_op jit(solution)/shard_map/all_to_all | solution.py:49
  60.4 3.5 %send_half.1 = (s16[48,4224]{1,0:T(8,128)(2,1)S(1)}, bf16[2,48,4352]{2,1,0:T(8,128)(2,1)S(1)}, f32[2,48,256]{2,1,0:T(8,128)S(1)}) custom-call(bf16[8,16,128]{2,1,0:T(8,128)(2,1)S(1)} %all_to_all.5.emb_ref, bf16[1024,256]{1,0:T(8,128)(2,1)S(1)} %get-tuple-element.15.proj_ref, f32[96,4096]{1,0:T(8,128)S(1)} %get-tuple-element.16.slope_ref, ...), custom_call_target="tpu_custom_call" | custom-call | tf_op jit(solution)/shard_map/send_half/pallas_call | solution.py:374
  64.0 0.1 collective-permute-start.3
  64.1 2.1 %keep_half.1.a_ref = f32[48,4096]{1,0:T(8,128)S(1)} custom-call(bf16[2,48,4352]{2,1,0:T(8,128)(2,1)S(1)} %get-tuple-element.18.dconv_ref, f32[2,48,256]{2,1,0:T(8,128)S(1)} %get-tuple-element.19.qk_ref, bf16[768,4096]{1,0:T(8,128)(2,1)S(1)} %get-tuple-element.17.pooled_ref), custom_call_target="tpu_custom_call" | custom-call | flops 1509949440 | bytes 12582912 | tf_op jit(solution)/shard_map/keep_half/pallas_call | solution.py:389
  66.1 0.0 collective-permute-done.3.b_ref
  66.1 0.4 add_half.2.a_ref
  66.5 1.6 %collective-permute-start.4 = (s16[48,4224]{1,0:T(8,128)(2,1)S(1)}, s16[48,4224]{1,0:T(8,128)(2,1)S(1)}, u32[]{:S(2)}, u32[]{:S(2)}) collective-permute-start(s16[48,4224]{1,0:T(8,128)(2,1)S(1)} %add_half.2.a_ref), channel_id=1, source_target_pairs={{0,16},{8,24},{16,0},{24,8},{1,17},{9,25},{17,1},{25,9},{2,18},{10... | collective-permute-start | bytes 1216520 | tf_op jit(solution)/shard_map/ppermute | solution.py:36
  68.1 10.2 %collective-permute-done.4.b_ref = s16[48,4224]{1,0:T(8,128)(2,1)S(1)} collective-permute-done((s16[48,4224]{1,0:T(8,128)(2,1)S(1)}, s16[48,4224]{1,0:T(8,128)(2,1)S(1)}, u32[]{:S(2)}, u32[]{:S(2)}) %collective-permute-start.4) | collective-permute-done | bytes 405536 | tf_op jit(solution)/shard_map/ppermute | solution.py:36
  78.4 0.5 add_half.3.mine_ref
  78.8 0.1 collective-permute-start.5
  78.9 1.7 %collective-permute-done.5.other_ref = s16[48,4224]{1,0:T(8,128)(2,1)S(1)} collective-permute-done((s16[48,4224]{1,0:T(8,128)(2,1)S(1)}, s16[48,4224]{1,0:T(8,128)(2,1)S(1)}, u32[]{:S(2)}, u32[]{:S(2)}) %collective-permute-start.5) | collective-permute-done | bytes 405536 | tf_op jit(solution)/shard_map/ppermute | solution.py:36
  80.6 1.3 %join.1 = (f32[96,3840]{1,0:T(8,128)}, f32[96,128]{1,0:T(8,128)}, f32[96,128]{1,0:T(8,128)}) custom-call(s16[48,4224]{1,0:T(8,128)(2,1)S(1)} %add_half.3.mine_ref, s16[48,4224]{1,0:T(8,128)(2,1)S(1)} %collective-permute-done.5.other_ref), custom_call_target="tpu_custom_call" | custom-call | tf_op jit(solution)/shard_map/join/pallas_call | solution.py:429
  (6 shorter events, 0.1 us)
Async XLA Ops:
  0.6 12.7 %copy-start.2 = (bf16[768,128]{1,0:T(8,128)(2,1)S(1)}, bf16[768,128]{1,0:T(8,128)(2,1)}, u32[]{:S(2)}) copy-start(bf16[768,128]{1,0:T(8,128)(2,1)} %wk_ref.1) | copy-start | bytes 589828
  0.6 12.7 %copy-start.1 = (bf16[768,128]{1,0:T(8,128)(2,1)S(1)}, bf16[768,128]{1,0:T(8,128)(2,1)}, u32[]{:S(2)}) copy-start(bf16[768,128]{1,0:T(8,128)(2,1)} %wq_ref.1) | copy-start | bytes 589828
  0.7 12.7 %copy-start = (bf16[96,3840]{1,0:T(8,128)(2,1)S(1)}, bf16[96,3840]{1,0:T(8,128)(2,1)}, u32[]{:S(2)}) copy-start(bf16[96,3840]{1,0:T(8,128)(2,1)} %w_ref.1) | copy-start | bytes 2211844
  1.8 13.4 %copy-start.3 = (f32[1,2,16]{2,1,0:T(2,128)S(1)}, f32[1,2,16]{2,1,0:T(2,128)}, u32[]{:S(2)}) copy-start(f32[1,2,16]{2,1,0:T(2,128)} %param.11) | copy-start | bytes 388
  1.8 4.6 %collective-permute-start = (bf16[1,16,256]{2,1,0:T(8,128)(2,1)S(1)}, bf16[1,16,256]{2,1,0:T(8,128)(2,1)S(1)}, u32[]{:S(2)}, u32[]{:S(2)}) collective-permute-start(bf16[1,16,256]{2,1,0:T(8,128)(2,1)S(1)} %bitcast.11), channel_id=1, source_target_pairs={{0,1},{1,0},{2,3},{3,2},{4,5},{5,4},{6,7},{7,6},{8,9},{9,8},{10,11... | collective-permute-start | bytes 24584 | tf_op jit(solution)/shard_map/ppermute | solution.py:36
  6.4 3.8 %collective-permute-start.1 = (bf16[2,16,256]{2,1,0:T(8,128)(2,1)S(1)}, bf16[2,16,256]{2,1,0:T(8,128)(2,1)S(1)}, u32[]{:S(2)}, u32[]{:S(2)}) collective-permute-start(bf16[2,16,256]{2,1,0:T(8,128)(2,1)S(1)} %pad_maximum_fusion.2), channel_id=1, source_target_pairs={{0,2},{1,3},{2,0},{3,1},{4,6},{5,7},{6,4},{7,5},{8,10},{9,11},{10,... | collective-permute-start | bytes 49160 | tf_op jit(solution)/shard_map/ppermute | solution.py:36
  10.2 4.9 %collective-permute-start.2 = (bf16[4,16,256]{2,1,0:T(8,128)(2,1)S(1)}, bf16[4,16,256]{2,1,0:T(8,128)(2,1)S(1)}, u32[]{:S(2)}, u32[]{:S(2)}) collective-permute-start(bf16[4,16,256]{2,1,0:T(8,128)(2,1)S(1)} %pad_maximum_fusion.1), channel_id=1, source_target_pairs={{0,4},{1,5},{2,6},{3,7},{4,0},{5,1},{6,2},{7,3},{8,12},{9,13},{10,... | collective-permute-start | bytes 98312 | tf_op jit(solution)/shard_map/ppermute | solution.py:36
  64.0 2.2 %collective-permute-start.3 = (s16[48,4224]{1,0:T(8,128)(2,1)S(1)}, s16[48,4224]{1,0:T(8,128)(2,1)S(1)}, u32[]{:S(2)}, u32[]{:S(2)}) collective-permute-start(s16[48,4224]{1,0:T(8,128)(2,1)S(1)} %get-tuple-element.20), channel_id=1, source_target_pairs={{0,8},{8,0},{16,24},{24,16},{1,9},{9,1},{17,25},{25,17},{2,10},{10... | collective-permute-start | bytes 1216520 | tf_op jit(solution)/shard_map/ppermute | solution.py:36
  66.5 11.8 %collective-permute-start.4 = (s16[48,4224]{1,0:T(8,128)(2,1)S(1)}, s16[48,4224]{1,0:T(8,128)(2,1)S(1)}, u32[]{:S(2)}, u32[]{:S(2)}) collective-permute-start(s16[48,4224]{1,0:T(8,128)(2,1)S(1)} %add_half.2.a_ref), channel_id=1, source_target_pairs={{0,16},{8,24},{16,0},{24,8},{1,17},{9,25},{17,1},{25,9},{2,18},{10... | collective-permute-start | bytes 1216520 | tf_op jit(solution)/shard_map/ppermute | solution.py:36
  78.8 1.8 %collective-permute-start.5 = (s16[48,4224]{1,0:T(8,128)(2,1)S(1)}, s16[48,4224]{1,0:T(8,128)(2,1)S(1)}, u32[]{:S(2)}, u32[]{:S(2)}) collective-permute-start(s16[48,4224]{1,0:T(8,128)(2,1)S(1)} %add_half.3.mine_ref), channel_id=1, source_target_pairs={{0,8},{8,0},{16,24},{24,16},{1,9},{9,1},{17,25},{25,17},{2,10},{10... | collective-permute-start | bytes 1216520 | tf_op jit(solution)/shard_map/ppermute | solution.py:36

commit v3 on v2

--- a/solution.py
+++ b/solution.py
@@ -87,7 +87,8 @@
 
 
 def stem_kernel(
-    n, rows_dev, co, pay_ref, table, weights, grad_ref, p_ref, slope_ref, emb_ref, bases, ybuf, prev, sums, sa, sb, slopes
+    n, rows_dev, co, pay_ref, table_ref, weights_ref, grad_ref, p_ref, slope_ref, emb_ref,
+    table, weights, bases, ybuf, prev, sums, sa, sb, slopes
 ):
     step = pl.program_id(0)
     rows = n * rows_dev
@@ -135,6 +136,8 @@
             first = PAD + slab * rows_dev
             bases[:, first : first + half] = block[:POOL]
             bases[:, first + half : first + 2 * half] = block[POOL:]
+        table[...] = table_ref[...]
+        weights[...] = weights_ref[...]
         ybuf[:, front + rows :] = jnp.zeros((K1 * co, PAD), jnp.float32)
         prev[...] = jnp.zeros(prev.shape, jnp.bfloat16)
         sums[...] = jnp.zeros(sums.shape, jnp.float32)
@@ -239,6 +242,8 @@
             jax.ShapeDtypeStruct((npos, SLOT), jnp.bfloat16),
         ],
         scratch_shapes=[
+            pltpu.VMEM(table.shape, jnp.bfloat16),
+            pltpu.VMEM(weights.shape, jnp.bfloat16),
             pltpu.VMEM((POOL, rows + 2 * PAD), jnp.float32),
             pltpu.VMEM((K1 * co, LAG * BLOCK + rows + 2 * PAD), jnp.float32),
             pltpu.VMEM((C0, BLOCK), jnp.bfloat16),

time: 82.2 us -> 82.6 us (level)
  no operation moved by 1% of the time
where the time goes in v3:
time: 82.6 us; the launch traced here: 82.3 us
  Pallas kernels  41 us (50%)
  waiting for transfers between devices  15.6 us (19%)
  blocking collectives  12.9 us (16%)
  starting transfers between devices  9.83 us (12%)
  local copies, waits for them, and re-layouts  1.39 us (2%)
  other arithmetic  0.9 us (1%)
    pallas_call x1, Pallas kernels, stem_and_conv(): pl.pallas_call(functools.partial(stem_kernel, n, rows_dev, co), grid=(blo...  32.7 us
    ppermute x6, waiting for transfers between devices, swap(): return lax.ppermute(x, axis, [(i, i ^ bit) for i in range(size)])  15.6 us
    all_to_all x1, blocking collectives, gather_direct(): lax.all_to_all(jnp.broadcast_to(x[None], (lax.axis_size(axis),) + x.shape...  12.9 us
    ppermute x6, starting transfers between devices, swap(): return lax.ppermute(x, axis, [(i, i ^ bit) for i in range(size)])  9.83 us
    pallas_call x1, Pallas kernels, send_half(): pl.pallas_call(functools.partial(send_kernel, n), out_shape=[jax.ShapeDty...  3.55 us
    pallas_call x1, Pallas kernels, keep_half(): pl.pallas_call(keep_kernel, out_shape=jax.ShapeDtypeStruct((size, WIDE),...  2.07 us
  transfers between devices with their start and end apart: 6, of which 5 were waited for; matrix products, arithmetic and copies ran while one was open for 1% of the time, Pallas kernels for 3%

profile of v3, /device:TPU:0, one launch (start us, length us, event | category | flops | bytes accessed | tf_op | source)
XLA Modules:
  0.0 82.3 jit_solution(16594178054506919080)
XLA Ops:
  0.6 0.0 copy-start.2
  0.6 0.0 copy-start.1
  0.7 0.0 copy-start
  0.7 0.9 %convert_reduce_fusion = bf16[4096]{0:T(1024)(128)(2,1)S(1)} fusion(s32[1,4096]{1,0:T(1,128)} %param.6), kind=kLoop, calls=%fused_computation.5 | loop fusion | flops 4096 | bytes 24576 | tf_op jit(solution)/shard_map/convert_element_type | solution.py:450
  1.5 0.2 reshape.13
  1.7 0.1 copy.11
  1.8 0.0 copy-start.3
  1.8 3.0 %collective-permute-start = (bf16[1,16,256]{2,1,0:T(8,128)(2,1)S(1)}, bf16[1,16,256]{2,1,0:T(8,128)(2,1)S(1)}, u32[]{:S(2)}, u32[]{:S(2)}) collective-permute-start(bf16[1,16,256]{2,1,0:T(8,128)(2,1)S(1)} %bitcast.11), channel_id=1, source_target_pairs={{0,1},{1,0},{2,3},{3,2},{4,5},{5,4},{6,7},{7,6},{8,9},{9,8},{10,11... | collective-permute-start | bytes 24584 | tf_op jit(solution)/shard_map/ppermute | solution.py:36
  4.8 1.6 %collective-permute-done = bf16[1,16,256]{2,1,0:T(8,128)(2,1)S(1)} collective-permute-done((bf16[1,16,256]{2,1,0:T(8,128)(2,1)S(1)}, bf16[1,16,256]{2,1,0:T(8,128)(2,1)S(1)}, u32[]{:S(2)}, u32[]{:S(2)}) %collective-permute-start) | collective-permute-done | bytes 8224 | tf_op jit(solution)/shard_map/ppermute | solution.py:36
  6.4 2.1 %collective-permute-start.1 = (bf16[2,16,256]{2,1,0:T(8,128)(2,1)S(1)}, bf16[2,16,256]{2,1,0:T(8,128)(2,1)S(1)}, u32[]{:S(2)}, u32[]{:S(2)}) collective-permute-start(bf16[2,16,256]{2,1,0:T(8,128)(2,1)S(1)} %pad_maximum_fusion.2), channel_id=1, source_target_pairs={{0,2},{1,3},{2,0},{3,1},{4,6},{5,7},{6,4},{7,5},{8,10},{9,11},{10,... | collective-permute-start | bytes 49160 | tf_op jit(solution)/shard_map/ppermute | solution.py:36
  8.5 0.9 %copy.15 = bf16[15,4,768]{2,0,1:T(8,128)(2,1)S(1)} copy(bf16[15,4,768]{2,1,0:T(4,128)(2,1)} %param.7) | data formatting | bytes 184320 | tf_op args[1]
  9.5 0.2 copy.13
  9.6 0.6 collective-permute-done.1
  10.2 3.0 %collective-permute-start.2 = (bf16[4,16,256]{2,1,0:T(8,128)(2,1)S(1)}, bf16[4,16,256]{2,1,0:T(8,128)(2,1)S(1)}, u32[]{:S(2)}, u32[]{:S(2)}) collective-permute-start(bf16[4,16,256]{2,1,0:T(8,128)(2,1)S(1)} %pad_maximum_fusion.1), channel_id=1, source_target_pairs={{0,4},{1,5},{2,6},{3,7},{4,0},{5,1},{6,2},{7,3},{8,12},{9,13},{10,... | collective-permute-start | bytes 98312 | tf_op jit(solution)/shard_map/ppermute | solution.py:36
  13.3 0.0 copy-done.2
  13.3 0.0 copy-done.1
  13.3 0.0 copy-done
  13.3 0.5 prepare.1
  13.8 1.3 %collective-permute-done.2 = bf16[4,16,256]{2,1,0:T(8,128)(2,1)S(1)} collective-permute-done((bf16[4,16,256]{2,1,0:T(8,128)(2,1)S(1)}, bf16[4,16,256]{2,1,0:T(8,128)(2,1)S(1)}, u32[]{:S(2)}, u32[]{:S(2)}) %collective-permute-start.2) | collective-permute-done | bytes 32800 | tf_op jit(solution)/shard_map/ppermute | solution.py:36
  15.2 0.0 copy-done.3
  15.2 32.7 %stem_and_conv.1 = (bf16[768,4096]{1,0:T(8,128)(2,1)S(1)}, f32[96,4096]{1,0:T(8,128)S(1)}, bf16[16,128]{1,0:T(8,128)(2,1)S(1)}) custom-call(bf16[8,16,256]{2,1,0:T(8,128)(2,1)S(1)} %pad_maximum_fusion.pay_ref, bf16[6144,128]{1,0:T(8,128)(2,1)S(1)} %get-tuple-element.12.table_ref, bf16[480,768]{1,0:T(8,128)(2,1)S(1)} %get-tuple-element.13.weights_ref, ...), custom_call_target="tpu_custom_call" | custom-call | tf_op jit(solution)/shard_map/stem_and_conv/pallas_call | solution.py:225
  47.9 12.9 %all_to_all.5.emb_ref = bf16[8,16,128]{2,1,0:T(8,128)(2,1)S(1)} all-to-all(bf16[8,16,128]{2,1,0:T(8,128)(2,1)S(1)} %broadcast_in_dim.2), channel_id=1, replica_groups=mesh['dp'=4,'seq'=8] {'seq'}, dimensions={0} | all-to-all | bytes 65536 | tf_op jit(solution)/shard_map/all_to_all | solution.py:49
  60.8 3.6 %send_half.1 = (s16[48,4224]{1,0:T(8,128)(2,1)S(1)}, bf16[2,48,4352]{2,1,0:T(8,128)(2,1)S(1)}, f32[2,48,256]{2,1,0:T(8,128)S(1)}) custom-call(bf16[8,16,128]{2,1,0:T(8,128)(2,1)S(1)} %all_to_all.5.emb_ref, bf16[1024,256]{1,0:T(8,128)(2,1)S(1)} %get-tuple-element.15.proj_ref, f32[96,4096]{1,0:T(8,128)S(1)} %get-tuple-element.16.slope_ref, ...), custom_call_target="tpu_custom_call" | custom-call | tf_op jit(solution)/shard_map/send_half/pallas_call | solution.py:379
  64.3 0.1 collective-permute-start.3
  64.4 2.1 %keep_half.1.a_ref = f32[48,4096]{1,0:T(8,128)S(1)} custom-call(bf16[2,48,4352]{2,1,0:T(8,128)(2,1)S(1)} %get-tuple-element.18.dconv_ref, f32[2,48,256]{2,1,0:T(8,128)S(1)} %get-tuple-element.19.qk_ref, bf16[768,4096]{1,0:T(8,128)(2,1)S(1)} %get-tuple-element.17.pooled_ref), custom_call_target="tpu_custom_call" | custom-call | flops 1509949440 | bytes 12582912 | tf_op jit(solution)/shard_map/keep_half/pallas_call | solution.py:394
  66.5 0.0 collective-permute-done.3.b_ref
  66.5 0.4 add_half.2.a_ref
  66.9 1.6 %collective-permute-start.4 = (s16[48,4224]{1,0:T(8,128)(2,1)S(1)}, s16[48,4224]{1,0:T(8,128)(2,1)S(1)}, u32[]{:S(2)}, u32[]{:S(2)}) collective-permute-start(s16[48,4224]{1,0:T(8,128)(2,1)S(1)} %add_half.2.a_ref), channel_id=1, source_target_pairs={{0,16},{8,24},{16,0},{24,8},{1,17},{9,25},{17,1},{25,9},{2,18},{10... | collective-permute-start | bytes 1216520 | tf_op jit(solution)/shard_map/ppermute | solution.py:36
  68.5 10.3 %collective-permute-done.4.b_ref = s16[48,4224]{1,0:T(8,128)(2,1)S(1)} collective-permute-done((s16[48,4224]{1,0:T(8,128)(2,1)S(1)}, s16[48,4224]{1,0:T(8,128)(2,1)S(1)}, u32[]{:S(2)}, u32[]{:S(2)}) %collective-permute-start.4) | collective-permute-done | bytes 405536 | tf_op jit(solution)/shard_map/ppermute | solution.py:36
  78.7 0.5 add_half.3.mine_ref
  79.2 0.1 collective-permute-start.5
  79.3 1.7 %collective-permute-done.5.other_ref = s16[48,4224]{1,0:T(8,128)(2,1)S(1)} collective-permute-done((s16[48,4224]{1,0:T(8,128)(2,1)S(1)}, s16[48,4224]{1,0:T(8,128)(2,1)S(1)}, u32[]{:S(2)}, u32[]{:S(2)}) %collective-permute-start.5) | collective-permute-done | bytes 405536 | tf_op jit(solution)/shard_map/ppermute | solution.py:36
  81.0 1.3 %join.1 = (f32[96,3840]{1,0:T(8,128)}, f32[96,128]{1,0:T(8,128)}, f32[96,128]{1,0:T(8,128)}) custom-call(s16[48,4224]{1,0:T(8,128)(2,1)S(1)} %add_half.3.mine_ref, s16[48,4224]{1,0:T(8,128)(2,1)S(1)} %collective-permute-done.5.other_ref), custom_call_target="tpu_custom_call" | custom-call | tf_op jit(solution)/shard_map/join/pallas_call | solution.py:434
  (6 shorter events, 0.1 us)
Async XLA Ops:
  0.6 12.7 %copy-start.2 = (bf16[768,128]{1,0:T(8,128)(2,1)S(1)}, bf16[768,128]{1,0:T(8,128)(2,1)}, u32[]{:S(2)}) copy-start(bf16[768,128]{1,0:T(8,128)(2,1)} %wk_ref.1) | copy-start | bytes 589828
  0.6 12.7 %copy-start.1 = (bf16[768,128]{1,0:T(8,128)(2,1)S(1)}, bf16[768,128]{1,0:T(8,128)(2,1)}, u32[]{:S(2)}) copy-start(bf16[768,128]{1,0:T(8,128)(2,1)} %wq_ref.1) | copy-start | bytes 589828
  0.7 12.7 %copy-start = (bf16[96,3840]{1,0:T(8,128)(2,1)S(1)}, bf16[96,3840]{1,0:T(8,128)(2,1)}, u32[]{:S(2)}) copy-start(bf16[96,3840]{1,0:T(8,128)(2,1)} %w_ref.1) | copy-start | bytes 2211844
  1.8 13.4 %copy-start.3 = (f32[1,2,16]{2,1,0:T(2,128)S(1)}, f32[1,2,16]{2,1,0:T(2,128)}, u32[]{:S(2)}) copy-start(f32[1,2,16]{2,1,0:T(2,128)} %param.11) | copy-start | bytes 388
  1.8 4.6 %collective-permute-start = (bf16[1,16,256]{2,1,0:T(8,128)(2,1)S(1)}, bf16[1,16,256]{2,1,0:T(8,128)(2,1)S(1)}, u32[]{:S(2)}, u32[]{:S(2)}) collective-permute-start(bf16[1,16,256]{2,1,0:T(8,128)(2,1)S(1)} %bitcast.11), channel_id=1, source_target_pairs={{0,1},{1,0},{2,3},{3,2},{4,5},{5,4},{6,7},{7,6},{8,9},{9,8},{10,11... | collective-permute-start | bytes 24584 | tf_op jit(solution)/shard_map/ppermute | solution.py:36
  6.4 3.8 %collective-permute-start.1 = (bf16[2,16,256]{2,1,0:T(8,128)(2,1)S(1)}, bf16[2,16,256]{2,1,0:T(8,128)(2,1)S(1)}, u32[]{:S(2)}, u32[]{:S(2)}) collective-permute-start(bf16[2,16,256]{2,1,0:T(8,128)(2,1)S(1)} %pad_maximum_fusion.2), channel_id=1, source_target_pairs={{0,2},{1,3},{2,0},{3,1},{4,6},{5,7},{6,4},{7,5},{8,10},{9,11},{10,... | collective-permute-start | bytes 49160 | tf_op jit(solution)/shard_map/ppermute | solution.py:36
  10.2 4.9 %collective-permute-start.2 = (bf16[4,16,256]{2,1,0:T(8,128)(2,1)S(1)}, bf16[4,16,256]{2,1,0:T(8,128)(2,1)S(1)}, u32[]{:S(2)}, u32[]{:S(2)}) collective-permute-start(bf16[4,16,256]{2,1,0:T(8,128)(2,1)S(1)} %pad_maximum_fusion.1), channel_id=1, source_target_pairs={{0,4},{1,5},{2,6},{3,7},{4,0},{5,1},{6,2},{7,3},{8,12},{9,13},{10,... | collective-permute-start | bytes 98312 | tf_op jit(solution)/shard_map/ppermute | solution.py:36
  64.3 2.1 %collective-permute-start.3 = (s16[48,4224]{1,0:T(8,128)(2,1)S(1)}, s16[48,4224]{1,0:T(8,128)(2,1)S(1)}, u32[]{:S(2)}, u32[]{:S(2)}) collective-permute-start(s16[48,4224]{1,0:T(8,128)(2,1)S(1)} %get-tuple-element.20), channel_id=1, source_target_pairs={{0,8},{8,0},{16,24},{24,16},{1,9},{9,1},{17,25},{25,17},{2,10},{10... | collective-permute-start | bytes 1216520 | tf_op jit(solution)/shard_map/ppermute | solution.py:36
  66.9 11.8 %collective-permute-start.4 = (s16[48,4224]{1,0:T(8,128)(2,1)S(1)}, s16[48,4224]{1,0:T(8,128)(2,1)S(1)}, u32[]{:S(2)}, u32[]{:S(2)}) collective-permute-start(s16[48,4224]{1,0:T(8,128)(2,1)S(1)} %add_half.2.a_ref), channel_id=1, source_target_pairs={{0,16},{8,24},{16,0},{24,8},{1,17},{9,25},{17,1},{25,9},{2,18},{10... | collective-permute-start | bytes 1216520 | tf_op jit(solution)/shard_map/ppermute | solution.py:36
  79.2 1.8 %collective-permute-start.5 = (s16[48,4224]{1,0:T(8,128)(2,1)S(1)}, s16[48,4224]{1,0:T(8,128)(2,1)S(1)}, u32[]{:S(2)}, u32[]{:S(2)}) collective-permute-start(s16[48,4224]{1,0:T(8,128)(2,1)S(1)} %add_half.3.mine_ref), channel_id=1, source_target_pairs={{0,8},{8,0},{16,24},{24,16},{1,9},{9,1},{17,25},{25,17},{2,10},{10... | collective-permute-start | bytes 1216520 | tf_op jit(solution)/shard_map/ppermute | solution.py:36

commit v4 on v3

--- a/solution.py
+++ b/solution.py
@@ -15,7 +15,7 @@
 POOL = 8
 BIN_ROWS = 256
 WINDOW = 24
-CHUNK = 128
+CHUNK = 64
 BLOCK = 512
 LAG = 3
 PAD = 128
@@ -61,7 +61,7 @@
             first = (chunk * POOL + pos) * CHUNK
             table_ref[first : first + CHUNK, :] = shifted.astype(jnp.bfloat16)
     for tap in range(K1):
-        weights_ref[tap * co : (tap + 1) * co, :] = w_ref[:, tap * C0 : (tap + 1) * C0]
+        weights_ref[tap * co : (tap + 1) * co, :] = w_ref[:, tap * C0 : (tap + 1) * C0] * 0.5
     for slot in range(n):
         rows = slice(slot * co, (slot + 1) * co)
         proj_ref[slot * SLOT : slot * SLOT + co, :PC] = wq_ref[rows, :]
@@ -88,7 +88,7 @@
 
 def stem_kernel(
     n, rows_dev, co, pay_ref, table_ref, weights_ref, grad_ref, p_ref, slope_ref, emb_ref,
-    table, weights, bases, ybuf, prev, sums, sa, sb, slopes
+    table, weights, bases, ybuf, prev, sums, sa, sb, slopes, codes
 ):
     step = pl.program_id(0)
     rows = n * rows_dev
@@ -156,35 +156,39 @@
         ).astype(jnp.bfloat16)
         convolve(step - LAG)
         taps(step - 1)
-        stage = (sa, sb)
-
-        def multiply(chunk, at):
-            stage[chunk % 2][:, at : at + piece] = jnp.dot(
-                table[chunk * POOL * CHUNK : (chunk + 1) * POOL * CHUNK, :],
-                onehot[:, at : at + piece],
+        codes[...] = onehot
+
+        def multiply(chunk, at, stage):
+            first = pl.multiple_of(chunk * (POOL * CHUNK), POOL * CHUNK)
+            stage[...] = jnp.dot(
+                table[pl.ds(first, POOL * CHUNK), :],
+                codes[:, at : at + piece],
                 preferred_element_type=jnp.float32,
             )
 
-        def pool(chunk, at):
-            stem = stage[chunk % 2]
+        def pool(chunk, at, stage):
             for row in range(0, CHUNK, 16):
-                most = least = stem[row : row + 16, at : at + piece]
+                most = least = stage[row : row + 16, :]
                 for pos in range(1, POOL):
-                    part = stem[pos * CHUNK + row : pos * CHUNK + row + 16, at : at + piece]
+                    part = stage[pos * CHUNK + row : pos * CHUNK + row + 16, :]
                     most = jnp.maximum(most, part)
                     least = jnp.minimum(least, part)
-                pooled = (0.5 * jnp.maximum(twice_gelu(most), twice_gelu(least))).astype(jnp.bfloat16)
-                to = chunk * CHUNK + row
-                prev[to : to + 16, at : at + piece] = pooled
+                to = pl.multiple_of(chunk * CHUNK + row, 16)
+                prev[pl.ds(to, 16), at : at + piece] = jnp.maximum(
+                    twice_gelu(most), twice_gelu(least)
+                ).astype(jnp.bfloat16)
 
         chunks = C0 // CHUNK
-        for at in range(0, BLOCK, piece):
-            multiply(0, at)
-        for chunk in range(chunks):
-            for at in range(0, BLOCK, piece):
-                if chunk + 1 < chunks:
-                    multiply(chunk + 1, at)
-                pool(chunk, at)
+        multiply(0, 0, sa)
+
+        def turn(chunk, carry):
+            multiply(chunk, piece, sb)
+            pool(chunk, 0, sa)
+            multiply(jnp.minimum(chunk + 1, chunks - 1), 0, sa)
+            pool(chunk, piece, sb)
+            return carry
+
+        lax.fori_loop(0, chunks, turn, 0)
         p_ref[...] = prev[...]
         slope_ref[...] = slopes[...]
 
@@ -248,9 +252,10 @@
             pltpu.VMEM((K1 * co, LAG * BLOCK + rows + 2 * PAD), jnp.float32),
             pltpu.VMEM((C0, BLOCK), jnp.bfloat16),
             pltpu.VMEM((128, 128), jnp.float32),
-            pltpu.VMEM((POOL * CHUNK, BLOCK), jnp.float32),
-            pltpu.VMEM((POOL * CHUNK, BLOCK), jnp.float32),
+            pltpu.VMEM((POOL * CHUNK, 256), jnp.float32),
+            pltpu.VMEM((POOL * CHUNK, 256), jnp.float32),
             pltpu.VMEM((co, BLOCK), jnp.float32),
+            pltpu.VMEM((128, BLOCK), jnp.bfloat16),
         ],
         compiler_params=params(36),
         name="stem_and_conv",
@@ -343,7 +348,7 @@
     dembed = lax.dot_general(
         proj_ref[own, :].astype(jnp.float32), cotangent,
         (((1,), (1,)), ((), ())), precision=HIGH, preferred_element_type=jnp.float32,
-    ) * (1.0 / BIN_ROWS)
+    ) * (0.5 / BIN_ROWS)
     qk = lax.dot_general(
         emb_ref[me].astype(jnp.float32), cotangent, (((0,), (0,)), ((), ())),
         precision=HIGH, preferred_element_type=jnp.float32,

time: 82.6 us -> 91.4 us (1.11)
  Pallas kernels: 41 us -> 49.8 us
    pallas_call x1, Pallas kernels: 32.7 us -> 41.5 us  [stem_and_conv(): pl.pallas_call(functools.partial(stem_kernel, n, rows_dev, co), grid=(blo...]
where the time goes in v4:
time: 91.4 us; the launch traced here: 91.1 us
  Pallas kernels  49.8 us (54%)
  waiting for transfers between devices  15.5 us (17%)
  blocking collectives  12.9 us (14%)
  starting transfers between devices  9.83 us (11%)
  local copies, waits for them, and re-layouts  1.39 us (2%)
    pallas_call x1, Pallas kernels, stem_and_conv(): pl.pallas_call(functools.partial(stem_kernel, n, rows_dev, co), grid=(blo...  41.5 us
    ppermute x6, waiting for transfers between devices, swap(): return lax.ppermute(x, axis, [(i, i ^ bit) for i in range(size)])  15.5 us
    all_to_all x1, blocking collectives, gather_direct(): lax.all_to_all(jnp.broadcast_to(x[None], (lax.axis_size(axis),) + x.shape...  12.9 us
    ppermute x6, starting transfers between devices, swap(): return lax.ppermute(x, axis, [(i, i ^ bit) for i in range(size)])  9.83 us
    pallas_call x1, Pallas kernels, send_half(): pl.pallas_call(functools.partial(send_kernel, n), out_shape=[jax.ShapeDty...  3.55 us
    pallas_call x1, Pallas kernels, keep_half(): pl.pallas_call(keep_kernel, out_shape=jax.ShapeDtypeStruct((size, WIDE),...  2.07 us
  transfers between devices with their start and end apart: 6, of which 5 were waited for; matrix products, arithmetic and copies ran while one was open for 1% of the time, Pallas kernels for 3%

profile of v4, /device:TPU:0, one launch (start us, length us, event | category | flops | bytes accessed | tf_op | source)
XLA Modules:
  0.0 91.1 jit_solution(14075460444640883642)
XLA Ops:
  0.6 0.0 copy-start.2
  0.6 0.0 copy-start.1
  0.7 0.0 copy-start
  0.7 0.9 convert_reduce_fusion
  1.5 0.2 reshape.13
  1.7 0.1 copy.11
  1.8 0.0 copy-start.3
  1.8 3.0 %collective-permute-start = (bf16[1,16,256]{2,1,0:T(8,128)(2,1)S(1)}, bf16[1,16,256]{2,1,0:T(8,128)(2,1)S(1)}, u32[]{:S(2)}, u32[]{:S(2)}) collective-permute-start(bf16[1,16,256]{2,1,0:T(8,128)(2,1)S(1)} %bitcast.11), channel_id=1, source_target_pairs={{0,1},{1,0},{2,3},{3,2},{4,5},{5,4},{6,7},{7,6},{8,9},{9,8},{10,11... | collective-permute-start | bytes 24584 | tf_op jit(solution)/shard_map/ppermute | solution.py:36
  4.8 1.6 %collective-permute-done = bf16[1,16,256]{2,1,0:T(8,128)(2,1)S(1)} collective-permute-done((bf16[1,16,256]{2,1,0:T(8,128)(2,1)S(1)}, bf16[1,16,256]{2,1,0:T(8,128)(2,1)S(1)}, u32[]{:S(2)}, u32[]{:S(2)}) %collective-permute-start) | collective-permute-done | bytes 8224 | tf_op jit(solution)/shard_map/ppermute | solution.py:36
  6.4 2.1 %collective-permute-start.1 = (bf16[2,16,256]{2,1,0:T(8,128)(2,1)S(1)}, bf16[2,16,256]{2,1,0:T(8,128)(2,1)S(1)}, u32[]{:S(2)}, u32[]{:S(2)}) collective-permute-start(bf16[2,16,256]{2,1,0:T(8,128)(2,1)S(1)} %pad_maximum_fusion.2), channel_id=1, source_target_pairs={{0,2},{1,3},{2,0},{3,1},{4,6},{5,7},{6,4},{7,5},{8,10},{9,11},{10,... | collective-permute-start | bytes 49160 | tf_op jit(solution)/shard_map/ppermute | solution.py:36
  8.5 0.9 copy.15
  9.5 0.2 copy.13
  9.6 0.6 collective-permute-done.1
  10.2 3.0 %collective-permute-start.2 = (bf16[4,16,256]{2,1,0:T(8,128)(2,1)S(1)}, bf16[4,16,256]{2,1,0:T(8,128)(2,1)S(1)}, u32[]{:S(2)}, u32[]{:S(2)}) collective-permute-start(bf16[4,16,256]{2,1,0:T(8,128)(2,1)S(1)} %pad_maximum_fusion.1), channel_id=1, source_target_pairs={{0,4},{1,5},{2,6},{3,7},{4,0},{5,1},{6,2},{7,3},{8,12},{9,13},{10,... | collective-permute-start | bytes 98312 | tf_op jit(solution)/shard_map/ppermute | solution.py:36
  13.3 0.0 copy-done.2
  13.3 0.0 copy-done.1
  13.3 0.0 copy-done
  13.3 0.5 prepare.1
  13.8 1.3 %collective-permute-done.2 = bf16[4,16,256]{2,1,0:T(8,128)(2,1)S(1)} collective-permute-done((bf16[4,16,256]{2,1,0:T(8,128)(2,1)S(1)}, bf16[4,16,256]{2,1,0:T(8,128)(2,1)S(1)}, u32[]{:S(2)}, u32[]{:S(2)}) %collective-permute-start.2) | collective-permute-done | bytes 32800 | tf_op jit(solution)/shard_map/ppermute | solution.py:36
  15.2 0.0 copy-done.3
  15.2 41.5 %stem_and_conv.1 = (bf16[768,4096]{1,0:T(8,128)(2,1)S(1)}, f32[96,4096]{1,0:T(8,128)S(1)}, bf16[16,128]{1,0:T(8,128)(2,1)S(1)}) custom-call(bf16[8,16,256]{2,1,0:T(8,128)(2,1)S(1)} %pad_maximum_fusion.pay_ref, bf16[6144,128]{1,0:T(8,128)(2,1)S(1)} %get-tuple-element.12.table_ref, bf16[480,768]{1,0:T(8,128)(2,1)S(1)} %get-tuple-element.13.weights_ref, ...), custom_call_target="tpu_custom_call" | custom-call | tf_op jit(solution)/shard_map/stem_and_conv/pallas_call | solution.py:229
  56.7 12.9 %all_to_all.5.emb_ref = bf16[8,16,128]{2,1,0:T(8,128)(2,1)S(1)} all-to-all(bf16[8,16,128]{2,1,0:T(8,128)(2,1)S(1)} %broadcast_in_dim.2), channel_id=1, replica_groups=mesh['dp'=4,'seq'=8] {'seq'}, dimensions={0} | all-to-all | bytes 65536 | tf_op jit(solution)/shard_map/all_to_all | solution.py:49
  69.6 3.5 %send_half.1 = (s16[48,4224]{1,0:T(8,128)(2,1)S(1)}, bf16[2,48,4352]{2,1,0:T(8,128)(2,1)S(1)}, f32[2,48,256]{2,1,0:T(8,128)S(1)}) custom-call(bf16[8,16,128]{2,1,0:T(8,128)(2,1)S(1)} %all_to_all.5.emb_ref, bf16[1024,256]{1,0:T(8,128)(2,1)S(1)} %get-tuple-element.15.proj_ref, f32[96,4096]{1,0:T(8,128)S(1)} %get-tuple-element.16.slope_ref, ...), custom_call_target="tpu_custom_call" | custom-call | tf_op jit(solution)/shard_map/send_half/pallas_call | solution.py:384
  73.1 0.1 collective-permute-start.3
  73.2 2.1 %keep_half.1.a_ref = f32[48,4096]{1,0:T(8,128)S(1)} custom-call(bf16[2,48,4352]{2,1,0:T(8,128)(2,1)S(1)} %get-tuple-element.18.dconv_ref, f32[2,48,256]{2,1,0:T(8,128)S(1)} %get-tuple-element.19.qk_ref, bf16[768,4096]{1,0:T(8,128)(2,1)S(1)} %get-tuple-element.17.pooled_ref), custom_call_target="tpu_custom_call" | custom-call | flops 1509949440 | bytes 12582912 | tf_op jit(solution)/shard_map/keep_half/pallas_call | solution.py:399
  75.3 0.0 collective-permute-done.3.b_ref
  75.3 0.4 add_half.2.a_ref
  75.7 1.6 %collective-permute-start.4 = (s16[48,4224]{1,0:T(8,128)(2,1)S(1)}, s16[48,4224]{1,0:T(8,128)(2,1)S(1)}, u32[]{:S(2)}, u32[]{:S(2)}) collective-permute-start(s16[48,4224]{1,0:T(8,128)(2,1)S(1)} %add_half.2.a_ref), channel_id=1, source_target_pairs={{0,16},{8,24},{16,0},{24,8},{1,17},{9,25},{17,1},{25,9},{2,18},{10... | collective-permute-start | bytes 1216520 | tf_op jit(solution)/shard_map/ppermute | solution.py:36
  77.2 10.3 %collective-permute-done.4.b_ref = s16[48,4224]{1,0:T(8,128)(2,1)S(1)} collective-permute-done((s16[48,4224]{1,0:T(8,128)(2,1)S(1)}, s16[48,4224]{1,0:T(8,128)(2,1)S(1)}, u32[]{:S(2)}, u32[]{:S(2)}) %collective-permute-start.4) | collective-permute-done | bytes 405536 | tf_op jit(solution)/shard_map/ppermute | solution.py:36
  87.5 0.5 add_half.3.mine_ref
  88.0 0.1 collective-permute-start.5
  88.1 1.7 %collective-permute-done.5.other_ref = s16[48,4224]{1,0:T(8,128)(2,1)S(1)} collective-permute-done((s16[48,4224]{1,0:T(8,128)(2,1)S(1)}, s16[48,4224]{1,0:T(8,128)(2,1)S(1)}, u32[]{:S(2)}, u32[]{:S(2)}) %collective-permute-start.5) | collective-permute-done | bytes 405536 | tf_op jit(solution)/shard_map/ppermute | solution.py:36
  89.8 1.3 %join.1 = (f32[96,3840]{1,0:T(8,128)}, f32[96,128]{1,0:T(8,128)}, f32[96,128]{1,0:T(8,128)}) custom-call(s16[48,4224]{1,0:T(8,128)(2,1)S(1)} %add_half.3.mine_ref, s16[48,4224]{1,0:T(8,128)(2,1)S(1)} %collective-permute-done.5.other_ref), custom_call_target="tpu_custom_call" | custom-call | tf_op jit(solution)/shard_map/join/pallas_call | solution.py:439
  (6 shorter events, 0.1 us)
Async XLA Ops:
  0.6 12.7 %copy-start.2 = (bf16[768,128]{1,0:T(8,128)(2,1)S(1)}, bf16[768,128]{1,0:T(8,128)(2,1)}, u32[]{:S(2)}) copy-start(bf16[768,128]{1,0:T(8,128)(2,1)} %wk_ref.1) | copy-start | bytes 589828
  0.6 12.7 %copy-start.1 = (bf16[768,128]{1,0:T(8,128)(2,1)S(1)}, bf16[768,128]{1,0:T(8,128)(2,1)}, u32[]{:S(2)}) copy-start(bf16[768,128]{1,0:T(8,128)(2,1)} %wq_ref.1) | copy-start | bytes 589828
  0.7 12.7 %copy-start = (bf16[96,3840]{1,0:T(8,128)(2,1)S(1)}, bf16[96,3840]{1,0:T(8,128)(2,1)}, u32[]{:S(2)}) copy-start(bf16[96,3840]{1,0:T(8,128)(2,1)} %w_ref.1) | copy-start | bytes 2211844
  1.8 13.4 %copy-start.3 = (f32[1,2,16]{2,1,0:T(2,128)S(1)}, f32[1,2,16]{2,1,0:T(2,128)}, u32[]{:S(2)}) copy-start(f32[1,2,16]{2,1,0:T(2,128)} %param.11) | copy-start | bytes 388
  1.8 4.6 %collective-permute-start = (bf16[1,16,256]{2,1,0:T(8,128)(2,1)S(1)}, bf16[1,16,256]{2,1,0:T(8,128)(2,1)S(1)}, u32[]{:S(2)}, u32[]{:S(2)}) collective-permute-start(bf16[1,16,256]{2,1,0:T(8,128)(2,1)S(1)} %bitcast.11), channel_id=1, source_target_pairs={{0,1},{1,0},{2,3},{3,2},{4,5},{5,4},{6,7},{7,6},{8,9},{9,8},{10,11... | collective-permute-start | bytes 24584 | tf_op jit(solution)/shard_map/ppermute | solution.py:36
  6.4 3.8 %collective-permute-start.1 = (bf16[2,16,256]{2,1,0:T(8,128)(2,1)S(1)}, bf16[2,16,256]{2,1,0:T(8,128)(2,1)S(1)}, u32[]{:S(2)}, u32[]{:S(2)}) collective-permute-start(bf16[2,16,256]{2,1,0:T(8,128)(2,1)S(1)} %pad_maximum_fusion.2), channel_id=1, source_target_pairs={{0,2},{1,3},{2,0},{3,1},{4,6},{5,7},{6,4},{7,5},{8,10},{9,11},{10,... | collective-permute-start | bytes 49160 | tf_op jit(solution)/shard_map/ppermute | solution.py:36
  10.2 4.9 %collective-permute-start.2 = (bf16[4,16,256]{2,1,0:T(8,128)(2,1)S(1)}, bf16[4,16,256]{2,1,0:T(8,128)(2,1)S(1)}, u32[]{:S(2)}, u32[]{:S(2)}) collective-permute-start(bf16[4,16,256]{2,1,0:T(8,128)(2,1)S(1)} %pad_maximum_fusion.1), channel_id=1, source_target_pairs={{0,4},{1,5},{2,6},{3,7},{4,0},{5,1},{6,2},{7,3},{8,12},{9,13},{10,... | collective-permute-start | bytes 98312 | tf_op jit(solution)/shard_map/ppermute | solution.py:36
  73.1 2.2 %collective-permute-start.3 = (s16[48,4224]{1,0:T(8,128)(2,1)S(1)}, s16[48,4224]{1,0:T(8,128)(2,1)S(1)}, u32[]{:S(2)}, u32[]{:S(2)}) collective-permute-start(s16[48,4224]{1,0:T(8,128)(2,1)S(1)} %get-tuple-element.20), channel_id=1, source_target_pairs={{0,8},{8,0},{16,24},{24,16},{1,9},{9,1},{17,25},{25,17},{2,10},{10... | collective-permute-start | bytes 1216520 | tf_op jit(solution)/shard_map/ppermute | solution.py:36
  75.7 11.8 %collective-permute-start.4 = (s16[48,4224]{1,0:T(8,128)(2,1)S(1)}, s16[48,4224]{1,0:T(8,128)(2,1)S(1)}, u32[]{:S(2)}, u32[]{:S(2)}) collective-permute-start(s16[48,4224]{1,0:T(8,128)(2,1)S(1)} %add_half.2.a_ref), channel_id=1, source_target_pairs={{0,16},{8,24},{16,0},{24,8},{1,17},{9,25},{17,1},{25,9},{2,18},{10... | collective-permute-start | bytes 1216520 | tf_op jit(solution)/shard_map/ppermute | solution.py:36
  88.0 1.8 %collective-permute-start.5 = (s16[48,4224]{1,0:T(8,128)(2,1)S(1)}, s16[48,4224]{1,0:T(8,128)(2,1)S(1)}, u32[]{:S(2)}, u32[]{:S(2)}) collective-permute-start(s16[48,4224]{1,0:T(8,128)(2,1)S(1)} %add_half.3.mine_ref), channel_id=1, source_target_pairs={{0,8},{8,0},{16,24},{24,16},{1,9},{9,1},{17,25},{25,17},{2,10},{10... | collective-permute-start | bytes 1216520 | tf_op jit(solution)/shard_map/ppermute | solution.py:36

commit v5 on v3

--- a/solution.py
+++ b/solution.py
@@ -61,7 +61,7 @@
             first = (chunk * POOL + pos) * CHUNK
             table_ref[first : first + CHUNK, :] = shifted.astype(jnp.bfloat16)
     for tap in range(K1):
-        weights_ref[tap * co : (tap + 1) * co, :] = w_ref[:, tap * C0 : (tap + 1) * C0]
+        weights_ref[tap * co : (tap + 1) * co, :] = w_ref[:, tap * C0 : (tap + 1) * C0] * 0.5
     for slot in range(n):
         rows = slice(slot * co, (slot + 1) * co)
         proj_ref[slot * SLOT : slot * SLOT + co, :PC] = wq_ref[rows, :]
@@ -94,7 +94,6 @@
     rows = n * rows_dev
     blocks = rows // BLOCK
     front = LAG * BLOCK + PAD
-    piece = 256
 
     def convolve(block):
         first = pl.multiple_of((block + LAG) * BLOCK, 128)
@@ -158,33 +157,32 @@
         taps(step - 1)
         stage = (sa, sb)
 
-        def multiply(chunk, at):
-            stage[chunk % 2][:, at : at + piece] = jnp.dot(
+        def multiply(chunk):
+            stage[chunk % 2][...] = jnp.dot(
                 table[chunk * POOL * CHUNK : (chunk + 1) * POOL * CHUNK, :],
-                onehot[:, at : at + piece],
+                onehot,
                 preferred_element_type=jnp.float32,
             )
 
-        def pool(chunk, at):
+        def pool(chunk):
             stem = stage[chunk % 2]
             for row in range(0, CHUNK, 16):
-                most = least = stem[row : row + 16, at : at + piece]
-                for pos in range(1, POOL):
-                    part = stem[pos * CHUNK + row : pos * CHUNK + row + 16, at : at + piece]
-                    most = jnp.maximum(most, part)
-                    least = jnp.minimum(least, part)
-                pooled = (0.5 * jnp.maximum(twice_gelu(most), twice_gelu(least))).astype(jnp.bfloat16)
-                to = chunk * CHUNK + row
-                prev[to : to + 16, at : at + piece] = pooled
+                for at in range(0, BLOCK, 256):
+                    most = least = stem[row : row + 16, at : at + 256]
+                    for pos in range(1, POOL):
+                        part = stem[pos * CHUNK + row : pos * CHUNK + row + 16, at : at + 256]
+                        most = jnp.maximum(most, part)
+                        least = jnp.minimum(least, part)
+                    prev[chunk * CHUNK + row : chunk * CHUNK + row + 16, at : at + 256] = (
+                        jnp.maximum(twice_gelu(most), twice_gelu(least)).astype(jnp.bfloat16)
+                    )
 
         chunks = C0 // CHUNK
-        for at in range(0, BLOCK, piece):
-            multiply(0, at)
+        multiply(0)
         for chunk in range(chunks):
-            for at in range(0, BLOCK, piece):
-                if chunk + 1 < chunks:
-                    multiply(chunk + 1, at)
-                pool(chunk, at)
+            if chunk + 1 < chunks:
+                multiply(chunk + 1)
+            pool(chunk)
         p_ref[...] = prev[...]
         slope_ref[...] = slopes[...]
 
@@ -343,7 +341,7 @@
     dembed = lax.dot_general(
         proj_ref[own, :].astype(jnp.float32), cotangent,
         (((1,), (1,)), ((), ())), precision=HIGH, preferred_element_type=jnp.float32,
-    ) * (1.0 / BIN_ROWS)
+    ) * (0.5 / BIN_ROWS)
     qk = lax.dot_general(
         emb_ref[me].astype(jnp.float32), cotangent, (((0,), (0,)), ((), ())),
         precision=HIGH, preferred_element_type=jnp.float32,

time: 82.6 us -> 82.2 us (level)
  no operation moved by 1% of the time
where the time goes in v5:
time: 82.2 us; the launch traced here: 81.9 us
  Pallas kernels  40.6 us (49%)
  waiting for transfers between devices  15.5 us (19%)
  blocking collectives  12.9 us (16%)
  starting transfers between devices  9.83 us (12%)
  local copies, waits for them, and re-layouts  1.39 us (2%)
  other arithmetic  0.9 us (1%)
    pallas_call x1, Pallas kernels, stem_and_conv(): pl.pallas_call(functools.partial(stem_kernel, n, rows_dev, co), grid=(blo...  32.3 us
    ppermute x6, waiting for transfers between devices, swap(): return lax.ppermute(x, axis, [(i, i ^ bit) for i in range(size)])  15.5 us
    all_to_all x1, blocking collectives, gather_direct(): lax.all_to_all(jnp.broadcast_to(x[None], (lax.axis_size(axis),) + x.shape...  12.9 us
    ppermute x6, starting transfers between devices, swap(): return lax.ppermute(x, axis, [(i, i ^ bit) for i in range(size)])  9.83 us
    pallas_call x1, Pallas kernels, send_half(): pl.pallas_call(functools.partial(send_kernel, n), out_shape=[jax.ShapeDty...  3.55 us
    pallas_call x1, Pallas kernels, keep_half(): pl.pallas_call(keep_kernel, out_shape=jax.ShapeDtypeStruct((size, WIDE),...  2.07 us
  transfers between devices with their start and end apart: 6, of which 5 were waited for; matrix products, arithmetic and copies ran while one was open for 1% of the time, Pallas kernels for 3%

profile of v5, /device:TPU:0, one launch (start us, length us, event | category | flops | bytes accessed | tf_op | source)
XLA Modules:
  0.0 81.9 jit_solution(11437341018289581896)
XLA Ops:
  0.6 0.0 copy-start.2
  0.6 0.0 copy-start.1
  0.7 0.0 copy-start
  0.7 0.9 %convert_reduce_fusion = bf16[4096]{0:T(1024)(128)(2,1)S(1)} fusion(s32[1,4096]{1,0:T(1,128)} %param.6), kind=kLoop, calls=%fused_computation.5 | loop fusion | flops 4096 | bytes 24576 | tf_op jit(solution)/shard_map/convert_element_type | solution.py:448
  1.5 0.2 reshape.13
  1.7 0.1 copy.11
  1.8 0.0 copy-start.3
  1.8 3.0 %collective-permute-start = (bf16[1,16,256]{2,1,0:T(8,128)(2,1)S(1)}, bf16[1,16,256]{2,1,0:T(8,128)(2,1)S(1)}, u32[]{:S(2)}, u32[]{:S(2)}) collective-permute-start(bf16[1,16,256]{2,1,0:T(8,128)(2,1)S(1)} %bitcast.11), channel_id=1, source_target_pairs={{0,1},{1,0},{2,3},{3,2},{4,5},{5,4},{6,7},{7,6},{8,9},{9,8},{10,11... | collective-permute-start | bytes 24584 | tf_op jit(solution)/shard_map/ppermute | solution.py:36
  4.8 1.6 %collective-permute-done = bf16[1,16,256]{2,1,0:T(8,128)(2,1)S(1)} collective-permute-done((bf16[1,16,256]{2,1,0:T(8,128)(2,1)S(1)}, bf16[1,16,256]{2,1,0:T(8,128)(2,1)S(1)}, u32[]{:S(2)}, u32[]{:S(2)}) %collective-permute-start) | collective-permute-done | bytes 8224 | tf_op jit(solution)/shard_map/ppermute | solution.py:36
  6.4 2.1 %collective-permute-start.1 = (bf16[2,16,256]{2,1,0:T(8,128)(2,1)S(1)}, bf16[2,16,256]{2,1,0:T(8,128)(2,1)S(1)}, u32[]{:S(2)}, u32[]{:S(2)}) collective-permute-start(bf16[2,16,256]{2,1,0:T(8,128)(2,1)S(1)} %pad_maximum_fusion.2), channel_id=1, source_target_pairs={{0,2},{1,3},{2,0},{3,1},{4,6},{5,7},{6,4},{7,5},{8,10},{9,11},{10,... | collective-permute-start | bytes 49160 | tf_op jit(solution)/shard_map/ppermute | solution.py:36
  8.5 0.9 %copy.15 = bf16[15,4,768]{2,0,1:T(8,128)(2,1)S(1)} copy(bf16[15,4,768]{2,1,0:T(4,128)(2,1)} %param.7) | data formatting | bytes 184320 | tf_op args[1]
  9.5 0.2 copy.13
  9.6 0.6 collective-permute-done.1
  10.2 3.0 %collective-permute-start.2 = (bf16[4,16,256]{2,1,0:T(8,128)(2,1)S(1)}, bf16[4,16,256]{2,1,0:T(8,128)(2,1)S(1)}, u32[]{:S(2)}, u32[]{:S(2)}) collective-permute-start(bf16[4,16,256]{2,1,0:T(8,128)(2,1)S(1)} %pad_maximum_fusion.1), channel_id=1, source_target_pairs={{0,4},{1,5},{2,6},{3,7},{4,0},{5,1},{6,2},{7,3},{8,12},{9,13},{10,... | collective-permute-start | bytes 98312 | tf_op jit(solution)/shard_map/ppermute | solution.py:36
  13.3 0.0 copy-done.2
  13.3 0.0 copy-done.1
  13.3 0.0 copy-done
  13.3 0.5 prepare.1
  13.8 1.3 %collective-permute-done.2 = bf16[4,16,256]{2,1,0:T(8,128)(2,1)S(1)} collective-permute-done((bf16[4,16,256]{2,1,0:T(8,128)(2,1)S(1)}, bf16[4,16,256]{2,1,0:T(8,128)(2,1)S(1)}, u32[]{:S(2)}, u32[]{:S(2)}) %collective-permute-start.2) | collective-permute-done | bytes 32800 | tf_op jit(solution)/shard_map/ppermute | solution.py:36
  15.2 0.0 copy-done.3
  15.2 32.3 %stem_and_conv.1 = (bf16[768,4096]{1,0:T(8,128)(2,1)S(1)}, f32[96,4096]{1,0:T(8,128)S(1)}, bf16[16,128]{1,0:T(8,128)(2,1)S(1)}) custom-call(bf16[8,16,256]{2,1,0:T(8,128)(2,1)S(1)} %pad_maximum_fusion.pay_ref, bf16[6144,128]{1,0:T(8,128)(2,1)S(1)} %get-tuple-element.12.table_ref, bf16[480,768]{1,0:T(8,128)(2,1)S(1)} %get-tuple-element.13.weights_ref, ...), custom_call_target="tpu_custom_call" | custom-call | tf_op jit(solution)/shard_map/stem_and_conv/pallas_call | solution.py:223
  47.5 12.9 %all_to_all.5.emb_ref = bf16[8,16,128]{2,1,0:T(8,128)(2,1)S(1)} all-to-all(bf16[8,16,128]{2,1,0:T(8,128)(2,1)S(1)} %broadcast_in_dim.2), channel_id=1, replica_groups=mesh['dp'=4,'seq'=8] {'seq'}, dimensions={0} | all-to-all | bytes 65536 | tf_op jit(solution)/shard_map/all_to_all | solution.py:49
  60.4 3.6 %send_half.1 = (s16[48,4224]{1,0:T(8,128)(2,1)S(1)}, bf16[2,48,4352]{2,1,0:T(8,128)(2,1)S(1)}, f32[2,48,256]{2,1,0:T(8,128)S(1)}) custom-call(bf16[8,16,128]{2,1,0:T(8,128)(2,1)S(1)} %all_to_all.5.emb_ref, bf16[1024,256]{1,0:T(8,128)(2,1)S(1)} %get-tuple-element.15.proj_ref, f32[96,4096]{1,0:T(8,128)S(1)} %get-tuple-element.16.slope_ref, ...), custom_call_target="tpu_custom_call" | custom-call | tf_op jit(solution)/shard_map/send_half/pallas_call | solution.py:377
  63.9 0.1 collective-permute-start.3
  64.0 2.1 %keep_half.1.a_ref = f32[48,4096]{1,0:T(8,128)S(1)} custom-call(bf16[2,48,4352]{2,1,0:T(8,128)(2,1)S(1)} %get-tuple-element.18.dconv_ref, f32[2,48,256]{2,1,0:T(8,128)S(1)} %get-tuple-element.19.qk_ref, bf16[768,4096]{1,0:T(8,128)(2,1)S(1)} %get-tuple-element.17.pooled_ref), custom_call_target="tpu_custom_call" | custom-call | flops 1509949440 | bytes 12582912 | tf_op jit(solution)/shard_map/keep_half/pallas_call | solution.py:392
  66.1 0.0 collective-permute-done.3.b_ref
  66.1 0.4 add_half.2.a_ref
  66.5 1.6 %collective-permute-start.4 = (s16[48,4224]{1,0:T(8,128)(2,1)S(1)}, s16[48,4224]{1,0:T(8,128)(2,1)S(1)}, u32[]{:S(2)}, u32[]{:S(2)}) collective-permute-start(s16[48,4224]{1,0:T(8,128)(2,1)S(1)} %add_half.2.a_ref), channel_id=1, source_target_pairs={{0,16},{8,24},{16,0},{24,8},{1,17},{9,25},{17,1},{25,9},{2,18},{10... | collective-permute-start | bytes 1216520 | tf_op jit(solution)/shard_map/ppermute | solution.py:36
  68.1 10.3 %collective-permute-done.4.b_ref = s16[48,4224]{1,0:T(8,128)(2,1)S(1)} collective-permute-done((s16[48,4224]{1,0:T(8,128)(2,1)S(1)}, s16[48,4224]{1,0:T(8,128)(2,1)S(1)}, u32[]{:S(2)}, u32[]{:S(2)}) %collective-permute-start.4) | collective-permute-done | bytes 405536 | tf_op jit(solution)/shard_map/ppermute | solution.py:36
  78.3 0.5 add_half.3.mine_ref
  78.8 0.1 collective-permute-start.5
  78.9 1.7 %collective-permute-done.5.other_ref = s16[48,4224]{1,0:T(8,128)(2,1)S(1)} collective-permute-done((s16[48,4224]{1,0:T(8,128)(2,1)S(1)}, s16[48,4224]{1,0:T(8,128)(2,1)S(1)}, u32[]{:S(2)}, u32[]{:S(2)}) %collective-permute-start.5) | collective-permute-done | bytes 405536 | tf_op jit(solution)/shard_map/ppermute | solution.py:36
  80.6 1.3 %join.1 = (f32[96,3840]{1,0:T(8,128)}, f32[96,128]{1,0:T(8,128)}, f32[96,128]{1,0:T(8,128)}) custom-call(s16[48,4224]{1,0:T(8,128)(2,1)S(1)} %add_half.3.mine_ref, s16[48,4224]{1,0:T(8,128)(2,1)S(1)} %collective-permute-done.5.other_ref), custom_call_target="tpu_custom_call" | custom-call | tf_op jit(solution)/shard_map/join/pallas_call | solution.py:432
  (6 shorter events, 0.1 us)
Async XLA Ops:
  0.6 12.7 %copy-start.2 = (bf16[768,128]{1,0:T(8,128)(2,1)S(1)}, bf16[768,128]{1,0:T(8,128)(2,1)}, u32[]{:S(2)}) copy-start(bf16[768,128]{1,0:T(8,128)(2,1)} %wk_ref.1) | copy-start | bytes 589828
  0.6 12.7 %copy-start.1 = (bf16[768,128]{1,0:T(8,128)(2,1)S(1)}, bf16[768,128]{1,0:T(8,128)(2,1)}, u32[]{:S(2)}) copy-start(bf16[768,128]{1,0:T(8,128)(2,1)} %wq_ref.1) | copy-start | bytes 589828
  0.7 12.7 %copy-start = (bf16[96,3840]{1,0:T(8,128)(2,1)S(1)}, bf16[96,3840]{1,0:T(8,128)(2,1)}, u32[]{:S(2)}) copy-start(bf16[96,3840]{1,0:T(8,128)(2,1)} %w_ref.1) | copy-start | bytes 2211844
  1.8 13.4 %copy-start.3 = (f32[1,2,16]{2,1,0:T(2,128)S(1)}, f32[1,2,16]{2,1,0:T(2,128)}, u32[]{:S(2)}) copy-start(f32[1,2,16]{2,1,0:T(2,128)} %param.11) | copy-start | bytes 388
  1.8 4.6 %collective-permute-start = (bf16[1,16,256]{2,1,0:T(8,128)(2,1)S(1)}, bf16[1,16,256]{2,1,0:T(8,128)(2,1)S(1)}, u32[]{:S(2)}, u32[]{:S(2)}) collective-permute-start(bf16[1,16,256]{2,1,0:T(8,128)(2,1)S(1)} %bitcast.11), channel_id=1, source_target_pairs={{0,1},{1,0},{2,3},{3,2},{4,5},{5,4},{6,7},{7,6},{8,9},{9,8},{10,11... | collective-permute-start | bytes 24584 | tf_op jit(solution)/shard_map/ppermute | solution.py:36
  6.4 3.8 %collective-permute-start.1 = (bf16[2,16,256]{2,1,0:T(8,128)(2,1)S(1)}, bf16[2,16,256]{2,1,0:T(8,128)(2,1)S(1)}, u32[]{:S(2)}, u32[]{:S(2)}) collective-permute-start(bf16[2,16,256]{2,1,0:T(8,128)(2,1)S(1)} %pad_maximum_fusion.2), channel_id=1, source_target_pairs={{0,2},{1,3},{2,0},{3,1},{4,6},{5,7},{6,4},{7,5},{8,10},{9,11},{10,... | collective-permute-start | bytes 49160 | tf_op jit(solution)/shard_map/ppermute | solution.py:36
  10.2 4.9 %collective-permute-start.2 = (bf16[4,16,256]{2,1,0:T(8,128)(2,1)S(1)}, bf16[4,16,256]{2,1,0:T(8,128)(2,1)S(1)}, u32[]{:S(2)}, u32[]{:S(2)}) collective-permute-start(bf16[4,16,256]{2,1,0:T(8,128)(2,1)S(1)} %pad_maximum_fusion.1), channel_id=1, source_target_pairs={{0,4},{1,5},{2,6},{3,7},{4,0},{5,1},{6,2},{7,3},{8,12},{9,13},{10,... | collective-permute-start | bytes 98312 | tf_op jit(solution)/shard_map/ppermute | solution.py:36
  63.9 2.1 %collective-permute-start.3 = (s16[48,4224]{1,0:T(8,128)(2,1)S(1)}, s16[48,4224]{1,0:T(8,128)(2,1)S(1)}, u32[]{:S(2)}, u32[]{:S(2)}) collective-permute-start(s16[48,4224]{1,0:T(8,128)(2,1)S(1)} %get-tuple-element.20), channel_id=1, source_target_pairs={{0,8},{8,0},{16,24},{24,16},{1,9},{9,1},{17,25},{25,17},{2,10},{10... | collective-permute-start | bytes 1216520 | tf_op jit(solution)/shard_map/ppermute | solution.py:36
  66.5 11.8 %collective-permute-start.4 = (s16[48,4224]{1,0:T(8,128)(2,1)S(1)}, s16[48,4224]{1,0:T(8,128)(2,1)S(1)}, u32[]{:S(2)}, u32[]{:S(2)}) collective-permute-start(s16[48,4224]{1,0:T(8,128)(2,1)S(1)} %add_half.2.a_ref), channel_id=1, source_target_pairs={{0,16},{8,24},{16,0},{24,8},{1,17},{9,25},{17,1},{25,9},{2,18},{10... | collective-permute-start | bytes 1216520 | tf_op jit(solution)/shard_map/ppermute | solution.py:36
  78.8 1.8 %collective-permute-start.5 = (s16[48,4224]{1,0:T(8,128)(2,1)S(1)}, s16[48,4224]{1,0:T(8,128)(2,1)S(1)}, u32[]{:S(2)}, u32[]{:S(2)}) collective-permute-start(s16[48,4224]{1,0:T(8,128)(2,1)S(1)} %add_half.3.mine_ref), channel_id=1, source_target_pairs={{0,8},{8,0},{16,24},{24,16},{1,9},{9,1},{17,25},{25,17},{2,10},{10... | collective-permute-start | bytes 1216520 | tf_op jit(solution)/shard_map/ppermute | solution.py:36

commit v6 on v5

--- a/solution.py
+++ b/solution.py
@@ -49,8 +49,12 @@
     return lax.all_to_all(jnp.broadcast_to(x[None], (lax.axis_size(axis),) + x.shape), axis, 0, 0)
 
 
-def twice_gelu(v):
-    return v + v * jnp.tanh(v * (ROOT + (ROOT * CUBE) * (v * v)))
+EXPO = -2.0 * ROOT * 1.4426950408889634
+
+
+def gelu_ratio(v):
+    power = jnp.exp2(v * (EXPO + (EXPO * CUBE) * (v * v)))
+    return v * pl.reciprocal(1.0 + power, approx=True)
 
 
 def prepare_kernel(n, co, t0_ref, w_ref, wq_ref, wk_ref, table_ref, weights_ref, proj_ref):
@@ -61,7 +65,7 @@
             first = (chunk * POOL + pos) * CHUNK
             table_ref[first : first + CHUNK, :] = shifted.astype(jnp.bfloat16)
     for tap in range(K1):
-        weights_ref[tap * co : (tap + 1) * co, :] = w_ref[:, tap * C0 : (tap + 1) * C0] * 0.5
+        weights_ref[tap * co : (tap + 1) * co, :] = w_ref[:, tap * C0 : (tap + 1) * C0]
     for slot in range(n):
         rows = slice(slot * co, (slot + 1) * co)
         proj_ref[slot * SLOT : slot * SLOT + co, :PC] = wq_ref[rows, :]
@@ -174,7 +178,7 @@
                         most = jnp.maximum(most, part)
                         least = jnp.minimum(least, part)
                     prev[chunk * CHUNK + row : chunk * CHUNK + row + 16, at : at + 256] = (
-                        jnp.maximum(twice_gelu(most), twice_gelu(least)).astype(jnp.bfloat16)
+                        jnp.maximum(gelu_ratio(most), gelu_ratio(least)).astype(jnp.bfloat16)
                     )
 
         chunks = C0 // CHUNK
@@ -341,7 +345,7 @@
     dembed = lax.dot_general(
         proj_ref[own, :].astype(jnp.float32), cotangent,
         (((1,), (1,)), ((), ())), precision=HIGH, preferred_element_type=jnp.float32,
-    ) * (0.5 / BIN_ROWS)
+    ) * (1.0 / BIN_ROWS)
     qk = lax.dot_general(
         emb_ref[me].astype(jnp.float32), cotangent, (((0,), (0,)), ((), ())),
         precision=HIGH, preferred_element_type=jnp.float32,

time: 82.2 us -> 83.4 us (1.015)
  Pallas kernels: 40.6 us -> 41.7 us
    pallas_call x1, Pallas kernels: 32.3 us -> 33.5 us  [stem_and_conv(): pl.pallas_call(functools.partial(stem_kernel, n, rows_dev, co), grid=(blo...]
where the time goes in v6:
time: 83.4 us; the launch traced here: 83.1 us
  Pallas kernels  41.7 us (50%)
  waiting for transfers between devices  15.5 us (19%)
  blocking collectives  12.9 us (15%)
  starting transfers between devices  9.83 us (12%)
  local copies, waits for them, and re-layouts  1.39 us (2%)
  other arithmetic  0.9 us (1%)
    pallas_call x1, Pallas kernels, stem_and_conv(): pl.pallas_call(functools.partial(stem_kernel, n, rows_dev, co), grid=(blo...  33.5 us
    ppermute x6, waiting for transfers between devices, swap(): return lax.ppermute(x, axis, [(i, i ^ bit) for i in range(size)])  15.5 us
    all_to_all x1, blocking collectives, gather_direct(): lax.all_to_all(jnp.broadcast_to(x[None], (lax.axis_size(axis),) + x.shape...  12.9 us
    ppermute x6, starting transfers between devices, swap(): return lax.ppermute(x, axis, [(i, i ^ bit) for i in range(size)])  9.83 us
    pallas_call x1, Pallas kernels, send_half(): pl.pallas_call(functools.partial(send_kernel, n), out_shape=[jax.ShapeDty...  3.54 us
    pallas_call x1, Pallas kernels, keep_half(): pl.pallas_call(keep_kernel, out_shape=jax.ShapeDtypeStruct((size, WIDE),...  2.07 us
  transfers between devices with their start and end apart: 6, of which 5 were waited for; matrix products, arithmetic and copies ran while one was open for 1% of the time, Pallas kernels for 3%

profile of v6, /device:TPU:0, one launch (start us, length us, event | category | flops | bytes accessed | tf_op | source)
XLA Modules:
  0.0 83.1 jit_solution(16253475807576011488)
XLA Ops:
  0.6 0.0 copy-start.2
  0.6 0.0 copy-start.1
  0.7 0.0 copy-start
  0.7 0.9 %convert_reduce_fusion = bf16[4096]{0:T(1024)(128)(2,1)S(1)} fusion(s32[1,4096]{1,0:T(1,128)} %param.6), kind=kLoop, calls=%fused_computation.5 | loop fusion | flops 4096 | bytes 24576 | tf_op jit(solution)/shard_map/convert_element_type | solution.py:452
  1.5 0.2 reshape.13
  1.7 0.1 copy.11
  1.8 0.0 copy-start.3
  1.8 3.0 %collective-permute-start = (bf16[1,16,256]{2,1,0:T(8,128)(2,1)S(1)}, bf16[1,16,256]{2,1,0:T(8,128)(2,1)S(1)}, u32[]{:S(2)}, u32[]{:S(2)}) collective-permute-start(bf16[1,16,256]{2,1,0:T(8,128)(2,1)S(1)} %bitcast.11), channel_id=1, source_target_pairs={{0,1},{1,0},{2,3},{3,2},{4,5},{5,4},{6,7},{7,6},{8,9},{9,8},{10,11... | collective-permute-start | bytes 24584 | tf_op jit(solution)/shard_map/ppermute | solution.py:36
  4.8 1.6 %collective-permute-done = bf16[1,16,256]{2,1,0:T(8,128)(2,1)S(1)} collective-permute-done((bf16[1,16,256]{2,1,0:T(8,128)(2,1)S(1)}, bf16[1,16,256]{2,1,0:T(8,128)(2,1)S(1)}, u32[]{:S(2)}, u32[]{:S(2)}) %collective-permute-start) | collective-permute-done | bytes 8224 | tf_op jit(solution)/shard_map/ppermute | solution.py:36
  6.4 2.1 %collective-permute-start.1 = (bf16[2,16,256]{2,1,0:T(8,128)(2,1)S(1)}, bf16[2,16,256]{2,1,0:T(8,128)(2,1)S(1)}, u32[]{:S(2)}, u32[]{:S(2)}) collective-permute-start(bf16[2,16,256]{2,1,0:T(8,128)(2,1)S(1)} %pad_maximum_fusion.2), channel_id=1, source_target_pairs={{0,2},{1,3},{2,0},{3,1},{4,6},{5,7},{6,4},{7,5},{8,10},{9,11},{10,... | collective-permute-start | bytes 49160 | tf_op jit(solution)/shard_map/ppermute | solution.py:36
  8.5 0.9 %copy.15 = bf16[15,4,768]{2,0,1:T(8,128)(2,1)S(1)} copy(bf16[15,4,768]{2,1,0:T(4,128)(2,1)} %param.7) | data formatting | bytes 184320 | tf_op args[1]
  9.5 0.2 copy.13
  9.6 0.6 collective-permute-done.1
  10.2 3.0 %collective-permute-start.2 = (bf16[4,16,256]{2,1,0:T(8,128)(2,1)S(1)}, bf16[4,16,256]{2,1,0:T(8,128)(2,1)S(1)}, u32[]{:S(2)}, u32[]{:S(2)}) collective-permute-start(bf16[4,16,256]{2,1,0:T(8,128)(2,1)S(1)} %pad_maximum_fusion.1), channel_id=1, source_target_pairs={{0,4},{1,5},{2,6},{3,7},{4,0},{5,1},{6,2},{7,3},{8,12},{9,13},{10,... | collective-permute-start | bytes 98312 | tf_op jit(solution)/shard_map/ppermute | solution.py:36
  13.3 0.0 copy-done.2
  13.3 0.0 copy-done.1
  13.3 0.0 copy-done
  13.3 0.5 prepare.1
  13.8 1.3 %collective-permute-done.2 = bf16[4,16,256]{2,1,0:T(8,128)(2,1)S(1)} collective-permute-done((bf16[4,16,256]{2,1,0:T(8,128)(2,1)S(1)}, bf16[4,16,256]{2,1,0:T(8,128)(2,1)S(1)}, u32[]{:S(2)}, u32[]{:S(2)}) %collective-permute-start.2) | collective-permute-done | bytes 32800 | tf_op jit(solution)/shard_map/ppermute | solution.py:36
  15.2 0.0 copy-done.3
  15.2 33.5 %stem_and_conv.1 = (bf16[768,4096]{1,0:T(8,128)(2,1)S(1)}, f32[96,4096]{1,0:T(8,128)S(1)}, bf16[16,128]{1,0:T(8,128)(2,1)S(1)}) custom-call(bf16[8,16,256]{2,1,0:T(8,128)(2,1)S(1)} %pad_maximum_fusion.pay_ref, bf16[6144,128]{1,0:T(8,128)(2,1)S(1)} %get-tuple-element.12.table_ref, bf16[480,768]{1,0:T(8,128)(2,1)S(1)} %get-tuple-element.13.weights_ref, ...), custom_call_target="tpu_custom_call" | custom-call | tf_op jit(solution)/shard_map/stem_and_conv/pallas_call | solution.py:227
  48.7 12.9 %all_to_all.5.emb_ref = bf16[8,16,128]{2,1,0:T(8,128)(2,1)S(1)} all-to-all(bf16[8,16,128]{2,1,0:T(8,128)(2,1)S(1)} %broadcast_in_dim.2), channel_id=1, replica_groups=mesh['dp'=4,'seq'=8] {'seq'}, dimensions={0} | all-to-all | bytes 65536 | tf_op jit(solution)/shard_map/all_to_all | solution.py:49
  61.6 3.5 %send_half.1 = (s16[48,4224]{1,0:T(8,128)(2,1)S(1)}, bf16[2,48,4352]{2,1,0:T(8,128)(2,1)S(1)}, f32[2,48,256]{2,1,0:T(8,128)S(1)}) custom-call(bf16[8,16,128]{2,1,0:T(8,128)(2,1)S(1)} %all_to_all.5.emb_ref, bf16[1024,256]{1,0:T(8,128)(2,1)S(1)} %get-tuple-element.15.proj_ref, f32[96,4096]{1,0:T(8,128)S(1)} %get-tuple-element.16.slope_ref, ...), custom_call_target="tpu_custom_call" | custom-call | tf_op jit(solution)/shard_map/send_half/pallas_call | solution.py:381
  65.1 0.1 collective-permute-start.3
  65.2 2.1 %keep_half.1.a_ref = f32[48,4096]{1,0:T(8,128)S(1)} custom-call(bf16[2,48,4352]{2,1,0:T(8,128)(2,1)S(1)} %get-tuple-element.18.dconv_ref, f32[2,48,256]{2,1,0:T(8,128)S(1)} %get-tuple-element.19.qk_ref, bf16[768,4096]{1,0:T(8,128)(2,1)S(1)} %get-tuple-element.17.pooled_ref), custom_call_target="tpu_custom_call" | custom-call | flops 1509949440 | bytes 12582912 | tf_op jit(solution)/shard_map/keep_half/pallas_call | solution.py:396
  67.3 0.0 collective-permute-done.3.b_ref
  67.3 0.4 add_half.2.a_ref
  67.7 1.6 %collective-permute-start.4 = (s16[48,4224]{1,0:T(8,128)(2,1)S(1)}, s16[48,4224]{1,0:T(8,128)(2,1)S(1)}, u32[]{:S(2)}, u32[]{:S(2)}) collective-permute-start(s16[48,4224]{1,0:T(8,128)(2,1)S(1)} %add_half.2.a_ref), channel_id=1, source_target_pairs={{0,16},{8,24},{16,0},{24,8},{1,17},{9,25},{17,1},{25,9},{2,18},{10... | collective-permute-start | bytes 1216520 | tf_op jit(solution)/shard_map/ppermute | solution.py:36
  69.2 10.3 %collective-permute-done.4.b_ref = s16[48,4224]{1,0:T(8,128)(2,1)S(1)} collective-permute-done((s16[48,4224]{1,0:T(8,128)(2,1)S(1)}, s16[48,4224]{1,0:T(8,128)(2,1)S(1)}, u32[]{:S(2)}, u32[]{:S(2)}) %collective-permute-start.4) | collective-permute-done | bytes 405536 | tf_op jit(solution)/shard_map/ppermute | solution.py:36
  79.5 0.5 add_half.3.mine_ref
  80.0 0.1 collective-permute-start.5
  80.1 1.7 %collective-permute-done.5.other_ref = s16[48,4224]{1,0:T(8,128)(2,1)S(1)} collective-permute-done((s16[48,4224]{1,0:T(8,128)(2,1)S(1)}, s16[48,4224]{1,0:T(8,128)(2,1)S(1)}, u32[]{:S(2)}, u32[]{:S(2)}) %collective-permute-start.5) | collective-permute-done | bytes 405536 | tf_op jit(solution)/shard_map/ppermute | solution.py:36
  81.8 1.3 %join.1 = (f32[96,3840]{1,0:T(8,128)}, f32[96,128]{1,0:T(8,128)}, f32[96,128]{1,0:T(8,128)}) custom-call(s16[48,4224]{1,0:T(8,128)(2,1)S(1)} %add_half.3.mine_ref, s16[48,4224]{1,0:T(8,128)(2,1)S(1)} %collective-permute-done.5.other_ref), custom_call_target="tpu_custom_call" | custom-call | tf_op jit(solution)/shard_map/join/pallas_call | solution.py:436
  (6 shorter events, 0.1 us)
Async XLA Ops:
  0.6 12.7 %copy-start.2 = (bf16[768,128]{1,0:T(8,128)(2,1)S(1)}, bf16[768,128]{1,0:T(8,128)(2,1)}, u32[]{:S(2)}) copy-start(bf16[768,128]{1,0:T(8,128)(2,1)} %wk_ref.1) | copy-start | bytes 589828
  0.6 12.7 %copy-start.1 = (bf16[768,128]{1,0:T(8,128)(2,1)S(1)}, bf16[768,128]{1,0:T(8,128)(2,1)}, u32[]{:S(2)}) copy-start(bf16[768,128]{1,0:T(8,128)(2,1)} %wq_ref.1) | copy-start | bytes 589828
  0.7 12.7 %copy-start = (bf16[96,3840]{1,0:T(8,128)(2,1)S(1)}, bf16[96,3840]{1,0:T(8,128)(2,1)}, u32[]{:S(2)}) copy-start(bf16[96,3840]{1,0:T(8,128)(2,1)} %w_ref.1) | copy-start | bytes 2211844
  1.8 13.4 %copy-start.3 = (f32[1,2,16]{2,1,0:T(2,128)S(1)}, f32[1,2,16]{2,1,0:T(2,128)}, u32[]{:S(2)}) copy-start(f32[1,2,16]{2,1,0:T(2,128)} %param.11) | copy-start | bytes 388
  1.8 4.6 %collective-permute-start = (bf16[1,16,256]{2,1,0:T(8,128)(2,1)S(1)}, bf16[1,16,256]{2,1,0:T(8,128)(2,1)S(1)}, u32[]{:S(2)}, u32[]{:S(2)}) collective-permute-start(bf16[1,16,256]{2,1,0:T(8,128)(2,1)S(1)} %bitcast.11), channel_id=1, source_target_pairs={{0,1},{1,0},{2,3},{3,2},{4,5},{5,4},{6,7},{7,6},{8,9},{9,8},{10,11... | collective-permute-start | bytes 24584 | tf_op jit(solution)/shard_map/ppermute | solution.py:36
  6.4 3.8 %collective-permute-start.1 = (bf16[2,16,256]{2,1,0:T(8,128)(2,1)S(1)}, bf16[2,16,256]{2,1,0:T(8,128)(2,1)S(1)}, u32[]{:S(2)}, u32[]{:S(2)}) collective-permute-start(bf16[2,16,256]{2,1,0:T(8,128)(2,1)S(1)} %pad_maximum_fusion.2), channel_id=1, source_target_pairs={{0,2},{1,3},{2,0},{3,1},{4,6},{5,7},{6,4},{7,5},{8,10},{9,11},{10,... | collective-permute-start | bytes 49160 | tf_op jit(solution)/shard_map/ppermute | solution.py:36
  10.2 4.9 %collective-permute-start.2 = (bf16[4,16,256]{2,1,0:T(8,128)(2,1)S(1)}, bf16[4,16,256]{2,1,0:T(8,128)(2,1)S(1)}, u32[]{:S(2)}, u32[]{:S(2)}) collective-permute-start(bf16[4,16,256]{2,1,0:T(8,128)(2,1)S(1)} %pad_maximum_fusion.1), channel_id=1, source_target_pairs={{0,4},{1,5},{2,6},{3,7},{4,0},{5,1},{6,2},{7,3},{8,12},{9,13},{10,... | collective-permute-start | bytes 98312 | tf_op jit(solution)/shard_map/ppermute | solution.py:36
  65.1 2.2 %collective-permute-start.3 = (s16[48,4224]{1,0:T(8,128)(2,1)S(1)}, s16[48,4224]{1,0:T(8,128)(2,1)S(1)}, u32[]{:S(2)}, u32[]{:S(2)}) collective-permute-start(s16[48,4224]{1,0:T(8,128)(2,1)S(1)} %get-tuple-element.20), channel_id=1, source_target_pairs={{0,8},{8,0},{16,24},{24,16},{1,9},{9,1},{17,25},{25,17},{2,10},{10... | collective-permute-start | bytes 1216520 | tf_op jit(solution)/shard_map/ppermute | solution.py:36
  67.7 11.8 %collective-permute-start.4 = (s16[48,4224]{1,0:T(8,128)(2,1)S(1)}, s16[48,4224]{1,0:T(8,128)(2,1)S(1)}, u32[]{:S(2)}, u32[]{:S(2)}) collective-permute-start(s16[48,4224]{1,0:T(8,128)(2,1)S(1)} %add_half.2.a_ref), channel_id=1, source_target_pairs={{0,16},{8,24},{16,0},{24,8},{1,17},{9,25},{17,1},{25,9},{2,18},{10... | collective-permute-start | bytes 1216520 | tf_op jit(solution)/shard_map/ppermute | solution.py:36
  80.0 1.8 %collective-permute-start.5 = (s16[48,4224]{1,0:T(8,128)(2,1)S(1)}, s16[48,4224]{1,0:T(8,128)(2,1)S(1)}, u32[]{:S(2)}, u32[]{:S(2)}) collective-permute-start(s16[48,4224]{1,0:T(8,128)(2,1)S(1)} %add_half.3.mine_ref), channel_id=1, source_target_pairs={{0,8},{8,0},{16,24},{24,16},{1,9},{9,1},{17,25},{25,17},{2,10},{10... | collective-permute-start | bytes 1216520 | tf_op jit(solution)/shard_map/ppermute | solution.py:36

commit v7 on v4

--- a/solution.py
+++ b/solution.py
@@ -15,7 +15,7 @@
 POOL = 8
 BIN_ROWS = 256
 WINDOW = 24
-CHUNK = 64
+CHUNK = 16
 BLOCK = 512
 LAG = 3
 PAD = 128
@@ -88,13 +88,12 @@
 
 def stem_kernel(
     n, rows_dev, co, pay_ref, table_ref, weights_ref, grad_ref, p_ref, slope_ref, emb_ref,
-    table, weights, bases, ybuf, prev, sums, sa, sb, slopes, codes
+    table, weights, bases, ybuf, prev, sums, slopes
 ):
     step = pl.program_id(0)
     rows = n * rows_dev
     blocks = rows // BLOCK
     front = LAG * BLOCK + PAD
-    piece = 256
 
     def convolve(block):
         first = pl.multiple_of((block + LAG) * BLOCK, 128)
@@ -156,39 +155,21 @@
         ).astype(jnp.bfloat16)
         convolve(step - LAG)
         taps(step - 1)
-        codes[...] = onehot
-
-        def multiply(chunk, at, stage):
-            first = pl.multiple_of(chunk * (POOL * CHUNK), POOL * CHUNK)
-            stage[...] = jnp.dot(
-                table[pl.ds(first, POOL * CHUNK), :],
-                codes[:, at : at + piece],
-                preferred_element_type=jnp.float32,
-            )
-
-        def pool(chunk, at, stage):
-            for row in range(0, CHUNK, 16):
-                most = least = stage[row : row + 16, :]
+        for chunk in range(C0 // CHUNK):
+            for at in range(0, BLOCK, 256):
+                stem = jnp.dot(
+                    table[chunk * POOL * CHUNK : (chunk + 1) * POOL * CHUNK, :],
+                    onehot[:, at : at + 256],
+                    preferred_element_type=jnp.float32,
+                )
+                most = least = stem[:CHUNK]
                 for pos in range(1, POOL):
-                    part = stage[pos * CHUNK + row : pos * CHUNK + row + 16, :]
+                    part = stem[pos * CHUNK : (pos + 1) * CHUNK]
                     most = jnp.maximum(most, part)
                     least = jnp.minimum(least, part)
-                to = pl.multiple_of(chunk * CHUNK + row, 16)
-                prev[pl.ds(to, 16), at : at + piece] = jnp.maximum(
+                prev[chunk * CHUNK : (chunk + 1) * CHUNK, at : at + 256] = jnp.maximum(
                     twice_gelu(most), twice_gelu(least)
                 ).astype(jnp.bfloat16)
-
-        chunks = C0 // CHUNK
-        multiply(0, 0, sa)
-
-        def turn(chunk, carry):
-            multiply(chunk, piece, sb)
-            pool(chunk, 0, sa)
-            multiply(jnp.minimum(chunk + 1, chunks - 1), 0, sa)
-            pool(chunk, piece, sb)
-            return carry
-
-        lax.fori_loop(0, chunks, turn, 0)
         p_ref[...] = prev[...]
         slope_ref[...] = slopes[...]
 
@@ -252,10 +233,7 @@
             pltpu.VMEM((K1 * co, LAG * BLOCK + rows + 2 * PAD), jnp.float32),
             pltpu.VMEM((C0, BLOCK), jnp.bfloat16),
             pltpu.VMEM((128, 128), jnp.float32),
-            pltpu.VMEM((POOL * CHUNK, 256), jnp.float32),
-            pltpu.VMEM((POOL * CHUNK, 256), jnp.float32),
             pltpu.VMEM((co, BLOCK), jnp.float32),
-            pltpu.VMEM((128, BLOCK), jnp.bfloat16),
         ],
         compiler_params=params(36),
         name="stem_and_conv",

time: 91.4 us -> 74.4 us (0.81)
  Pallas kernels: 49.8 us -> 32.8 us
    pallas_call x1, Pallas kernels: 41.5 us -> 24.5 us  [stem_and_conv(): pl.pallas_call(functools.partial(stem_kernel, n, rows_dev, co), grid=(blo...]
  transfers between devices with their start and end apart: 6 -> 6, of which waited for: 5 -> 5; matrix products, arithmetic and copies ran while one was open for 1% -> 2% of each run, Pallas kernels for 3% -> 3%
where the time goes in v7:
time: 74.4 us; the launch traced here: 74.1 us
  Pallas kernels  32.8 us (44%)
  waiting for transfers between devices  15.5 us (21%)
  blocking collectives  12.9 us (17%)
  starting transfers between devices  9.83 us (13%)
  local copies, waits for them, and re-layouts  1.39 us (2%)
  other arithmetic  0.9 us (1%)
  between operations  0.79 us (1%)
    pallas_call x1, Pallas kernels, stem_and_conv(): pl.pallas_call(functools.partial(stem_kernel, n, rows_dev, co), grid=(blo...  24.5 us
    ppermute x6, waiting for transfers between devices, swap(): return lax.ppermute(x, axis, [(i, i ^ bit) for i in range(size)])  15.5 us
    all_to_all x1, blocking collectives, gather_direct(): lax.all_to_all(jnp.broadcast_to(x[None], (lax.axis_size(axis),) + x.shape...  12.9 us
    ppermute x6, starting transfers between devices, swap(): return lax.ppermute(x, axis, [(i, i ^ bit) for i in range(size)])  9.83 us
    pallas_call x1, Pallas kernels, send_half(): pl.pallas_call(functools.partial(send_kernel, n), out_shape=[jax.ShapeDty...  3.55 us
    pallas_call x1, Pallas kernels, keep_half(): pl.pallas_call(keep_kernel, out_shape=jax.ShapeDtypeStruct((size, WIDE),...  2.08 us
  transfers between devices with their start and end apart: 6, of which 5 were waited for; matrix products, arithmetic and copies ran while one was open for 2% of the time, Pallas kernels for 3%

profile of v7, /device:TPU:0, one launch (start us, length us, event | category | flops | bytes accessed | tf_op | source)
XLA Modules:
  0.0 74.1 jit_solution(4608075242744381986)
XLA Ops:
  0.6 0.0 copy-start.2
  0.6 0.0 copy-start.1
  0.7 0.0 copy-start
  0.7 0.9 %convert_reduce_fusion = bf16[4096]{0:T(1024)(128)(2,1)S(1)} fusion(s32[1,4096]{1,0:T(1,128)} %param.6), kind=kLoop, calls=%fused_computation.5 | loop fusion | flops 4096 | bytes 24576 | tf_op jit(solution)/shard_map/convert_element_type | solution.py:433
  1.5 0.2 reshape.13
  1.7 0.1 copy.11
  1.8 0.0 copy-start.3
  1.8 3.0 %collective-permute-start = (bf16[1,16,256]{2,1,0:T(8,128)(2,1)S(1)}, bf16[1,16,256]{2,1,0:T(8,128)(2,1)S(1)}, u32[]{:S(2)}, u32[]{:S(2)}) collective-permute-start(bf16[1,16,256]{2,1,0:T(8,128)(2,1)S(1)} %bitcast.11), channel_id=1, source_target_pairs={{0,1},{1,0},{2,3},{3,2},{4,5},{5,4},{6,7},{7,6},{8,9},{9,8},{10,11... | collective-permute-start | bytes 24584 | tf_op jit(solution)/shard_map/ppermute | solution.py:36
  4.8 1.6 %collective-permute-done = bf16[1,16,256]{2,1,0:T(8,128)(2,1)S(1)} collective-permute-done((bf16[1,16,256]{2,1,0:T(8,128)(2,1)S(1)}, bf16[1,16,256]{2,1,0:T(8,128)(2,1)S(1)}, u32[]{:S(2)}, u32[]{:S(2)}) %collective-permute-start) | collective-permute-done | bytes 8224 | tf_op jit(solution)/shard_map/ppermute | solution.py:36
  6.4 2.1 %collective-permute-start.1 = (bf16[2,16,256]{2,1,0:T(8,128)(2,1)S(1)}, bf16[2,16,256]{2,1,0:T(8,128)(2,1)S(1)}, u32[]{:S(2)}, u32[]{:S(2)}) collective-permute-start(bf16[2,16,256]{2,1,0:T(8,128)(2,1)S(1)} %pad_maximum_fusion.2), channel_id=1, source_target_pairs={{0,2},{1,3},{2,0},{3,1},{4,6},{5,7},{6,4},{7,5},{8,10},{9,11},{10,... | collective-permute-start | bytes 49160 | tf_op jit(solution)/shard_map/ppermute | solution.py:36
  8.5 0.9 %copy.15 = bf16[15,4,768]{2,0,1:T(8,128)(2,1)S(1)} copy(bf16[15,4,768]{2,1,0:T(4,128)(2,1)} %param.7) | data formatting | bytes 184320 | tf_op args[1]
  9.5 0.2 copy.13
  9.6 0.6 collective-permute-done.1
  10.2 3.0 %collective-permute-start.2 = (bf16[4,16,256]{2,1,0:T(8,128)(2,1)S(1)}, bf16[4,16,256]{2,1,0:T(8,128)(2,1)S(1)}, u32[]{:S(2)}, u32[]{:S(2)}) collective-permute-start(bf16[4,16,256]{2,1,0:T(8,128)(2,1)S(1)} %pad_maximum_fusion.1), channel_id=1, source_target_pairs={{0,4},{1,5},{2,6},{3,7},{4,0},{5,1},{6,2},{7,3},{8,12},{9,13},{10,... | collective-permute-start | bytes 98312 | tf_op jit(solution)/shard_map/ppermute | solution.py:36
  13.3 0.0 copy-done.2
  13.3 0.0 copy-done.1
  13.3 0.0 copy-done
  13.3 0.5 prepare.1
  13.8 1.3 %collective-permute-done.2 = bf16[4,16,256]{2,1,0:T(8,128)(2,1)S(1)} collective-permute-done((bf16[4,16,256]{2,1,0:T(8,128)(2,1)S(1)}, bf16[4,16,256]{2,1,0:T(8,128)(2,1)S(1)}, u32[]{:S(2)}, u32[]{:S(2)}) %collective-permute-start.2) | collective-permute-done | bytes 32800 | tf_op jit(solution)/shard_map/ppermute | solution.py:36
  15.2 0.0 copy-done.3
  15.2 24.5 %stem_and_conv.1 = (bf16[768,4096]{1,0:T(8,128)(2,1)S(1)}, f32[96,4096]{1,0:T(8,128)S(1)}, bf16[16,128]{1,0:T(8,128)(2,1)S(1)}) custom-call(bf16[8,16,256]{2,1,0:T(8,128)(2,1)S(1)} %pad_maximum_fusion.pay_ref, bf16[6144,128]{1,0:T(8,128)(2,1)S(1)} %get-tuple-element.12.table_ref, bf16[480,768]{1,0:T(8,128)(2,1)S(1)} %get-tuple-element.13.weights_ref, ...), custom_call_target="tpu_custom_call" | custom-call | tf_op jit(solution)/shard_map/stem_and_conv/pallas_call | solution.py:210
  39.7 12.9 %all_to_all.5.emb_ref = bf16[8,16,128]{2,1,0:T(8,128)(2,1)S(1)} all-to-all(bf16[8,16,128]{2,1,0:T(8,128)(2,1)S(1)} %broadcast_in_dim.2), channel_id=1, replica_groups=mesh['dp'=4,'seq'=8] {'seq'}, dimensions={0} | all-to-all | bytes 65536 | tf_op jit(solution)/shard_map/all_to_all | solution.py:49
  52.6 3.5 %send_half.1 = (s16[48,4224]{1,0:T(8,128)(2,1)S(1)}, bf16[2,48,4352]{2,1,0:T(8,128)(2,1)S(1)}, f32[2,48,256]{2,1,0:T(8,128)S(1)}) custom-call(bf16[8,16,128]{2,1,0:T(8,128)(2,1)S(1)} %all_to_all.5.emb_ref, bf16[1024,256]{1,0:T(8,128)(2,1)S(1)} %get-tuple-element.15.proj_ref, f32[96,4096]{1,0:T(8,128)S(1)} %get-tuple-element.16.slope_ref, ...), custom_call_target="tpu_custom_call" | custom-call | tf_op jit(solution)/shard_map/send_half/pallas_call | solution.py:362
  56.1 0.1 collective-permute-start.3
  56.2 2.1 %keep_half.1.a_ref = f32[48,4096]{1,0:T(8,128)S(1)} custom-call(bf16[2,48,4352]{2,1,0:T(8,128)(2,1)S(1)} %get-tuple-element.18.dconv_ref, f32[2,48,256]{2,1,0:T(8,128)S(1)} %get-tuple-element.19.qk_ref, bf16[768,4096]{1,0:T(8,128)(2,1)S(1)} %get-tuple-element.17.pooled_ref), custom_call_target="tpu_custom_call" | custom-call | flops 1509949440 | bytes 12582912 | tf_op jit(solution)/shard_map/keep_half/pallas_call | solution.py:377
  58.3 0.0 collective-permute-done.3.b_ref
  58.3 0.4 add_half.2.a_ref
  58.7 1.6 %collective-permute-start.4 = (s16[48,4224]{1,0:T(8,128)(2,1)S(1)}, s16[48,4224]{1,0:T(8,128)(2,1)S(1)}, u32[]{:S(2)}, u32[]{:S(2)}) collective-permute-start(s16[48,4224]{1,0:T(8,128)(2,1)S(1)} %add_half.2.a_ref), channel_id=1, source_target_pairs={{0,16},{8,24},{16,0},{24,8},{1,17},{9,25},{17,1},{25,9},{2,18},{10... | collective-permute-start | bytes 1216520 | tf_op jit(solution)/shard_map/ppermute | solution.py:36
  60.3 10.2 %collective-permute-done.4.b_ref = s16[48,4224]{1,0:T(8,128)(2,1)S(1)} collective-permute-done((s16[48,4224]{1,0:T(8,128)(2,1)S(1)}, s16[48,4224]{1,0:T(8,128)(2,1)S(1)}, u32[]{:S(2)}, u32[]{:S(2)}) %collective-permute-start.4) | collective-permute-done | bytes 405536 | tf_op jit(solution)/shard_map/ppermute | solution.py:36
  70.5 0.5 add_half.3.mine_ref
  71.0 0.1 collective-permute-start.5
  71.1 1.7 %collective-permute-done.5.other_ref = s16[48,4224]{1,0:T(8,128)(2,1)S(1)} collective-permute-done((s16[48,4224]{1,0:T(8,128)(2,1)S(1)}, s16[48,4224]{1,0:T(8,128)(2,1)S(1)}, u32[]{:S(2)}, u32[]{:S(2)}) %collective-permute-start.5) | collective-permute-done | bytes 405536 | tf_op jit(solution)/shard_map/ppermute | solution.py:36
  72.8 1.3 %join.1 = (f32[96,3840]{1,0:T(8,128)}, f32[96,128]{1,0:T(8,128)}, f32[96,128]{1,0:T(8,128)}) custom-call(s16[48,4224]{1,0:T(8,128)(2,1)S(1)} %add_half.3.mine_ref, s16[48,4224]{1,0:T(8,128)(2,1)S(1)} %collective-permute-done.5.other_ref), custom_call_target="tpu_custom_call" | custom-call | tf_op jit(solution)/shard_map/join/pallas_call | solution.py:417
  (6 shorter events, 0.1 us)
Async XLA Ops:
  0.6 12.7 %copy-start.2 = (bf16[768,128]{1,0:T(8,128)(2,1)S(1)}, bf16[768,128]{1,0:T(8,128)(2,1)}, u32[]{:S(2)}) copy-start(bf16[768,128]{1,0:T(8,128)(2,1)} %wk_ref.1) | copy-start | bytes 589828
  0.6 12.7 %copy-start.1 = (bf16[768,128]{1,0:T(8,128)(2,1)S(1)}, bf16[768,128]{1,0:T(8,128)(2,1)}, u32[]{:S(2)}) copy-start(bf16[768,128]{1,0:T(8,128)(2,1)} %wq_ref.1) | copy-start | bytes 589828
  0.7 12.7 %copy-start = (bf16[96,3840]{1,0:T(8,128)(2,1)S(1)}, bf16[96,3840]{1,0:T(8,128)(2,1)}, u32[]{:S(2)}) copy-start(bf16[96,3840]{1,0:T(8,128)(2,1)} %w_ref.1) | copy-start | bytes 2211844
  1.8 13.4 %copy-start.3 = (f32[1,2,16]{2,1,0:T(2,128)S(1)}, f32[1,2,16]{2,1,0:T(2,128)}, u32[]{:S(2)}) copy-start(f32[1,2,16]{2,1,0:T(2,128)} %param.11) | copy-start | bytes 388
  1.8 4.6 %collective-permute-start = (bf16[1,16,256]{2,1,0:T(8,128)(2,1)S(1)}, bf16[1,16,256]{2,1,0:T(8,128)(2,1)S(1)}, u32[]{:S(2)}, u32[]{:S(2)}) collective-permute-start(bf16[1,16,256]{2,1,0:T(8,128)(2,1)S(1)} %bitcast.11), channel_id=1, source_target_pairs={{0,1},{1,0},{2,3},{3,2},{4,5},{5,4},{6,7},{7,6},{8,9},{9,8},{10,11... | collective-permute-start | bytes 24584 | tf_op jit(solution)/shard_map/ppermute | solution.py:36
  6.4 3.8 %collective-permute-start.1 = (bf16[2,16,256]{2,1,0:T(8,128)(2,1)S(1)}, bf16[2,16,256]{2,1,0:T(8,128)(2,1)S(1)}, u32[]{:S(2)}, u32[]{:S(2)}) collective-permute-start(bf16[2,16,256]{2,1,0:T(8,128)(2,1)S(1)} %pad_maximum_fusion.2), channel_id=1, source_target_pairs={{0,2},{1,3},{2,0},{3,1},{4,6},{5,7},{6,4},{7,5},{8,10},{9,11},{10,... | collective-permute-start | bytes 49160 | tf_op jit(solution)/shard_map/ppermute | solution.py:36
  10.2 4.9 %collective-permute-start.2 = (bf16[4,16,256]{2,1,0:T(8,128)(2,1)S(1)}, bf16[4,16,256]{2,1,0:T(8,128)(2,1)S(1)}, u32[]{:S(2)}, u32[]{:S(2)}) collective-permute-start(bf16[4,16,256]{2,1,0:T(8,128)(2,1)S(1)} %pad_maximum_fusion.1), channel_id=1, source_target_pairs={{0,4},{1,5},{2,6},{3,7},{4,0},{5,1},{6,2},{7,3},{8,12},{9,13},{10,... | collective-permute-start | bytes 98312 | tf_op jit(solution)/shard_map/ppermute | solution.py:36
  56.1 2.2 %collective-permute-start.3 = (s16[48,4224]{1,0:T(8,128)(2,1)S(1)}, s16[48,4224]{1,0:T(8,128)(2,1)S(1)}, u32[]{:S(2)}, u32[]{:S(2)}) collective-permute-start(s16[48,4224]{1,0:T(8,128)(2,1)S(1)} %get-tuple-element.20), channel_id=1, source_target_pairs={{0,8},{8,0},{16,24},{24,16},{1,9},{9,1},{17,25},{25,17},{2,10},{10... | collective-permute-start | bytes 1216520 | tf_op jit(solution)/shard_map/ppermute | solution.py:36
  58.7 11.8 %collective-permute-start.4 = (s16[48,4224]{1,0:T(8,128)(2,1)S(1)}, s16[48,4224]{1,0:T(8,128)(2,1)S(1)}, u32[]{:S(2)}, u32[]{:S(2)}) collective-permute-start(s16[48,4224]{1,0:T(8,128)(2,1)S(1)} %add_half.2.a_ref), channel_id=1, source_target_pairs={{0,16},{8,24},{16,0},{24,8},{1,17},{9,25},{17,1},{25,9},{2,18},{10... | collective-permute-start | bytes 1216520 | tf_op jit(solution)/shard_map/ppermute | solution.py:36
  71.0 1.8 %collective-permute-start.5 = (s16[48,4224]{1,0:T(8,128)(2,1)S(1)}, s16[48,4224]{1,0:T(8,128)(2,1)S(1)}, u32[]{:S(2)}, u32[]{:S(2)}) collective-permute-start(s16[48,4224]{1,0:T(8,128)(2,1)S(1)} %add_half.3.mine_ref), channel_id=1, source_target_pairs={{0,8},{8,0},{16,24},{24,16},{1,9},{9,1},{17,25},{25,17},{2,10},{10... | collective-permute-start | bytes 1216520 | tf_op jit(solution)/shard_map/ppermute | solution.py:36

commit v8 on v7

--- a/solution.py
+++ b/solution.py
@@ -15,7 +15,7 @@
 POOL = 8
 BIN_ROWS = 256
 WINDOW = 24
-CHUNK = 16
+CHUNK = 32
 BLOCK = 512
 LAG = 3
 PAD = 128
@@ -87,8 +87,8 @@
 
 
 def stem_kernel(
-    n, rows_dev, co, pay_ref, table_ref, weights_ref, grad_ref, p_ref, slope_ref, emb_ref,
-    table, weights, bases, ybuf, prev, sums, slopes
+    n, rows_dev, co, pay_ref, table, weights, grad_ref, p_ref, slope_ref, emb_ref,
+    bases, ybuf, prev, sums, slopes
 ):
     step = pl.program_id(0)
     rows = n * rows_dev
@@ -135,8 +135,6 @@
             first = PAD + slab * rows_dev
             bases[:, first : first + half] = block[:POOL]
             bases[:, first + half : first + 2 * half] = block[POOL:]
-        table[...] = table_ref[...]
-        weights[...] = weights_ref[...]
         ybuf[:, front + rows :] = jnp.zeros((K1 * co, PAD), jnp.float32)
         prev[...] = jnp.zeros(prev.shape, jnp.bfloat16)
         sums[...] = jnp.zeros(sums.shape, jnp.float32)
@@ -155,8 +153,8 @@
         ).astype(jnp.bfloat16)
         convolve(step - LAG)
         taps(step - 1)
-        for chunk in range(C0 // CHUNK):
-            for at in range(0, BLOCK, 256):
+        for at in range(0, BLOCK, 256):
+            for chunk in range(C0 // CHUNK):
                 stem = jnp.dot(
                     table[chunk * POOL * CHUNK : (chunk + 1) * POOL * CHUNK, :],
                     onehot[:, at : at + 256],
@@ -167,10 +165,9 @@
                     part = stem[pos * CHUNK : (pos + 1) * CHUNK]
                     most = jnp.maximum(most, part)
                     least = jnp.minimum(least, part)
-                prev[chunk * CHUNK : (chunk + 1) * CHUNK, at : at + 256] = jnp.maximum(
-                    twice_gelu(most), twice_gelu(least)
-                ).astype(jnp.bfloat16)
-        p_ref[...] = prev[...]
+                pooled = jnp.maximum(twice_gelu(most), twice_gelu(least)).astype(jnp.bfloat16)
+                prev[chunk * CHUNK : (chunk + 1) * CHUNK, at : at + 256] = pooled
+                p_ref[chunk * CHUNK : (chunk + 1) * CHUNK, at : at + 256] = pooled
         slope_ref[...] = slopes[...]
 
     @pl.when(step >= blocks)
@@ -227,8 +224,6 @@
             jax.ShapeDtypeStruct((npos, SLOT), jnp.bfloat16),
         ],
         scratch_shapes=[
-            pltpu.VMEM(table.shape, jnp.bfloat16),
-            pltpu.VMEM(weights.shape, jnp.bfloat16),
             pltpu.VMEM((POOL, rows + 2 * PAD), jnp.float32),
             pltpu.VMEM((K1 * co, LAG * BLOCK + rows + 2 * PAD), jnp.float32),
             pltpu.VMEM((C0, BLOCK), jnp.bfloat16),

time: 74.4 us -> 75.7 us (1.017)
  Pallas kernels: 32.8 us -> 34.1 us
    pallas_call x1, Pallas kernels: 24.5 us -> 25.8 us  [stem_and_conv(): pl.pallas_call(functools.partial(stem_kernel, n, rows_dev, co), grid=(blo...]
where the time goes in v8:
time: 75.7 us; the launch traced here: 75.4 us
  Pallas kernels  34.1 us (45%)
  waiting for transfers between devices  15.5 us (20%)
  blocking collectives  12.9 us (17%)
  starting transfers between devices  9.83 us (13%)
  local copies, waits for them, and re-layouts  1.39 us (2%)
  other arithmetic  0.9 us (1%)
  between operations  0.79 us (1%)
    pallas_call x1, Pallas kernels, stem_and_conv(): pl.pallas_call(functools.partial(stem_kernel, n, rows_dev, co), grid=(blo...  25.8 us
    ppermute x6, waiting for transfers between devices, swap(): return lax.ppermute(x, axis, [(i, i ^ bit) for i in range(size)])  15.5 us
    all_to_all x1, blocking collectives, gather_direct(): lax.all_to_all(jnp.broadcast_to(x[None], (lax.axis_size(axis),) + x.shape...  12.9 us
    ppermute x6, starting transfers between devices, swap(): return lax.ppermute(x, axis, [(i, i ^ bit) for i in range(size)])  9.83 us
    pallas_call x1, Pallas kernels, send_half(): pl.pallas_call(functools.partial(send_kernel, n), out_shape=[jax.ShapeDty...  3.55 us
    pallas_call x1, Pallas kernels, keep_half(): pl.pallas_call(keep_kernel, out_shape=jax.ShapeDtypeStruct((size, WIDE),...  2.07 us
  transfers between devices with their start and end apart: 6, of which 5 were waited for; matrix products, arithmetic and copies ran while one was open for 2% of the time, Pallas kernels for 3%

profile of v8, /device:TPU:0, one launch (start us, length us, event | category | flops | bytes accessed | tf_op | source)
XLA Modules:
  0.0 75.4 jit_solution(2436191612061268972)
XLA Ops:
  0.6 0.0 copy-start.2
  0.6 0.0 copy-start.1
  0.7 0.0 copy-start
  0.7 0.9 %convert_reduce_fusion = bf16[4096]{0:T(1024)(128)(2,1)S(1)} fusion(s32[1,4096]{1,0:T(1,128)} %param.6), kind=kLoop, calls=%fused_computation.5 | loop fusion | flops 4096 | bytes 24576 | tf_op jit(solution)/shard_map/convert_element_type | solution.py:428
  1.5 0.2 reshape.13
  1.7 0.1 copy.11
  1.8 0.0 copy-start.3
  1.8 3.0 %collective-permute-start = (bf16[1,16,256]{2,1,0:T(8,128)(2,1)S(1)}, bf16[1,16,256]{2,1,0:T(8,128)(2,1)S(1)}, u32[]{:S(2)}, u32[]{:S(2)}) collective-permute-start(bf16[1,16,256]{2,1,0:T(8,128)(2,1)S(1)} %bitcast.11), channel_id=1, source_target_pairs={{0,1},{1,0},{2,3},{3,2},{4,5},{5,4},{6,7},{7,6},{8,9},{9,8},{10,11... | collective-permute-start | bytes 24584 | tf_op jit(solution)/shard_map/ppermute | solution.py:36
  4.8 1.6 %collective-permute-done = bf16[1,16,256]{2,1,0:T(8,128)(2,1)S(1)} collective-permute-done((bf16[1,16,256]{2,1,0:T(8,128)(2,1)S(1)}, bf16[1,16,256]{2,1,0:T(8,128)(2,1)S(1)}, u32[]{:S(2)}, u32[]{:S(2)}) %collective-permute-start) | collective-permute-done | bytes 8224 | tf_op jit(solution)/shard_map/ppermute | solution.py:36
  6.4 2.1 %collective-permute-start.1 = (bf16[2,16,256]{2,1,0:T(8,128)(2,1)S(1)}, bf16[2,16,256]{2,1,0:T(8,128)(2,1)S(1)}, u32[]{:S(2)}, u32[]{:S(2)}) collective-permute-start(bf16[2,16,256]{2,1,0:T(8,128)(2,1)S(1)} %pad_maximum_fusion.2), channel_id=1, source_target_pairs={{0,2},{1,3},{2,0},{3,1},{4,6},{5,7},{6,4},{7,5},{8,10},{9,11},{10,... | collective-permute-start | bytes 49160 | tf_op jit(solution)/shard_map/ppermute | solution.py:36
  8.5 0.9 %copy.15 = bf16[15,4,768]{2,0,1:T(8,128)(2,1)S(1)} copy(bf16[15,4,768]{2,1,0:T(4,128)(2,1)} %param.7) | data formatting | bytes 184320 | tf_op args[1]
  9.5 0.2 copy.13
  9.6 0.6 collective-permute-done.1
  10.2 3.0 %collective-permute-start.2 = (bf16[4,16,256]{2,1,0:T(8,128)(2,1)S(1)}, bf16[4,16,256]{2,1,0:T(8,128)(2,1)S(1)}, u32[]{:S(2)}, u32[]{:S(2)}) collective-permute-start(bf16[4,16,256]{2,1,0:T(8,128)(2,1)S(1)} %pad_maximum_fusion.1), channel_id=1, source_target_pairs={{0,4},{1,5},{2,6},{3,7},{4,0},{5,1},{6,2},{7,3},{8,12},{9,13},{10,... | collective-permute-start | bytes 98312 | tf_op jit(solution)/shard_map/ppermute | solution.py:36
  13.3 0.0 copy-done.2
  13.3 0.0 copy-done.1
  13.3 0.0 copy-done
  13.3 0.5 prepare.1
  13.8 1.3 %collective-permute-done.2 = bf16[4,16,256]{2,1,0:T(8,128)(2,1)S(1)} collective-permute-done((bf16[4,16,256]{2,1,0:T(8,128)(2,1)S(1)}, bf16[4,16,256]{2,1,0:T(8,128)(2,1)S(1)}, u32[]{:S(2)}, u32[]{:S(2)}) %collective-permute-start.2) | collective-permute-done | bytes 32800 | tf_op jit(solution)/shard_map/ppermute | solution.py:36
  15.2 0.0 copy-done.3
  15.2 25.8 %stem_and_conv.1 = (bf16[768,4096]{1,0:T(8,128)(2,1)S(1)}, f32[96,4096]{1,0:T(8,128)S(1)}, bf16[16,128]{1,0:T(8,128)(2,1)S(1)}) custom-call(bf16[8,16,256]{2,1,0:T(8,128)(2,1)S(1)} %pad_maximum_fusion.pay_ref, bf16[6144,128]{1,0:T(8,128)(2,1)S(1)} %get-tuple-element.12.table, bf16[480,768]{1,0:T(8,128)(2,1)S(1)} %get-tuple-element.13.weights, ...), custom_call_target="tpu_custom_call" | custom-call | tf_op jit(solution)/shard_map/stem_and_conv/pallas_call | solution.py:207
  41.0 12.9 %all_to_all.5.emb_ref = bf16[8,16,128]{2,1,0:T(8,128)(2,1)S(1)} all-to-all(bf16[8,16,128]{2,1,0:T(8,128)(2,1)S(1)} %broadcast_in_dim.2), channel_id=1, replica_groups=mesh['dp'=4,'seq'=8] {'seq'}, dimensions={0} | all-to-all | bytes 65536 | tf_op jit(solution)/shard_map/all_to_all | solution.py:49
  53.9 3.6 %send_half.1 = (s16[48,4224]{1,0:T(8,128)(2,1)S(1)}, bf16[2,48,4352]{2,1,0:T(8,128)(2,1)S(1)}, f32[2,48,256]{2,1,0:T(8,128)S(1)}) custom-call(bf16[8,16,128]{2,1,0:T(8,128)(2,1)S(1)} %all_to_all.5.emb_ref, bf16[1024,256]{1,0:T(8,128)(2,1)S(1)} %get-tuple-element.15.proj_ref, f32[96,4096]{1,0:T(8,128)S(1)} %get-tuple-element.16.slope_ref, ...), custom_call_target="tpu_custom_call" | custom-call | tf_op jit(solution)/shard_map/send_half/pallas_call | solution.py:357
  57.4 0.1 collective-permute-start.3
  57.5 2.1 %keep_half.1.a_ref = f32[48,4096]{1,0:T(8,128)S(1)} custom-call(bf16[2,48,4352]{2,1,0:T(8,128)(2,1)S(1)} %get-tuple-element.18.dconv_ref, f32[2,48,256]{2,1,0:T(8,128)S(1)} %get-tuple-element.19.qk_ref, bf16[768,4096]{1,0:T(8,128)(2,1)S(1)} %get-tuple-element.17.pooled_ref), custom_call_target="tpu_custom_call" | custom-call | flops 1509949440 | bytes 12582912 | tf_op jit(solution)/shard_map/keep_half/pallas_call | solution.py:372
  59.6 0.0 collective-permute-done.3.b_ref
  59.6 0.4 add_half.2.a_ref
  60.0 1.6 %collective-permute-start.4 = (s16[48,4224]{1,0:T(8,128)(2,1)S(1)}, s16[48,4224]{1,0:T(8,128)(2,1)S(1)}, u32[]{:S(2)}, u32[]{:S(2)}) collective-permute-start(s16[48,4224]{1,0:T(8,128)(2,1)S(1)} %add_half.2.a_ref), channel_id=1, source_target_pairs={{0,16},{8,24},{16,0},{24,8},{1,17},{9,25},{17,1},{25,9},{2,18},{10... | collective-permute-start | bytes 1216520 | tf_op jit(solution)/shard_map/ppermute | solution.py:36
  61.6 10.3 %collective-permute-done.4.b_ref = s16[48,4224]{1,0:T(8,128)(2,1)S(1)} collective-permute-done((s16[48,4224]{1,0:T(8,128)(2,1)S(1)}, s16[48,4224]{1,0:T(8,128)(2,1)S(1)}, u32[]{:S(2)}, u32[]{:S(2)}) %collective-permute-start.4) | collective-permute-done | bytes 405536 | tf_op jit(solution)/shard_map/ppermute | solution.py:36
  71.8 0.5 add_half.3.mine_ref
  72.3 0.1 collective-permute-start.5
  72.4 1.7 %collective-permute-done.5.other_ref = s16[48,4224]{1,0:T(8,128)(2,1)S(1)} collective-permute-done((s16[48,4224]{1,0:T(8,128)(2,1)S(1)}, s16[48,4224]{1,0:T(8,128)(2,1)S(1)}, u32[]{:S(2)}, u32[]{:S(2)}) %collective-permute-start.5) | collective-permute-done | bytes 405536 | tf_op jit(solution)/shard_map/ppermute | solution.py:36
  74.1 1.3 %join.1 = (f32[96,3840]{1,0:T(8,128)}, f32[96,128]{1,0:T(8,128)}, f32[96,128]{1,0:T(8,128)}) custom-call(s16[48,4224]{1,0:T(8,128)(2,1)S(1)} %add_half.3.mine_ref, s16[48,4224]{1,0:T(8,128)(2,1)S(1)} %collective-permute-done.5.other_ref), custom_call_target="tpu_custom_call" | custom-call | tf_op jit(solution)/shard_map/join/pallas_call | solution.py:412
  (6 shorter events, 0.1 us)
Async XLA Ops:
  0.6 12.7 %copy-start.2 = (bf16[768,128]{1,0:T(8,128)(2,1)S(1)}, bf16[768,128]{1,0:T(8,128)(2,1)}, u32[]{:S(2)}) copy-start(bf16[768,128]{1,0:T(8,128)(2,1)} %wk_ref.1) | copy-start | bytes 589828
  0.6 12.7 %copy-start.1 = (bf16[768,128]{1,0:T(8,128)(2,1)S(1)}, bf16[768,128]{1,0:T(8,128)(2,1)}, u32[]{:S(2)}) copy-start(bf16[768,128]{1,0:T(8,128)(2,1)} %wq_ref.1) | copy-start | bytes 589828
  0.7 12.7 %copy-start = (bf16[96,3840]{1,0:T(8,128)(2,1)S(1)}, bf16[96,3840]{1,0:T(8,128)(2,1)}, u32[]{:S(2)}) copy-start(bf16[96,3840]{1,0:T(8,128)(2,1)} %w_ref.1) | copy-start | bytes 2211844
  1.8 13.4 %copy-start.3 = (f32[1,2,16]{2,1,0:T(2,128)S(1)}, f32[1,2,16]{2,1,0:T(2,128)}, u32[]{:S(2)}) copy-start(f32[1,2,16]{2,1,0:T(2,128)} %param.11) | copy-start | bytes 388
  1.8 4.6 %collective-permute-start = (bf16[1,16,256]{2,1,0:T(8,128)(2,1)S(1)}, bf16[1,16,256]{2,1,0:T(8,128)(2,1)S(1)}, u32[]{:S(2)}, u32[]{:S(2)}) collective-permute-start(bf16[1,16,256]{2,1,0:T(8,128)(2,1)S(1)} %bitcast.11), channel_id=1, source_target_pairs={{0,1},{1,0},{2,3},{3,2},{4,5},{5,4},{6,7},{7,6},{8,9},{9,8},{10,11... | collective-permute-start | bytes 24584 | tf_op jit(solution)/shard_map/ppermute | solution.py:36
  6.4 3.8 %collective-permute-start.1 = (bf16[2,16,256]{2,1,0:T(8,128)(2,1)S(1)}, bf16[2,16,256]{2,1,0:T(8,128)(2,1)S(1)}, u32[]{:S(2)}, u32[]{:S(2)}) collective-permute-start(bf16[2,16,256]{2,1,0:T(8,128)(2,1)S(1)} %pad_maximum_fusion.2), channel_id=1, source_target_pairs={{0,2},{1,3},{2,0},{3,1},{4,6},{5,7},{6,4},{7,5},{8,10},{9,11},{10,... | collective-permute-start | bytes 49160 | tf_op jit(solution)/shard_map/ppermute | solution.py:36
  10.2 4.9 %collective-permute-start.2 = (bf16[4,16,256]{2,1,0:T(8,128)(2,1)S(1)}, bf16[4,16,256]{2,1,0:T(8,128)(2,1)S(1)}, u32[]{:S(2)}, u32[]{:S(2)}) collective-permute-start(bf16[4,16,256]{2,1,0:T(8,128)(2,1)S(1)} %pad_maximum_fusion.1), channel_id=1, source_target_pairs={{0,4},{1,5},{2,6},{3,7},{4,0},{5,1},{6,2},{7,3},{8,12},{9,13},{10,... | collective-permute-start | bytes 98312 | tf_op jit(solution)/shard_map/ppermute | solution.py:36
  57.4 2.1 %collective-permute-start.3 = (s16[48,4224]{1,0:T(8,128)(2,1)S(1)}, s16[48,4224]{1,0:T(8,128)(2,1)S(1)}, u32[]{:S(2)}, u32[]{:S(2)}) collective-permute-start(s16[48,4224]{1,0:T(8,128)(2,1)S(1)} %get-tuple-element.20), channel_id=1, source_target_pairs={{0,8},{8,0},{16,24},{24,16},{1,9},{9,1},{17,25},{25,17},{2,10},{10... | collective-permute-start | bytes 1216520 | tf_op jit(solution)/shard_map/ppermute | solution.py:36
  60.0 11.8 %collective-permute-start.4 = (s16[48,4224]{1,0:T(8,128)(2,1)S(1)}, s16[48,4224]{1,0:T(8,128)(2,1)S(1)}, u32[]{:S(2)}, u32[]{:S(2)}) collective-permute-start(s16[48,4224]{1,0:T(8,128)(2,1)S(1)} %add_half.2.a_ref), channel_id=1, source_target_pairs={{0,16},{8,24},{16,0},{24,8},{1,17},{9,25},{17,1},{25,9},{2,18},{10... | collective-permute-start | bytes 1216520 | tf_op jit(solution)/shard_map/ppermute | solution.py:36
  72.3 1.8 %collective-permute-start.5 = (s16[48,4224]{1,0:T(8,128)(2,1)S(1)}, s16[48,4224]{1,0:T(8,128)(2,1)S(1)}, u32[]{:S(2)}, u32[]{:S(2)}) collective-permute-start(s16[48,4224]{1,0:T(8,128)(2,1)S(1)} %add_half.3.mine_ref), channel_id=1, source_target_pairs={{0,8},{8,0},{16,24},{24,16},{1,9},{9,1},{17,25},{25,17},{2,10},{10... | collective-permute-start | bytes 1216520 | tf_op jit(solution)/shard_map/ppermute | solution.py:36

commit v9 on v8

--- a/solution.py
+++ b/solution.py
@@ -15,7 +15,7 @@
 POOL = 8
 BIN_ROWS = 256
 WINDOW = 24
-CHUNK = 32
+CHUNK = 16
 BLOCK = 512
 LAG = 3
 PAD = 128
@@ -43,10 +43,6 @@
         x = jnp.concatenate([x, swap(x, axis, bit)], axis=0)
         bit *= 2
     return x
-
-
-def gather_direct(x, axis):
-    return lax.all_to_all(jnp.broadcast_to(x[None], (lax.axis_size(axis),) + x.shape), axis, 0, 0)
 
 
 def twice_gelu(v):
@@ -88,9 +84,8 @@
 
 def stem_kernel(
     n, rows_dev, co, pay_ref, table, weights, grad_ref, p_ref, slope_ref, emb_ref,
-    bases, ybuf, prev, sums, slopes
+    bases, ybuf, sums
 ):
-    step = pl.program_id(0)
     rows = n * rows_dev
     blocks = rows // BLOCK
     front = LAG * BLOCK + PAD
@@ -107,7 +102,8 @@
         tangent = jnp.tanh(conv * (ROOT + (ROOT * CUBE) * square))
         half = 0.5 * conv
         gelu = half + half * tangent
-        slopes[...] = (0.5 + 0.5 * tangent) + half * (1.0 - tangent * tangent) * (
+        to = pl.multiple_of(jnp.maximum(block, 0) * BLOCK, 128)
+        slope_ref[:, pl.ds(to, BLOCK)] = (0.5 + 0.5 * tangent) + half * (1.0 - tangent * tangent) * (
             ROOT + (3.0 * ROOT * CUBE) * square
         )
         lane = lax.broadcasted_iota(jnp.int32, (co, 128), 1)
@@ -121,26 +117,25 @@
 
     def taps(block):
         ybuf[:, pl.ds(pl.multiple_of(front + block * BLOCK, 128), BLOCK)] = jnp.dot(
-            weights[...], prev[...], preferred_element_type=jnp.float32
+            weights[...],
+            p_ref[:, pl.ds(pl.multiple_of(jnp.maximum(block, 0) * BLOCK, 128), BLOCK)],
+            preferred_element_type=jnp.float32,
         )
 
-    @pl.when(step == 0)
-    def _():
-        me = lax.axis_index("seq")
-        bases[:, :PAD] = jnp.full((POOL, PAD), -1.0, jnp.float32)
-        bases[:, PAD + rows :] = jnp.full((POOL, PAD), -1.0, jnp.float32)
-        half = rows_dev // 2
-        for slab in range(n):
-            block = pay_ref[jnp.bitwise_xor(me, slab)].astype(jnp.float32)
-            first = PAD + slab * rows_dev
-            bases[:, first : first + half] = block[:POOL]
-            bases[:, first + half : first + 2 * half] = block[POOL:]
-        ybuf[:, front + rows :] = jnp.zeros((K1 * co, PAD), jnp.float32)
-        prev[...] = jnp.zeros(prev.shape, jnp.bfloat16)
-        sums[...] = jnp.zeros(sums.shape, jnp.float32)
-
-    @pl.when(step < blocks)
-    def _():
+    me = lax.axis_index("seq")
+    bases[:, :PAD] = jnp.full((POOL, PAD), -1.0, jnp.float32)
+    bases[:, PAD + rows :] = jnp.full((POOL, PAD), -1.0, jnp.float32)
+    half = rows_dev // 2
+    for slab in range(n):
+        block = pay_ref[jnp.bitwise_xor(me, slab)].astype(jnp.float32)
+        first = PAD + slab * rows_dev
+        bases[:, first : first + half] = block[:POOL]
+        bases[:, first + half : first + 2 * half] = block[POOL:]
+    ybuf[:, front + rows :] = jnp.zeros((K1 * co, PAD), jnp.float32)
+    p_ref[:, :BLOCK] = jnp.zeros((C0, BLOCK), jnp.bfloat16)
+    sums[...] = jnp.zeros(sums.shape, jnp.float32)
+
+    def main(step, carry):
         first = pl.multiple_of(step * BLOCK, 128)
         near = bases[:, pl.ds(first, BLOCK + 2 * PAD)]
         window = jnp.concatenate(
@@ -153,8 +148,8 @@
         ).astype(jnp.bfloat16)
         convolve(step - LAG)
         taps(step - 1)
-        for at in range(0, BLOCK, 256):
-            for chunk in range(C0 // CHUNK):
+        for chunk in range(C0 // CHUNK):
+            for at in range(0, BLOCK, 256):
                 stem = jnp.dot(
                     table[chunk * POOL * CHUNK : (chunk + 1) * POOL * CHUNK, :],
                     onehot[:, at : at + 256],
@@ -165,36 +160,30 @@
                     part = stem[pos * CHUNK : (pos + 1) * CHUNK]
                     most = jnp.maximum(most, part)
                     least = jnp.minimum(least, part)
-                pooled = jnp.maximum(twice_gelu(most), twice_gelu(least)).astype(jnp.bfloat16)
-                prev[chunk * CHUNK : (chunk + 1) * CHUNK, at : at + 256] = pooled
-                p_ref[chunk * CHUNK : (chunk + 1) * CHUNK, at : at + 256] = pooled
-        slope_ref[...] = slopes[...]
-
-    @pl.when(step >= blocks)
-    def _():
-        @pl.when(step == blocks)
-        def _():
-            taps(blocks - 1)
-
-        convolve(step - LAG)
-        slope_ref[...] = slopes[...]
-
-    @pl.when(step == blocks + LAG - 1)
-    def _():
-        own_pos, npos = grad_ref.shape
-        embed = sums[...].T[:npos, :].astype(jnp.bfloat16).astype(jnp.float32)
-        rest = grad_ref[...]
-        parts = []
-        for _ in range(3):
-            part = rest.astype(jnp.bfloat16).astype(jnp.float32)
-            parts.append(part)
-            rest = rest - part
-        grads = jnp.concatenate(
-            parts + [jnp.zeros((npos - 3 * own_pos, npos), jnp.float32)], axis=0
-        )
-        emb_ref[...] = jnp.concatenate(
-            [embed[:, :co], grads, jnp.zeros((npos, SLOT - co - npos), jnp.float32)], axis=1
-        ).astype(jnp.bfloat16)
+                p_ref[
+                    chunk * CHUNK : (chunk + 1) * CHUNK, pl.ds(pl.multiple_of(first + at, 128), 256)
+                ] = jnp.maximum(twice_gelu(most), twice_gelu(least)).astype(jnp.bfloat16)
+        return carry
+
+    lax.fori_loop(0, blocks, main, 0)
+    taps(blocks - 1)
+    for last in range(LAG):
+        convolve(blocks - LAG + last)
+
+    own_pos, npos = grad_ref.shape
+    embed = sums[...].T[:npos, :].astype(jnp.bfloat16).astype(jnp.float32)
+    rest = grad_ref[...]
+    parts = []
+    for _ in range(3):
+        part = rest.astype(jnp.bfloat16).astype(jnp.float32)
+        parts.append(part)
+        rest = rest - part
+    grads = jnp.concatenate(
+        parts + [jnp.zeros((npos - 3 * own_pos, npos), jnp.float32)], axis=0
+    )
+    emb_ref[...] = jnp.concatenate(
+        [embed[:, :co], grads, jnp.zeros((npos, SLOT - co - npos), jnp.float32)], axis=1
+    ).astype(jnp.bfloat16)
 
 
 def stem_and_conv(n, payload, table, weights, pair_grad):
@@ -202,22 +191,8 @@
     rows_dev = payload.shape[2] * 2
     rows = n * rows_dev
     npos = rows // BIN_ROWS
-    blocks = rows // BLOCK
-    whole = lambda i: (0, 0)
     return pl.pallas_call(
         functools.partial(stem_kernel, n, rows_dev, co),
-        grid=(blocks + LAG,),
-        in_specs=[
-            pl.BlockSpec(payload.shape, lambda i: (0, 0, 0)),
-            pl.BlockSpec(table.shape, whole),
-            pl.BlockSpec(weights.shape, whole),
-            pl.BlockSpec(pair_grad.shape, whole),
-        ],
-        out_specs=[
-            pl.BlockSpec((C0, BLOCK), lambda i: (0, jnp.minimum(i, blocks - 1))),
-            pl.BlockSpec((co, BLOCK), lambda i: (0, jnp.maximum(i - LAG, 0))),
-            pl.BlockSpec((npos, SLOT), whole),
-        ],
         out_shape=[
             jax.ShapeDtypeStruct((C0, rows), jnp.bfloat16),
             jax.ShapeDtypeStruct((co, rows), jnp.float32),
@@ -226,9 +201,7 @@
         scratch_shapes=[
             pltpu.VMEM((POOL, rows + 2 * PAD), jnp.float32),
             pltpu.VMEM((K1 * co, LAG * BLOCK + rows + 2 * PAD), jnp.float32),
-            pltpu.VMEM((C0, BLOCK), jnp.bfloat16),
             pltpu.VMEM((128, 128), jnp.float32),
-            pltpu.VMEM((co, BLOCK), jnp.float32),
         ],
         compiler_params=params(36),
         name="stem_and_conv",
@@ -295,14 +268,14 @@
     scale = PC**-0.5
     me = lax.axis_index("seq")
     both = jnp.dot(
-        jnp.concatenate([emb_ref[slot] for slot in range(n)], axis=1),
+        jnp.concatenate([emb_ref[jnp.bitwise_xor(me, slab)] for slab in range(n)], axis=1),
         proj_ref[...],
         preferred_element_type=jnp.float32,
     )
     query, keys = both[:, :PC], both[:, PC:]
     pieces = []
     for slab in range(n):
-        block = emb_ref[slab].astype(jnp.float32)
+        block = emb_ref[jnp.bitwise_xor(me, slab)].astype(jnp.float32)
         total = block[:own_pos]
         for part in range(1, 3):
             total = total + block[part * own_pos : (part + 1) * own_pos]
@@ -323,7 +296,7 @@
         (((1,), (1,)), ((), ())), precision=HIGH, preferred_element_type=jnp.float32,
     ) * (0.5 / BIN_ROWS)
     qk = lax.dot_general(
-        emb_ref[me].astype(jnp.float32), cotangent, (((0,), (0,)), ((), ())),
+        emb_ref[0].astype(jnp.float32), cotangent, (((0,), (0,)), ((), ())),
         precision=HIGH, preferred_element_type=jnp.float32,
     )
     edge = jnp.zeros((held, PAD), jnp.bfloat16)
@@ -435,7 +408,7 @@
     table, weights, proj = prepare(n, first_table, conv_weight, query_weight, key_weight)
 
     pooled, slope, embed = stem_and_conv(n, payload, table, weights, pair_grad[0])
-    embed_all = gather_direct(embed, "seq")
+    embed_all = gather_xor(embed, "seq")
     send, dconv, qk = send_half(n, embed_all, proj, slope, pooled)
     received = swap(send, "dp", 1)
     keep = keep_half(dconv, qk, pooled)

time: 75.7 us -> 71.5 us (0.945)
  blocking collectives: 12.9 us -> 0 us
  starting transfers between devices: 9.83 us -> 16.9 us
  waiting for transfers between devices: 15.5 us -> 20.5 us
  Pallas kernels: 34.1 us -> 30.8 us
    all_to_all x1 -> x0, blocking collectives: 12.9 us -> none  [gather_direct(): lax.all_to_all(jnp.broadcast_to(x[None], (lax.axis_size(axis),) + x.shape...]
    ppermute x6 -> x9, starting transfers between devices: 9.83 us -> 16.9 us  [swap(): return lax.ppermute(x, axis, [(i, i ^ bit) for i in range(size)])]
    ppermute x6 -> x9, waiting for transfers between devices: 15.5 us -> 20.5 us  [swap(): return lax.ppermute(x, axis, [(i, i ^ bit) for i in range(size)])]
    pallas_call x1, Pallas kernels: 25.8 us -> 22.5 us  [stem_and_conv(): pl.pallas_call(functools.partial(stem_kernel, n, rows_dev, co), out_shape...]
  transfers between devices with their start and end apart: 6 -> 9, of which waited for: 5 -> 8; matrix products, arithmetic and copies ran while one was open for 2% -> 2% of each run, Pallas kernels for 3% -> 4%
where the time goes in v9:
time: 71.5 us; the launch traced here: 71.2 us
  Pallas kernels  30.8 us (43%)
  waiting for transfers between devices  20.5 us (29%)
  starting transfers between devices  16.9 us (24%)
  local copies, waits for them, and re-layouts  1.38 us (2%)
  other arithmetic  0.92 us (1%)
  between operations  0.78 us (1%)
    pallas_call x1, Pallas kernels, stem_and_conv(): pl.pallas_call(functools.partial(stem_kernel, n, rows_dev, co), out_shape...  22.5 us
    ppermute x9, waiting for transfers between devices, swap(): return lax.ppermute(x, axis, [(i, i ^ bit) for i in range(size)])  20.5 us
    ppermute x9, starting transfers between devices, swap(): return lax.ppermute(x, axis, [(i, i ^ bit) for i in range(size)])  16.9 us
    pallas_call x1, Pallas kernels, send_half(): pl.pallas_call(functools.partial(send_kernel, n), out_shape=[jax.ShapeDty...  3.56 us
    pallas_call x1, Pallas kernels, keep_half(): pl.pallas_call(keep_kernel, out_shape=jax.ShapeDtypeStruct((size, WIDE),...  2.07 us
  transfers between devices with their start and end apart: 9, of which 8 were waited for; matrix products, arithmetic and copies ran while one was open for 2% of the time, Pallas kernels for 4%

profile of v9, /device:TPU:0, one launch (start us, length us, event | category | flops | bytes accessed | tf_op | source)
XLA Modules:
  0.0 71.2 jit_solution(7650308027074202341)
XLA Ops:
  0.6 0.0 copy-start.2
  0.6 0.0 copy-start.1
  0.7 0.0 copy-start
  0.7 0.9 %convert_reduce_fusion = bf16[4096]{0:T(1024)(128)(2,1)S(1)} fusion(s32[1,4096]{1,0:T(1,128)} %param.6), kind=kLoop, calls=%fused_computation.7 | loop fusion | flops 4096 | bytes 24576 | tf_op jit(solution)/shard_map/convert_element_type | solution.py:401
  1.5 0.2 reshape.12
  1.7 0.1 copy.11
  1.8 0.0 copy-start.3
  1.8 3.0 %collective-permute-start = (bf16[1,16,256]{2,1,0:T(8,128)(2,1)S(1)}, bf16[1,16,256]{2,1,0:T(8,128)(2,1)S(1)}, u32[]{:S(2)}, u32[]{:S(2)}) collective-permute-start(bf16[1,16,256]{2,1,0:T(8,128)(2,1)S(1)} %bitcast.16), channel_id=1, source_target_pairs={{0,1},{1,0},{2,3},{3,2},{4,5},{5,4},{6,7},{7,6},{8,9},{9,8},{10,11... | collective-permute-start | bytes 24584 | tf_op jit(solution)/shard_map/ppermute | solution.py:36
  4.8 1.6 %collective-permute-done = bf16[1,16,256]{2,1,0:T(8,128)(2,1)S(1)} collective-permute-done((bf16[1,16,256]{2,1,0:T(8,128)(2,1)S(1)}, bf16[1,16,256]{2,1,0:T(8,128)(2,1)S(1)}, u32[]{:S(2)}, u32[]{:S(2)}) %collective-permute-start) | collective-permute-done | bytes 8224 | tf_op jit(solution)/shard_map/ppermute | solution.py:36
  6.4 2.1 %collective-permute-start.1 = (bf16[2,16,256]{2,1,0:T(8,128)(2,1)S(1)}, bf16[2,16,256]{2,1,0:T(8,128)(2,1)S(1)}, u32[]{:S(2)}, u32[]{:S(2)}) collective-permute-start(bf16[2,16,256]{2,1,0:T(8,128)(2,1)S(1)} %pad_maximum_fusion.3), channel_id=1, source_target_pairs={{0,2},{1,3},{2,0},{3,1},{4,6},{5,7},{6,4},{7,5},{8,10},{9,11},{10,... | collective-permute-start | bytes 49160 | tf_op jit(solution)/shard_map/ppermute | solution.py:36
  8.5 0.9 %copy.15 = bf16[15,4,768]{2,0,1:T(8,128)(2,1)S(1)} copy(bf16[15,4,768]{2,1,0:T(4,128)(2,1)} %param.7) | data formatting | bytes 184320 | tf_op args[1]
  9.5 0.2 copy.13
  9.6 0.6 collective-permute-done.1
  10.2 3.0 %collective-permute-start.2 = (bf16[4,16,256]{2,1,0:T(8,128)(2,1)S(1)}, bf16[4,16,256]{2,1,0:T(8,128)(2,1)S(1)}, u32[]{:S(2)}, u32[]{:S(2)}) collective-permute-start(bf16[4,16,256]{2,1,0:T(8,128)(2,1)S(1)} %pad_maximum_fusion.1), channel_id=1, source_target_pairs={{0,4},{1,5},{2,6},{3,7},{4,0},{5,1},{6,2},{7,3},{8,12},{9,13},{10,... | collective-permute-start | bytes 98312 | tf_op jit(solution)/shard_map/ppermute | solution.py:36
  13.3 0.0 copy-done.2
  13.3 0.0 copy-done.1
  13.3 0.0 copy-done
  13.3 0.5 prepare.1
  13.8 1.3 %collective-permute-done.2 = bf16[4,16,256]{2,1,0:T(8,128)(2,1)S(1)} collective-permute-done((bf16[4,16,256]{2,1,0:T(8,128)(2,1)S(1)}, bf16[4,16,256]{2,1,0:T(8,128)(2,1)S(1)}, u32[]{:S(2)}, u32[]{:S(2)}) %collective-permute-start.2) | collective-permute-done | bytes 32800 | tf_op jit(solution)/shard_map/ppermute | solution.py:36
  15.2 0.0 copy-done.3
  15.2 22.5 %stem_and_conv.1 = (bf16[768,4096]{1,0:T(8,128)(2,1)S(1)}, f32[96,4096]{1,0:T(8,128)S(1)}, bf16[16,128]{1,0:T(8,128)(2,1)S(1)}) custom-call(bf16[8,16,256]{2,1,0:T(8,128)(2,1)S(1)} %pad_maximum_fusion.pay_ref, bf16[6144,128]{1,0:T(8,128)(2,1)S(1)} %get-tuple-element.12.table, bf16[480,768]{1,0:T(8,128)(2,1)S(1)} %get-tuple-element.13.weights, ...), custom_call_target="tpu_custom_call" | custom-call | tf_op jit(solution)/shard_map/stem_and_conv/pallas_call | solution.py:194
  37.7 1.9 %collective-permute-start.3 = (bf16[1,16,128]{2,1,0:T(8,128)(2,1)S(1)}, bf16[1,16,128]{2,1,0:T(8,128)(2,1)S(1)}, u32[]{:S(2)}, u32[]{:S(2)}) collective-permute-start(bf16[1,16,128]{2,1,0:T(8,128)(2,1)S(1)} %bitcast.8), channel_id=1, source_target_pairs={{0,1},{1,0},{2,3},{3,2},{4,5},{5,4},{6,7},{7,6},{8,9},{9,8},{10,11... | collective-permute-start | bytes 12296 | tf_op jit(solution)/shard_map/ppermute | solution.py:36
  39.6 1.8 %collective-permute-done.3 = bf16[1,16,128]{2,1,0:T(8,128)(2,1)S(1)} collective-permute-done((bf16[1,16,128]{2,1,0:T(8,128)(2,1)S(1)}, bf16[1,16,128]{2,1,0:T(8,128)(2,1)S(1)}, u32[]{:S(2)}, u32[]{:S(2)}) %collective-permute-start.3) | collective-permute-done | bytes 4128 | tf_op jit(solution)/shard_map/ppermute | solution.py:36
  41.3 1.9 %collective-permute-start.4 = (bf16[2,16,128]{2,1,0:T(8,128)(2,1)S(1)}, bf16[2,16,128]{2,1,0:T(8,128)(2,1)S(1)}, u32[]{:S(2)}, u32[]{:S(2)}) collective-permute-start(bf16[2,16,128]{2,1,0:T(8,128)(2,1)S(1)} %pad_maximum_fusion.5), channel_id=1, source_target_pairs={{0,2},{1,3},{2,0},{3,1},{4,6},{5,7},{6,4},{7,5},{8,10},{9,11},{10,... | collective-permute-start | bytes 24584 | tf_op jit(solution)/shard_map/ppermute | solution.py:36
  43.2 1.7 %collective-permute-done.4 = bf16[2,16,128]{2,1,0:T(8,128)(2,1)S(1)} collective-permute-done((bf16[2,16,128]{2,1,0:T(8,128)(2,1)S(1)}, bf16[2,16,128]{2,1,0:T(8,128)(2,1)S(1)}, u32[]{:S(2)}, u32[]{:S(2)}) %collective-permute-start.4) | collective-permute-done | bytes 8224 | tf_op jit(solution)/shard_map/ppermute | solution.py:36
  45.0 2.9 %collective-permute-start.5 = (bf16[4,16,128]{2,1,0:T(8,128)(2,1)S(1)}, bf16[4,16,128]{2,1,0:T(8,128)(2,1)S(1)}, u32[]{:S(2)}, u32[]{:S(2)}) collective-permute-start(bf16[4,16,128]{2,1,0:T(8,128)(2,1)S(1)} %pad_maximum_fusion.4), channel_id=1, source_target_pairs={{0,4},{1,5},{2,6},{3,7},{4,0},{5,1},{6,2},{7,3},{8,12},{9,13},{10,... | collective-permute-start | bytes 49160 | tf_op jit(solution)/shard_map/ppermute | solution.py:36
  47.9 1.7 %collective-permute-done.5 = bf16[4,16,128]{2,1,0:T(8,128)(2,1)S(1)} collective-permute-done((bf16[4,16,128]{2,1,0:T(8,128)(2,1)S(1)}, bf16[4,16,128]{2,1,0:T(8,128)(2,1)S(1)}, u32[]{:S(2)}, u32[]{:S(2)}) %collective-permute-start.5) | collective-permute-done | bytes 16416 | tf_op jit(solution)/shard_map/ppermute | solution.py:36
  49.6 3.6 %send_half.1 = (s16[48,4224]{1,0:T(8,128)(2,1)S(1)}, bf16[2,48,4352]{2,1,0:T(8,128)(2,1)S(1)}, f32[2,48,256]{2,1,0:T(8,128)S(1)}) custom-call(bf16[8,16,128]{2,1,0:T(8,128)(2,1)S(1)} %pad_maximum_fusion.2.emb_ref, bf16[1024,256]{1,0:T(8,128)(2,1)S(1)} %get-tuple-element.15.proj_ref, f32[96,4096]{1,0:T(8,128)S(1)} %get-tuple-element.16.slope_ref, ...), custom_call_target="tpu_custom_call" | custom-call | tf_op jit(solution)/shard_map/send_half/pallas_call | solution.py:330
  53.2 0.1 collective-permute-start.6
  53.3 2.1 %keep_half.1.a_ref = f32[48,4096]{1,0:T(8,128)S(1)} custom-call(bf16[2,48,4352]{2,1,0:T(8,128)(2,1)S(1)} %get-tuple-element.18.dconv_ref, f32[2,48,256]{2,1,0:T(8,128)S(1)} %get-tuple-element.19.qk_ref, bf16[768,4096]{1,0:T(8,128)(2,1)S(1)} %get-tuple-element.17.pooled_ref), custom_call_target="tpu_custom_call" | custom-call | flops 1509949440 | bytes 12582912 | tf_op jit(solution)/shard_map/keep_half/pallas_call | solution.py:345
  55.4 0.0 collective-permute-done.6.b_ref
  55.4 0.4 add_half.2.a_ref
  55.8 1.9 %collective-permute-start.7 = (s16[48,4224]{1,0:T(8,128)(2,1)S(1)}, s16[48,4224]{1,0:T(8,128)(2,1)S(1)}, u32[]{:S(2)}, u32[]{:S(2)}) collective-permute-start(s16[48,4224]{1,0:T(8,128)(2,1)S(1)} %add_half.2.a_ref), channel_id=1, source_target_pairs={{0,16},{8,24},{16,0},{24,8},{1,17},{9,25},{17,1},{25,9},{2,18},{10... | collective-permute-start | bytes 1216520 | tf_op jit(solution)/shard_map/ppermute | solution.py:36
  57.6 10.0 %collective-permute-done.7.b_ref = s16[48,4224]{1,0:T(8,128)(2,1)S(1)} collective-permute-done((s16[48,4224]{1,0:T(8,128)(2,1)S(1)}, s16[48,4224]{1,0:T(8,128)(2,1)S(1)}, u32[]{:S(2)}, u32[]{:S(2)}) %collective-permute-start.7) | collective-permute-done | bytes 405536 | tf_op jit(solution)/shard_map/ppermute | solution.py:36
  67.7 0.5 add_half.3.mine_ref
  68.1 0.1 collective-permute-start.8
  68.2 1.7 %collective-permute-done.8.other_ref = s16[48,4224]{1,0:T(8,128)(2,1)S(1)} collective-permute-done((s16[48,4224]{1,0:T(8,128)(2,1)S(1)}, s16[48,4224]{1,0:T(8,128)(2,1)S(1)}, u32[]{:S(2)}, u32[]{:S(2)}) %collective-permute-start.8) | collective-permute-done | bytes 405536 | tf_op jit(solution)/shard_map/ppermute | solution.py:36
  69.9 1.3 %join.1 = (f32[96,3840]{1,0:T(8,128)}, f32[96,128]{1,0:T(8,128)}, f32[96,128]{1,0:T(8,128)}) custom-call(s16[48,4224]{1,0:T(8,128)(2,1)S(1)} %add_half.3.mine_ref, s16[48,4224]{1,0:T(8,128)(2,1)S(1)} %collective-permute-done.8.other_ref), custom_call_target="tpu_custom_call" | custom-call | tf_op jit(solution)/shard_map/join/pallas_call | solution.py:385
  (8 shorter events, 0.1 us)
Async XLA Ops:
  0.6 12.7 %copy-start.2 = (bf16[768,128]{1,0:T(8,128)(2,1)S(1)}, bf16[768,128]{1,0:T(8,128)(2,1)}, u32[]{:S(2)}) copy-start(bf16[768,128]{1,0:T(8,128)(2,1)} %wk_ref.1) | copy-start | bytes 589828
  0.6 12.7 %copy-start.1 = (bf16[768,128]{1,0:T(8,128)(2,1)S(1)}, bf16[768,128]{1,0:T(8,128)(2,1)}, u32[]{:S(2)}) copy-start(bf16[768,128]{1,0:T(8,128)(2,1)} %wq_ref.1) | copy-start | bytes 589828
  0.7 12.7 %copy-start = (bf16[96,3840]{1,0:T(8,128)(2,1)S(1)}, bf16[96,3840]{1,0:T(8,128)(2,1)}, u32[]{:S(2)}) copy-start(bf16[96,3840]{1,0:T(8,128)(2,1)} %w_ref.1) | copy-start | bytes 2211844
  1.8 13.4 %copy-start.3 = (f32[1,2,16]{2,1,0:T(2,128)S(1)}, f32[1,2,16]{2,1,0:T(2,128)}, u32[]{:S(2)}) copy-start(f32[1,2,16]{2,1,0:T(2,128)} %param.11) | copy-start | bytes 388
  1.8 4.6 %collective-permute-start = (bf16[1,16,256]{2,1,0:T(8,128)(2,1)S(1)}, bf16[1,16,256]{2,1,0:T(8,128)(2,1)S(1)}, u32[]{:S(2)}, u32[]{:S(2)}) collective-permute-start(bf16[1,16,256]{2,1,0:T(8,128)(2,1)S(1)} %bitcast.16), channel_id=1, source_target_pairs={{0,1},{1,0},{2,3},{3,2},{4,5},{5,4},{6,7},{7,6},{8,9},{9,8},{10,11... | collective-permute-start | bytes 24584 | tf_op jit(solution)/shard_map/ppermute | solution.py:36
  6.4 3.8 %collective-permute-start.1 = (bf16[2,16,256]{2,1,0:T(8,128)(2,1)S(1)}, bf16[2,16,256]{2,1,0:T(8,128)(2,1)S(1)}, u32[]{:S(2)}, u32[]{:S(2)}) collective-permute-start(bf16[2,16,256]{2,1,0:T(8,128)(2,1)S(1)} %pad_maximum_fusion.3), channel_id=1, source_target_pairs={{0,2},{1,3},{2,0},{3,1},{4,6},{5,7},{6,4},{7,5},{8,10},{9,11},{10,... | collective-permute-start | bytes 49160 | tf_op jit(solution)/shard_map/ppermute | solution.py:36
  10.2 4.9 %collective-permute-start.2 = (bf16[4,16,256]{2,1,0:T(8,128)(2,1)S(1)}, bf16[4,16,256]{2,1,0:T(8,128)(2,1)S(1)}, u32[]{:S(2)}, u32[]{:S(2)}) collective-permute-start(bf16[4,16,256]{2,1,0:T(8,128)(2,1)S(1)} %pad_maximum_fusion.1), channel_id=1, source_target_pairs={{0,4},{1,5},{2,6},{3,7},{4,0},{5,1},{6,2},{7,3},{8,12},{9,13},{10,... | collective-permute-start | bytes 98312 | tf_op jit(solution)/shard_map/ppermute | solution.py:36
  37.7 3.6 %collective-permute-start.3 = (bf16[1,16,128]{2,1,0:T(8,128)(2,1)S(1)}, bf16[1,16,128]{2,1,0:T(8,128)(2,1)S(1)}, u32[]{:S(2)}, u32[]{:S(2)}) collective-permute-start(bf16[1,16,128]{2,1,0:T(8,128)(2,1)S(1)} %bitcast.8), channel_id=1, source_target_pairs={{0,1},{1,0},{2,3},{3,2},{4,5},{5,4},{6,7},{7,6},{8,9},{9,8},{10,11... | collective-permute-start | bytes 12296 | tf_op jit(solution)/shard_map/ppermute | solution.py:36
  41.3 3.7 %collective-permute-start.4 = (bf16[2,16,128]{2,1,0:T(8,128)(2,1)S(1)}, bf16[2,16,128]{2,1,0:T(8,128)(2,1)S(1)}, u32[]{:S(2)}, u32[]{:S(2)}) collective-permute-start(bf16[2,16,128]{2,1,0:T(8,128)(2,1)S(1)} %pad_maximum_fusion.5), channel_id=1, source_target_pairs={{0,2},{1,3},{2,0},{3,1},{4,6},{5,7},{6,4},{7,5},{8,10},{9,11},{10,... | collective-permute-start | bytes 24584 | tf_op jit(solution)/shard_map/ppermute | solution.py:36
  45.0 4.7 %collective-permute-start.5 = (bf16[4,16,128]{2,1,0:T(8,128)(2,1)S(1)}, bf16[4,16,128]{2,1,0:T(8,128)(2,1)S(1)}, u32[]{:S(2)}, u32[]{:S(2)}) collective-permute-start(bf16[4,16,128]{2,1,0:T(8,128)(2,1)S(1)} %pad_maximum_fusion.4), channel_id=1, source_target_pairs={{0,4},{1,5},{2,6},{3,7},{4,0},{5,1},{6,2},{7,3},{8,12},{9,13},{10,... | collective-permute-start | bytes 49160 | tf_op jit(solution)/shard_map/ppermute | solution.py:36
  53.2 2.1 %collective-permute-start.6 = (s16[48,4224]{1,0:T(8,128)(2,1)S(1)}, s16[48,4224]{1,0:T(8,128)(2,1)S(1)}, u32[]{:S(2)}, u32[]{:S(2)}) collective-permute-start(s16[48,4224]{1,0:T(8,128)(2,1)S(1)} %get-tuple-element.20), channel_id=1, source_target_pairs={{0,8},{8,0},{16,24},{24,16},{1,9},{9,1},{17,25},{25,17},{2,10},{10... | collective-permute-start | bytes 1216520 | tf_op jit(solution)/shard_map/ppermute | solution.py:36
  55.8 11.9 %collective-permute-start.7 = (s16[48,4224]{1,0:T(8,128)(2,1)S(1)}, s16[48,4224]{1,0:T(8,128)(2,1)S(1)}, u32[]{:S(2)}, u32[]{:S(2)}) collective-permute-start(s16[48,4224]{1,0:T(8,128)(2,1)S(1)} %add_half.2.a_ref), channel_id=1, source_target_pairs={{0,16},{8,24},{16,0},{24,8},{1,17},{9,25},{17,1},{25,9},{2,18},{10... | collective-permute-start | bytes 1216520 | tf_op jit(solution)/shard_map/ppermute | solution.py:36
  68.1 1.8 %collective-permute-start.8 = (s16[48,4224]{1,0:T(8,128)(2,1)S(1)}, s16[48,4224]{1,0:T(8,128)(2,1)S(1)}, u32[]{:S(2)}, u32[]{:S(2)}) collective-permute-start(s16[48,4224]{1,0:T(8,128)(2,1)S(1)} %add_half.3.mine_ref), channel_id=1, source_target_pairs={{0,8},{8,0},{16,24},{24,16},{1,9},{9,1},{17,25},{25,17},{2,10},{10... | collective-permute-start | bytes 1216520 | tf_op jit(solution)/shard_map/ppermute | solution.py:36

commit v10 on v9

--- a/solution.py
+++ b/solution.py
@@ -47,6 +47,39 @@
 
 def twice_gelu(v):
     return v + v * jnp.tanh(v * (ROOT + (ROOT * CUBE) * (v * v)))
+
+
+def regroup_kernel(bases_ref, out_ref):
+    lines, width = bases_ref.shape
+    per = width // POOL
+    rows = lines * per
+    line = lax.broadcasted_iota(jnp.int32, (lines, rows), 0)
+    column = lax.broadcasted_iota(jnp.int32, (lines, rows), 1)
+    spread = lax.dot_general(
+        bases_ref[...].astype(jnp.float32).astype(jnp.bfloat16),
+        (column // per == line).astype(jnp.float32).astype(jnp.bfloat16),
+        (((0,), (0,)), ((), ())),
+        preferred_element_type=jnp.float32,
+    )
+    place = lax.broadcasted_iota(jnp.int32, (width, rows), 0) // POOL
+    column = lax.broadcasted_iota(jnp.int32, (width, rows), 1)
+    spread = jnp.where(place == column % per, spread, 0.0)
+    grouped = spread[:POOL]
+    for i in range(1, per):
+        grouped = grouped + spread[i * POOL : (i + 1) * POOL]
+    out_ref[...] = jnp.concatenate(
+        [grouped[:, : rows // 2], grouped[:, rows // 2 :]], axis=0
+    ).astype(jnp.bfloat16)
+
+
+def regroup(bases):
+    rows = bases.shape[1] // POOL
+    return pl.pallas_call(
+        regroup_kernel,
+        out_shape=jax.ShapeDtypeStruct((2 * POOL, rows // 2), jnp.bfloat16),
+        compiler_params=params(4),
+        name="regroup",
+    )(bases.reshape(bases.shape[1] // 128, 128))
 
 
 def prepare_kernel(n, co, t0_ref, w_ref, wq_ref, wk_ref, table_ref, weights_ref, proj_ref):
@@ -148,8 +181,8 @@
         ).astype(jnp.bfloat16)
         convolve(step - LAG)
         taps(step - 1)
-        for chunk in range(C0 // CHUNK):
-            for at in range(0, BLOCK, 256):
+        for at in range(0, BLOCK, 256):
+            for chunk in range(C0 // CHUNK):
                 stem = jnp.dot(
                     table[chunk * POOL * CHUNK : (chunk + 1) * POOL * CHUNK, :],
                     onehot[:, at : at + 256],
@@ -396,10 +429,7 @@
 
 def body(bases, stem_table, conv_weight, query_weight, key_weight, pair_grad):
     n = lax.axis_size("seq")
-    rows_dev = bases.shape[1] // POOL
-
-    own = bases.astype(jnp.bfloat16).reshape(2, rows_dev // 2, POOL).transpose(0, 2, 1)
-    payload = gather_xor(own.reshape(2 * POOL, rows_dev // 2), "seq")
+    payload = gather_xor(regroup(bases), "seq")
 
     first_table = jnp.pad(
         stem_table.transpose(2, 1, 0), ((0, 0), (0, 0), (1, WINDOW - 1 - K0))

time: 71.5 us -> 71.1 us (level)
  other arithmetic: 0.92 us -> 0.06 us
    convert_element_type x1 -> x0, other arithmetic: 0.86 us -> none  [body(): bases.astype(jnp.bfloat16).reshape(2, rows_dev // 2, POOL)]
    unnamed x9 -> x11, local copies, waits for them, and re-layouts: 0.92 us -> 1.72 us
where the time goes in v10:
time: 71.1 us; the launch traced here: 70.9 us
  Pallas kernels  30.7 us (43%)
  waiting for transfers between devices  20.5 us (29%)
  starting transfers between devices  16.9 us (24%)
  local copies, waits for them, and re-layouts  1.92 us (3%)
  between operations  0.79 us (1%)
    pallas_call x1, Pallas kernels, stem_and_conv(): pl.pallas_call(functools.partial(stem_kernel, n, rows_dev, co), out_shape...  22.2 us
    ppermute x9, waiting for transfers between devices, swap(): return lax.ppermute(x, axis, [(i, i ^ bit) for i in range(size)])  20.5 us
    ppermute x9, starting transfers between devices, swap(): return lax.ppermute(x, axis, [(i, i ^ bit) for i in range(size)])  16.9 us
    pallas_call x1, Pallas kernels, send_half(): pl.pallas_call(functools.partial(send_kernel, n), out_shape=[jax.ShapeDty...  3.54 us
    pallas_call x1, Pallas kernels, keep_half(): pl.pallas_call(keep_kernel, out_shape=jax.ShapeDtypeStruct((size, WIDE),...  2.07 us
    unnamed x11, local copies, waits for them, and re-layouts  1.72 us
  transfers between devices with their start and end apart: 9, of which 8 were waited for; matrix products, arithmetic and copies ran while one was open for 2% of the time, Pallas kernels for 4%

profile of v10, /device:TPU:0, one launch (start us, length us, event | category | flops | bytes accessed | tf_op | source)
XLA Modules:
  0.0 70.9 jit_solution(11262074467899155476)
XLA Ops:
  0.6 0.0 copy-start.2
  0.6 0.0 copy-start.1
  0.7 0.0 copy-start
  0.7 0.0 copy-start.3
  0.7 0.8 %copy-done.3 = s32[1,4096]{1,0:T(1,128)S(1)} copy-done((s32[1,4096]{1,0:T(1,128)S(1)}, s32[1,4096]{1,0:T(1,128)}, u32[]{:S(2)}) %copy-start.3) | copy-done | bytes 16408
  1.5 0.2 regroup.1
  1.7 0.0 copy-start.4
  1.7 3.0 %collective-permute-start = (bf16[1,16,256]{2,1,0:T(8,128)(2,1)S(1)}, bf16[1,16,256]{2,1,0:T(8,128)(2,1)S(1)}, u32[]{:S(2)}, u32[]{:S(2)}) collective-permute-start(bf16[1,16,256]{2,1,0:T(8,128)(2,1)S(1)} %bitcast.8), channel_id=1, source_target_pairs={{0,1},{1,0},{2,3},{3,2},{4,5},{5,4},{6,7},{7,6},{8,9},{9,8},{10,11... | collective-permute-start | bytes 24584 | tf_op jit(solution)/shard_map/ppermute | solution.py:36
  4.7 1.6 %collective-permute-done = bf16[1,16,256]{2,1,0:T(8,128)(2,1)S(1)} collective-permute-done((bf16[1,16,256]{2,1,0:T(8,128)(2,1)S(1)}, bf16[1,16,256]{2,1,0:T(8,128)(2,1)S(1)}, u32[]{:S(2)}, u32[]{:S(2)}) %collective-permute-start) | collective-permute-done | bytes 8224 | tf_op jit(solution)/shard_map/ppermute | solution.py:36
  6.4 2.1 %collective-permute-start.1 = (bf16[2,16,256]{2,1,0:T(8,128)(2,1)S(1)}, bf16[2,16,256]{2,1,0:T(8,128)(2,1)S(1)}, u32[]{:S(2)}, u32[]{:S(2)}) collective-permute-start(bf16[2,16,256]{2,1,0:T(8,128)(2,1)S(1)} %pad_maximum_fusion.3), channel_id=1, source_target_pairs={{0,2},{1,3},{2,0},{3,1},{4,6},{5,7},{6,4},{7,5},{8,10},{9,11},{10,... | collective-permute-start | bytes 49160 | tf_op jit(solution)/shard_map/ppermute | solution.py:36
  8.4 0.9 %copy.13 = bf16[15,4,768]{2,0,1:T(8,128)(2,1)S(1)} copy(bf16[15,4,768]{2,1,0:T(4,128)(2,1)} %param.7) | data formatting | bytes 184320 | tf_op args[1]
  9.4 0.2 copy.11
  9.6 0.6 collective-permute-done.1
  10.2 3.0 %collective-permute-start.2 = (bf16[4,16,256]{2,1,0:T(8,128)(2,1)S(1)}, bf16[4,16,256]{2,1,0:T(8,128)(2,1)S(1)}, u32[]{:S(2)}, u32[]{:S(2)}) collective-permute-start(bf16[4,16,256]{2,1,0:T(8,128)(2,1)S(1)} %pad_maximum_fusion.1), channel_id=1, source_target_pairs={{0,4},{1,5},{2,6},{3,7},{4,0},{5,1},{6,2},{7,3},{8,12},{9,13},{10,... | collective-permute-start | bytes 98312 | tf_op jit(solution)/shard_map/ppermute | solution.py:36
  13.2 0.0 copy-done.2
  13.2 0.0 copy-done.1
  13.3 0.0 copy-done
  13.3 0.5 prepare.1
  13.8 1.3 %collective-permute-done.2 = bf16[4,16,256]{2,1,0:T(8,128)(2,1)S(1)} collective-permute-done((bf16[4,16,256]{2,1,0:T(8,128)(2,1)S(1)}, bf16[4,16,256]{2,1,0:T(8,128)(2,1)S(1)}, u32[]{:S(2)}, u32[]{:S(2)}) %collective-permute-start.2) | collective-permute-done | bytes 32800 | tf_op jit(solution)/shard_map/ppermute | solution.py:36
  15.1 0.0 copy-done.4
  15.1 22.2 %stem_and_conv.1 = (bf16[768,4096]{1,0:T(8,128)(2,1)S(1)}, f32[96,4096]{1,0:T(8,128)S(1)}, bf16[16,128]{1,0:T(8,128)(2,1)S(1)}) custom-call(bf16[8,16,256]{2,1,0:T(8,128)(2,1)S(1)} %pad_maximum_fusion.pay_ref, bf16[6144,128]{1,0:T(8,128)(2,1)S(1)} %get-tuple-element.12.table, bf16[480,768]{1,0:T(8,128)(2,1)S(1)} %get-tuple-element.13.weights, ...), custom_call_target="tpu_custom_call" | custom-call | tf_op jit(solution)/shard_map/stem_and_conv/pallas_call | solution.py:227
  37.3 1.9 %collective-permute-start.3 = (bf16[1,16,128]{2,1,0:T(8,128)(2,1)S(1)}, bf16[1,16,128]{2,1,0:T(8,128)(2,1)S(1)}, u32[]{:S(2)}, u32[]{:S(2)}) collective-permute-start(bf16[1,16,128]{2,1,0:T(8,128)(2,1)S(1)} %bitcast.12), channel_id=1, source_target_pairs={{0,1},{1,0},{2,3},{3,2},{4,5},{5,4},{6,7},{7,6},{8,9},{9,8},{10,11... | collective-permute-start | bytes 12296 | tf_op jit(solution)/shard_map/ppermute | solution.py:36
  39.2 1.8 %collective-permute-done.3 = bf16[1,16,128]{2,1,0:T(8,128)(2,1)S(1)} collective-permute-done((bf16[1,16,128]{2,1,0:T(8,128)(2,1)S(1)}, bf16[1,16,128]{2,1,0:T(8,128)(2,1)S(1)}, u32[]{:S(2)}, u32[]{:S(2)}) %collective-permute-start.3) | collective-permute-done | bytes 4128 | tf_op jit(solution)/shard_map/ppermute | solution.py:36
  41.0 1.9 %collective-permute-start.4 = (bf16[2,16,128]{2,1,0:T(8,128)(2,1)S(1)}, bf16[2,16,128]{2,1,0:T(8,128)(2,1)S(1)}, u32[]{:S(2)}, u32[]{:S(2)}) collective-permute-start(bf16[2,16,128]{2,1,0:T(8,128)(2,1)S(1)} %pad_maximum_fusion.5), channel_id=1, source_target_pairs={{0,2},{1,3},{2,0},{3,1},{4,6},{5,7},{6,4},{7,5},{8,10},{9,11},{10,... | collective-permute-start | bytes 24584 | tf_op jit(solution)/shard_map/ppermute | solution.py:36
  42.9 1.7 %collective-permute-done.4 = bf16[2,16,128]{2,1,0:T(8,128)(2,1)S(1)} collective-permute-done((bf16[2,16,128]{2,1,0:T(8,128)(2,1)S(1)}, bf16[2,16,128]{2,1,0:T(8,128)(2,1)S(1)}, u32[]{:S(2)}, u32[]{:S(2)}) %collective-permute-start.4) | collective-permute-done | bytes 8224 | tf_op jit(solution)/shard_map/ppermute | solution.py:36
  44.6 2.9 %collective-permute-start.5 = (bf16[4,16,128]{2,1,0:T(8,128)(2,1)S(1)}, bf16[4,16,128]{2,1,0:T(8,128)(2,1)S(1)}, u32[]{:S(2)}, u32[]{:S(2)}) collective-permute-start(bf16[4,16,128]{2,1,0:T(8,128)(2,1)S(1)} %pad_maximum_fusion.4), channel_id=1, source_target_pairs={{0,4},{1,5},{2,6},{3,7},{4,0},{5,1},{6,2},{7,3},{8,12},{9,13},{10,... | collective-permute-start | bytes 49160 | tf_op jit(solution)/shard_map/ppermute | solution.py:36
  47.6 1.7 %collective-permute-done.5 = bf16[4,16,128]{2,1,0:T(8,128)(2,1)S(1)} collective-permute-done((bf16[4,16,128]{2,1,0:T(8,128)(2,1)S(1)}, bf16[4,16,128]{2,1,0:T(8,128)(2,1)S(1)}, u32[]{:S(2)}, u32[]{:S(2)}) %collective-permute-start.5) | collective-permute-done | bytes 16416 | tf_op jit(solution)/shard_map/ppermute | solution.py:36
  49.3 3.5 %send_half.1 = (s16[48,4224]{1,0:T(8,128)(2,1)S(1)}, bf16[2,48,4352]{2,1,0:T(8,128)(2,1)S(1)}, f32[2,48,256]{2,1,0:T(8,128)S(1)}) custom-call(bf16[8,16,128]{2,1,0:T(8,128)(2,1)S(1)} %pad_maximum_fusion.2.emb_ref, bf16[1024,256]{1,0:T(8,128)(2,1)S(1)} %get-tuple-element.15.proj_ref, f32[96,4096]{1,0:T(8,128)S(1)} %get-tuple-element.16.slope_ref, ...), custom_call_target="tpu_custom_call" | custom-call | tf_op jit(solution)/shard_map/send_half/pallas_call | solution.py:363
  52.8 0.1 collective-permute-start.6
  52.9 2.1 %keep_half.1.a_ref = f32[48,4096]{1,0:T(8,128)S(1)} custom-call(bf16[2,48,4352]{2,1,0:T(8,128)(2,1)S(1)} %get-tuple-element.18.dconv_ref, f32[2,48,256]{2,1,0:T(8,128)S(1)} %get-tuple-element.19.qk_ref, bf16[768,4096]{1,0:T(8,128)(2,1)S(1)} %get-tuple-element.17.pooled_ref), custom_call_target="tpu_custom_call" | custom-call | flops 1509949440 | bytes 12582912 | tf_op jit(solution)/shard_map/keep_half/pallas_call | solution.py:378
  55.0 0.0 collective-permute-done.6.b_ref
  55.0 0.4 add_half.2.a_ref
  55.4 1.9 %collective-permute-start.7 = (s16[48,4224]{1,0:T(8,128)(2,1)S(1)}, s16[48,4224]{1,0:T(8,128)(2,1)S(1)}, u32[]{:S(2)}, u32[]{:S(2)}) collective-permute-start(s16[48,4224]{1,0:T(8,128)(2,1)S(1)} %add_half.2.a_ref), channel_id=1, source_target_pairs={{0,16},{8,24},{16,0},{24,8},{1,17},{9,25},{17,1},{25,9},{2,18},{10... | collective-permute-start | bytes 1216520 | tf_op jit(solution)/shard_map/ppermute | solution.py:36
  57.3 10.0 %collective-permute-done.7.b_ref = s16[48,4224]{1,0:T(8,128)(2,1)S(1)} collective-permute-done((s16[48,4224]{1,0:T(8,128)(2,1)S(1)}, s16[48,4224]{1,0:T(8,128)(2,1)S(1)}, u32[]{:S(2)}, u32[]{:S(2)}) %collective-permute-start.7) | collective-permute-done | bytes 405536 | tf_op jit(solution)/shard_map/ppermute | solution.py:36
  67.3 0.5 add_half.3.mine_ref
  67.8 0.1 collective-permute-start.8
  67.9 1.7 %collective-permute-done.8.other_ref = s16[48,4224]{1,0:T(8,128)(2,1)S(1)} collective-permute-done((s16[48,4224]{1,0:T(8,128)(2,1)S(1)}, s16[48,4224]{1,0:T(8,128)(2,1)S(1)}, u32[]{:S(2)}, u32[]{:S(2)}) %collective-permute-start.8) | collective-permute-done | bytes 405536 | tf_op jit(solution)/shard_map/ppermute | solution.py:36
  69.6 1.3 %join.1 = (f32[96,3840]{1,0:T(8,128)}, f32[96,128]{1,0:T(8,128)}, f32[96,128]{1,0:T(8,128)}) custom-call(s16[48,4224]{1,0:T(8,128)(2,1)S(1)} %add_half.3.mine_ref, s16[48,4224]{1,0:T(8,128)(2,1)S(1)} %collective-permute-done.8.other_ref), custom_call_target="tpu_custom_call" | custom-call | tf_op jit(solution)/shard_map/join/pallas_call | solution.py:418
  (8 shorter events, 0.1 us)
Async XLA Ops:
  0.6 12.6 %copy-start.2 = (bf16[768,128]{1,0:T(8,128)(2,1)S(1)}, bf16[768,128]{1,0:T(8,128)(2,1)}, u32[]{:S(2)}) copy-start(bf16[768,128]{1,0:T(8,128)(2,1)} %wk_ref.1) | copy-start | bytes 589828
  0.6 12.6 %copy-start.1 = (bf16[768,128]{1,0:T(8,128)(2,1)S(1)}, bf16[768,128]{1,0:T(8,128)(2,1)}, u32[]{:S(2)}) copy-start(bf16[768,128]{1,0:T(8,128)(2,1)} %wq_ref.1) | copy-start | bytes 589828
  0.7 12.6 %copy-start = (bf16[96,3840]{1,0:T(8,128)(2,1)S(1)}, bf16[96,3840]{1,0:T(8,128)(2,1)}, u32[]{:S(2)}) copy-start(bf16[96,3840]{1,0:T(8,128)(2,1)} %w_ref.1) | copy-start | bytes 2211844
  0.7 0.8 %copy-start.3 = (s32[1,4096]{1,0:T(1,128)S(1)}, s32[1,4096]{1,0:T(1,128)}, u32[]{:S(2)}) copy-start(s32[1,4096]{1,0:T(1,128)} %param.6) | copy-start | bytes 49156
  1.7 13.4 %copy-start.4 = (f32[1,2,16]{2,1,0:T(2,128)S(1)}, f32[1,2,16]{2,1,0:T(2,128)}, u32[]{:S(2)}) copy-start(f32[1,2,16]{2,1,0:T(2,128)} %param.11) | copy-start | bytes 388
  1.7 4.7 %collective-permute-start = (bf16[1,16,256]{2,1,0:T(8,128)(2,1)S(1)}, bf16[1,16,256]{2,1,0:T(8,128)(2,1)S(1)}, u32[]{:S(2)}, u32[]{:S(2)}) collective-permute-start(bf16[1,16,256]{2,1,0:T(8,128)(2,1)S(1)} %bitcast.8), channel_id=1, source_target_pairs={{0,1},{1,0},{2,3},{3,2},{4,5},{5,4},{6,7},{7,6},{8,9},{9,8},{10,11... | collective-permute-start | bytes 24584 | tf_op jit(solution)/shard_map/ppermute | solution.py:36
  6.4 3.8 %collective-permute-start.1 = (bf16[2,16,256]{2,1,0:T(8,128)(2,1)S(1)}, bf16[2,16,256]{2,1,0:T(8,128)(2,1)S(1)}, u32[]{:S(2)}, u32[]{:S(2)}) collective-permute-start(bf16[2,16,256]{2,1,0:T(8,128)(2,1)S(1)} %pad_maximum_fusion.3), channel_id=1, source_target_pairs={{0,2},{1,3},{2,0},{3,1},{4,6},{5,7},{6,4},{7,5},{8,10},{9,11},{10,... | collective-permute-start | bytes 49160 | tf_op jit(solution)/shard_map/ppermute | solution.py:36
  10.2 4.9 %collective-permute-start.2 = (bf16[4,16,256]{2,1,0:T(8,128)(2,1)S(1)}, bf16[4,16,256]{2,1,0:T(8,128)(2,1)S(1)}, u32[]{:S(2)}, u32[]{:S(2)}) collective-permute-start(bf16[4,16,256]{2,1,0:T(8,128)(2,1)S(1)} %pad_maximum_fusion.1), channel_id=1, source_target_pairs={{0,4},{1,5},{2,6},{3,7},{4,0},{5,1},{6,2},{7,3},{8,12},{9,13},{10,... | collective-permute-start | bytes 98312 | tf_op jit(solution)/shard_map/ppermute | solution.py:36
  37.3 3.6 %collective-permute-start.3 = (bf16[1,16,128]{2,1,0:T(8,128)(2,1)S(1)}, bf16[1,16,128]{2,1,0:T(8,128)(2,1)S(1)}, u32[]{:S(2)}, u32[]{:S(2)}) collective-permute-start(bf16[1,16,128]{2,1,0:T(8,128)(2,1)S(1)} %bitcast.12), channel_id=1, source_target_pairs={{0,1},{1,0},{2,3},{3,2},{4,5},{5,4},{6,7},{7,6},{8,9},{9,8},{10,11... | collective-permute-start | bytes 12296 | tf_op jit(solution)/shard_map/ppermute | solution.py:36
  41.0 3.7 %collective-permute-start.4 = (bf16[2,16,128]{2,1,0:T(8,128)(2,1)S(1)}, bf16[2,16,128]{2,1,0:T(8,128)(2,1)S(1)}, u32[]{:S(2)}, u32[]{:S(2)}) collective-permute-start(bf16[2,16,128]{2,1,0:T(8,128)(2,1)S(1)} %pad_maximum_fusion.5), channel_id=1, source_target_pairs={{0,2},{1,3},{2,0},{3,1},{4,6},{5,7},{6,4},{7,5},{8,10},{9,11},{10,... | collective-permute-start | bytes 24584 | tf_op jit(solution)/shard_map/ppermute | solution.py:36
  44.6 4.7 %collective-permute-start.5 = (bf16[4,16,128]{2,1,0:T(8,128)(2,1)S(1)}, bf16[4,16,128]{2,1,0:T(8,128)(2,1)S(1)}, u32[]{:S(2)}, u32[]{:S(2)}) collective-permute-start(bf16[4,16,128]{2,1,0:T(8,128)(2,1)S(1)} %pad_maximum_fusion.4), channel_id=1, source_target_pairs={{0,4},{1,5},{2,6},{3,7},{4,0},{5,1},{6,2},{7,3},{8,12},{9,13},{10,... | collective-permute-start | bytes 49160 | tf_op jit(solution)/shard_map/ppermute | solution.py:36
  52.8 2.2 %collective-permute-start.6 = (s16[48,4224]{1,0:T(8,128)(2,1)S(1)}, s16[48,4224]{1,0:T(8,128)(2,1)S(1)}, u32[]{:S(2)}, u32[]{:S(2)}) collective-permute-start(s16[48,4224]{1,0:T(8,128)(2,1)S(1)} %get-tuple-element.20), channel_id=1, source_target_pairs={{0,8},{8,0},{16,24},{24,16},{1,9},{9,1},{17,25},{25,17},{2,10},{10... | collective-permute-start | bytes 1216520 | tf_op jit(solution)/shard_map/ppermute | solution.py:36
  55.4 11.9 %collective-permute-start.7 = (s16[48,4224]{1,0:T(8,128)(2,1)S(1)}, s16[48,4224]{1,0:T(8,128)(2,1)S(1)}, u32[]{:S(2)}, u32[]{:S(2)}) collective-permute-start(s16[48,4224]{1,0:T(8,128)(2,1)S(1)} %add_half.2.a_ref), channel_id=1, source_target_pairs={{0,16},{8,24},{16,0},{24,8},{1,17},{9,25},{17,1},{25,9},{2,18},{10... | collective-permute-start | bytes 1216520 | tf_op jit(solution)/shard_map/ppermute | solution.py:36
  67.8 1.8 %collective-permute-start.8 = (s16[48,4224]{1,0:T(8,128)(2,1)S(1)}, s16[48,4224]{1,0:T(8,128)(2,1)S(1)}, u32[]{:S(2)}, u32[]{:S(2)}) collective-permute-start(s16[48,4224]{1,0:T(8,128)(2,1)S(1)} %add_half.3.mine_ref), channel_id=1, source_target_pairs={{0,8},{8,0},{16,24},{24,16},{1,9},{9,1},{17,25},{25,17},{2,10},{10... | collective-permute-start | bytes 1216520 | tf_op jit(solution)/shard_map/ppermute | solution.py:36

commit v11 on v10

--- a/solution.py
+++ b/solution.py
@@ -123,30 +123,29 @@
     blocks = rows // BLOCK
     front = LAG * BLOCK + PAD
 
-    def convolve(block):
-        first = pl.multiple_of((block + LAG) * BLOCK, 128)
+    group = 16
+
+    def convolve(block, row, part):
+        first = pl.multiple_of((block + LAG) * BLOCK + part * BIN_ROWS, 128)
         conv = None
         for tap in range(K1):
-            near = ybuf[tap * co : (tap + 1) * co, pl.ds(first, BLOCK + 2 * PAD)]
+            near = ybuf[tap * co + row : tap * co + row + group, pl.ds(first, BIN_ROWS + 2 * PAD)]
             begin = PAD + tap - K1 // 2
-            part = near[:, begin : begin + BLOCK]
-            conv = part if conv is None else conv + part
+            shifted = near[:, begin : begin + BIN_ROWS]
+            conv = shifted if conv is None else conv + shifted
         square = conv * conv
         tangent = jnp.tanh(conv * (ROOT + (ROOT * CUBE) * square))
         half = 0.5 * conv
         gelu = half + half * tangent
-        to = pl.multiple_of(jnp.maximum(block, 0) * BLOCK, 128)
-        slope_ref[:, pl.ds(to, BLOCK)] = (0.5 + 0.5 * tangent) + half * (1.0 - tangent * tangent) * (
-            ROOT + (3.0 * ROOT * CUBE) * square
+        to = pl.multiple_of(jnp.maximum(block, 0) * BLOCK + part * BIN_ROWS, 128)
+        slope_ref[row : row + group, pl.ds(to, BIN_ROWS)] = (0.5 + 0.5 * tangent) + half * (
+            1.0 - tangent * tangent
+        ) * (ROOT + (3.0 * ROOT * CUBE) * square)
+        mean = jnp.sum(gelu, axis=1, keepdims=True) * (1.0 / BIN_ROWS)
+        lane = lax.broadcasted_iota(jnp.int32, (group, 128), 1)
+        sums[row : row + group, :] = jnp.where(
+            lane == block * (BLOCK // BIN_ROWS) + part, mean, sums[row : row + group, :]
         )
-        lane = lax.broadcasted_iota(jnp.int32, (co, 128), 1)
-        total = sums[:co, :]
-        for part in range(BLOCK // BIN_ROWS):
-            mean = jnp.sum(
-                gelu[:, part * BIN_ROWS : (part + 1) * BIN_ROWS], axis=1, keepdims=True
-            ) * (1.0 / BIN_ROWS)
-            total = jnp.where(lane == block * (BLOCK // BIN_ROWS) + part, mean, total)
-        sums[:co, :] = total
 
     def taps(block):
         ybuf[:, pl.ds(pl.multiple_of(front + block * BLOCK, 128), BLOCK)] = jnp.dot(
@@ -179,10 +178,12 @@
             + [jnp.zeros((128 - 4 * WINDOW, BLOCK), jnp.float32)],
             axis=0,
         ).astype(jnp.bfloat16)
-        convolve(step - LAG)
         taps(step - 1)
+        every = (C0 // CHUNK) // (co // group)
         for at in range(0, BLOCK, 256):
             for chunk in range(C0 // CHUNK):
+                if chunk % every == 0:
+                    convolve(step - LAG, chunk // every * group, at // 256)
                 stem = jnp.dot(
                     table[chunk * POOL * CHUNK : (chunk + 1) * POOL * CHUNK, :],
                     onehot[:, at : at + 256],
@@ -201,7 +202,9 @@
     lax.fori_loop(0, blocks, main, 0)
     taps(blocks - 1)
     for last in range(LAG):
-        convolve(blocks - LAG + last)
+        for row in range(0, co, group):
+            for part in range(BLOCK // BIN_ROWS):
+                convolve(blocks - LAG + last, row, part)
 
     own_pos, npos = grad_ref.shape
     embed = sums[...].T[:npos, :].astype(jnp.bfloat16).astype(jnp.float32)

time: 71.1 us -> 76.7 us (1.079)
  Pallas kernels: 30.7 us -> 36.2 us
    pallas_call x1, Pallas kernels: 22.2 us -> 27.7 us  [stem_and_conv(): pl.pallas_call(functools.partial(stem_kernel, n, rows_dev, co), out_shape...]
  transfers between devices with their start and end apart: 9 -> 9, of which waited for: 8 -> 8; matrix products, arithmetic and copies ran while one was open for 2% -> 1% of each run, Pallas kernels for 4% -> 3%
where the time goes in v11:
time: 76.7 us; the launch traced here: 76.4 us
  Pallas kernels  36.2 us (47%)
  waiting for transfers between devices  20.5 us (27%)
  starting transfers between devices  16.9 us (22%)
  local copies, waits for them, and re-layouts  1.92 us (3%)
  between operations  0.79 us (1%)
    pallas_call x1, Pallas kernels, stem_and_conv(): pl.pallas_call(functools.partial(stem_kernel, n, rows_dev, co), out_shape...  27.7 us
    ppermute x9, waiting for transfers between devices, swap(): return lax.ppermute(x, axis, [(i, i ^ bit) for i in range(size)])  20.5 us
    ppermute x9, starting transfers between devices, swap(): return lax.ppermute(x, axis, [(i, i ^ bit) for i in range(size)])  16.9 us
    pallas_call x1, Pallas kernels, send_half(): pl.pallas_call(functools.partial(send_kernel, n), out_shape=[jax.ShapeDty...  3.54 us
    pallas_call x1, Pallas kernels, keep_half(): pl.pallas_call(keep_kernel, out_shape=jax.ShapeDtypeStruct((size, WIDE),...  2.07 us
    unnamed x11, local copies, waits for them, and re-layouts  1.72 us
  transfers between devices with their start and end apart: 9, of which 8 were waited for; matrix products, arithmetic and copies ran while one was open for 1% of the time, Pallas kernels for 3%

profile of v11, /device:TPU:0, one launch (start us, length us, event | category | flops | bytes accessed | tf_op | source)
XLA Modules:
  0.0 76.4 jit_solution(1375198918970524000)
XLA Ops:
  0.6 0.0 copy-start.2
  0.6 0.0 copy-start.1
  0.7 0.0 copy-start
  0.7 0.0 copy-start.3
  0.7 0.8 %copy-done.3 = s32[1,4096]{1,0:T(1,128)S(1)} copy-done((s32[1,4096]{1,0:T(1,128)S(1)}, s32[1,4096]{1,0:T(1,128)}, u32[]{:S(2)}) %copy-start.3) | copy-done | bytes 16408
  1.5 0.2 regroup.1
  1.7 0.0 copy-start.4
  1.7 3.0 %collective-permute-start = (bf16[1,16,256]{2,1,0:T(8,128)(2,1)S(1)}, bf16[1,16,256]{2,1,0:T(8,128)(2,1)S(1)}, u32[]{:S(2)}, u32[]{:S(2)}) collective-permute-start(bf16[1,16,256]{2,1,0:T(8,128)(2,1)S(1)} %bitcast.8), channel_id=1, source_target_pairs={{0,1},{1,0},{2,3},{3,2},{4,5},{5,4},{6,7},{7,6},{8,9},{9,8},{10,11... | collective-permute-start | bytes 24584 | tf_op jit(solution)/shard_map/ppermute | solution.py:36
  4.7 1.6 %collective-permute-done = bf16[1,16,256]{2,1,0:T(8,128)(2,1)S(1)} collective-permute-done((bf16[1,16,256]{2,1,0:T(8,128)(2,1)S(1)}, bf16[1,16,256]{2,1,0:T(8,128)(2,1)S(1)}, u32[]{:S(2)}, u32[]{:S(2)}) %collective-permute-start) | collective-permute-done | bytes 8224 | tf_op jit(solution)/shard_map/ppermute | solution.py:36
  6.4 2.1 %collective-permute-start.1 = (bf16[2,16,256]{2,1,0:T(8,128)(2,1)S(1)}, bf16[2,16,256]{2,1,0:T(8,128)(2,1)S(1)}, u32[]{:S(2)}, u32[]{:S(2)}) collective-permute-start(bf16[2,16,256]{2,1,0:T(8,128)(2,1)S(1)} %pad_maximum_fusion.3), channel_id=1, source_target_pairs={{0,2},{1,3},{2,0},{3,1},{4,6},{5,7},{6,4},{7,5},{8,10},{9,11},{10,... | collective-permute-start | bytes 49160 | tf_op jit(solution)/shard_map/ppermute | solution.py:36
  8.4 0.9 %copy.13 = bf16[15,4,768]{2,0,1:T(8,128)(2,1)S(1)} copy(bf16[15,4,768]{2,1,0:T(4,128)(2,1)} %param.7) | data formatting | bytes 184320 | tf_op args[1]
  9.4 0.2 copy.11
  9.6 0.6 collective-permute-done.1
  10.2 3.0 %collective-permute-start.2 = (bf16[4,16,256]{2,1,0:T(8,128)(2,1)S(1)}, bf16[4,16,256]{2,1,0:T(8,128)(2,1)S(1)}, u32[]{:S(2)}, u32[]{:S(2)}) collective-permute-start(bf16[4,16,256]{2,1,0:T(8,128)(2,1)S(1)} %pad_maximum_fusion.1), channel_id=1, source_target_pairs={{0,4},{1,5},{2,6},{3,7},{4,0},{5,1},{6,2},{7,3},{8,12},{9,13},{10,... | collective-permute-start | bytes 98312 | tf_op jit(solution)/shard_map/ppermute | solution.py:36
  13.2 0.0 copy-done.2
  13.2 0.0 copy-done.1
  13.3 0.0 copy-done
  13.3 0.5 prepare.1
  13.8 1.3 %collective-permute-done.2 = bf16[4,16,256]{2,1,0:T(8,128)(2,1)S(1)} collective-permute-done((bf16[4,16,256]{2,1,0:T(8,128)(2,1)S(1)}, bf16[4,16,256]{2,1,0:T(8,128)(2,1)S(1)}, u32[]{:S(2)}, u32[]{:S(2)}) %collective-permute-start.2) | collective-permute-done | bytes 32800 | tf_op jit(solution)/shard_map/ppermute | solution.py:36
  15.1 0.0 copy-done.4
  15.1 27.7 %stem_and_conv.1 = (bf16[768,4096]{1,0:T(8,128)(2,1)S(1)}, f32[96,4096]{1,0:T(8,128)S(1)}, bf16[16,128]{1,0:T(8,128)(2,1)S(1)}) custom-call(bf16[8,16,256]{2,1,0:T(8,128)(2,1)S(1)} %pad_maximum_fusion.pay_ref, bf16[6144,128]{1,0:T(8,128)(2,1)S(1)} %get-tuple-element.12.table, bf16[480,768]{1,0:T(8,128)(2,1)S(1)} %get-tuple-element.13.weights, ...), custom_call_target="tpu_custom_call" | custom-call | tf_op jit(solution)/shard_map/stem_and_conv/pallas_call | solution.py:230
  42.9 1.9 %collective-permute-start.3 = (bf16[1,16,128]{2,1,0:T(8,128)(2,1)S(1)}, bf16[1,16,128]{2,1,0:T(8,128)(2,1)S(1)}, u32[]{:S(2)}, u32[]{:S(2)}) collective-permute-start(bf16[1,16,128]{2,1,0:T(8,128)(2,1)S(1)} %bitcast.12), channel_id=1, source_target_pairs={{0,1},{1,0},{2,3},{3,2},{4,5},{5,4},{6,7},{7,6},{8,9},{9,8},{10,11... | collective-permute-start | bytes 12296 | tf_op jit(solution)/shard_map/ppermute | solution.py:36
  44.7 1.8 %collective-permute-done.3 = bf16[1,16,128]{2,1,0:T(8,128)(2,1)S(1)} collective-permute-done((bf16[1,16,128]{2,1,0:T(8,128)(2,1)S(1)}, bf16[1,16,128]{2,1,0:T(8,128)(2,1)S(1)}, u32[]{:S(2)}, u32[]{:S(2)}) %collective-permute-start.3) | collective-permute-done | bytes 4128 | tf_op jit(solution)/shard_map/ppermute | solution.py:36
  46.5 1.9 %collective-permute-start.4 = (bf16[2,16,128]{2,1,0:T(8,128)(2,1)S(1)}, bf16[2,16,128]{2,1,0:T(8,128)(2,1)S(1)}, u32[]{:S(2)}, u32[]{:S(2)}) collective-permute-start(bf16[2,16,128]{2,1,0:T(8,128)(2,1)S(1)} %pad_maximum_fusion.5), channel_id=1, source_target_pairs={{0,2},{1,3},{2,0},{3,1},{4,6},{5,7},{6,4},{7,5},{8,10},{9,11},{10,... | collective-permute-start | bytes 24584 | tf_op jit(solution)/shard_map/ppermute | solution.py:36
  48.4 1.7 %collective-permute-done.4 = bf16[2,16,128]{2,1,0:T(8,128)(2,1)S(1)} collective-permute-done((bf16[2,16,128]{2,1,0:T(8,128)(2,1)S(1)}, bf16[2,16,128]{2,1,0:T(8,128)(2,1)S(1)}, u32[]{:S(2)}, u32[]{:S(2)}) %collective-permute-start.4) | collective-permute-done | bytes 8224 | tf_op jit(solution)/shard_map/ppermute | solution.py:36
  50.2 2.9 %collective-permute-start.5 = (bf16[4,16,128]{2,1,0:T(8,128)(2,1)S(1)}, bf16[4,16,128]{2,1,0:T(8,128)(2,1)S(1)}, u32[]{:S(2)}, u32[]{:S(2)}) collective-permute-start(bf16[4,16,128]{2,1,0:T(8,128)(2,1)S(1)} %pad_maximum_fusion.4), channel_id=1, source_target_pairs={{0,4},{1,5},{2,6},{3,7},{4,0},{5,1},{6,2},{7,3},{8,12},{9,13},{10,... | collective-permute-start | bytes 49160 | tf_op jit(solution)/shard_map/ppermute | solution.py:36
  53.1 1.7 %collective-permute-done.5 = bf16[4,16,128]{2,1,0:T(8,128)(2,1)S(1)} collective-permute-done((bf16[4,16,128]{2,1,0:T(8,128)(2,1)S(1)}, bf16[4,16,128]{2,1,0:T(8,128)(2,1)S(1)}, u32[]{:S(2)}, u32[]{:S(2)}) %collective-permute-start.5) | collective-permute-done | bytes 16416 | tf_op jit(solution)/shard_map/ppermute | solution.py:36
  54.8 3.5 %send_half.1 = (s16[48,4224]{1,0:T(8,128)(2,1)S(1)}, bf16[2,48,4352]{2,1,0:T(8,128)(2,1)S(1)}, f32[2,48,256]{2,1,0:T(8,128)S(1)}) custom-call(bf16[8,16,128]{2,1,0:T(8,128)(2,1)S(1)} %pad_maximum_fusion.2.emb_ref, bf16[1024,256]{1,0:T(8,128)(2,1)S(1)} %get-tuple-element.15.proj_ref, f32[96,4096]{1,0:T(8,128)S(1)} %get-tuple-element.16.slope_ref, ...), custom_call_target="tpu_custom_call" | custom-call | tf_op jit(solution)/shard_map/send_half/pallas_call | solution.py:366
  58.4 0.1 collective-permute-start.6
  58.5 2.1 %keep_half.1.a_ref = f32[48,4096]{1,0:T(8,128)S(1)} custom-call(bf16[2,48,4352]{2,1,0:T(8,128)(2,1)S(1)} %get-tuple-element.18.dconv_ref, f32[2,48,256]{2,1,0:T(8,128)S(1)} %get-tuple-element.19.qk_ref, bf16[768,4096]{1,0:T(8,128)(2,1)S(1)} %get-tuple-element.17.pooled_ref), custom_call_target="tpu_custom_call" | custom-call | flops 1509949440 | bytes 12582912 | tf_op jit(solution)/shard_map/keep_half/pallas_call | solution.py:381
  60.5 0.0 collective-permute-done.6.b_ref
  60.5 0.4 add_half.2.a_ref
  60.9 1.9 %collective-permute-start.7 = (s16[48,4224]{1,0:T(8,128)(2,1)S(1)}, s16[48,4224]{1,0:T(8,128)(2,1)S(1)}, u32[]{:S(2)}, u32[]{:S(2)}) collective-permute-start(s16[48,4224]{1,0:T(8,128)(2,1)S(1)} %add_half.2.a_ref), channel_id=1, source_target_pairs={{0,16},{8,24},{16,0},{24,8},{1,17},{9,25},{17,1},{25,9},{2,18},{10... | collective-permute-start | bytes 1216520 | tf_op jit(solution)/shard_map/ppermute | solution.py:36
  62.8 10.0 %collective-permute-done.7.b_ref = s16[48,4224]{1,0:T(8,128)(2,1)S(1)} collective-permute-done((s16[48,4224]{1,0:T(8,128)(2,1)S(1)}, s16[48,4224]{1,0:T(8,128)(2,1)S(1)}, u32[]{:S(2)}, u32[]{:S(2)}) %collective-permute-start.7) | collective-permute-done | bytes 405536 | tf_op jit(solution)/shard_map/ppermute | solution.py:36
  72.8 0.5 add_half.3.mine_ref
  73.3 0.1 collective-permute-start.8
  73.4 1.7 %collective-permute-done.8.other_ref = s16[48,4224]{1,0:T(8,128)(2,1)S(1)} collective-permute-done((s16[48,4224]{1,0:T(8,128)(2,1)S(1)}, s16[48,4224]{1,0:T(8,128)(2,1)S(1)}, u32[]{:S(2)}, u32[]{:S(2)}) %collective-permute-start.8) | collective-permute-done | bytes 405536 | tf_op jit(solution)/shard_map/ppermute | solution.py:36
  75.1 1.3 %join.1 = (f32[96,3840]{1,0:T(8,128)}, f32[96,128]{1,0:T(8,128)}, f32[96,128]{1,0:T(8,128)}) custom-call(s16[48,4224]{1,0:T(8,128)(2,1)S(1)} %add_half.3.mine_ref, s16[48,4224]{1,0:T(8,128)(2,1)S(1)} %collective-permute-done.8.other_ref), custom_call_target="tpu_custom_call" | custom-call | tf_op jit(solution)/shard_map/join/pallas_call | solution.py:421
  (8 shorter events, 0.1 us)
Async XLA Ops:
  0.6 12.6 %copy-start.2 = (bf16[768,128]{1,0:T(8,128)(2,1)S(1)}, bf16[768,128]{1,0:T(8,128)(2,1)}, u32[]{:S(2)}) copy-start(bf16[768,128]{1,0:T(8,128)(2,1)} %wk_ref.1) | copy-start | bytes 589828
  0.6 12.6 %copy-start.1 = (bf16[768,128]{1,0:T(8,128)(2,1)S(1)}, bf16[768,128]{1,0:T(8,128)(2,1)}, u32[]{:S(2)}) copy-start(bf16[768,128]{1,0:T(8,128)(2,1)} %wq_ref.1) | copy-start | bytes 589828
  0.7 12.6 %copy-start = (bf16[96,3840]{1,0:T(8,128)(2,1)S(1)}, bf16[96,3840]{1,0:T(8,128)(2,1)}, u32[]{:S(2)}) copy-start(bf16[96,3840]{1,0:T(8,128)(2,1)} %w_ref.1) | copy-start | bytes 2211844
  0.7 0.8 %copy-start.3 = (s32[1,4096]{1,0:T(1,128)S(1)}, s32[1,4096]{1,0:T(1,128)}, u32[]{:S(2)}) copy-start(s32[1,4096]{1,0:T(1,128)} %param.6) | copy-start | bytes 49156
  1.7 13.4 %copy-start.4 = (f32[1,2,16]{2,1,0:T(2,128)S(1)}, f32[1,2,16]{2,1,0:T(2,128)}, u32[]{:S(2)}) copy-start(f32[1,2,16]{2,1,0:T(2,128)} %param.11) | copy-start | bytes 388
  1.7 4.7 %collective-permute-start = (bf16[1,16,256]{2,1,0:T(8,128)(2,1)S(1)}, bf16[1,16,256]{2,1,0:T(8,128)(2,1)S(1)}, u32[]{:S(2)}, u32[]{:S(2)}) collective-permute-start(bf16[1,16,256]{2,1,0:T(8,128)(2,1)S(1)} %bitcast.8), channel_id=1, source_target_pairs={{0,1},{1,0},{2,3},{3,2},{4,5},{5,4},{6,7},{7,6},{8,9},{9,8},{10,11... | collective-permute-start | bytes 24584 | tf_op jit(solution)/shard_map/ppermute | solution.py:36
  6.4 3.8 %collective-permute-start.1 = (bf16[2,16,256]{2,1,0:T(8,128)(2,1)S(1)}, bf16[2,16,256]{2,1,0:T(8,128)(2,1)S(1)}, u32[]{:S(2)}, u32[]{:S(2)}) collective-permute-start(bf16[2,16,256]{2,1,0:T(8,128)(2,1)S(1)} %pad_maximum_fusion.3), channel_id=1, source_target_pairs={{0,2},{1,3},{2,0},{3,1},{4,6},{5,7},{6,4},{7,5},{8,10},{9,11},{10,... | collective-permute-start | bytes 49160 | tf_op jit(solution)/shard_map/ppermute | solution.py:36
  10.2 4.9 %collective-permute-start.2 = (bf16[4,16,256]{2,1,0:T(8,128)(2,1)S(1)}, bf16[4,16,256]{2,1,0:T(8,128)(2,1)S(1)}, u32[]{:S(2)}, u32[]{:S(2)}) collective-permute-start(bf16[4,16,256]{2,1,0:T(8,128)(2,1)S(1)} %pad_maximum_fusion.1), channel_id=1, source_target_pairs={{0,4},{1,5},{2,6},{3,7},{4,0},{5,1},{6,2},{7,3},{8,12},{9,13},{10,... | collective-permute-start | bytes 98312 | tf_op jit(solution)/shard_map/ppermute | solution.py:36
  42.9 3.6 %collective-permute-start.3 = (bf16[1,16,128]{2,1,0:T(8,128)(2,1)S(1)}, bf16[1,16,128]{2,1,0:T(8,128)(2,1)S(1)}, u32[]{:S(2)}, u32[]{:S(2)}) collective-permute-start(bf16[1,16,128]{2,1,0:T(8,128)(2,1)S(1)} %bitcast.12), channel_id=1, source_target_pairs={{0,1},{1,0},{2,3},{3,2},{4,5},{5,4},{6,7},{7,6},{8,9},{9,8},{10,11... | collective-permute-start | bytes 12296 | tf_op jit(solution)/shard_map/ppermute | solution.py:36
  46.5 3.7 %collective-permute-start.4 = (bf16[2,16,128]{2,1,0:T(8,128)(2,1)S(1)}, bf16[2,16,128]{2,1,0:T(8,128)(2,1)S(1)}, u32[]{:S(2)}, u32[]{:S(2)}) collective-permute-start(bf16[2,16,128]{2,1,0:T(8,128)(2,1)S(1)} %pad_maximum_fusion.5), channel_id=1, source_target_pairs={{0,2},{1,3},{2,0},{3,1},{4,6},{5,7},{6,4},{7,5},{8,10},{9,11},{10,... | collective-permute-start | bytes 24584 | tf_op jit(solution)/shard_map/ppermute | solution.py:36
  50.2 4.7 %collective-permute-start.5 = (bf16[4,16,128]{2,1,0:T(8,128)(2,1)S(1)}, bf16[4,16,128]{2,1,0:T(8,128)(2,1)S(1)}, u32[]{:S(2)}, u32[]{:S(2)}) collective-permute-start(bf16[4,16,128]{2,1,0:T(8,128)(2,1)S(1)} %pad_maximum_fusion.4), channel_id=1, source_target_pairs={{0,4},{1,5},{2,6},{3,7},{4,0},{5,1},{6,2},{7,3},{8,12},{9,13},{10,... | collective-permute-start | bytes 49160 | tf_op jit(solution)/shard_map/ppermute | solution.py:36
  58.4 2.2 %collective-permute-start.6 = (s16[48,4224]{1,0:T(8,128)(2,1)S(1)}, s16[48,4224]{1,0:T(8,128)(2,1)S(1)}, u32[]{:S(2)}, u32[]{:S(2)}) collective-permute-start(s16[48,4224]{1,0:T(8,128)(2,1)S(1)} %get-tuple-element.20), channel_id=1, source_target_pairs={{0,8},{8,0},{16,24},{24,16},{1,9},{9,1},{17,25},{25,17},{2,10},{10... | collective-permute-start | bytes 1216520 | tf_op jit(solution)/shard_map/ppermute | solution.py:36
  60.9 11.9 %collective-permute-start.7 = (s16[48,4224]{1,0:T(8,128)(2,1)S(1)}, s16[48,4224]{1,0:T(8,128)(2,1)S(1)}, u32[]{:S(2)}, u32[]{:S(2)}) collective-permute-start(s16[48,4224]{1,0:T(8,128)(2,1)S(1)} %add_half.2.a_ref), channel_id=1, source_target_pairs={{0,16},{8,24},{16,0},{24,8},{1,17},{9,25},{17,1},{25,9},{2,18},{10... | collective-permute-start | bytes 1216520 | tf_op jit(solution)/shard_map/ppermute | solution.py:36
  73.3 1.8 %collective-permute-start.8 = (s16[48,4224]{1,0:T(8,128)(2,1)S(1)}, s16[48,4224]{1,0:T(8,128)(2,1)S(1)}, u32[]{:S(2)}, u32[]{:S(2)}) collective-permute-start(s16[48,4224]{1,0:T(8,128)(2,1)S(1)} %add_half.3.mine_ref), channel_id=1, source_target_pairs={{0,8},{8,0},{16,24},{24,16},{1,9},{9,1},{17,25},{25,17},{2,10},{10... | collective-permute-start | bytes 1216520 | tf_op jit(solution)/shard_map/ppermute | solution.py:36

commit v12 on v10

--- a/solution.py
+++ b/solution.py
@@ -16,7 +16,7 @@
 BIN_ROWS = 256
 WINDOW = 24
 CHUNK = 16
-BLOCK = 512
+BLOCK = 1024
 LAG = 3
 PAD = 128
 SLOT = 128
@@ -241,8 +241,9 @@
     )(payload, table, weights, pair_grad)
 
 
-WIDE = K1 * C0 + 2 * PC
-PARTS = ((0, K1 * C0), (K1 * C0, K1 * C0 + PC), (K1 * C0 + PC, WIDE))
+COLS = C0 // 2
+PARTS = ((0, K1 * COLS), (K1 * COLS, K1 * COLS + PC))
+WIDE = K1 * COLS + PC
 CODED = WIDE + 128
 
 
@@ -255,7 +256,7 @@
         out_ref[:, begin:end] = scaled.astype(jnp.int32).astype(jnp.int16)
         exponents.append(exponent)
     lane = lax.broadcasted_iota(jnp.int32, (out_ref.shape[0], 128), 1)
-    packed = jnp.where(lane == 0, exponents[0], jnp.where(lane == 1, exponents[1], exponents[2]))
+    packed = jnp.where(lane == 0, exponents[0], exponents[1])
     out_ref[:, WIDE:] = packed.astype(jnp.int32).astype(jnp.int16)
 
 
@@ -267,10 +268,9 @@
     ]
 
 
-def half_gradient(half, dconv, qk_ref, pooled_ref, out_ref, shifted):
-    size = out_ref.shape[0]
+def build_shifted(half, dconv, shifted):
     held = dconv.shape[1]
-    rows = pooled_ref.shape[1]
+    rows = shifted.shape[1]
     shifted[K1 * held :, :] = jnp.zeros((shifted.shape[0] - K1 * held, rows), jnp.bfloat16)
     for first in range(0, rows, BLOCK):
         near = dconv[half, :, first : first + BLOCK + 2 * PAD]
@@ -279,21 +279,29 @@
             shifted[tap * held : (tap + 1) * held, first : first + BLOCK] = near[
                 :, begin : begin + BLOCK
             ]
+
+
+def gradient(half, part, shifted, qk_ref, pooled_ref, out_ref):
+    size = out_ref.shape[0]
+    held = -(-size // 16) * 16
     product = lax.dot_general(
-        pooled_ref[...], shifted[...], (((1,), (1,)), ((), ())), preferred_element_type=jnp.float32
+        pooled_ref[part * COLS : (part + 1) * COLS, :], shifted[...],
+        (((1,), (1,)), ((), ())), preferred_element_type=jnp.float32,
     ).T
     conv = jnp.concatenate(
         [product[tap * held : tap * held + size, :] for tap in range(K1)], axis=1
     )
+    proj = qk_ref[half][:, part * PC : (part + 1) * PC]
     if out_ref.dtype == jnp.int16:
-        qk = qk_ref[half]
-        encode((conv, qk[:, :PC], qk[:, PC:]), out_ref)
+        encode((conv, proj), out_ref)
     else:
-        out_ref[:, : K1 * C0] = conv
-        out_ref[:, K1 * C0 :] = qk_ref[half]
-
-
-def send_kernel(n, emb_ref, proj_ref, slope_ref, pooled_ref, send_ref, dconv_ref, qk_ref, shifted):
+        out_ref[:, : K1 * COLS] = conv
+        out_ref[:, K1 * COLS :] = proj
+
+
+def first_kernel(
+    n, emb_ref, proj_ref, slope_ref, pooled_ref, send_ref, give_ref, stay_ref, qk_ref, dconv_ref
+):
     co, rows = slope_ref.shape
     size, held = co // 2, dconv_ref.shape[1]
     npos = rows // BIN_ROWS
@@ -349,45 +357,73 @@
             dconv_ref[half, :, PAD + pos * BIN_ROWS : PAD + (pos + 1) * BIN_ROWS] = part.astype(
                 jnp.bfloat16
             )
-    half_gradient(1 - lax.axis_index("dp") % 2, dconv_ref, qk_ref, pooled_ref, send_ref, shifted)
-
-
-def keep_kernel(dconv_ref, qk_ref, pooled_ref, keep_ref, shifted):
-    half_gradient(lax.axis_index("dp") % 2, dconv_ref, qk_ref, pooled_ref, keep_ref, shifted)
-
-
-def send_half(n, embed, proj, slope, pooled):
+    core = lax.axis_index("dp") % 2
+    build_shifted(1 - core, dconv_ref, give_ref)
+    gradient(1 - core, 0, give_ref, qk_ref, pooled_ref, send_ref)
+    build_shifted(core, dconv_ref, stay_ref)
+
+
+def middle_kernel(give_ref, stay_ref, qk_ref, pooled_ref, keep_ref, send_ref):
+    core = lax.axis_index("dp") % 2
+    gradient(core, 0, stay_ref, qk_ref, pooled_ref, keep_ref)
+    gradient(1 - core, 1, give_ref, qk_ref, pooled_ref, send_ref)
+
+
+def last_kernel(stay_ref, qk_ref, pooled_ref, after_ref, keep_ref):
+    gradient(lax.axis_index("dp") % 2, 1, stay_ref, qk_ref, pooled_ref, keep_ref)
+
+
+def first_part(n, embed, proj, slope, pooled):
     co, rows = slope.shape
     size = co // 2
     held = -(-size // 16) * 16
     return pl.pallas_call(
-        functools.partial(send_kernel, n),
+        functools.partial(first_kernel, n),
         out_shape=[
             jax.ShapeDtypeStruct((size, CODED), jnp.int16),
-            jax.ShapeDtypeStruct((2, held, rows + 2 * PAD), jnp.bfloat16),
+            jax.ShapeDtypeStruct((256, rows), jnp.bfloat16),
+            jax.ShapeDtypeStruct((256, rows), jnp.bfloat16),
             jax.ShapeDtypeStruct((2, size, 2 * PC), jnp.float32),
         ],
-        scratch_shapes=[pltpu.VMEM((256, rows), jnp.bfloat16)],
-        compiler_params=params(32),
-        name="send_half",
+        scratch_shapes=[pltpu.VMEM((2, held, rows + 2 * PAD), jnp.bfloat16)],
+        compiler_params=params(28),
+        name="first_part",
     )(embed, proj, slope, pooled)
 
 
-def keep_half(dconv, qk, pooled):
+def gradient_cost(size, rows, count):
+    return pl.CostEstimate(
+        flops=2 * 256 * COLS * rows * count, bytes_accessed=6 * MIB * count, transcendentals=0
+    )
+
+
+def middle_part(give, stay, qk, pooled):
     size, rows = qk.shape[1], pooled.shape[1]
     return pl.pallas_call(
-        keep_kernel,
+        middle_kernel,
+        out_shape=[
+            jax.ShapeDtypeStruct((size, WIDE), jnp.float32),
+            jax.ShapeDtypeStruct((size, CODED), jnp.int16),
+        ],
+        compiler_params=params(28),
+        cost_estimate=gradient_cost(size, rows, 2),
+        name="middle_part",
+    )(give, stay, qk, pooled)
+
+
+def last_part(stay, qk, pooled, after):
+    size, rows = qk.shape[1], pooled.shape[1]
+    return pl.pallas_call(
+        last_kernel,
         out_shape=jax.ShapeDtypeStruct((size, WIDE), jnp.float32),
-        scratch_shapes=[pltpu.VMEM((256, rows), jnp.bfloat16)],
-        compiler_params=params(32),
-        cost_estimate=pl.CostEstimate(
-            flops=2 * K1 * size * C0 * rows, bytes_accessed=12 * MIB, transcendentals=0
-        ),
-        name="keep_half",
-    )(dconv, qk, pooled)
-
-
-def add_kernel(a_ref, b_ref, out_ref):
+        compiler_params=params(28),
+        in_specs=[pl.BlockSpec(memory_space=pltpu.VMEM)] * 3 + [pl.BlockSpec(memory_space=pl.ANY)],
+        cost_estimate=gradient_cost(size, rows, 1),
+        name="last_part",
+    )(stay, qk, pooled, after)
+
+
+def add_kernel(a_ref, b_ref, after_ref, out_ref):
     if a_ref.dtype == jnp.int16:
         a = decode(a_ref)
     else:
@@ -395,26 +431,32 @@
     encode([x + y for x, y in zip(a, decode(b_ref))], out_ref)
 
 
-def add_half(a, b):
+def add_half(a, b, after=None):
     return pl.pallas_call(
         add_kernel,
         out_shape=jax.ShapeDtypeStruct(b.shape, jnp.int16),
+        in_specs=[pl.BlockSpec(memory_space=pltpu.VMEM)] * 2 + [pl.BlockSpec(memory_space=pl.ANY)],
         compiler_params=params(8),
         name="add_half",
-    )(a, b)
-
-
-def join_kernel(mine_ref, other_ref, conv_ref, query_ref, key_ref):
-    size = mine_ref.shape[0]
+    )(a, b, a if after is None else after)
+
+
+def join_kernel(*refs):
+    conv_ref, query_ref, key_ref = refs[4:]
+    size = refs[0].shape[0]
     core = lax.axis_index("dp") % 2
-    for half, ref in ((core, mine_ref), (1 - core, other_ref)):
-        rows = pl.ds(pl.multiple_of(half * size, 8), size)
-        for x, out_ref in zip(decode(ref), (conv_ref, query_ref, key_ref)):
-            out_ref[rows, :] = x
-
-
-def join(mine, other):
-    co = 2 * mine.shape[0]
+    for part, out_ref in ((0, query_ref), (1, key_ref)):
+        for half, ref in ((core, refs[2 * part]), (1 - core, refs[2 * part + 1])):
+            rows = pl.ds(pl.multiple_of(half * size, 8), size)
+            conv, proj = decode(ref)
+            for tap in range(K1):
+                first = tap * C0 + part * COLS
+                conv_ref[rows, first : first + COLS] = conv[:, tap * COLS : (tap + 1) * COLS]
+            out_ref[rows, :] = proj
+
+
+def join(*halves):
+    co = 2 * halves[0].shape[0]
     return pl.pallas_call(
         join_kernel,
         out_shape=[
@@ -424,7 +466,7 @@
         ],
         compiler_params=params(8),
         name="join",
-    )(mine, other)
+    )(*halves)
 
 
 def body(bases, stem_table, conv_weight, query_weight, key_weight, pair_grad):
@@ -439,16 +481,17 @@
 
     pooled, slope, embed = stem_and_conv(n, payload, table, weights, pair_grad[0])
     embed_all = gather_xor(embed, "seq")
-    send, dconv, qk = send_half(n, embed_all, proj, slope, pooled)
-    received = swap(send, "dp", 1)
-    keep = keep_half(dconv, qk, pooled)
-
-    mine = add_half(keep, received)
+    send_a, give, stay, qk = first_part(n, embed_all, proj, slope, pooled)
+    keep_a, send_b = middle_part(give, stay, qk, pooled)
+    mine_a = add_half(keep_a, swap(send_a, "dp", 1))
+    mine_b = add_half(last_part(stay, qk, pooled, mine_a), swap(send_b, "dp", 1))
     bit = 2
     while bit < lax.axis_size("dp"):
-        mine = add_half(mine, swap(mine, "dp", bit))
+        other_b = swap(mine_b, "dp", bit)
+        mine_a = add_half(mine_a, swap(mine_a, "dp", bit))
+        mine_b = add_half(mine_b, other_b, mine_a)
         bit *= 2
-    return tuple(join(mine, swap(mine, "dp", 1)))
+    return tuple(join(mine_a, swap(mine_a, "dp", 1), mine_b, swap(mine_b, "dp", 1)))
 
 
 def solution(mesh):

time: 71.1 us -> 73.6 us (1.035)
  local copies, waits for them, and re-layouts: 1.92 us -> 4.79 us
  Pallas kernels: 30.7 us -> 33 us
  waiting for transfers between devices: 20.5 us -> 18.7 us
  starting transfers between devices: 16.9 us -> 16 us
    unnamed x11, local copies, waits for them, and re-layouts: 1.72 us -> 4.59 us
    ppermute x9 -> x12, waiting for transfers between devices: 20.5 us -> 18.7 us  [swap(): return lax.ppermute(x, axis, [(i, i ^ bit) for i in range(size)])]
    pallas_call x1, Pallas kernels: 22.2 us -> 23.9 us  [stem_and_conv(): pl.pallas_call(functools.partial(stem_kernel, n, rows_dev, co), out_shape...]
    ppermute x9 -> x12, starting transfers between devices: 16.9 us -> 16 us  [swap(): return lax.ppermute(x, axis, [(i, i ^ bit) for i in range(size)])]
    pallas_call x2 -> x3, Pallas kernels: 5.61 us -> 5.89 us  [the longest x1 2.67 us: first_part(): pl.pallas_call(functools.partial(first_kernel, n), out_shape=[jax.ShapeDt...]
  transfers between devices with their start and end apart: 9 -> 12, of which waited for: 8 -> 9; matrix products, arithmetic and copies ran while one was open for 2% -> 2% of each run, Pallas kernels for 4% -> 6%
where the time goes in v12:
time: 73.6 us; the launch traced here: 73.3 us
  Pallas kernels  33 us (45%)
  waiting for transfers between devices  18.7 us (25%)
  starting transfers between devices  16 us (22%)
  local copies, waits for them, and re-layouts  4.79 us (7%)
  between operations  0.79 us (1%)
    pallas_call x1, Pallas kernels, stem_and_conv(): pl.pallas_call(functools.partial(stem_kernel, n, rows_dev, co), out_shape...  23.9 us
    ppermute x12, waiting for transfers between devices, swap(): return lax.ppermute(x, axis, [(i, i ^ bit) for i in range(size)])  18.7 us
    ppermute x12, starting transfers between devices, swap(): return lax.ppermute(x, axis, [(i, i ^ bit) for i in range(size)])  16 us
    unnamed x11, local copies, waits for them, and re-layouts  4.59 us
    pallas_call x1, Pallas kernels, first_part(): pl.pallas_call(functools.partial(first_kernel, n), out_shape=[jax.ShapeDt...  2.67 us
    pallas_call x1, Pallas kernels, middle_part(): pl.pallas_call(middle_kernel, out_shape=[jax.ShapeDtypeStruct((size, WIDE...  2.15 us
  transfers between devices with their start and end apart: 12, of which 9 were waited for; matrix products, arithmetic and copies ran while one was open for 2% of the time, Pallas kernels for 6%

profile of v12, /device:TPU:0, one launch (start us, length us, event | category | flops | bytes accessed | tf_op | source)
XLA Modules:
  0.0 73.3 jit_solution(14998208238038927235)
XLA Ops:
  0.6 0.0 copy-start.4
  0.6 0.0 copy-start.3
  0.6 0.7 copy-done.3
  1.4 0.2 regroup.1
  1.6 3.0 %collective-permute-start = (bf16[1,16,256]{2,1,0:T(8,128)(2,1)S(1)}, bf16[1,16,256]{2,1,0:T(8,128)(2,1)S(1)}, u32[]{:S(2)}, u32[]{:S(2)}) collective-permute-start(bf16[1,16,256]{2,1,0:T(8,128)(2,1)S(1)} %bitcast.8), channel_id=1, source_target_pairs={{0,1},{1,0},{2,3},{3,2},{4,5},{5,4},{6,7},{7,6},{8,9},{9,8},{10,11... | collective-permute-start | bytes 24584 | tf_op jit(solution)/shard_map/ppermute | solution.py:36
  4.6 1.6 %collective-permute-done = bf16[1,16,256]{2,1,0:T(8,128)(2,1)S(1)} collective-permute-done((bf16[1,16,256]{2,1,0:T(8,128)(2,1)S(1)}, bf16[1,16,256]{2,1,0:T(8,128)(2,1)S(1)}, u32[]{:S(2)}, u32[]{:S(2)}) %collective-permute-start) | collective-permute-done | bytes 8224 | tf_op jit(solution)/shard_map/ppermute | solution.py:36
  6.2 2.1 %collective-permute-start.1 = (bf16[2,16,256]{2,1,0:T(8,128)(2,1)S(1)}, bf16[2,16,256]{2,1,0:T(8,128)(2,1)S(1)}, u32[]{:S(2)}, u32[]{:S(2)}) collective-permute-start(bf16[2,16,256]{2,1,0:T(8,128)(2,1)S(1)} %pad_maximum_fusion.3), channel_id=1, source_target_pairs={{0,2},{1,3},{2,0},{3,1},{4,6},{5,7},{6,4},{7,5},{8,10},{9,11},{10,... | collective-permute-start | bytes 49160 | tf_op jit(solution)/shard_map/ppermute | solution.py:36
  8.3 0.9 %copy.13 = bf16[15,4,768]{2,0,1:T(8,128)(2,1)S(1)} copy(bf16[15,4,768]{2,1,0:T(4,128)(2,1)} %param.7) | data formatting | bytes 184320 | tf_op args[1]
  9.3 0.2 copy.11
  9.4 0.6 collective-permute-done.1
  10.0 3.0 %collective-permute-start.2 = (bf16[4,16,256]{2,1,0:T(8,128)(2,1)S(1)}, bf16[4,16,256]{2,1,0:T(8,128)(2,1)S(1)}, u32[]{:S(2)}, u32[]{:S(2)}) collective-permute-start(bf16[4,16,256]{2,1,0:T(8,128)(2,1)S(1)} %pad_maximum_fusion.1), channel_id=1, source_target_pairs={{0,4},{1,5},{2,6},{3,7},{4,0},{5,1},{6,2},{7,3},{8,12},{9,13},{10,... | collective-permute-start | bytes 98312 | tf_op jit(solution)/shard_map/ppermute | solution.py:36
  13.1 0.0 copy-start
  13.1 1.1 %copy-done = bf16[96,3840]{1,0:T(8,128)(2,1)S(1)} copy-done((bf16[96,3840]{1,0:T(8,128)(2,1)S(1)}, bf16[96,3840]{1,0:T(8,128)(2,1)}, u32[]{:S(2)}) %copy-start) | copy-done | bytes 737304
  14.2 0.0 copy-start.1
  14.2 0.9 %copy-done.1 = bf16[768,128]{1,0:T(8,128)(2,1)S(1)} copy-done((bf16[768,128]{1,0:T(8,128)(2,1)S(1)}, bf16[768,128]{1,0:T(8,128)(2,1)}, u32[]{:S(2)}) %copy-start.1) | copy-done | bytes 196632
  15.2 0.0 copy-start.2
  15.2 0.9 %copy-done.2 = bf16[768,128]{1,0:T(8,128)(2,1)S(1)} copy-done((bf16[768,128]{1,0:T(8,128)(2,1)S(1)}, bf16[768,128]{1,0:T(8,128)(2,1)}, u32[]{:S(2)}) %copy-start.2) | copy-done | bytes 196632
  16.1 0.5 prepare.1
  16.6 0.0 collective-permute-done.2
  16.6 0.0 copy-done.4
  16.6 23.9 %stem_and_conv.1 = (bf16[768,4096]{1,0:T(8,128)(2,1)S(1)}, f32[96,4096]{1,0:T(8,128)S(1)}, bf16[16,128]{1,0:T(8,128)(2,1)S(1)}) custom-call(bf16[8,16,256]{2,1,0:T(8,128)(2,1)S(1)} %pad_maximum_fusion.pay_ref, bf16[6144,128]{1,0:T(8,128)(2,1)S(1)} %get-tuple-element.15.table, bf16[480,768]{1,0:T(8,128)(2,1)S(1)} %get-tuple-element.16.weights, ...), custom_call_target="tpu_custom_call" | custom-call | tf_op jit(solution)/shard_map/stem_and_conv/pallas_call | solution.py:227
  40.5 1.6 %collective-permute-start.3 = (bf16[1,16,128]{2,1,0:T(8,128)(2,1)S(1)}, bf16[1,16,128]{2,1,0:T(8,128)(2,1)S(1)}, u32[]{:S(2)}, u32[]{:S(2)}) collective-permute-start(bf16[1,16,128]{2,1,0:T(8,128)(2,1)S(1)} %bitcast.12), channel_id=1, source_target_pairs={{0,1},{1,0},{2,3},{3,2},{4,5},{5,4},{6,7},{7,6},{8,9},{9,8},{10,11... | collective-permute-start | bytes 12296 | tf_op jit(solution)/shard_map/ppermute | solution.py:36
  42.0 2.1 %collective-permute-done.3 = bf16[1,16,128]{2,1,0:T(8,128)(2,1)S(1)} collective-permute-done((bf16[1,16,128]{2,1,0:T(8,128)(2,1)S(1)}, bf16[1,16,128]{2,1,0:T(8,128)(2,1)S(1)}, u32[]{:S(2)}, u32[]{:S(2)}) %collective-permute-start.3) | collective-permute-done | bytes 4128 | tf_op jit(solution)/shard_map/ppermute | solution.py:36
  44.1 1.6 %collective-permute-start.4 = (bf16[2,16,128]{2,1,0:T(8,128)(2,1)S(1)}, bf16[2,16,128]{2,1,0:T(8,128)(2,1)S(1)}, u32[]{:S(2)}, u32[]{:S(2)}) collective-permute-start(bf16[2,16,128]{2,1,0:T(8,128)(2,1)S(1)} %pad_maximum_fusion.5), channel_id=1, source_target_pairs={{0,2},{1,3},{2,0},{3,1},{4,6},{5,7},{6,4},{7,5},{8,10},{9,11},{10,... | collective-permute-start | bytes 24584 | tf_op jit(solution)/shard_map/ppermute | solution.py:36
  45.7 2.1 %collective-permute-done.4 = bf16[2,16,128]{2,1,0:T(8,128)(2,1)S(1)} collective-permute-done((bf16[2,16,128]{2,1,0:T(8,128)(2,1)S(1)}, bf16[2,16,128]{2,1,0:T(8,128)(2,1)S(1)}, u32[]{:S(2)}, u32[]{:S(2)}) %collective-permute-start.4) | collective-permute-done | bytes 8224 | tf_op jit(solution)/shard_map/ppermute | solution.py:36
  47.8 1.3 %collective-permute-start.5 = (bf16[4,16,128]{2,1,0:T(8,128)(2,1)S(1)}, bf16[4,16,128]{2,1,0:T(8,128)(2,1)S(1)}, u32[]{:S(2)}, u32[]{:S(2)}) collective-permute-start(bf16[4,16,128]{2,1,0:T(8,128)(2,1)S(1)} %pad_maximum_fusion.4), channel_id=1, source_target_pairs={{0,4},{1,5},{2,6},{3,7},{4,0},{5,1},{6,2},{7,3},{8,12},{9,13},{10,... | collective-permute-start | bytes 49160 | tf_op jit(solution)/shard_map/ppermute | solution.py:36
  49.1 3.3 %collective-permute-done.5 = bf16[4,16,128]{2,1,0:T(8,128)(2,1)S(1)} collective-permute-done((bf16[4,16,128]{2,1,0:T(8,128)(2,1)S(1)}, bf16[4,16,128]{2,1,0:T(8,128)(2,1)S(1)}, u32[]{:S(2)}, u32[]{:S(2)}) %collective-permute-start.5) | collective-permute-done | bytes 16416 | tf_op jit(solution)/shard_map/ppermute | solution.py:36
  52.4 2.7 %first_part.1 = (s16[48,2176]{1,0:T(8,128)(2,1)S(1)}, bf16[256,4096]{1,0:T(8,128)(2,1)S(1)}, bf16[256,4096]{1,0:T(8,128)(2,1)S(1)}, f32[2,48,256]{2,1,0:T(8,128)S(1)}) custom-call(bf16[8,16,128]{2,1,0:T(8,128)(2,1)S(1)} %pad_maximum_fusion.2.emb_ref, bf16[1024,256]{1,0:T(8,128)(2,1)S(1)} %get-tuple-element.18.proj_ref, ...), custom_call_target="tpu_custom_call" | custom-call | tf_op jit(solution)/shard_map/first_part/pallas_call | solution.py:380
  55.1 0.1 collective-permute-start.6
  55.2 2.2 %middle_part.1 = (f32[48,2048]{1,0:T(8,128)S(1)}, s16[48,2176]{1,0:T(8,128)(2,1)S(1)}) custom-call(bf16[256,4096]{1,0:T(8,128)(2,1)S(1)} %get-tuple-element.21.give_ref, bf16[256,4096]{1,0:T(8,128)(2,1)S(1)} %get-tuple-element.22.stay_ref, f32[2,48,256]{2,1,0:T(8,128)S(1)} %get-tuple-element.23.qk_ref, bf16[768,4096]{1,0:T(8,128)(2,1)S(1)} %get-tuple-element.20.pooled_ref), custom_call_target="tpu_custom_call" | custom-call | flops 1610612736 | bytes 12582912 | tf_op jit(solution)/shard_map/middle_part/pallas_call | solution.py:402
  57.3 0.6 collective-permute-start.9
  57.9 0.0 collective-permute-done.6.b_ref
  57.9 0.3 add_half.4.a_ref.after_ref
  58.2 1.5 %collective-permute-start.7 = (s16[48,2176]{1,0:T(8,128)(2,1)S(1)}, s16[48,2176]{1,0:T(8,128)(2,1)S(1)}, u32[]{:S(2)}, u32[]{:S(2)}) collective-permute-start(s16[48,2176]{1,0:T(8,128)(2,1)S(1)} %add_half.4.a_ref.after_ref), channel_id=1, source_target_pairs={{0,16},{8,24},{16,0},{24,8},{1,17},{9,25},{17,1},{25,9},{2,18},{10... | collective-permute-start | bytes 626696 | tf_op jit(solution)/shard_map/ppermute | solution.py:36
  59.7 1.1 %last_part.1.a_ref.after_ref = f32[48,2048]{1,0:T(8,128)S(1)} custom-call(bf16[256,4096]{1,0:T(8,128)(2,1)S(1)} %get-tuple-element.22.stay_ref, f32[2,48,256]{2,1,0:T(8,128)S(1)} %get-tuple-element.23.qk_ref, bf16[768,4096]{1,0:T(8,128)(2,1)S(1)} %get-tuple-element.20.pooled_ref, s16[48,2176]{1,0:T(8,128)(2,1)S(1)} %add_half.4.a_ref.after_ref), custom_call_target="tpu_custom_call" | custom-call | flops 805306368 | bytes 6291456 | tf_op jit(solution)/shard_map/last_part/pallas_call | solution.py:416
  60.8 0.0 collective-permute-done.9.b_ref
  60.8 0.3 add_half.6.a_ref
  61.1 0.6 collective-permute-start.10
  61.7 4.5 %collective-permute-done.7.b_ref = s16[48,2176]{1,0:T(8,128)(2,1)S(1)} collective-permute-done((s16[48,2176]{1,0:T(8,128)(2,1)S(1)}, s16[48,2176]{1,0:T(8,128)(2,1)S(1)}, u32[]{:S(2)}, u32[]{:S(2)}) %collective-permute-start.7) | collective-permute-done | bytes 208928 | tf_op jit(solution)/shard_map/ppermute | solution.py:36
  66.3 0.3 add_half.5.after_ref.refs_0_
  66.6 3.2 %collective-permute-done.10.b_ref = s16[48,2176]{1,0:T(8,128)(2,1)S(1)} collective-permute-done((s16[48,2176]{1,0:T(8,128)(2,1)S(1)}, s16[48,2176]{1,0:T(8,128)(2,1)S(1)}, u32[]{:S(2)}, u32[]{:S(2)}) %collective-permute-start.10) | collective-permute-done | bytes 208928 | tf_op jit(solution)/shard_map/ppermute | solution.py:36
  69.8 0.3 add_half.7.refs_2_
  70.1 0.1 collective-permute-start.11
  70.2 0.5 collective-permute-start.8
  70.7 0.9 %collective-permute-done.11.refs_3_ = s16[48,2176]{1,0:T(8,128)(2,1)S(1)} collective-permute-done((s16[48,2176]{1,0:T(8,128)(2,1)S(1)}, s16[48,2176]{1,0:T(8,128)(2,1)S(1)}, u32[]{:S(2)}, u32[]{:S(2)}) %collective-permute-start.11) | collective-permute-done | bytes 208928 | tf_op jit(solution)/shard_map/ppermute | solution.py:36
  71.7 0.3 collective-permute-done.8.refs_1_
  72.0 1.3 %join.1 = (f32[96,3840]{1,0:T(8,128)}, f32[96,128]{1,0:T(8,128)}, f32[96,128]{1,0:T(8,128)}) custom-call(s16[48,2176]{1,0:T(8,128)(2,1)S(1)} %add_half.5.after_ref.refs_0_, s16[48,2176]{1,0:T(8,128)(2,1)S(1)} %collective-permute-done.8.refs_1_, s16[48,2176]{1,0:T(8,128)(2,1)S(1)} %add_half.7.refs_2_, s16[48,2176]{1,0:T(8,128)(2,1)S(1)} %collective-permute-done.11.refs_3_), custom_call_target="tpu_custom_call" | custom-call | tf_op jit(solution)/shard_map/join/pallas_call | solution.py:460
  (8 shorter events, 0.1 us)
Async XLA Ops:
  0.6 16.0 %copy-start.4 = (f32[1,2,16]{2,1,0:T(2,128)S(1)}, f32[1,2,16]{2,1,0:T(2,128)}, u32[]{:S(2)}) copy-start(f32[1,2,16]{2,1,0:T(2,128)} %param.11) | copy-start | bytes 388
  0.6 0.7 copy-start.3
  1.6 4.7 %collective-permute-start = (bf16[1,16,256]{2,1,0:T(8,128)(2,1)S(1)}, bf16[1,16,256]{2,1,0:T(8,128)(2,1)S(1)}, u32[]{:S(2)}, u32[]{:S(2)}) collective-permute-start(bf16[1,16,256]{2,1,0:T(8,128)(2,1)S(1)} %bitcast.8), channel_id=1, source_target_pairs={{0,1},{1,0},{2,3},{3,2},{4,5},{5,4},{6,7},{7,6},{8,9},{9,8},{10,11... | collective-permute-start | bytes 24584 | tf_op jit(solution)/shard_map/ppermute | solution.py:36
  6.2 3.8 %collective-permute-start.1 = (bf16[2,16,256]{2,1,0:T(8,128)(2,1)S(1)}, bf16[2,16,256]{2,1,0:T(8,128)(2,1)S(1)}, u32[]{:S(2)}, u32[]{:S(2)}) collective-permute-start(bf16[2,16,256]{2,1,0:T(8,128)(2,1)S(1)} %pad_maximum_fusion.3), channel_id=1, source_target_pairs={{0,2},{1,3},{2,0},{3,1},{4,6},{5,7},{6,4},{7,5},{8,10},{9,11},{10,... | collective-permute-start | bytes 49160 | tf_op jit(solution)/shard_map/ppermute | solution.py:36
  10.0 6.5 %collective-permute-start.2 = (bf16[4,16,256]{2,1,0:T(8,128)(2,1)S(1)}, bf16[4,16,256]{2,1,0:T(8,128)(2,1)S(1)}, u32[]{:S(2)}, u32[]{:S(2)}) collective-permute-start(bf16[4,16,256]{2,1,0:T(8,128)(2,1)S(1)} %pad_maximum_fusion.1), channel_id=1, source_target_pairs={{0,4},{1,5},{2,6},{3,7},{4,0},{5,1},{6,2},{7,3},{8,12},{9,13},{10,... | collective-permute-start | bytes 98312 | tf_op jit(solution)/shard_map/ppermute | solution.py:36
  13.1 1.1 %copy-start = (bf16[96,3840]{1,0:T(8,128)(2,1)S(1)}, bf16[96,3840]{1,0:T(8,128)(2,1)}, u32[]{:S(2)}) copy-start(bf16[96,3840]{1,0:T(8,128)(2,1)} %w_ref.1) | copy-start | bytes 2211844
  14.2 0.9 %copy-start.1 = (bf16[768,128]{1,0:T(8,128)(2,1)S(1)}, bf16[768,128]{1,0:T(8,128)(2,1)}, u32[]{:S(2)}) copy-start(bf16[768,128]{1,0:T(8,128)(2,1)} %wq_ref.1) | copy-start | bytes 589828
  15.2 0.9 %copy-start.2 = (bf16[768,128]{1,0:T(8,128)(2,1)S(1)}, bf16[768,128]{1,0:T(8,128)(2,1)}, u32[]{:S(2)}) copy-start(bf16[768,128]{1,0:T(8,128)(2,1)} %wk_ref.1) | copy-start | bytes 589828
  40.5 3.6 %collective-permute-start.3 = (bf16[1,16,128]{2,1,0:T(8,128)(2,1)S(1)}, bf16[1,16,128]{2,1,0:T(8,128)(2,1)S(1)}, u32[]{:S(2)}, u32[]{:S(2)}) collective-permute-start(bf16[1,16,128]{2,1,0:T(8,128)(2,1)S(1)} %bitcast.12), channel_id=1, source_target_pairs={{0,1},{1,0},{2,3},{3,2},{4,5},{5,4},{6,7},{7,6},{8,9},{9,8},{10,11... | collective-permute-start | bytes 12296 | tf_op jit(solution)/shard_map/ppermute | solution.py:36
  44.1 3.7 %collective-permute-start.4 = (bf16[2,16,128]{2,1,0:T(8,128)(2,1)S(1)}, bf16[2,16,128]{2,1,0:T(8,128)(2,1)S(1)}, u32[]{:S(2)}, u32[]{:S(2)}) collective-permute-start(bf16[2,16,128]{2,1,0:T(8,128)(2,1)S(1)} %pad_maximum_fusion.5), channel_id=1, source_target_pairs={{0,2},{1,3},{2,0},{3,1},{4,6},{5,7},{6,4},{7,5},{8,10},{9,11},{10,... | collective-permute-start | bytes 24584 | tf_op jit(solution)/shard_map/ppermute | solution.py:36
  47.8 4.6 %collective-permute-start.5 = (bf16[4,16,128]{2,1,0:T(8,128)(2,1)S(1)}, bf16[4,16,128]{2,1,0:T(8,128)(2,1)S(1)}, u32[]{:S(2)}, u32[]{:S(2)}) collective-permute-start(bf16[4,16,128]{2,1,0:T(8,128)(2,1)S(1)} %pad_maximum_fusion.4), channel_id=1, source_target_pairs={{0,4},{1,5},{2,6},{3,7},{4,0},{5,1},{6,2},{7,3},{8,12},{9,13},{10,... | collective-permute-start | bytes 49160 | tf_op jit(solution)/shard_map/ppermute | solution.py:36
  55.1 2.8 %collective-permute-start.6 = (s16[48,2176]{1,0:T(8,128)(2,1)S(1)}, s16[48,2176]{1,0:T(8,128)(2,1)S(1)}, u32[]{:S(2)}, u32[]{:S(2)}) collective-permute-start(s16[48,2176]{1,0:T(8,128)(2,1)S(1)} %get-tuple-element.25), channel_id=1, source_target_pairs={{0,8},{8,0},{16,24},{24,16},{1,9},{9,1},{17,25},{25,17},{2,10},{10... | collective-permute-start | bytes 626696 | tf_op jit(solution)/shard_map/ppermute | solution.py:36
  57.3 3.5 %collective-permute-start.9 = (s16[48,2176]{1,0:T(8,128)(2,1)S(1)}, s16[48,2176]{1,0:T(8,128)(2,1)S(1)}, u32[]{:S(2)}, u32[]{:S(2)}) collective-permute-start(s16[48,2176]{1,0:T(8,128)(2,1)S(1)} %get-tuple-element.26), channel_id=1, source_target_pairs={{0,8},{8,0},{16,24},{24,16},{1,9},{9,1},{17,25},{25,17},{2,10},{10... | collective-permute-start | bytes 626696 | tf_op jit(solution)/shard_map/ppermute | solution.py:36
  58.2 8.1 %collective-permute-start.7 = (s16[48,2176]{1,0:T(8,128)(2,1)S(1)}, s16[48,2176]{1,0:T(8,128)(2,1)S(1)}, u32[]{:S(2)}, u32[]{:S(2)}) collective-permute-start(s16[48,2176]{1,0:T(8,128)(2,1)S(1)} %add_half.4.a_ref.after_ref), channel_id=1, source_target_pairs={{0,16},{8,24},{16,0},{24,8},{1,17},{9,25},{17,1},{25,9},{2,18},{10... | collective-permute-start | bytes 626696 | tf_op jit(solution)/shard_map/ppermute | solution.py:36
  61.1 8.7 %collective-permute-start.10 = (s16[48,2176]{1,0:T(8,128)(2,1)S(1)}, s16[48,2176]{1,0:T(8,128)(2,1)S(1)}, u32[]{:S(2)}, u32[]{:S(2)}) collective-permute-start(s16[48,2176]{1,0:T(8,128)(2,1)S(1)} %add_half.6.a_ref), channel_id=1, source_target_pairs={{0,16},{8,24},{16,0},{24,8},{1,17},{9,25},{17,1},{25,9},{2,18},{10... | collective-permute-start | bytes 626696 | tf_op jit(solution)/shard_map/ppermute | solution.py:36
  70.1 1.5 %collective-permute-start.11 = (s16[48,2176]{1,0:T(8,128)(2,1)S(1)}, s16[48,2176]{1,0:T(8,128)(2,1)S(1)}, u32[]{:S(2)}, u32[]{:S(2)}) collective-permute-start(s16[48,2176]{1,0:T(8,128)(2,1)S(1)} %add_half.7.refs_2_), channel_id=1, source_target_pairs={{0,8},{8,0},{16,24},{24,16},{1,9},{9,1},{17,25},{25,17},{2,10},{10... | collective-permute-start | bytes 626696 | tf_op jit(solution)/shard_map/ppermute | solution.py:36
  70.2 1.7 %collective-permute-start.8 = (s16[48,2176]{1,0:T(8,128)(2,1)S(1)}, s16[48,2176]{1,0:T(8,128)(2,1)S(1)}, u32[]{:S(2)}, u32[]{:S(2)}) collective-permute-start(s16[48,2176]{1,0:T(8,128)(2,1)S(1)} %add_half.5.after_ref.refs_0_), channel_id=1, source_target_pairs={{0,8},{8,0},{16,24},{24,16},{1,9},{9,1},{17,25},{25,17},{2,10},{10... | collective-permute-start | bytes 626696 | tf_op jit(solution)/shard_map/ppermute | solution.py:36

commit v13 on v12

--- a/solution.py
+++ b/solution.py
@@ -16,7 +16,8 @@
 BIN_ROWS = 256
 WINDOW = 24
 CHUNK = 16
-BLOCK = 1024
+BLOCK = 256
+SHIFT_BLOCK = 512
 LAG = 3
 PAD = 128
 SLOT = 128
@@ -272,12 +273,12 @@
     held = dconv.shape[1]
     rows = shifted.shape[1]
     shifted[K1 * held :, :] = jnp.zeros((shifted.shape[0] - K1 * held, rows), jnp.bfloat16)
-    for first in range(0, rows, BLOCK):
-        near = dconv[half, :, first : first + BLOCK + 2 * PAD]
+    for first in range(0, rows, SHIFT_BLOCK):
+        near = dconv[half, :, first : first + SHIFT_BLOCK + 2 * PAD]
         for tap in range(K1):
             begin = PAD - tap + K1 // 2
-            shifted[tap * held : (tap + 1) * held, first : first + BLOCK] = near[
-                :, begin : begin + BLOCK
+            shifted[tap * held : (tap + 1) * held, first : first + SHIFT_BLOCK] = near[
+                :, begin : begin + SHIFT_BLOCK
             ]
 
 

time: 73.6 us -> 74.5 us (1.012)
  Pallas kernels: 33 us -> 33.9 us
where the time goes in v13:
time: 74.5 us; the launch traced here: 74.3 us
  Pallas kernels  33.9 us (46%)
  waiting for transfers between devices  18.7 us (25%)
  starting transfers between devices  16 us (21%)
  local copies, waits for them, and re-layouts  4.79 us (6%)
  between operations  0.79 us (1%)
    pallas_call x1, Pallas kernels, stem_and_conv(): pl.pallas_call(functools.partial(stem_kernel, n, rows_dev, co), out_shape...  24.6 us
    ppermute x12, waiting for transfers between devices, swap(): return lax.ppermute(x, axis, [(i, i ^ bit) for i in range(size)])  18.7 us
    ppermute x12, starting transfers between devices, swap(): return lax.ppermute(x, axis, [(i, i ^ bit) for i in range(size)])  16 us
    unnamed x11, local copies, waits for them, and re-layouts  4.59 us
    pallas_call x1, Pallas kernels, first_part(): pl.pallas_call(functools.partial(first_kernel, n), out_shape=[jax.ShapeDt...  2.89 us
    pallas_call x1, Pallas kernels, middle_part(): pl.pallas_call(middle_kernel, out_shape=[jax.ShapeDtypeStruct((size, WIDE...  2.15 us
  transfers between devices with their start and end apart: 12, of which 9 were waited for; matrix products, arithmetic and copies ran while one was open for 2% of the time, Pallas kernels for 6%

profile of v13, /device:TPU:0, one launch (start us, length us, event | category | flops | bytes accessed | tf_op | source)
XLA Modules:
  0.0 74.3 jit_solution(7831454113219602390)
XLA Ops:
  0.6 0.0 copy-start.4
  0.6 0.0 copy-start.3
  0.6 0.7 copy-done.3
  1.4 0.2 regroup.1
  1.6 3.0 %collective-permute-start = (bf16[1,16,256]{2,1,0:T(8,128)(2,1)S(1)}, bf16[1,16,256]{2,1,0:T(8,128)(2,1)S(1)}, u32[]{:S(2)}, u32[]{:S(2)}) collective-permute-start(bf16[1,16,256]{2,1,0:T(8,128)(2,1)S(1)} %bitcast.8), channel_id=1, source_target_pairs={{0,1},{1,0},{2,3},{3,2},{4,5},{5,4},{6,7},{7,6},{8,9},{9,8},{10,11... | collective-permute-start | bytes 24584 | tf_op jit(solution)/shard_map/ppermute | solution.py:37
  4.6 1.6 %collective-permute-done = bf16[1,16,256]{2,1,0:T(8,128)(2,1)S(1)} collective-permute-done((bf16[1,16,256]{2,1,0:T(8,128)(2,1)S(1)}, bf16[1,16,256]{2,1,0:T(8,128)(2,1)S(1)}, u32[]{:S(2)}, u32[]{:S(2)}) %collective-permute-start) | collective-permute-done | bytes 8224 | tf_op jit(solution)/shard_map/ppermute | solution.py:37
  6.2 2.1 %collective-permute-start.1 = (bf16[2,16,256]{2,1,0:T(8,128)(2,1)S(1)}, bf16[2,16,256]{2,1,0:T(8,128)(2,1)S(1)}, u32[]{:S(2)}, u32[]{:S(2)}) collective-permute-start(bf16[2,16,256]{2,1,0:T(8,128)(2,1)S(1)} %pad_maximum_fusion.3), channel_id=1, source_target_pairs={{0,2},{1,3},{2,0},{3,1},{4,6},{5,7},{6,4},{7,5},{8,10},{9,11},{10,... | collective-permute-start | bytes 49160 | tf_op jit(solution)/shard_map/ppermute | solution.py:37
  8.3 0.9 %copy.13 = bf16[15,4,768]{2,0,1:T(8,128)(2,1)S(1)} copy(bf16[15,4,768]{2,1,0:T(4,128)(2,1)} %param.7) | data formatting | bytes 184320 | tf_op args[1]
  9.3 0.2 copy.11
  9.4 0.6 collective-permute-done.1
  10.0 3.0 %collective-permute-start.2 = (bf16[4,16,256]{2,1,0:T(8,128)(2,1)S(1)}, bf16[4,16,256]{2,1,0:T(8,128)(2,1)S(1)}, u32[]{:S(2)}, u32[]{:S(2)}) collective-permute-start(bf16[4,16,256]{2,1,0:T(8,128)(2,1)S(1)} %pad_maximum_fusion.1), channel_id=1, source_target_pairs={{0,4},{1,5},{2,6},{3,7},{4,0},{5,1},{6,2},{7,3},{8,12},{9,13},{10,... | collective-permute-start | bytes 98312 | tf_op jit(solution)/shard_map/ppermute | solution.py:37
  13.1 0.0 copy-start
  13.1 1.1 %copy-done = bf16[96,3840]{1,0:T(8,128)(2,1)S(1)} copy-done((bf16[96,3840]{1,0:T(8,128)(2,1)S(1)}, bf16[96,3840]{1,0:T(8,128)(2,1)}, u32[]{:S(2)}) %copy-start) | copy-done | bytes 737304
  14.2 0.0 copy-start.1
  14.2 0.9 %copy-done.1 = bf16[768,128]{1,0:T(8,128)(2,1)S(1)} copy-done((bf16[768,128]{1,0:T(8,128)(2,1)S(1)}, bf16[768,128]{1,0:T(8,128)(2,1)}, u32[]{:S(2)}) %copy-start.1) | copy-done | bytes 196632
  15.2 0.0 copy-start.2
  15.2 0.9 %copy-done.2 = bf16[768,128]{1,0:T(8,128)(2,1)S(1)} copy-done((bf16[768,128]{1,0:T(8,128)(2,1)S(1)}, bf16[768,128]{1,0:T(8,128)(2,1)}, u32[]{:S(2)}) %copy-start.2) | copy-done | bytes 196632
  16.1 0.5 prepare.1
  16.6 0.0 collective-permute-done.2
  16.6 0.0 copy-done.4
  16.6 24.6 %stem_and_conv.1 = (bf16[768,4096]{1,0:T(8,128)(2,1)S(1)}, f32[96,4096]{1,0:T(8,128)S(1)}, bf16[16,128]{1,0:T(8,128)(2,1)S(1)}) custom-call(bf16[8,16,256]{2,1,0:T(8,128)(2,1)S(1)} %pad_maximum_fusion.pay_ref, bf16[6144,128]{1,0:T(8,128)(2,1)S(1)} %get-tuple-element.15.table, bf16[480,768]{1,0:T(8,128)(2,1)S(1)} %get-tuple-element.16.weights, ...), custom_call_target="tpu_custom_call" | custom-call | tf_op jit(solution)/shard_map/stem_and_conv/pallas_call | solution.py:228
  41.2 1.6 %collective-permute-start.3 = (bf16[1,16,128]{2,1,0:T(8,128)(2,1)S(1)}, bf16[1,16,128]{2,1,0:T(8,128)(2,1)S(1)}, u32[]{:S(2)}, u32[]{:S(2)}) collective-permute-start(bf16[1,16,128]{2,1,0:T(8,128)(2,1)S(1)} %bitcast.12), channel_id=1, source_target_pairs={{0,1},{1,0},{2,3},{3,2},{4,5},{5,4},{6,7},{7,6},{8,9},{9,8},{10,11... | collective-permute-start | bytes 12296 | tf_op jit(solution)/shard_map/ppermute | solution.py:37
  42.8 2.1 %collective-permute-done.3 = bf16[1,16,128]{2,1,0:T(8,128)(2,1)S(1)} collective-permute-done((bf16[1,16,128]{2,1,0:T(8,128)(2,1)S(1)}, bf16[1,16,128]{2,1,0:T(8,128)(2,1)S(1)}, u32[]{:S(2)}, u32[]{:S(2)}) %collective-permute-start.3) | collective-permute-done | bytes 4128 | tf_op jit(solution)/shard_map/ppermute | solution.py:37
  44.9 1.6 %collective-permute-start.4 = (bf16[2,16,128]{2,1,0:T(8,128)(2,1)S(1)}, bf16[2,16,128]{2,1,0:T(8,128)(2,1)S(1)}, u32[]{:S(2)}, u32[]{:S(2)}) collective-permute-start(bf16[2,16,128]{2,1,0:T(8,128)(2,1)S(1)} %pad_maximum_fusion.5), channel_id=1, source_target_pairs={{0,2},{1,3},{2,0},{3,1},{4,6},{5,7},{6,4},{7,5},{8,10},{9,11},{10,... | collective-permute-start | bytes 24584 | tf_op jit(solution)/shard_map/ppermute | solution.py:37
  46.5 2.1 %collective-permute-done.4 = bf16[2,16,128]{2,1,0:T(8,128)(2,1)S(1)} collective-permute-done((bf16[2,16,128]{2,1,0:T(8,128)(2,1)S(1)}, bf16[2,16,128]{2,1,0:T(8,128)(2,1)S(1)}, u32[]{:S(2)}, u32[]{:S(2)}) %collective-permute-start.4) | collective-permute-done | bytes 8224 | tf_op jit(solution)/shard_map/ppermute | solution.py:37
  48.5 1.3 %collective-permute-start.5 = (bf16[4,16,128]{2,1,0:T(8,128)(2,1)S(1)}, bf16[4,16,128]{2,1,0:T(8,128)(2,1)S(1)}, u32[]{:S(2)}, u32[]{:S(2)}) collective-permute-start(bf16[4,16,128]{2,1,0:T(8,128)(2,1)S(1)} %pad_maximum_fusion.4), channel_id=1, source_target_pairs={{0,4},{1,5},{2,6},{3,7},{4,0},{5,1},{6,2},{7,3},{8,12},{9,13},{10,... | collective-permute-start | bytes 49160 | tf_op jit(solution)/shard_map/ppermute | solution.py:37
  49.9 3.3 %collective-permute-done.5 = bf16[4,16,128]{2,1,0:T(8,128)(2,1)S(1)} collective-permute-done((bf16[4,16,128]{2,1,0:T(8,128)(2,1)S(1)}, bf16[4,16,128]{2,1,0:T(8,128)(2,1)S(1)}, u32[]{:S(2)}, u32[]{:S(2)}) %collective-permute-start.5) | collective-permute-done | bytes 16416 | tf_op jit(solution)/shard_map/ppermute | solution.py:37
  53.2 2.9 %first_part.1 = (s16[48,2176]{1,0:T(8,128)(2,1)S(1)}, bf16[256,4096]{1,0:T(8,128)(2,1)S(1)}, bf16[256,4096]{1,0:T(8,128)(2,1)S(1)}, f32[2,48,256]{2,1,0:T(8,128)S(1)}) custom-call(bf16[8,16,128]{2,1,0:T(8,128)(2,1)S(1)} %pad_maximum_fusion.2.emb_ref, bf16[1024,256]{1,0:T(8,128)(2,1)S(1)} %get-tuple-element.18.proj_ref, ...), custom_call_target="tpu_custom_call" | custom-call | tf_op jit(solution)/shard_map/first_part/pallas_call | solution.py:381
  56.1 0.1 collective-permute-start.6
  56.2 2.2 %middle_part.1 = (f32[48,2048]{1,0:T(8,128)S(1)}, s16[48,2176]{1,0:T(8,128)(2,1)S(1)}) custom-call(bf16[256,4096]{1,0:T(8,128)(2,1)S(1)} %get-tuple-element.21.give_ref, bf16[256,4096]{1,0:T(8,128)(2,1)S(1)} %get-tuple-element.22.stay_ref, f32[2,48,256]{2,1,0:T(8,128)S(1)} %get-tuple-element.23.qk_ref, bf16[768,4096]{1,0:T(8,128)(2,1)S(1)} %get-tuple-element.20.pooled_ref), custom_call_target="tpu_custom_call" | custom-call | flops 1610612736 | bytes 12582912 | tf_op jit(solution)/shard_map/middle_part/pallas_call | solution.py:403
  58.3 0.6 collective-permute-start.9
  58.9 0.0 collective-permute-done.6.b_ref
  58.9 0.3 add_half.4.a_ref.after_ref
  59.2 1.6 %collective-permute-start.7 = (s16[48,2176]{1,0:T(8,128)(2,1)S(1)}, s16[48,2176]{1,0:T(8,128)(2,1)S(1)}, u32[]{:S(2)}, u32[]{:S(2)}) collective-permute-start(s16[48,2176]{1,0:T(8,128)(2,1)S(1)} %add_half.4.a_ref.after_ref), channel_id=1, source_target_pairs={{0,16},{8,24},{16,0},{24,8},{1,17},{9,25},{17,1},{25,9},{2,18},{10... | collective-permute-start | bytes 626696 | tf_op jit(solution)/shard_map/ppermute | solution.py:37
  60.7 1.1 %last_part.1.a_ref.after_ref = f32[48,2048]{1,0:T(8,128)S(1)} custom-call(bf16[256,4096]{1,0:T(8,128)(2,1)S(1)} %get-tuple-element.22.stay_ref, f32[2,48,256]{2,1,0:T(8,128)S(1)} %get-tuple-element.23.qk_ref, bf16[768,4096]{1,0:T(8,128)(2,1)S(1)} %get-tuple-element.20.pooled_ref, s16[48,2176]{1,0:T(8,128)(2,1)S(1)} %add_half.4.a_ref.after_ref), custom_call_target="tpu_custom_call" | custom-call | flops 805306368 | bytes 6291456 | tf_op jit(solution)/shard_map/last_part/pallas_call | solution.py:417
  61.8 0.0 collective-permute-done.9.b_ref
  61.8 0.3 add_half.6.a_ref
  62.1 0.6 collective-permute-start.10
  62.7 4.5 %collective-permute-done.7.b_ref = s16[48,2176]{1,0:T(8,128)(2,1)S(1)} collective-permute-done((s16[48,2176]{1,0:T(8,128)(2,1)S(1)}, s16[48,2176]{1,0:T(8,128)(2,1)S(1)}, u32[]{:S(2)}, u32[]{:S(2)}) %collective-permute-start.7) | collective-permute-done | bytes 208928 | tf_op jit(solution)/shard_map/ppermute | solution.py:37
  67.3 0.3 add_half.5.after_ref.refs_0_
  67.6 3.2 %collective-permute-done.10.b_ref = s16[48,2176]{1,0:T(8,128)(2,1)S(1)} collective-permute-done((s16[48,2176]{1,0:T(8,128)(2,1)S(1)}, s16[48,2176]{1,0:T(8,128)(2,1)S(1)}, u32[]{:S(2)}, u32[]{:S(2)}) %collective-permute-start.10) | collective-permute-done | bytes 208928 | tf_op jit(solution)/shard_map/ppermute | solution.py:37
  70.8 0.3 add_half.7.refs_2_
  71.1 0.1 collective-permute-start.11
  71.2 0.5 collective-permute-start.8
  71.7 0.9 %collective-permute-done.11.refs_3_ = s16[48,2176]{1,0:T(8,128)(2,1)S(1)} collective-permute-done((s16[48,2176]{1,0:T(8,128)(2,1)S(1)}, s16[48,2176]{1,0:T(8,128)(2,1)S(1)}, u32[]{:S(2)}, u32[]{:S(2)}) %collective-permute-start.11) | collective-permute-done | bytes 208928 | tf_op jit(solution)/shard_map/ppermute | solution.py:37
  72.6 0.3 collective-permute-done.8.refs_1_
  72.9 1.3 %join.1 = (f32[96,3840]{1,0:T(8,128)}, f32[96,128]{1,0:T(8,128)}, f32[96,128]{1,0:T(8,128)}) custom-call(s16[48,2176]{1,0:T(8,128)(2,1)S(1)} %add_half.5.after_ref.refs_0_, s16[48,2176]{1,0:T(8,128)(2,1)S(1)} %collective-permute-done.8.refs_1_, s16[48,2176]{1,0:T(8,128)(2,1)S(1)} %add_half.7.refs_2_, s16[48,2176]{1,0:T(8,128)(2,1)S(1)} %collective-permute-done.11.refs_3_), custom_call_target="tpu_custom_call" | custom-call | tf_op jit(solution)/shard_map/join/pallas_call | solution.py:461
  (8 shorter events, 0.1 us)
Async XLA Ops:
  0.6 16.0 %copy-start.4 = (f32[1,2,16]{2,1,0:T(2,128)S(1)}, f32[1,2,16]{2,1,0:T(2,128)}, u32[]{:S(2)}) copy-start(f32[1,2,16]{2,1,0:T(2,128)} %param.11) | copy-start | bytes 388
  0.6 0.7 copy-start.3
  1.6 4.7 %collective-permute-start = (bf16[1,16,256]{2,1,0:T(8,128)(2,1)S(1)}, bf16[1,16,256]{2,1,0:T(8,128)(2,1)S(1)}, u32[]{:S(2)}, u32[]{:S(2)}) collective-permute-start(bf16[1,16,256]{2,1,0:T(8,128)(2,1)S(1)} %bitcast.8), channel_id=1, source_target_pairs={{0,1},{1,0},{2,3},{3,2},{4,5},{5,4},{6,7},{7,6},{8,9},{9,8},{10,11... | collective-permute-start | bytes 24584 | tf_op jit(solution)/shard_map/ppermute | solution.py:37
  6.2 3.8 %collective-permute-start.1 = (bf16[2,16,256]{2,1,0:T(8,128)(2,1)S(1)}, bf16[2,16,256]{2,1,0:T(8,128)(2,1)S(1)}, u32[]{:S(2)}, u32[]{:S(2)}) collective-permute-start(bf16[2,16,256]{2,1,0:T(8,128)(2,1)S(1)} %pad_maximum_fusion.3), channel_id=1, source_target_pairs={{0,2},{1,3},{2,0},{3,1},{4,6},{5,7},{6,4},{7,5},{8,10},{9,11},{10,... | collective-permute-start | bytes 49160 | tf_op jit(solution)/shard_map/ppermute | solution.py:37
  10.0 6.5 %collective-permute-start.2 = (bf16[4,16,256]{2,1,0:T(8,128)(2,1)S(1)}, bf16[4,16,256]{2,1,0:T(8,128)(2,1)S(1)}, u32[]{:S(2)}, u32[]{:S(2)}) collective-permute-start(bf16[4,16,256]{2,1,0:T(8,128)(2,1)S(1)} %pad_maximum_fusion.1), channel_id=1, source_target_pairs={{0,4},{1,5},{2,6},{3,7},{4,0},{5,1},{6,2},{7,3},{8,12},{9,13},{10,... | collective-permute-start | bytes 98312 | tf_op jit(solution)/shard_map/ppermute | solution.py:37
  13.1 1.1 %copy-start = (bf16[96,3840]{1,0:T(8,128)(2,1)S(1)}, bf16[96,3840]{1,0:T(8,128)(2,1)}, u32[]{:S(2)}) copy-start(bf16[96,3840]{1,0:T(8,128)(2,1)} %w_ref.1) | copy-start | bytes 2211844
  14.2 0.9 %copy-start.1 = (bf16[768,128]{1,0:T(8,128)(2,1)S(1)}, bf16[768,128]{1,0:T(8,128)(2,1)}, u32[]{:S(2)}) copy-start(bf16[768,128]{1,0:T(8,128)(2,1)} %wq_ref.1) | copy-start | bytes 589828
  15.2 0.9 %copy-start.2 = (bf16[768,128]{1,0:T(8,128)(2,1)S(1)}, bf16[768,128]{1,0:T(8,128)(2,1)}, u32[]{:S(2)}) copy-start(bf16[768,128]{1,0:T(8,128)(2,1)} %wk_ref.1) | copy-start | bytes 589828
  41.2 3.7 %collective-permute-start.3 = (bf16[1,16,128]{2,1,0:T(8,128)(2,1)S(1)}, bf16[1,16,128]{2,1,0:T(8,128)(2,1)S(1)}, u32[]{:S(2)}, u32[]{:S(2)}) collective-permute-start(bf16[1,16,128]{2,1,0:T(8,128)(2,1)S(1)} %bitcast.12), channel_id=1, source_target_pairs={{0,1},{1,0},{2,3},{3,2},{4,5},{5,4},{6,7},{7,6},{8,9},{9,8},{10,11... | collective-permute-start | bytes 12296 | tf_op jit(solution)/shard_map/ppermute | solution.py:37
  44.9 3.7 %collective-permute-start.4 = (bf16[2,16,128]{2,1,0:T(8,128)(2,1)S(1)}, bf16[2,16,128]{2,1,0:T(8,128)(2,1)S(1)}, u32[]{:S(2)}, u32[]{:S(2)}) collective-permute-start(bf16[2,16,128]{2,1,0:T(8,128)(2,1)S(1)} %pad_maximum_fusion.5), channel_id=1, source_target_pairs={{0,2},{1,3},{2,0},{3,1},{4,6},{5,7},{6,4},{7,5},{8,10},{9,11},{10,... | collective-permute-start | bytes 24584 | tf_op jit(solution)/shard_map/ppermute | solution.py:37
  48.5 4.6 %collective-permute-start.5 = (bf16[4,16,128]{2,1,0:T(8,128)(2,1)S(1)}, bf16[4,16,128]{2,1,0:T(8,128)(2,1)S(1)}, u32[]{:S(2)}, u32[]{:S(2)}) collective-permute-start(bf16[4,16,128]{2,1,0:T(8,128)(2,1)S(1)} %pad_maximum_fusion.4), channel_id=1, source_target_pairs={{0,4},{1,5},{2,6},{3,7},{4,0},{5,1},{6,2},{7,3},{8,12},{9,13},{10,... | collective-permute-start | bytes 49160 | tf_op jit(solution)/shard_map/ppermute | solution.py:37
  56.1 2.8 %collective-permute-start.6 = (s16[48,2176]{1,0:T(8,128)(2,1)S(1)}, s16[48,2176]{1,0:T(8,128)(2,1)S(1)}, u32[]{:S(2)}, u32[]{:S(2)}) collective-permute-start(s16[48,2176]{1,0:T(8,128)(2,1)S(1)} %get-tuple-element.25), channel_id=1, source_target_pairs={{0,8},{8,0},{16,24},{24,16},{1,9},{9,1},{17,25},{25,17},{2,10},{10... | collective-permute-start | bytes 626696 | tf_op jit(solution)/shard_map/ppermute | solution.py:37
  58.3 3.5 %collective-permute-start.9 = (s16[48,2176]{1,0:T(8,128)(2,1)S(1)}, s16[48,2176]{1,0:T(8,128)(2,1)S(1)}, u32[]{:S(2)}, u32[]{:S(2)}) collective-permute-start(s16[48,2176]{1,0:T(8,128)(2,1)S(1)} %get-tuple-element.26), channel_id=1, source_target_pairs={{0,8},{8,0},{16,24},{24,16},{1,9},{9,1},{17,25},{25,17},{2,10},{10... | collective-permute-start | bytes 626696 | tf_op jit(solution)/shard_map/ppermute | solution.py:37
  59.2 8.1 %collective-permute-start.7 = (s16[48,2176]{1,0:T(8,128)(2,1)S(1)}, s16[48,2176]{1,0:T(8,128)(2,1)S(1)}, u32[]{:S(2)}, u32[]{:S(2)}) collective-permute-start(s16[48,2176]{1,0:T(8,128)(2,1)S(1)} %add_half.4.a_ref.after_ref), channel_id=1, source_target_pairs={{0,16},{8,24},{16,0},{24,8},{1,17},{9,25},{17,1},{25,9},{2,18},{10... | collective-permute-start | bytes 626696 | tf_op jit(solution)/shard_map/ppermute | solution.py:37
  62.1 8.7 %collective-permute-start.10 = (s16[48,2176]{1,0:T(8,128)(2,1)S(1)}, s16[48,2176]{1,0:T(8,128)(2,1)S(1)}, u32[]{:S(2)}, u32[]{:S(2)}) collective-permute-start(s16[48,2176]{1,0:T(8,128)(2,1)S(1)} %add_half.6.a_ref), channel_id=1, source_target_pairs={{0,16},{8,24},{16,0},{24,8},{1,17},{9,25},{17,1},{25,9},{2,18},{10... | collective-permute-start | bytes 626696 | tf_op jit(solution)/shard_map/ppermute | solution.py:37
  71.1 1.5 %collective-permute-start.11 = (s16[48,2176]{1,0:T(8,128)(2,1)S(1)}, s16[48,2176]{1,0:T(8,128)(2,1)S(1)}, u32[]{:S(2)}, u32[]{:S(2)}) collective-permute-start(s16[48,2176]{1,0:T(8,128)(2,1)S(1)} %add_half.7.refs_2_), channel_id=1, source_target_pairs={{0,8},{8,0},{16,24},{24,16},{1,9},{9,1},{17,25},{25,17},{2,10},{10... | collective-permute-start | bytes 626696 | tf_op jit(solution)/shard_map/ppermute | solution.py:37
  71.2 1.7 %collective-permute-start.8 = (s16[48,2176]{1,0:T(8,128)(2,1)S(1)}, s16[48,2176]{1,0:T(8,128)(2,1)S(1)}, u32[]{:S(2)}, u32[]{:S(2)}) collective-permute-start(s16[48,2176]{1,0:T(8,128)(2,1)S(1)} %add_half.5.after_ref.refs_0_), channel_id=1, source_target_pairs={{0,8},{8,0},{16,24},{24,16},{1,9},{9,1},{17,25},{25,17},{2,10},{10... | collective-permute-start | bytes 626696 | tf_op jit(solution)/shard_map/ppermute | solution.py:37

commit v14 on v13

--- a/solution.py
+++ b/solution.py
@@ -16,7 +16,7 @@
 BIN_ROWS = 256
 WINDOW = 24
 CHUNK = 16
-BLOCK = 256
+BLOCK = 512
 SHIFT_BLOCK = 512
 LAG = 3
 PAD = 128
@@ -83,7 +83,7 @@
     )(bases.reshape(bases.shape[1] // 128, 128))
 
 
-def prepare_kernel(n, co, t0_ref, w_ref, wq_ref, wk_ref, table_ref, weights_ref, proj_ref):
+def prepare_kernel(n, co, t0_ref, w_ref, both_ref, table_ref, weights_ref, proj_ref):
     for chunk in range(C0 // CHUNK):
         part = t0_ref[chunk * CHUNK : (chunk + 1) * CHUNK, :]
         for pos in range(POOL):
@@ -91,17 +91,16 @@
             first = (chunk * POOL + pos) * CHUNK
             table_ref[first : first + CHUNK, :] = shifted.astype(jnp.bfloat16)
     for tap in range(K1):
-        weights_ref[tap * co : (tap + 1) * co, :] = w_ref[:, tap * C0 : (tap + 1) * C0] * 0.5
+        weights_ref[tap * co : (tap + 1) * co, :] = w_ref[:, tap * C0 : (tap + 1) * C0]
     for slot in range(n):
         rows = slice(slot * co, (slot + 1) * co)
-        proj_ref[slot * SLOT : slot * SLOT + co, :PC] = wq_ref[rows, :]
-        proj_ref[slot * SLOT : slot * SLOT + co, PC:] = wk_ref[rows, :]
+        proj_ref[slot * SLOT : slot * SLOT + co, :] = both_ref[rows, :]
         proj_ref[slot * SLOT + co : (slot + 1) * SLOT, :] = jnp.zeros(
             (SLOT - co, 2 * PC), jnp.bfloat16
         )
 
 
-def prepare(n, first_table, conv_weight, query_weight, key_weight):
+def prepare(n, first_table, conv_weight, both):
     co = conv_weight.shape[0]
     return pl.pallas_call(
         functools.partial(prepare_kernel, n, co),
@@ -113,7 +112,7 @@
         compiler_params=params(8),
         cost_estimate=pl.CostEstimate(flops=0, bytes_accessed=5 * MIB, transcendentals=0),
         name="prepare",
-    )(first_table, conv_weight, query_weight, key_weight)
+    )(first_table, conv_weight, both)
 
 
 def stem_kernel(
@@ -478,7 +477,12 @@
         stem_table.transpose(2, 1, 0), ((0, 0), (0, 0), (1, WINDOW - 1 - K0))
     ).reshape(C0, 4 * WINDOW)
     first_table = jnp.pad(first_table, ((0, 0), (0, 128 - 4 * WINDOW))).astype(jnp.float32)
-    table, weights, proj = prepare(n, first_table, conv_weight, query_weight, key_weight)
+    table, weights, proj = prepare(
+        n,
+        first_table,
+        conv_weight * jnp.bfloat16(0.5),
+        jnp.concatenate([query_weight, key_weight], axis=1),
+    )
 
     pooled, slope, embed = stem_and_conv(n, payload, table, weights, pair_grad[0])
     embed_all = gather_xor(embed, "seq")

time: 74.5 us -> 71 us (0.953)
  local copies, waits for them, and re-layouts: 4.79 us -> 1.84 us
  Pallas kernels: 33.9 us -> 31.5 us
  other arithmetic: 0.06 us -> 1.29 us
    unnamed x11 -> x9, local copies, waits for them, and re-layouts: 4.59 us -> 1.63 us
    pallas_call x1, Pallas kernels: 24.6 us -> 22.2 us  [stem_and_conv(): pl.pallas_call(functools.partial(stem_kernel, n, rows_dev, co), out_shape...]
    mul x0 -> x1, other arithmetic: none -> 1.18 us  [body(): conv_weight * jnp.bfloat16(0.5)]
  transfers between devices with their start and end apart: 12 -> 12, of which waited for: 9 -> 9; matrix products, arithmetic and copies ran while one was open for 2% -> 3% of each run, Pallas kernels for 6% -> 6%
where the time goes in v14:
time: 71 us; the launch traced here: 70.8 us
  Pallas kernels  31.5 us (44%)
  waiting for transfers between devices  19.3 us (27%)
  starting transfers between devices  16.1 us (23%)
  local copies, waits for them, and re-layouts  1.84 us (3%)
  other arithmetic  1.29 us (2%)
  between operations  0.79 us (1%)
    pallas_call x1, Pallas kernels, stem_and_conv(): pl.pallas_call(functools.partial(stem_kernel, n, rows_dev, co), out_shape...  22.2 us
    ppermute x12, waiting for transfers between devices, swap(): return lax.ppermute(x, axis, [(i, i ^ bit) for i in range(size)])  19.3 us
    ppermute x12, starting transfers between devices, swap(): return lax.ppermute(x, axis, [(i, i ^ bit) for i in range(size)])  16.1 us
    pallas_call x1, Pallas kernels, first_part(): pl.pallas_call(functools.partial(first_kernel, n), out_shape=[jax.ShapeDt...  2.9 us
    pallas_call x1, Pallas kernels, middle_part(): pl.pallas_call(middle_kernel, out_shape=[jax.ShapeDtypeStruct((size, WIDE...  2.15 us
    unnamed x9, local copies, waits for them, and re-layouts  1.63 us
  transfers between devices with their start and end apart: 12, of which 9 were waited for; matrix products, arithmetic and copies ran while one was open for 3% of the time, Pallas kernels for 6%

profile of v14, /device:TPU:0, one launch (start us, length us, event | category | flops | bytes accessed | tf_op | source)
XLA Modules:
  0.0 70.8 jit_solution(13870367393265679604)
XLA Ops:
  0.6 0.0 copy-start
  0.6 0.7 %copy-done = s32[1,4096]{1,0:T(1,128)S(1)} copy-done((s32[1,4096]{1,0:T(1,128)S(1)}, s32[1,4096]{1,0:T(1,128)}, u32[]{:S(2)}) %copy-start) | copy-done | bytes 16408
  1.3 0.0 copy-start.2
  1.4 0.0 copy-start.3
  1.4 0.2 regroup.1
  1.6 3.0 %collective-permute-start = (bf16[1,16,256]{2,1,0:T(8,128)(2,1)S(1)}, bf16[1,16,256]{2,1,0:T(8,128)(2,1)S(1)}, u32[]{:S(2)}, u32[]{:S(2)}) collective-permute-start(bf16[1,16,256]{2,1,0:T(8,128)(2,1)S(1)} %bitcast.8), channel_id=1, source_target_pairs={{0,1},{1,0},{2,3},{3,2},{4,5},{5,4},{6,7},{7,6},{8,9},{9,8},{10,11... | collective-permute-start | bytes 24584 | tf_op jit(solution)/shard_map/ppermute | solution.py:37
  4.6 1.2 %broadcast_multiply_fusion.w_ref = bf16[96,3840]{1,0:T(8,128)(2,1)S(1)} fusion(bf16[96,3840]{1,0:T(8,128)(2,1)} %param.8), kind=kLoop, calls=%fused_computation.1 | loop fusion | flops 368640 | bytes 1474560 | tf_op jit(solution)/shard_map/mul | solution.py:483
  5.8 0.0 copy-start.1
  5.8 0.9 %copy.13 = bf16[15,4,768]{2,0,1:T(8,128)(2,1)S(1)} copy(bf16[15,4,768]{2,1,0:T(4,128)(2,1)} %param.7) | data formatting | bytes 184320 | tf_op args[1]
  6.8 0.2 copy.11
  6.9 0.0 collective-permute-done
  6.9 1.6 %collective-permute-start.1 = (bf16[2,16,256]{2,1,0:T(8,128)(2,1)S(1)}, bf16[2,16,256]{2,1,0:T(8,128)(2,1)S(1)}, u32[]{:S(2)}, u32[]{:S(2)}) collective-permute-start(bf16[2,16,256]{2,1,0:T(8,128)(2,1)S(1)} %pad_maximum_fusion.4), channel_id=1, source_target_pairs={{0,2},{1,3},{2,0},{3,1},{4,6},{5,7},{6,4},{7,5},{8,10},{9,11},{10,... | collective-permute-start | bytes 49160 | tf_op jit(solution)/shard_map/ppermute | solution.py:37
  8.6 2.1 %collective-permute-done.1 = bf16[2,16,256]{2,1,0:T(8,128)(2,1)S(1)} collective-permute-done((bf16[2,16,256]{2,1,0:T(8,128)(2,1)S(1)}, bf16[2,16,256]{2,1,0:T(8,128)(2,1)S(1)}, u32[]{:S(2)}, u32[]{:S(2)}) %collective-permute-start.1) | collective-permute-done | bytes 16416 | tf_op jit(solution)/shard_map/ppermute | solution.py:37
  10.8 2.6 %collective-permute-start.2 = (bf16[4,16,256]{2,1,0:T(8,128)(2,1)S(1)}, bf16[4,16,256]{2,1,0:T(8,128)(2,1)S(1)}, u32[]{:S(2)}, u32[]{:S(2)}) collective-permute-start(bf16[4,16,256]{2,1,0:T(8,128)(2,1)S(1)} %pad_maximum_fusion.2), channel_id=1, source_target_pairs={{0,4},{1,5},{2,6},{3,7},{4,0},{5,1},{6,2},{7,3},{8,12},{9,13},{10,... | collective-permute-start | bytes 98312 | tf_op jit(solution)/shard_map/ppermute | solution.py:37
  13.3 0.0 copy-done.2
  13.4 0.0 copy-done.3
  13.4 0.4 prepare.1
  13.9 1.7 %collective-permute-done.2 = bf16[4,16,256]{2,1,0:T(8,128)(2,1)S(1)} collective-permute-done((bf16[4,16,256]{2,1,0:T(8,128)(2,1)S(1)}, bf16[4,16,256]{2,1,0:T(8,128)(2,1)S(1)}, u32[]{:S(2)}, u32[]{:S(2)}) %collective-permute-start.2) | collective-permute-done | bytes 32800 | tf_op jit(solution)/shard_map/ppermute | solution.py:37
  15.6 0.0 copy-done.1
  15.6 22.2 %stem_and_conv.1 = (bf16[768,4096]{1,0:T(8,128)(2,1)S(1)}, f32[96,4096]{1,0:T(8,128)S(1)}, bf16[16,128]{1,0:T(8,128)(2,1)S(1)}) custom-call(bf16[8,16,256]{2,1,0:T(8,128)(2,1)S(1)} %pad_maximum_fusion.1.pay_ref, bf16[6144,128]{1,0:T(8,128)(2,1)S(1)} %get-tuple-element.15.table, bf16[480,768]{1,0:T(8,128)(2,1)S(1)} %get-tuple-element.16.weights, ...), custom_call_target="tpu_custom_call" | custom-call | tf_op jit(solution)/shard_map/stem_and_conv/pallas_call | solution.py:227
  37.8 1.3 %collective-permute-start.3 = (bf16[1,16,128]{2,1,0:T(8,128)(2,1)S(1)}, bf16[1,16,128]{2,1,0:T(8,128)(2,1)S(1)}, u32[]{:S(2)}, u32[]{:S(2)}) collective-permute-start(bf16[1,16,128]{2,1,0:T(8,128)(2,1)S(1)} %bitcast.12), channel_id=1, source_target_pairs={{0,1},{1,0},{2,3},{3,2},{4,5},{5,4},{6,7},{7,6},{8,9},{9,8},{10,11... | collective-permute-start | bytes 12296 | tf_op jit(solution)/shard_map/ppermute | solution.py:37
  39.0 2.4 %collective-permute-done.3 = bf16[1,16,128]{2,1,0:T(8,128)(2,1)S(1)} collective-permute-done((bf16[1,16,128]{2,1,0:T(8,128)(2,1)S(1)}, bf16[1,16,128]{2,1,0:T(8,128)(2,1)S(1)}, u32[]{:S(2)}, u32[]{:S(2)}) %collective-permute-start.3) | collective-permute-done | bytes 4128 | tf_op jit(solution)/shard_map/ppermute | solution.py:37
  41.4 1.6 %collective-permute-start.4 = (bf16[2,16,128]{2,1,0:T(8,128)(2,1)S(1)}, bf16[2,16,128]{2,1,0:T(8,128)(2,1)S(1)}, u32[]{:S(2)}, u32[]{:S(2)}) collective-permute-start(bf16[2,16,128]{2,1,0:T(8,128)(2,1)S(1)} %pad_maximum_fusion.6), channel_id=1, source_target_pairs={{0,2},{1,3},{2,0},{3,1},{4,6},{5,7},{6,4},{7,5},{8,10},{9,11},{10,... | collective-permute-start | bytes 24584 | tf_op jit(solution)/shard_map/ppermute | solution.py:37
  43.0 2.1 %collective-permute-done.4 = bf16[2,16,128]{2,1,0:T(8,128)(2,1)S(1)} collective-permute-done((bf16[2,16,128]{2,1,0:T(8,128)(2,1)S(1)}, bf16[2,16,128]{2,1,0:T(8,128)(2,1)S(1)}, u32[]{:S(2)}, u32[]{:S(2)}) %collective-permute-start.4) | collective-permute-done | bytes 8224 | tf_op jit(solution)/shard_map/ppermute | solution.py:37
  45.1 2.6 %collective-permute-start.5 = (bf16[4,16,128]{2,1,0:T(8,128)(2,1)S(1)}, bf16[4,16,128]{2,1,0:T(8,128)(2,1)S(1)}, u32[]{:S(2)}, u32[]{:S(2)}) collective-permute-start(bf16[4,16,128]{2,1,0:T(8,128)(2,1)S(1)} %pad_maximum_fusion.5), channel_id=1, source_target_pairs={{0,4},{1,5},{2,6},{3,7},{4,0},{5,1},{6,2},{7,3},{8,12},{9,13},{10,... | collective-permute-start | bytes 49160 | tf_op jit(solution)/shard_map/ppermute | solution.py:37
  47.7 2.0 %collective-permute-done.5 = bf16[4,16,128]{2,1,0:T(8,128)(2,1)S(1)} collective-permute-done((bf16[4,16,128]{2,1,0:T(8,128)(2,1)S(1)}, bf16[4,16,128]{2,1,0:T(8,128)(2,1)S(1)}, u32[]{:S(2)}, u32[]{:S(2)}) %collective-permute-start.5) | collective-permute-done | bytes 16416 | tf_op jit(solution)/shard_map/ppermute | solution.py:37
  49.7 2.9 %first_part.1 = (s16[48,2176]{1,0:T(8,128)(2,1)S(1)}, bf16[256,4096]{1,0:T(8,128)(2,1)S(1)}, bf16[256,4096]{1,0:T(8,128)(2,1)S(1)}, f32[2,48,256]{2,1,0:T(8,128)S(1)}) custom-call(bf16[8,16,128]{2,1,0:T(8,128)(2,1)S(1)} %pad_maximum_fusion.3.emb_ref, bf16[1024,256]{1,0:T(8,128)(2,1)S(1)} %get-tuple-element.18.proj_ref, ...), custom_call_target="tpu_custom_call" | custom-call | tf_op jit(solution)/shard_map/first_part/pallas_call | solution.py:380
  52.6 0.1 collective-permute-start.6
  52.7 2.2 %middle_part.1 = (f32[48,2048]{1,0:T(8,128)S(1)}, s16[48,2176]{1,0:T(8,128)(2,1)S(1)}) custom-call(bf16[256,4096]{1,0:T(8,128)(2,1)S(1)} %get-tuple-element.21.give_ref, bf16[256,4096]{1,0:T(8,128)(2,1)S(1)} %get-tuple-element.22.stay_ref, f32[2,48,256]{2,1,0:T(8,128)S(1)} %get-tuple-element.23.qk_ref, bf16[768,4096]{1,0:T(8,128)(2,1)S(1)} %get-tuple-element.20.pooled_ref), custom_call_target="tpu_custom_call" | custom-call | flops 1610612736 | bytes 12582912 | tf_op jit(solution)/shard_map/middle_part/pallas_call | solution.py:402
  54.9 0.6 collective-permute-start.9
  55.4 0.0 collective-permute-done.6.b_ref
  55.4 0.3 add_half.4.a_ref.after_ref
  55.7 1.6 %collective-permute-start.7 = (s16[48,2176]{1,0:T(8,128)(2,1)S(1)}, s16[48,2176]{1,0:T(8,128)(2,1)S(1)}, u32[]{:S(2)}, u32[]{:S(2)}) collective-permute-start(s16[48,2176]{1,0:T(8,128)(2,1)S(1)} %add_half.4.a_ref.after_ref), channel_id=1, source_target_pairs={{0,16},{8,24},{16,0},{24,8},{1,17},{9,25},{17,1},{25,9},{2,18},{10... | collective-permute-start | bytes 626696 | tf_op jit(solution)/shard_map/ppermute | solution.py:37
  57.3 1.1 %last_part.1.a_ref.after_ref = f32[48,2048]{1,0:T(8,128)S(1)} custom-call(bf16[256,4096]{1,0:T(8,128)(2,1)S(1)} %get-tuple-element.22.stay_ref, f32[2,48,256]{2,1,0:T(8,128)S(1)} %get-tuple-element.23.qk_ref, bf16[768,4096]{1,0:T(8,128)(2,1)S(1)} %get-tuple-element.20.pooled_ref, s16[48,2176]{1,0:T(8,128)(2,1)S(1)} %add_half.4.a_ref.after_ref), custom_call_target="tpu_custom_call" | custom-call | flops 805306368 | bytes 6291456 | tf_op jit(solution)/shard_map/last_part/pallas_call | solution.py:416
  58.3 0.0 collective-permute-done.9.b_ref
  58.4 0.3 add_half.6.a_ref
  58.7 0.6 collective-permute-start.10
  59.3 4.5 %collective-permute-done.7.b_ref = s16[48,2176]{1,0:T(8,128)(2,1)S(1)} collective-permute-done((s16[48,2176]{1,0:T(8,128)(2,1)S(1)}, s16[48,2176]{1,0:T(8,128)(2,1)S(1)}, u32[]{:S(2)}, u32[]{:S(2)}) %collective-permute-start.7) | collective-permute-done | bytes 208928 | tf_op jit(solution)/shard_map/ppermute | solution.py:37
  63.8 0.3 add_half.5.after_ref.refs_0_
  64.1 3.2 %collective-permute-done.10.b_ref = s16[48,2176]{1,0:T(8,128)(2,1)S(1)} collective-permute-done((s16[48,2176]{1,0:T(8,128)(2,1)S(1)}, s16[48,2176]{1,0:T(8,128)(2,1)S(1)}, u32[]{:S(2)}, u32[]{:S(2)}) %collective-permute-start.10) | collective-permute-done | bytes 208928 | tf_op jit(solution)/shard_map/ppermute | solution.py:37
  67.3 0.3 add_half.7.refs_2_
  67.7 0.1 collective-permute-start.11
  67.7 0.5 collective-permute-start.8
  68.2 0.9 %collective-permute-done.11.refs_3_ = s16[48,2176]{1,0:T(8,128)(2,1)S(1)} collective-permute-done((s16[48,2176]{1,0:T(8,128)(2,1)S(1)}, s16[48,2176]{1,0:T(8,128)(2,1)S(1)}, u32[]{:S(2)}, u32[]{:S(2)}) %collective-permute-start.11) | collective-permute-done | bytes 208928 | tf_op jit(solution)/shard_map/ppermute | solution.py:37
  69.2 0.3 collective-permute-done.8.refs_1_
  69.5 1.3 %join.1 = (f32[96,3840]{1,0:T(8,128)}, f32[96,128]{1,0:T(8,128)}, f32[96,128]{1,0:T(8,128)}) custom-call(s16[48,2176]{1,0:T(8,128)(2,1)S(1)} %add_half.5.after_ref.refs_0_, s16[48,2176]{1,0:T(8,128)(2,1)S(1)} %collective-permute-done.8.refs_1_, s16[48,2176]{1,0:T(8,128)(2,1)S(1)} %add_half.7.refs_2_, s16[48,2176]{1,0:T(8,128)(2,1)S(1)} %collective-permute-done.11.refs_3_), custom_call_target="tpu_custom_call" | custom-call | tf_op jit(solution)/shard_map/join/pallas_call | solution.py:460
  (9 shorter events, 0.1 us)
Async XLA Ops:
  0.6 0.7 %copy-start = (s32[1,4096]{1,0:T(1,128)S(1)}, s32[1,4096]{1,0:T(1,128)}, u32[]{:S(2)}) copy-start(s32[1,4096]{1,0:T(1,128)} %param.6) | copy-start | bytes 49156
  1.3 12.0 %copy-start.2 = (bf16[768,128]{1,0:T(8,128)(2,1)S(1)}, bf16[768,128]{1,0:T(8,128)(2,1)}, u32[]{:S(2)}) copy-start(bf16[768,128]{1,0:T(8,128)(2,1)} %param.10) | copy-start | bytes 589828
  1.4 12.0 %copy-start.3 = (bf16[768,128]{1,0:T(8,128)(2,1)S(1)}, bf16[768,128]{1,0:T(8,128)(2,1)}, u32[]{:S(2)}) copy-start(bf16[768,128]{1,0:T(8,128)(2,1)} %param.9) | copy-start | bytes 589828
  1.6 5.4 %collective-permute-start = (bf16[1,16,256]{2,1,0:T(8,128)(2,1)S(1)}, bf16[1,16,256]{2,1,0:T(8,128)(2,1)S(1)}, u32[]{:S(2)}, u32[]{:S(2)}) collective-permute-start(bf16[1,16,256]{2,1,0:T(8,128)(2,1)S(1)} %bitcast.8), channel_id=1, source_target_pairs={{0,1},{1,0},{2,3},{3,2},{4,5},{5,4},{6,7},{7,6},{8,9},{9,8},{10,11... | collective-permute-start | bytes 24584 | tf_op jit(solution)/shard_map/ppermute | solution.py:37
  5.8 9.8 %copy-start.1 = (f32[1,2,16]{2,1,0:T(2,128)S(1)}, f32[1,2,16]{2,1,0:T(2,128)}, u32[]{:S(2)}) copy-start(f32[1,2,16]{2,1,0:T(2,128)} %param.11) | copy-start | bytes 388
  6.9 3.8 %collective-permute-start.1 = (bf16[2,16,256]{2,1,0:T(8,128)(2,1)S(1)}, bf16[2,16,256]{2,1,0:T(8,128)(2,1)S(1)}, u32[]{:S(2)}, u32[]{:S(2)}) collective-permute-start(bf16[2,16,256]{2,1,0:T(8,128)(2,1)S(1)} %pad_maximum_fusion.4), channel_id=1, source_target_pairs={{0,2},{1,3},{2,0},{3,1},{4,6},{5,7},{6,4},{7,5},{8,10},{9,11},{10,... | collective-permute-start | bytes 49160 | tf_op jit(solution)/shard_map/ppermute | solution.py:37
  10.8 4.8 %collective-permute-start.2 = (bf16[4,16,256]{2,1,0:T(8,128)(2,1)S(1)}, bf16[4,16,256]{2,1,0:T(8,128)(2,1)S(1)}, u32[]{:S(2)}, u32[]{:S(2)}) collective-permute-start(bf16[4,16,256]{2,1,0:T(8,128)(2,1)S(1)} %pad_maximum_fusion.2), channel_id=1, source_target_pairs={{0,4},{1,5},{2,6},{3,7},{4,0},{5,1},{6,2},{7,3},{8,12},{9,13},{10,... | collective-permute-start | bytes 98312 | tf_op jit(solution)/shard_map/ppermute | solution.py:37
  37.8 3.6 %collective-permute-start.3 = (bf16[1,16,128]{2,1,0:T(8,128)(2,1)S(1)}, bf16[1,16,128]{2,1,0:T(8,128)(2,1)S(1)}, u32[]{:S(2)}, u32[]{:S(2)}) collective-permute-start(bf16[1,16,128]{2,1,0:T(8,128)(2,1)S(1)} %bitcast.12), channel_id=1, source_target_pairs={{0,1},{1,0},{2,3},{3,2},{4,5},{5,4},{6,7},{7,6},{8,9},{9,8},{10,11... | collective-permute-start | bytes 12296 | tf_op jit(solution)/shard_map/ppermute | solution.py:37
  41.4 3.7 %collective-permute-start.4 = (bf16[2,16,128]{2,1,0:T(8,128)(2,1)S(1)}, bf16[2,16,128]{2,1,0:T(8,128)(2,1)S(1)}, u32[]{:S(2)}, u32[]{:S(2)}) collective-permute-start(bf16[2,16,128]{2,1,0:T(8,128)(2,1)S(1)} %pad_maximum_fusion.6), channel_id=1, source_target_pairs={{0,2},{1,3},{2,0},{3,1},{4,6},{5,7},{6,4},{7,5},{8,10},{9,11},{10,... | collective-permute-start | bytes 24584 | tf_op jit(solution)/shard_map/ppermute | solution.py:37
  45.1 4.6 %collective-permute-start.5 = (bf16[4,16,128]{2,1,0:T(8,128)(2,1)S(1)}, bf16[4,16,128]{2,1,0:T(8,128)(2,1)S(1)}, u32[]{:S(2)}, u32[]{:S(2)}) collective-permute-start(bf16[4,16,128]{2,1,0:T(8,128)(2,1)S(1)} %pad_maximum_fusion.5), channel_id=1, source_target_pairs={{0,4},{1,5},{2,6},{3,7},{4,0},{5,1},{6,2},{7,3},{8,12},{9,13},{10,... | collective-permute-start | bytes 49160 | tf_op jit(solution)/shard_map/ppermute | solution.py:37
  52.6 2.8 %collective-permute-start.6 = (s16[48,2176]{1,0:T(8,128)(2,1)S(1)}, s16[48,2176]{1,0:T(8,128)(2,1)S(1)}, u32[]{:S(2)}, u32[]{:S(2)}) collective-permute-start(s16[48,2176]{1,0:T(8,128)(2,1)S(1)} %get-tuple-element.25), channel_id=1, source_target_pairs={{0,8},{8,0},{16,24},{24,16},{1,9},{9,1},{17,25},{25,17},{2,10},{10... | collective-permute-start | bytes 626696 | tf_op jit(solution)/shard_map/ppermute | solution.py:37
  54.9 3.5 %collective-permute-start.9 = (s16[48,2176]{1,0:T(8,128)(2,1)S(1)}, s16[48,2176]{1,0:T(8,128)(2,1)S(1)}, u32[]{:S(2)}, u32[]{:S(2)}) collective-permute-start(s16[48,2176]{1,0:T(8,128)(2,1)S(1)} %get-tuple-element.26), channel_id=1, source_target_pairs={{0,8},{8,0},{16,24},{24,16},{1,9},{9,1},{17,25},{25,17},{2,10},{10... | collective-permute-start | bytes 626696 | tf_op jit(solution)/shard_map/ppermute | solution.py:37
  55.7 8.1 %collective-permute-start.7 = (s16[48,2176]{1,0:T(8,128)(2,1)S(1)}, s16[48,2176]{1,0:T(8,128)(2,1)S(1)}, u32[]{:S(2)}, u32[]{:S(2)}) collective-permute-start(s16[48,2176]{1,0:T(8,128)(2,1)S(1)} %add_half.4.a_ref.after_ref), channel_id=1, source_target_pairs={{0,16},{8,24},{16,0},{24,8},{1,17},{9,25},{17,1},{25,9},{2,18},{10... | collective-permute-start | bytes 626696 | tf_op jit(solution)/shard_map/ppermute | solution.py:37
  58.7 8.7 %collective-permute-start.10 = (s16[48,2176]{1,0:T(8,128)(2,1)S(1)}, s16[48,2176]{1,0:T(8,128)(2,1)S(1)}, u32[]{:S(2)}, u32[]{:S(2)}) collective-permute-start(s16[48,2176]{1,0:T(8,128)(2,1)S(1)} %add_half.6.a_ref), channel_id=1, source_target_pairs={{0,16},{8,24},{16,0},{24,8},{1,17},{9,25},{17,1},{25,9},{2,18},{10... | collective-permute-start | bytes 626696 | tf_op jit(solution)/shard_map/ppermute | solution.py:37
  67.7 1.5 %collective-permute-start.11 = (s16[48,2176]{1,0:T(8,128)(2,1)S(1)}, s16[48,2176]{1,0:T(8,128)(2,1)S(1)}, u32[]{:S(2)}, u32[]{:S(2)}) collective-permute-start(s16[48,2176]{1,0:T(8,128)(2,1)S(1)} %add_half.7.refs_2_), channel_id=1, source_target_pairs={{0,8},{8,0},{16,24},{24,16},{1,9},{9,1},{17,25},{25,17},{2,10},{10... | collective-permute-start | bytes 626696 | tf_op jit(solution)/shard_map/ppermute | solution.py:37
  67.7 1.7 %collective-permute-start.8 = (s16[48,2176]{1,0:T(8,128)(2,1)S(1)}, s16[48,2176]{1,0:T(8,128)(2,1)S(1)}, u32[]{:S(2)}, u32[]{:S(2)}) collective-permute-start(s16[48,2176]{1,0:T(8,128)(2,1)S(1)} %add_half.5.after_ref.refs_0_), channel_id=1, source_target_pairs={{0,8},{8,0},{16,24},{24,16},{1,9},{9,1},{17,25},{25,17},{2,10},{10... | collective-permute-start | bytes 626696 | tf_op jit(solution)/shard_map/ppermute | solution.py:37

commit v15 on v14

--- a/solution.py
+++ b/solution.py
@@ -91,7 +91,7 @@
             first = (chunk * POOL + pos) * CHUNK
             table_ref[first : first + CHUNK, :] = shifted.astype(jnp.bfloat16)
     for tap in range(K1):
-        weights_ref[tap * co : (tap + 1) * co, :] = w_ref[:, tap * C0 : (tap + 1) * C0]
+        weights_ref[tap * co : (tap + 1) * co, :] = w_ref[:, tap * C0 : (tap + 1) * C0] * 0.5
     for slot in range(n):
         rows = slice(slot * co, (slot + 1) * co)
         proj_ref[slot * SLOT : slot * SLOT + co, :] = both_ref[rows, :]
@@ -480,7 +480,7 @@
     table, weights, proj = prepare(
         n,
         first_table,
-        conv_weight * jnp.bfloat16(0.5),
+        conv_weight,
         jnp.concatenate([query_weight, key_weight], axis=1),
     )
 

time: 71 us -> 70.6 us (level)
  waiting for transfers between devices: 19.3 us -> 16.9 us
  starting transfers between devices: 16.1 us -> 18.2 us
    ppermute x12, waiting for transfers between devices: 19.3 us -> 16.9 us  [swap(): return lax.ppermute(x, axis, [(i, i ^ bit) for i in range(size)])]
    ppermute x12, starting transfers between devices: 16.1 us -> 18.2 us  [swap(): return lax.ppermute(x, axis, [(i, i ^ bit) for i in range(size)])]
    mul x1 -> x0, other arithmetic: 1.18 us -> none  [body(): conv_weight * jnp.bfloat16(0.5)]
    concatenate x1, other arithmetic: 0.04 us -> 1.06 us  [body(): jnp.concatenate([query_weight, key_weight], axis=1)]
    unnamed x9 -> x7, local copies, waits for them, and re-layouts: 1.63 us -> 1.69 us
  transfers between devices with their start and end apart: 12 -> 12, of which waited for: 9 -> 10; matrix products, arithmetic and copies ran while one was open for 3% -> 3% of each run, Pallas kernels for 6% -> 6%
where the time goes in v15:
time: 70.6 us; the launch traced here: 70.4 us
  Pallas kernels  31.5 us (45%)
  starting transfers between devices  18.2 us (26%)
  waiting for transfers between devices  16.9 us (24%)
  local copies, waits for them, and re-layouts  1.89 us (3%)
  other arithmetic  1.13 us (2%)
  between operations  0.78 us (1%)
    pallas_call x1, Pallas kernels, stem_and_conv(): pl.pallas_call(functools.partial(stem_kernel, n, rows_dev, co), out_shape...  22.2 us
    ppermute x12, starting transfers between devices, swap(): return lax.ppermute(x, axis, [(i, i ^ bit) for i in range(size)])  18.2 us
    ppermute x12, waiting for transfers between devices, swap(): return lax.ppermute(x, axis, [(i, i ^ bit) for i in range(size)])  16.9 us
    pallas_call x1, Pallas kernels, first_part(): pl.pallas_call(functools.partial(first_kernel, n), out_shape=[jax.ShapeDt...  2.89 us
    pallas_call x1, Pallas kernels, middle_part(): pl.pallas_call(middle_kernel, out_shape=[jax.ShapeDtypeStruct((size, WIDE...  2.15 us
    unnamed x7, local copies, waits for them, and re-layouts  1.69 us
  transfers between devices with their start and end apart: 12, of which 10 were waited for; matrix products, arithmetic and copies ran while one was open for 3% of the time, Pallas kernels for 6%

profile of v15, /device:TPU:0, one launch (start us, length us, event | category | flops | bytes accessed | tf_op | source)
XLA Modules:
  0.0 70.4 jit_solution(1261509340738754346)
XLA Ops:
  0.6 0.0 copy-start
  0.6 0.0 copy-start.1
  0.7 0.8 %copy-done.1 = s32[1,4096]{1,0:T(1,128)S(1)} copy-done((s32[1,4096]{1,0:T(1,128)S(1)}, s32[1,4096]{1,0:T(1,128)}, u32[]{:S(2)}) %copy-start.1) | copy-done | bytes 16408
  1.4 0.0 copy-start.2
  1.4 0.2 regroup.1
  1.6 3.0 %collective-permute-start = (bf16[1,16,256]{2,1,0:T(8,128)(2,1)S(1)}, bf16[1,16,256]{2,1,0:T(8,128)(2,1)S(1)}, u32[]{:S(2)}, u32[]{:S(2)}) collective-permute-start(bf16[1,16,256]{2,1,0:T(8,128)(2,1)S(1)} %bitcast.8), channel_id=1, source_target_pairs={{0,1},{1,0},{2,3},{3,2},{4,5},{5,4},{6,7},{7,6},{8,9},{9,8},{10,11... | collective-permute-start | bytes 24584 | tf_op jit(solution)/shard_map/ppermute | solution.py:37
  4.7 0.9 %copy.13 = bf16[15,4,768]{2,0,1:T(8,128)(2,1)S(1)} copy(bf16[15,4,768]{2,1,0:T(4,128)(2,1)} %param.7) | data formatting | bytes 184320 | tf_op args[1]
  5.6 0.2 copy.11
  5.8 0.5 collective-permute-done
  6.3 2.1 %collective-permute-start.1 = (bf16[2,16,256]{2,1,0:T(8,128)(2,1)S(1)}, bf16[2,16,256]{2,1,0:T(8,128)(2,1)S(1)}, u32[]{:S(2)}, u32[]{:S(2)}) collective-permute-start(bf16[2,16,256]{2,1,0:T(8,128)(2,1)S(1)} %pad_maximum_fusion.4), channel_id=1, source_target_pairs={{0,2},{1,3},{2,0},{3,1},{4,6},{5,7},{6,4},{7,5},{8,10},{9,11},{10,... | collective-permute-start | bytes 49160 | tf_op jit(solution)/shard_map/ppermute | solution.py:37
  8.4 1.7 %collective-permute-done.1 = bf16[2,16,256]{2,1,0:T(8,128)(2,1)S(1)} collective-permute-done((bf16[2,16,256]{2,1,0:T(8,128)(2,1)S(1)}, bf16[2,16,256]{2,1,0:T(8,128)(2,1)S(1)}, u32[]{:S(2)}, u32[]{:S(2)}) %collective-permute-start.1) | collective-permute-done | bytes 16416 | tf_op jit(solution)/shard_map/ppermute | solution.py:37
  10.1 3.0 %collective-permute-start.2 = (bf16[4,16,256]{2,1,0:T(8,128)(2,1)S(1)}, bf16[4,16,256]{2,1,0:T(8,128)(2,1)S(1)}, u32[]{:S(2)}, u32[]{:S(2)}) collective-permute-start(bf16[4,16,256]{2,1,0:T(8,128)(2,1)S(1)} %pad_maximum_fusion.2), channel_id=1, source_target_pairs={{0,4},{1,5},{2,6},{3,7},{4,0},{5,1},{6,2},{7,3},{8,12},{9,13},{10,... | collective-permute-start | bytes 98312 | tf_op jit(solution)/shard_map/ppermute | solution.py:37
  13.2 1.1 %pad_maximum_fusion.both_ref = bf16[768,256]{1,0:T(8,128)(2,1)S(1)} fusion(bf16[768,128]{1,0:T(8,128)(2,1)} %param.10, bf16[768,128]{1,0:T(8,128)(2,1)} %param.9), kind=kLoop, calls=%fused_computation | loop fusion | flops 786432 | bytes 786432 | tf_op jit(solution)/shard_map/concatenate | solution.py:484
  14.2 0.0 copy-done
  14.2 0.4 prepare.1
  14.7 0.4 collective-permute-done.2
  15.1 0.0 copy-done.2
  15.1 22.2 %stem_and_conv.1 = (bf16[768,4096]{1,0:T(8,128)(2,1)S(1)}, f32[96,4096]{1,0:T(8,128)S(1)}, bf16[16,128]{1,0:T(8,128)(2,1)S(1)}) custom-call(bf16[8,16,256]{2,1,0:T(8,128)(2,1)S(1)} %pad_maximum_fusion.1.pay_ref, bf16[6144,128]{1,0:T(8,128)(2,1)S(1)} %get-tuple-element.15.table, bf16[480,768]{1,0:T(8,128)(2,1)S(1)} %get-tuple-element.16.weights, ...), custom_call_target="tpu_custom_call" | custom-call | tf_op jit(solution)/shard_map/stem_and_conv/pallas_call | solution.py:227
  37.3 1.9 %collective-permute-start.3 = (bf16[1,16,128]{2,1,0:T(8,128)(2,1)S(1)}, bf16[1,16,128]{2,1,0:T(8,128)(2,1)S(1)}, u32[]{:S(2)}, u32[]{:S(2)}) collective-permute-start(bf16[1,16,128]{2,1,0:T(8,128)(2,1)S(1)} %bitcast.12), channel_id=1, source_target_pairs={{0,1},{1,0},{2,3},{3,2},{4,5},{5,4},{6,7},{7,6},{8,9},{9,8},{10,11... | collective-permute-start | bytes 12296 | tf_op jit(solution)/shard_map/ppermute | solution.py:37
  39.2 1.8 %collective-permute-done.3 = bf16[1,16,128]{2,1,0:T(8,128)(2,1)S(1)} collective-permute-done((bf16[1,16,128]{2,1,0:T(8,128)(2,1)S(1)}, bf16[1,16,128]{2,1,0:T(8,128)(2,1)S(1)}, u32[]{:S(2)}, u32[]{:S(2)}) %collective-permute-start.3) | collective-permute-done | bytes 4128 | tf_op jit(solution)/shard_map/ppermute | solution.py:37
  40.9 1.9 %collective-permute-start.4 = (bf16[2,16,128]{2,1,0:T(8,128)(2,1)S(1)}, bf16[2,16,128]{2,1,0:T(8,128)(2,1)S(1)}, u32[]{:S(2)}, u32[]{:S(2)}) collective-permute-start(bf16[2,16,128]{2,1,0:T(8,128)(2,1)S(1)} %pad_maximum_fusion.6), channel_id=1, source_target_pairs={{0,2},{1,3},{2,0},{3,1},{4,6},{5,7},{6,4},{7,5},{8,10},{9,11},{10,... | collective-permute-start | bytes 24584 | tf_op jit(solution)/shard_map/ppermute | solution.py:37
  42.8 1.7 %collective-permute-done.4 = bf16[2,16,128]{2,1,0:T(8,128)(2,1)S(1)} collective-permute-done((bf16[2,16,128]{2,1,0:T(8,128)(2,1)S(1)}, bf16[2,16,128]{2,1,0:T(8,128)(2,1)S(1)}, u32[]{:S(2)}, u32[]{:S(2)}) %collective-permute-start.4) | collective-permute-done | bytes 8224 | tf_op jit(solution)/shard_map/ppermute | solution.py:37
  44.6 2.9 %collective-permute-start.5 = (bf16[4,16,128]{2,1,0:T(8,128)(2,1)S(1)}, bf16[4,16,128]{2,1,0:T(8,128)(2,1)S(1)}, u32[]{:S(2)}, u32[]{:S(2)}) collective-permute-start(bf16[4,16,128]{2,1,0:T(8,128)(2,1)S(1)} %pad_maximum_fusion.5), channel_id=1, source_target_pairs={{0,4},{1,5},{2,6},{3,7},{4,0},{5,1},{6,2},{7,3},{8,12},{9,13},{10,... | collective-permute-start | bytes 49160 | tf_op jit(solution)/shard_map/ppermute | solution.py:37
  47.5 1.7 %collective-permute-done.5 = bf16[4,16,128]{2,1,0:T(8,128)(2,1)S(1)} collective-permute-done((bf16[4,16,128]{2,1,0:T(8,128)(2,1)S(1)}, bf16[4,16,128]{2,1,0:T(8,128)(2,1)S(1)}, u32[]{:S(2)}, u32[]{:S(2)}) %collective-permute-start.5) | collective-permute-done | bytes 16416 | tf_op jit(solution)/shard_map/ppermute | solution.py:37
  49.2 2.9 %first_part.1 = (s16[48,2176]{1,0:T(8,128)(2,1)S(1)}, bf16[256,4096]{1,0:T(8,128)(2,1)S(1)}, bf16[256,4096]{1,0:T(8,128)(2,1)S(1)}, f32[2,48,256]{2,1,0:T(8,128)S(1)}) custom-call(bf16[8,16,128]{2,1,0:T(8,128)(2,1)S(1)} %pad_maximum_fusion.3.emb_ref, bf16[1024,256]{1,0:T(8,128)(2,1)S(1)} %get-tuple-element.18.proj_ref, ...), custom_call_target="tpu_custom_call" | custom-call | tf_op jit(solution)/shard_map/first_part/pallas_call | solution.py:380
  52.1 0.1 collective-permute-start.6
  52.2 2.2 %middle_part.1 = (f32[48,2048]{1,0:T(8,128)S(1)}, s16[48,2176]{1,0:T(8,128)(2,1)S(1)}) custom-call(bf16[256,4096]{1,0:T(8,128)(2,1)S(1)} %get-tuple-element.21.give_ref, bf16[256,4096]{1,0:T(8,128)(2,1)S(1)} %get-tuple-element.22.stay_ref, f32[2,48,256]{2,1,0:T(8,128)S(1)} %get-tuple-element.23.qk_ref, bf16[768,4096]{1,0:T(8,128)(2,1)S(1)} %get-tuple-element.20.pooled_ref), custom_call_target="tpu_custom_call" | custom-call | flops 1610612736 | bytes 12582912 | tf_op jit(solution)/shard_map/middle_part/pallas_call | solution.py:402
  54.4 0.6 collective-permute-start.9
  54.9 0.0 collective-permute-done.6.b_ref
  54.9 0.3 add_half.4.a_ref.after_ref
  55.2 1.9 %collective-permute-start.7 = (s16[48,2176]{1,0:T(8,128)(2,1)S(1)}, s16[48,2176]{1,0:T(8,128)(2,1)S(1)}, u32[]{:S(2)}, u32[]{:S(2)}) collective-permute-start(s16[48,2176]{1,0:T(8,128)(2,1)S(1)} %add_half.4.a_ref.after_ref), channel_id=1, source_target_pairs={{0,16},{8,24},{16,0},{24,8},{1,17},{9,25},{17,1},{25,9},{2,18},{10... | collective-permute-start | bytes 626696 | tf_op jit(solution)/shard_map/ppermute | solution.py:37
  57.1 1.1 %last_part.1.a_ref.after_ref = f32[48,2048]{1,0:T(8,128)S(1)} custom-call(bf16[256,4096]{1,0:T(8,128)(2,1)S(1)} %get-tuple-element.22.stay_ref, f32[2,48,256]{2,1,0:T(8,128)S(1)} %get-tuple-element.23.qk_ref, bf16[768,4096]{1,0:T(8,128)(2,1)S(1)} %get-tuple-element.20.pooled_ref, s16[48,2176]{1,0:T(8,128)(2,1)S(1)} %add_half.4.a_ref.after_ref), custom_call_target="tpu_custom_call" | custom-call | flops 805306368 | bytes 6291456 | tf_op jit(solution)/shard_map/last_part/pallas_call | solution.py:416
  58.2 0.0 collective-permute-done.9.b_ref
  58.2 0.3 add_half.6.a_ref
  58.5 0.3 collective-permute-start.10
  58.8 4.5 %collective-permute-done.7.b_ref = s16[48,2176]{1,0:T(8,128)(2,1)S(1)} collective-permute-done((s16[48,2176]{1,0:T(8,128)(2,1)S(1)}, s16[48,2176]{1,0:T(8,128)(2,1)S(1)}, u32[]{:S(2)}, u32[]{:S(2)}) %collective-permute-start.7) | collective-permute-done | bytes 208928 | tf_op jit(solution)/shard_map/ppermute | solution.py:37
  63.3 0.3 add_half.5.after_ref.refs_0_
  63.6 3.3 %collective-permute-done.10.b_ref = s16[48,2176]{1,0:T(8,128)(2,1)S(1)} collective-permute-done((s16[48,2176]{1,0:T(8,128)(2,1)S(1)}, s16[48,2176]{1,0:T(8,128)(2,1)S(1)}, u32[]{:S(2)}, u32[]{:S(2)}) %collective-permute-start.10) | collective-permute-done | bytes 208928 | tf_op jit(solution)/shard_map/ppermute | solution.py:37
  66.9 0.3 add_half.7.refs_2_
  67.3 0.1 collective-permute-start.11
  67.3 0.5 collective-permute-start.8
  67.8 0.9 %collective-permute-done.11.refs_3_ = s16[48,2176]{1,0:T(8,128)(2,1)S(1)} collective-permute-done((s16[48,2176]{1,0:T(8,128)(2,1)S(1)}, s16[48,2176]{1,0:T(8,128)(2,1)S(1)}, u32[]{:S(2)}, u32[]{:S(2)}) %collective-permute-start.11) | collective-permute-done | bytes 208928 | tf_op jit(solution)/shard_map/ppermute | solution.py:37
  68.8 0.3 collective-permute-done.8.refs_1_
  69.1 1.3 %join.1 = (f32[96,3840]{1,0:T(8,128)}, f32[96,128]{1,0:T(8,128)}, f32[96,128]{1,0:T(8,128)}) custom-call(s16[48,2176]{1,0:T(8,128)(2,1)S(1)} %add_half.5.after_ref.refs_0_, s16[48,2176]{1,0:T(8,128)(2,1)S(1)} %collective-permute-done.8.refs_1_, s16[48,2176]{1,0:T(8,128)(2,1)S(1)} %add_half.7.refs_2_, s16[48,2176]{1,0:T(8,128)(2,1)S(1)} %collective-permute-done.11.refs_3_), custom_call_target="tpu_custom_call" | custom-call | tf_op jit(solution)/shard_map/join/pallas_call | solution.py:460
  (8 shorter events, 0.1 us)
Async XLA Ops:
  0.6 13.6 %copy-start = (bf16[96,3840]{1,0:T(8,128)(2,1)S(1)}, bf16[96,3840]{1,0:T(8,128)(2,1)}, u32[]{:S(2)}) copy-start(bf16[96,3840]{1,0:T(8,128)(2,1)} %w_ref.1) | copy-start | bytes 2211844
  0.6 0.8 %copy-start.1 = (s32[1,4096]{1,0:T(1,128)S(1)}, s32[1,4096]{1,0:T(1,128)}, u32[]{:S(2)}) copy-start(s32[1,4096]{1,0:T(1,128)} %param.6) | copy-start | bytes 49156
  1.4 13.6 %copy-start.2 = (f32[1,2,16]{2,1,0:T(2,128)S(1)}, f32[1,2,16]{2,1,0:T(2,128)}, u32[]{:S(2)}) copy-start(f32[1,2,16]{2,1,0:T(2,128)} %param.11) | copy-start | bytes 388
  1.6 4.7 %collective-permute-start = (bf16[1,16,256]{2,1,0:T(8,128)(2,1)S(1)}, bf16[1,16,256]{2,1,0:T(8,128)(2,1)S(1)}, u32[]{:S(2)}, u32[]{:S(2)}) collective-permute-start(bf16[1,16,256]{2,1,0:T(8,128)(2,1)S(1)} %bitcast.8), channel_id=1, source_target_pairs={{0,1},{1,0},{2,3},{3,2},{4,5},{5,4},{6,7},{7,6},{8,9},{9,8},{10,11... | collective-permute-start | bytes 24584 | tf_op jit(solution)/shard_map/ppermute | solution.py:37
  6.3 3.8 %collective-permute-start.1 = (bf16[2,16,256]{2,1,0:T(8,128)(2,1)S(1)}, bf16[2,16,256]{2,1,0:T(8,128)(2,1)S(1)}, u32[]{:S(2)}, u32[]{:S(2)}) collective-permute-start(bf16[2,16,256]{2,1,0:T(8,128)(2,1)S(1)} %pad_maximum_fusion.4), channel_id=1, source_target_pairs={{0,2},{1,3},{2,0},{3,1},{4,6},{5,7},{6,4},{7,5},{8,10},{9,11},{10,... | collective-permute-start | bytes 49160 | tf_op jit(solution)/shard_map/ppermute | solution.py:37
  10.1 4.9 %collective-permute-start.2 = (bf16[4,16,256]{2,1,0:T(8,128)(2,1)S(1)}, bf16[4,16,256]{2,1,0:T(8,128)(2,1)S(1)}, u32[]{:S(2)}, u32[]{:S(2)}) collective-permute-start(bf16[4,16,256]{2,1,0:T(8,128)(2,1)S(1)} %pad_maximum_fusion.2), channel_id=1, source_target_pairs={{0,4},{1,5},{2,6},{3,7},{4,0},{5,1},{6,2},{7,3},{8,12},{9,13},{10,... | collective-permute-start | bytes 98312 | tf_op jit(solution)/shard_map/ppermute | solution.py:37
  37.3 3.6 %collective-permute-start.3 = (bf16[1,16,128]{2,1,0:T(8,128)(2,1)S(1)}, bf16[1,16,128]{2,1,0:T(8,128)(2,1)S(1)}, u32[]{:S(2)}, u32[]{:S(2)}) collective-permute-start(bf16[1,16,128]{2,1,0:T(8,128)(2,1)S(1)} %bitcast.12), channel_id=1, source_target_pairs={{0,1},{1,0},{2,3},{3,2},{4,5},{5,4},{6,7},{7,6},{8,9},{9,8},{10,11... | collective-permute-start | bytes 12296 | tf_op jit(solution)/shard_map/ppermute | solution.py:37
  40.9 3.7 %collective-permute-start.4 = (bf16[2,16,128]{2,1,0:T(8,128)(2,1)S(1)}, bf16[2,16,128]{2,1,0:T(8,128)(2,1)S(1)}, u32[]{:S(2)}, u32[]{:S(2)}) collective-permute-start(bf16[2,16,128]{2,1,0:T(8,128)(2,1)S(1)} %pad_maximum_fusion.6), channel_id=1, source_target_pairs={{0,2},{1,3},{2,0},{3,1},{4,6},{5,7},{6,4},{7,5},{8,10},{9,11},{10,... | collective-permute-start | bytes 24584 | tf_op jit(solution)/shard_map/ppermute | solution.py:37
  44.6 4.7 %collective-permute-start.5 = (bf16[4,16,128]{2,1,0:T(8,128)(2,1)S(1)}, bf16[4,16,128]{2,1,0:T(8,128)(2,1)S(1)}, u32[]{:S(2)}, u32[]{:S(2)}) collective-permute-start(bf16[4,16,128]{2,1,0:T(8,128)(2,1)S(1)} %pad_maximum_fusion.5), channel_id=1, source_target_pairs={{0,4},{1,5},{2,6},{3,7},{4,0},{5,1},{6,2},{7,3},{8,12},{9,13},{10,... | collective-permute-start | bytes 49160 | tf_op jit(solution)/shard_map/ppermute | solution.py:37
  52.1 2.8 %collective-permute-start.6 = (s16[48,2176]{1,0:T(8,128)(2,1)S(1)}, s16[48,2176]{1,0:T(8,128)(2,1)S(1)}, u32[]{:S(2)}, u32[]{:S(2)}) collective-permute-start(s16[48,2176]{1,0:T(8,128)(2,1)S(1)} %get-tuple-element.25), channel_id=1, source_target_pairs={{0,8},{8,0},{16,24},{24,16},{1,9},{9,1},{17,25},{25,17},{2,10},{10... | collective-permute-start | bytes 626696 | tf_op jit(solution)/shard_map/ppermute | solution.py:37
  54.4 3.8 %collective-permute-start.9 = (s16[48,2176]{1,0:T(8,128)(2,1)S(1)}, s16[48,2176]{1,0:T(8,128)(2,1)S(1)}, u32[]{:S(2)}, u32[]{:S(2)}) collective-permute-start(s16[48,2176]{1,0:T(8,128)(2,1)S(1)} %get-tuple-element.26), channel_id=1, source_target_pairs={{0,8},{8,0},{16,24},{24,16},{1,9},{9,1},{17,25},{25,17},{2,10},{10... | collective-permute-start | bytes 626696 | tf_op jit(solution)/shard_map/ppermute | solution.py:37
  55.2 8.1 %collective-permute-start.7 = (s16[48,2176]{1,0:T(8,128)(2,1)S(1)}, s16[48,2176]{1,0:T(8,128)(2,1)S(1)}, u32[]{:S(2)}, u32[]{:S(2)}) collective-permute-start(s16[48,2176]{1,0:T(8,128)(2,1)S(1)} %add_half.4.a_ref.after_ref), channel_id=1, source_target_pairs={{0,16},{8,24},{16,0},{24,8},{1,17},{9,25},{17,1},{25,9},{2,18},{10... | collective-permute-start | bytes 626696 | tf_op jit(solution)/shard_map/ppermute | solution.py:37
  58.5 8.4 %collective-permute-start.10 = (s16[48,2176]{1,0:T(8,128)(2,1)S(1)}, s16[48,2176]{1,0:T(8,128)(2,1)S(1)}, u32[]{:S(2)}, u32[]{:S(2)}) collective-permute-start(s16[48,2176]{1,0:T(8,128)(2,1)S(1)} %add_half.6.a_ref), channel_id=1, source_target_pairs={{0,16},{8,24},{16,0},{24,8},{1,17},{9,25},{17,1},{25,9},{2,18},{10... | collective-permute-start | bytes 626696 | tf_op jit(solution)/shard_map/ppermute | solution.py:37
  67.3 1.5 %collective-permute-start.11 = (s16[48,2176]{1,0:T(8,128)(2,1)S(1)}, s16[48,2176]{1,0:T(8,128)(2,1)S(1)}, u32[]{:S(2)}, u32[]{:S(2)}) collective-permute-start(s16[48,2176]{1,0:T(8,128)(2,1)S(1)} %add_half.7.refs_2_), channel_id=1, source_target_pairs={{0,8},{8,0},{16,24},{24,16},{1,9},{9,1},{17,25},{25,17},{2,10},{10... | collective-permute-start | bytes 626696 | tf_op jit(solution)/shard_map/ppermute | solution.py:37
  67.3 1.7 %collective-permute-start.8 = (s16[48,2176]{1,0:T(8,128)(2,1)S(1)}, s16[48,2176]{1,0:T(8,128)(2,1)S(1)}, u32[]{:S(2)}, u32[]{:S(2)}) collective-permute-start(s16[48,2176]{1,0:T(8,128)(2,1)S(1)} %add_half.5.after_ref.refs_0_), channel_id=1, source_target_pairs={{0,8},{8,0},{16,24},{24,16},{1,9},{9,1},{17,25},{25,17},{2,10},{10... | collective-permute-start | bytes 626696 | tf_op jit(solution)/shard_map/ppermute | solution.py:37
